TPU v7x, 32 devices: a whole 2x2x4 slice. The times are simulated.
32 devices in a mesh: brick: 4 (over y, core), grp: 8 (over z, x).
Axes of the slice: x: 2, y: 2, z: 4, core: 2. Of those that a mesh axis runs over, the one named last changes fastest.
Arguments:
- source: float32 [8, 4, 2, 32, 1024], P('grp', 'brick'), may hold values from -21 to 21
- uptake: float32 [8, 4, 2, 32, 1024], P('grp', 'brick'), may hold values from 0.00015 to 0.006
- conductance: float32 [8, 4, 6, 2, 32, 1024], P('grp', 'brick'), may hold values from 0 to 3, as said below
- occupancy: int32 [8, 2, 4], replicated, may hold values from 0 to 1, as said below
- assignment: int32 [4], replicated, may hold values from 0 to 3, as said below
Outputs:
- solution_field: float32 [8, 4, 2, 32, 1024], P('grp', 'brick')
- residual: float32 [8, 4, 2, 32, 1024], P('grp', 'brick')
Inputs may be any that keep to these rules, and one draw needn't show every extreme that they name: `occupancy`: 1 marks an occupied brick; in every draw one patch of some slab has all its bricks occupied. `assignment`: each patch is held by exactly one index of brick. `conductance`: equal at both ends of a bond: the value toward +x at a cell is the value toward -x at its +x neighbour, likewise for y and z, the lattice being read cyclically; values toward +z and -z are 0.3 or more.
All inputs are finite; a program needn't handle non-finite values.
Results may differ from a plain program's by a relative error of at most 0.0003.
Values sent between devices are 32-bit elements; how exact they have to be, the bound alone decides.
No kernel may reach another device: no remote copies, remote signals or barrier semaphores. Data moves between devices by JAX's collectives and lax.ppermute only.
A program may use at most 128 MiB of HBM per device.

v0:
```python
import jax
import jax.numpy as jnp
from jax import lax
from jax.sharding import PartitionSpec as P

BS = 32
PATCH_X = 1
PATCH_Y = 2
ITERS = 3


OMEGA = 0.6


def extended_2(block, sides, width):
    for axis, dim in sides:
        count = lax.axis_size(axis)
        forward = [(i, i + 1) for i in range(count - 1)]
        backward = [(target, source) for source, target in forward]
        low = lax.ppermute(
            lax.slice_in_dim(block, block.shape[dim] - width, None, axis=dim), axis, forward
        )
        high = lax.ppermute(lax.slice_in_dim(block, 0, width, axis=dim), axis, backward)
        block = jnp.concatenate([low, block, high], axis=dim)
    return block


def assemble(coarse_diag, couplings, strides):
    extent = coarse_diag.shape[0]
    matrix = jnp.diag(coarse_diag)
    for coupling, stride in zip(couplings, strides):
        banded = coupling[: extent - stride]
        matrix = matrix - jnp.diag(banded, stride) - jnp.diag(banded, -stride)
    return matrix


def pad_rows(block, capacity):
    return jnp.pad(block, ((0, capacity - block.shape[0]), (0, 0)))


def on_device(source, uptake, conductance, occupancy, assignment):
    face_size = BS * BS
    capacity = max(PATCH_X, PATCH_Y)
    slot_count = PATCH_X * PATCH_Y
    slab_index = lax.axis_index("grp")
    brick_index = lax.axis_index("brick")
    brick_count = lax.axis_size("brick")
    across = brick_count // 2
    peer_ids = jnp.arange(brick_count, dtype=jnp.int32)
    patch_index = assignment[brick_index]
    patch_row = patch_index // across
    patch_column = patch_index % across

    def owner_of(row_shift, column_shift):
        row_target = patch_row + row_shift
        column_target = patch_column + column_shift
        inside = (
            (row_target >= 0) & (row_target < 2) & (column_target >= 0) & (column_target < across)
        )
        holder = jnp.sum(jnp.where(assignment == row_target * across + column_target, peer_ids, 0))
        return jnp.where(inside, holder, -1)

    wanted = jnp.stack([owner_of(1, 0), owner_of(-1, 0), owner_of(0, 1), owner_of(0, -1)])
    padded = jnp.pad(occupancy, 1)
    window = lax.dynamic_slice(
        padded,
        (slab_index, patch_row * PATCH_X, patch_column * PATCH_Y),
        (3, PATCH_X + 2, PATCH_Y + 2),
    ).astype(jnp.float32)
    centre = window[1, 1:-1, 1:-1].reshape(slot_count)
    toward = [
        window[1, 2:, 1:-1],
        window[1, :-2, 1:-1],
        window[1, 1:-1, 2:],
        window[1, 1:-1, :-2],
        window[2, 1:-1, 1:-1],
        window[0, 1:-1, 1:-1],
    ]
    first_axis = lax.broadcasted_iota(jnp.int32, (1, BS, face_size), 1)
    flat_axis = lax.broadcasted_iota(jnp.int32, (1, BS, face_size), 2)
    second_axis = flat_axis // BS
    third_axis = flat_axis % BS
    cube_third = lax.broadcasted_iota(jnp.int32, (1, BS, BS, BS), 3)
    borders = [
        first_axis == BS - 1,
        first_axis == 0,
        second_axis == BS - 1,
        second_axis == 0,
        third_axis == BS - 1,
        third_axis == 0,
    ]
    bonds = conductance[0, 0]
    live_here = centre[:, None, None]
    effective = []
    for direction in range(6):
        neighbour_live = toward[direction].reshape(slot_count)[:, None, None]
        active = jnp.where(borders[direction], live_here * neighbour_live, live_here)
        effective.append(bonds[direction] * active)
    absorb = uptake[0, 0]
    diagonal = absorb
    for direction in range(6):
        diagonal = diagonal + effective[direction]

    def apply_operator(field):
        lower_x = field[:, 0, :]
        upper_x = field[:, BS - 1, :]
        lower_y = field[:, :, :BS].reshape(slot_count, face_size)
        upper_y = field[:, :, face_size - BS :].reshape(slot_count, face_size)
        cube = field.reshape(slot_count, BS, BS, BS)
        lower_z = cube[:, :, :, 0].reshape(slot_count, face_size)
        upper_z = cube[:, :, :, BS - 1].reshape(slot_count, face_size)
        grid_lower_x = lower_x.reshape(PATCH_X, PATCH_Y, face_size)
        grid_upper_x = upper_x.reshape(PATCH_X, PATCH_Y, face_size)
        grid_lower_y = lower_y.reshape(PATCH_X, PATCH_Y, face_size)
        grid_upper_y = upper_y.reshape(PATCH_X, PATCH_Y, face_size)
        outgoing_sides = jnp.stack(
            [
                pad_rows(grid_lower_x[0], capacity),
                pad_rows(grid_upper_x[PATCH_X - 1], capacity),
                pad_rows(grid_lower_y[:, 0], capacity),
                pad_rows(grid_upper_y[:, PATCH_Y - 1], capacity),
            ]
        )
        portion = lax.all_gather(outgoing_sides[None], "brick", axis=0, tiled=True)
        sources = jnp.arange(portion.shape[0], dtype=jnp.int32)
        matches = sources[:, None] == wanted[None, :]
        remote = jnp.zeros((4, capacity, face_size), jnp.float32) + jnp.sum(
            jnp.where(matches[:, :, None, None], portion, 0.0), axis=0
        )
        stacked = jnp.stack([lower_z, upper_z])
        extended = extended_2(stacked, (("grp", 0),), 1)
        from_below = extended[0].reshape(slot_count, BS, BS, 1)
        from_above = extended[3].reshape(slot_count, BS, BS, 1)
        beyond_xplus = jnp.concatenate(
            [grid_lower_x[1:], remote[0, :PATCH_Y][None]], axis=0
        ).reshape(slot_count, face_size)
        beyond_xminus = jnp.concatenate(
            [remote[1, :PATCH_Y][None], grid_upper_x[:-1]], axis=0
        ).reshape(slot_count, face_size)
        beyond_yplus = jnp.concatenate(
            [grid_lower_y[:, 1:], remote[2, :PATCH_X][:, None]], axis=1
        ).reshape(slot_count, BS, BS)
        beyond_yminus = jnp.concatenate(
            [remote[3, :PATCH_X][:, None], grid_upper_y[:, :-1]], axis=1
        ).reshape(slot_count, BS, BS)
        upper_neighbour = jnp.where(
            cube_third == BS - 1, from_above, jnp.roll(cube, -1, axis=3)
        ).reshape(slot_count, BS, face_size)
        lower_neighbour = jnp.where(cube_third == 0, from_below, jnp.roll(cube, 1, axis=3)).reshape(
            slot_count, BS, face_size
        )
        total = diagonal * field
        total = total - effective[0] * jnp.concatenate(
            [field[:, 1:, :], beyond_xplus[:, None, :]], axis=1
        )
        total = total - effective[1] * jnp.concatenate(
            [beyond_xminus[:, None, :], field[:, :-1, :]], axis=1
        )
        total = total - effective[2] * jnp.concatenate([field[:, :, BS:], beyond_yplus], axis=2)
        total = total - effective[3] * jnp.concatenate(
            [beyond_yminus, field[:, :, : face_size - BS]], axis=2
        )
        total = total - effective[4] * upper_neighbour
        total = total - effective[5] * lower_neighbour
        return total

    slot_ids = jnp.arange(slot_count)
    brick_first = slot_ids // PATCH_Y
    brick_second = slot_ids % PATCH_Y
    inside = [
        (brick_first < PATCH_X - 1).astype(jnp.float32),
        (brick_first > 0).astype(jnp.float32),
        (brick_second < PATCH_Y - 1).astype(jnp.float32),
        (brick_second > 0).astype(jnp.float32),
    ]
    face_sums = [
        jnp.sum(effective[0][:, BS - 1, :], axis=1),
        jnp.sum(effective[1][:, 0, :], axis=1),
        jnp.sum(effective[2][:, :, face_size - BS :], axis=(1, 2)),
        jnp.sum(effective[3][:, :, :BS], axis=(1, 2)),
        jnp.sum(effective[4].reshape(slot_count, BS, BS, BS)[:, :, :, BS - 1], axis=(1, 2)),
        jnp.sum(effective[5].reshape(slot_count, BS, BS, BS)[:, :, :, 0], axis=(1, 2)),
    ]
    coarse_diag = jnp.sum(absorb, axis=(1, 2))
    for direction in range(4):
        coarse_diag = coarse_diag + face_sums[direction] * inside[direction]
    coarse_diag = coarse_diag + face_sums[4] + face_sums[5]
    record = jnp.stack(
        [coarse_diag, face_sums[0] * inside[0], face_sums[2] * inside[2], face_sums[4]]
    )[None]
    gathered = lax.all_gather(record, "grp", axis=0, tiled=True)
    columns = jnp.transpose(gathered, (1, 0, 2)).reshape(4, -1)
    matrix = assemble(columns[0], (columns[1], columns[2], columns[3]), (PATCH_Y, 1, slot_count))
    factor = jnp.linalg.cholesky(matrix)

    def coarse_solve(residual_field):
        totals = jnp.sum(residual_field, axis=(1, 2))
        gathered_terms = lax.all_gather(totals[None], "grp", axis=0, tiled=True).reshape(-1, 1)
        middle = lax.linalg.triangular_solve(factor, gathered_terms, left_side=True, lower=True)
        result = lax.linalg.triangular_solve(
            factor, middle, left_side=True, lower=True, transpose_a=True
        )
        return lax.dynamic_slice_in_dim(result[:, 0], slab_index * slot_count, slot_count)

    def precondition(residual_field):
        smoothed = OMEGA * residual_field / diagonal
        smoothed = smoothed + OMEGA * (residual_field - apply_operator(smoothed)) / diagonal
        return smoothed + coarse_solve(residual_field)[:, None, None]

    forcing = source[0, 0] * live_here
    solution_field = jnp.zeros_like(forcing)
    residual = forcing

    def paired(first_terms, second_terms):
        return lax.psum((jnp.sum(first_terms), jnp.sum(second_terms)), ("brick", "grp"))

    smoothed = precondition(residual)
    mapped = apply_operator(smoothed)
    energy, curvature = paired(residual * smoothed, mapped * smoothed)
    step_size = energy / curvature
    search = smoothed
    mapped_search = mapped
    for iteration in range(ITERS):
        solution_field = solution_field + step_size * search
        residual = residual - step_size * mapped_search
        if iteration + 1 < ITERS:
            smoothed = precondition(residual)
            mapped = apply_operator(smoothed)
            renewed, curvature = paired(residual * smoothed, mapped * smoothed)
            growth = renewed / energy
            step_size = renewed / (curvature - growth * renewed / step_size)
            search = smoothed + growth * search
            mapped_search = mapped + growth * mapped_search
            energy = renewed
    return (solution_field[None, None], residual[None, None])


def solution(mesh):
    return jax.shard_map(
        on_device,
        mesh=mesh,
        in_specs=(
            P("grp", "brick", None, None, None),
            P("grp", "brick", None, None, None),
            P("grp", "brick", None, None, None, None),
            P(),
            P(),
        ),
        out_specs=(P("grp", "brick", None, None, None), P("grp", "brick", None, None, None)),
        check_vma=False,
    )
```

profile of v0, /device:TPU:0, one launch (start us, length us, event | category | flops | bytes accessed | tf_op | source)
XLA Modules:
  0.0 819.7 jit_solution(3065018746639250551)
XLA Ops:
  25.5 5.3 multiply_divide_fusion.2
  33.4 5.4 collective-permute-start.1
  49.6 5.4 all-gather
  64.5 21.9 %all-gather.10 = f32[8,4,2]{1,2,0:T(2,128)S(1)} all-gather(f32[1,4,2]{1,2,0:T(2,128)S(1)} %bitcast.622), channel_id=3, replica_groups=mesh['brick'=4,'grp'=8] {'grp'}, dimensions={0}, use_global_device_ids=true | all-gather | bytes 288 | tf_op jit(solution)/shard_map/all_gather | solution.py:191
  91.9 17.3 %all-reduce.18 = f32[16]{0:T(128)S(1)} all-reduce(f32[16]{0:T(128)S(1)} %dynamic-update-slice.3), channel_id=4, replica_groups=mesh['brick'=4,'grp'=8] {'grp'}, use_global_device_ids=true, to_apply=%add.18 | all-reduce | flops 16 | bytes 128 | tf_op jit(solution)/shard_map/triangular_solve/reshape.87 | solution.py:199
  137.5 8.8 %fusion.47 = (f32[2,32,32,32]{3,2,1,0:T(8,128)S(1)}, f32[2,32,32,32]{3,2,1,0:T(8,128)}, f32[2,32,32,32]{3,2,1,0:T(8,128)}) fusion(f32[2,32,32,32]{3,2,1,0:T(8,128)} %get-tuple-element.79, f32[2,32,32,32]{3,2,1,0:T(8,128)} %get-tuple-element.78, f32[2,32,32,32]{3,2,1,0:T(8,128)} %concatenate.659, f32[2,32,32,32]{3,2,1,0:T(8,128)} %concatenate.658, ...), kind=kLoop, calls=%fused_computation.88 | loop fusion | flops 2686976 | bytes 4538480 | tf_op jit(solution)/shard_map/add | solution.py:208
  146.3 2.4 concatenate.643
  148.7 2.4 concatenate.645
  153.2 2.4 broadcast_in_dim.696
  157.7 2.4 broadcast_in_dim.702
  170.9 5.4 all-gather.3
  188.4 4.5 collective-permute-start.3
  195.7 3.0 pad_maximum_fusion.2
  221.3 2.4 concatenate.726
  247.3 2.4 broadcast_in_dim.726
  249.7 3.8 multiply_reduce_fusion.3
  253.5 39.5 %all-reduce.23 = (f32[]{:T(128)}, f32[]{:T(128)}) all-reduce(f32[]{:T(128)} %get-tuple-element.23, f32[]{:T(128)} %get-tuple-element.22), channel_id=1, replica_groups=mesh['brick'=4,'grp'=8] {'brick','grp'}, use_global_device_ids=true, to_apply=%region_16.19 | all-reduce | flops 2 | bytes 16 | tf_op jit(solution)/shard_map/psum | solution.py:215
  304.5 6.1 all-gather.4
  320.3 8.3 %multiply_divide_fusion.1 = f32[2,32,32,32]{3,2,1,0:T(8,128)S(1)} fusion(f32[2,32,32,32]{3,2,1,0:T(8,128)} %squeeze.116, f32[2,32,32,32]{3,2,1,0:T(8,128)} %get-tuple-element.79, f32[2,32,32,32]{3,2,1,0:T(8,128)} %get-tuple-element.78, f32[2,32,32,32]{3,2,1,0:T(8,128)} %concatenate.691, f32[2,32,32,32]{3,2,1,0:T(8,128)} %concatenate.690, ...), kind=kLoop, calls=%fused_computation.76 | loop fusion | flops 2490368 | bytes 4276332 | tf_op jit(solution)/shard_map/div | solution.py:206
  334.5 2.4 broadcast_in_dim.761
  337.0 20.8 %all-reduce.19 = f32[16]{0:T(128)} all-reduce(f32[16]{0:T(128)} %dynamic-update-slice.4), channel_id=7, replica_groups=mesh['brick'=4,'grp'=8] {'grp'}, use_global_device_ids=true, to_apply=%add.19 | all-reduce | flops 16 | bytes 128 | tf_op jit(solution)/shard_map/triangular_solve/reshape.87 | solution.py:199
  374.7 4.0 fusion.95
  398.7 13.3 %fusion.46 = (f32[2,32,32,32]{3,2,1,0:T(8,128)}, f32[2,32,32,32]{3,2,1,0:T(8,128)}, f32[2,32,32,32]{3,2,1,0:T(8,128)}) fusion(f32[2,32,32,32]{3,2,1,0:T(8,128)} %get-tuple-element.79, f32[2,32,32,32]{3,2,1,0:T(8,128)} %get-tuple-element.78, f32[2,32,32,32]{3,2,1,0:T(8,128)} %concatenate.709, f32[2,32,32,32]{3,2,1,0:T(8,128)} %concatenate.708, ...), kind=kLoop, calls=%fused_computation.87 | loop fusion | flops 4063232 | bytes 6389876 | tf_op jit(solution)/shard_map/add | solution.py:208
  412.0 2.4 concatenate.693
  436.6 5.4 all-gather.6
  454.1 5.1 collective-permute-start.7
  462.0 3.0 pad_maximum_fusion.6
  489.9 2.4 concatenate.711
  505.1 2.4 broadcast_in_dim.760
  511.1 2.4 broadcast_in_dim.757
  513.5 3.8 multiply_reduce_fusion.1
  517.3 40.9 %all-reduce.22 = (f32[]{:T(128)}, f32[]{:T(128)}) all-reduce(f32[]{:T(128)} %get-tuple-element.21, f32[]{:T(128)} %get-tuple-element.20), channel_id=1, replica_groups=mesh['brick'=4,'grp'=8] {'brick','grp'}, use_global_device_ids=true, to_apply=%region_23.26 | all-reduce | flops 2 | bytes 16 | tf_op jit(solution)/shard_map/psum | solution.py:215
  572.7 12.4 %multiply_divide_fusion = f32[2,32,32,32]{3,2,1,0:T(8,128)S(1)} fusion(f32[]{:T(128)S(6)} %div.162, f32[2,32,32,32]{3,2,1,0:T(8,128)} %get-tuple-element.79, f32[2,32,32,32]{3,2,1,0:T(8,128)} %get-tuple-element.78, f32[2,32,32,32]{3,2,1,0:T(8,128)} %concatenate.755, f32[2,32,32,32]{3,2,1,0:T(8,128)} %concatenate.754, f32[2,31,32,32]{3,2,1,0:T(8,128)} %concatenate.752, ...), kind=kLoop, calls=%fused_computation.75 | loop fusion | flops 3997696 | bytes 6127732 | tf_op jit(solution)/shard_map/div | solution.py:206
  596.2 6.1 all-gather.7
  607.5 20.3 %all-reduce.20 = f32[16]{0:T(128)} all-reduce(f32[16]{0:T(128)} %dynamic-update-slice.5), channel_id=10, replica_groups=mesh['brick'=4,'grp'=8] {'grp'}, use_global_device_ids=true, to_apply=%add.20 | all-reduce | flops 16 | bytes 128 | tf_op jit(solution)/shard_map/triangular_solve/reshape.87 | solution.py:199
  646.9 2.4 broadcast_in_dim.780
  668.7 16.1 %fusion.45 = (f32[2,32,32,32]{3,2,1,0:T(8,128)}, f32[2,32,32,32]{3,2,1,0:T(8,128)}, f32[2,32,32,32]{3,2,1,0:T(8,128)}) fusion(f32[2,32,32,32]{3,2,1,0:T(8,128)} %get-tuple-element.79, f32[2,32,32,32]{3,2,1,0:T(8,128)} %get-tuple-element.78, f32[2,32,32,32]{3,2,1,0:T(8,128)} %concatenate.773, f32[2,32,32,32]{3,2,1,0:T(8,128)} %concatenate.772, ...), kind=kLoop, calls=%fused_computation.86 | loop fusion | flops 5570560 | bytes 8241276 | tf_op jit(solution)/shard_map/add | solution.py:208
  684.9 2.5 concatenate.757
  689.9 2.5 broadcast_in_dim.768
  693.7 2.4 broadcast_in_dim.771
  696.2 2.6 multiply_reduce_fusion
  703.7 5.4 all-gather.9
  717.5 4.5 collective-permute-start.11
  724.4 3.0 pad_maximum_fusion.11
  746.0 2.5 concatenate.819
  764.5 2.6 fusion.154
  767.1 41.2 %all-reduce.21 = (f32[]{:T(128)}, f32[]{:T(128)}) all-reduce(f32[]{:T(128)} %get-tuple-element.51, f32[]{:T(128)} %fusion.154), channel_id=1, replica_groups=mesh['brick'=4,'grp'=8] {'brick','grp'}, use_global_device_ids=true, to_apply=%region_30.33 | all-reduce | flops 2 | bytes 16 | tf_op jit(solution)/shard_map/psum | solution.py:215
  812.4 6.0 fusion.148
  (541 shorter events, 411.2 us)
Async XLA Ops:
  0.6 8.8 %copy-start.10 = (f32[1,1,2,32,1024]{4,3,2,1,0:T(8,128)S(1)}, f32[1,1,2,32,1024]{4,3,2,1,0:T(8,128)}, u32[]{:S(2)}) copy-start(f32[1,1,2,32,1024]{4,3,2,1,0:T(8,128)} %param.9) | copy-start | bytes 786436
  0.6 10.1 %copy-start = (f32[1,1,6,2,32,1024]{5,4,3,2,1,0:T(8,128)S(1)}, f32[1,1,6,2,32,1024]{5,4,3,2,1,0:T(8,128)}, u32[]{:S(2)}) copy-start(f32[1,1,6,2,32,1024]{5,4,3,2,1,0:T(8,128)} %param.11) | copy-start | bytes 4718596
  4.7 38.2 %copy-start.48 = (pred[32]{0:T(512)(128)(4,1)}, pred[32]{0:T(512)(128)(4,1)S(1)}, u32[]{:S(2)}) copy-start(pred[32]{0:T(512)(128)(4,1)S(1)} %get-tuple-element.280) | copy-start | bytes 100
  9.4 16.0 %copy-start.2 = (f32[2,32,32,32]{3,2,1,0:T(8,128)}, f32[2,32,32,32]{3,2,1,0:T(8,128)S(1)}, u32[]{:S(2)}) copy-start(f32[2,32,32,32]{3,2,1,0:T(8,128)S(1)} %squeeze.117) | copy-start | bytes 786436
  24.4 6.4 copy-start.27
  25.4 17.4 %copy-start.54 = (f32[2]{0:T(128)}, f32[2]{0:T(128)S(1)}, u32[]{:S(2)}) copy-start(f32[2]{0:T(128)S(1)} %get-tuple-element.270) | copy-start | bytes 28
  30.8 12.1 %copy-start.25 = (f32[1,1,2,32,1024]{4,3,2,1,0:T(8,128)S(1)}, f32[1,1,2,32,1024]{4,3,2,1,0:T(8,128)}, u32[]{:S(2)}) copy-start(f32[1,1,2,32,1024]{4,3,2,1,0:T(8,128)} %param.10) | copy-start | bytes 786436
  30.9 12.0 %copy-start.56 = (f32[2]{0:T(128)S(1)}, f32[2]{0:T(128)}, u32[]{:S(2)}) copy-start(f32[2]{0:T(128)} %copy-done.55) | copy-start | bytes 28
  30.9 12.0 %copy-start.58 = (f32[2]{0:T(128)S(1)}, f32[2]{0:T(128)}, u32[]{:S(2)}) copy-start(f32[2]{0:T(128)} %copy-done.57) | copy-start | bytes 28
  30.9 12.0 %copy-start.61 = (f32[2]{0:T(128)S(1)}, f32[2]{0:T(128)}, u32[]{:S(2)}) copy-start(f32[2]{0:T(128)} %copy-done.60) | copy-start | bytes 28
  30.9 12.0 %copy-start.63 = (f32[2]{0:T(128)S(1)}, f32[2]{0:T(128)}, u32[]{:S(2)}) copy-start(f32[2]{0:T(128)} %copy-done.62) | copy-start | bytes 28
  30.9 12.0 %copy-start.65 = (f32[2]{0:T(128)S(1)}, f32[2]{0:T(128)}, u32[]{:S(2)}) copy-start(f32[2]{0:T(128)} %copy-done.64) | copy-start | bytes 28
  33.4 102.7 %collective-permute-start.1 = (f32[1,2,1024]{2,1,0:T(2,128)}, f32[1,2,1024]{2,1,0:T(2,128)}, u32[]{:S(2)}, u32[]{:S(2)}) collective-permute-start(f32[1,2,1024]{2,1,0:T(2,128)} %stack_reshape_squeeze.37), channel_id=1, source_target_pairs={{0,1},{1,2},{2,3},{3,4},{4,5},{5,6},{6,7},{8,9},{9,10},{10,11},{11... | collective-permute-start | bytes 24584 | tf_op jit(solution)/shard_map/ppermute | solution.py:20
  39.6 95.2 %collective-permute-start = (f32[1,2,1024]{2,1,0:T(2,128)}, f32[1,2,1024]{2,1,0:T(2,128)}, u32[]{:S(2)}, u32[]{:S(2)}) collective-permute-start(f32[1,2,1024]{2,1,0:T(2,128)} %stack_reshape_squeeze.36), channel_id=1, source_target_pairs={{1,0},{2,1},{3,2},{4,3},{5,4},{6,5},{7,6},{9,8},{10,9},{11,10},{12... | collective-permute-start | bytes 24584 | tf_op jit(solution)/shard_map/ppermute | solution.py:23
  48.1 7.7 copy-start.68
  48.9 9.7 %copy-start.22 = (f32[2,32,1024]{2,1,0:T(8,128)S(1)}, f32[2,32,1024]{2,1,0:T(8,128)}, u32[]{:S(2)}) copy-start(f32[2,32,1024]{2,1,0:T(8,128)} %copy-done.21) | copy-start | bytes 786436
  56.4 7.3 copy-start.3
  64.1 23.2 %copy-start.9 = (f32[2,32,32,32]{3,2,1,0:T(8,128)S(1)}, f32[2,32,32,32]{3,2,1,0:T(8,128)}, u32[]{:S(2)}) copy-start(f32[2,32,32,32]{3,2,1,0:T(8,128)} %copy-done.8) | copy-start | bytes 786436
  89.0 39.7 %copy-start.49 = (pred[32]{0:T(512)(128)(4,1)S(1)}, pred[32]{0:T(512)(128)(4,1)}, u32[]{:S(2)}) copy-start(pred[32]{0:T(512)(128)(4,1)} %copy-done.48) | copy-start | bytes 100
  109.9 22.1 %copy-start.42 = (f32[2,32,32]{2,1,0:T(8,128)}, f32[2,32,32]{2,1,0:T(8,128)S(1)}, u32[]{:S(2)}) copy-start(f32[2,32,32]{2,1,0:T(8,128)S(1)} %reshape.2206) | copy-start | bytes 24580
  110.7 21.3 %copy-start.43 = (f32[2,32,32]{2,1,0:T(8,128)}, f32[2,32,32]{2,1,0:T(8,128)S(1)}, u32[]{:S(2)}) copy-start(f32[2,32,32]{2,1,0:T(8,128)S(1)} %reshape.2205) | copy-start | bytes 24580
  119.6 12.5 %copy-start.35 = (f32[2,31,1024]{2,1,0:T(8,128)S(1)}, f32[2,31,1024]{2,1,0:T(8,128)}, u32[]{:S(2)}) copy-start(f32[2,31,1024]{2,1,0:T(8,128)} %get-tuple-element.144) | copy-start | bytes 761860
  168.7 11.7 %copy-start.17 = (f32[2,32,1024]{2,1,0:T(8,128)S(1)}, f32[2,32,1024]{2,1,0:T(8,128)}, u32[]{:S(2)}) copy-start(f32[2,32,1024]{2,1,0:T(8,128)} %copy-done.16) | copy-start | bytes 786436
  188.4 47.1 %collective-permute-start.3 = (f32[1,2,1024]{2,1,0:T(2,128)}, f32[1,2,1024]{2,1,0:T(2,128)}, u32[]{:S(2)}, u32[]{:S(2)}) collective-permute-start(f32[1,2,1024]{2,1,0:T(2,128)} %stack_reshape_squeeze.39), channel_id=1, source_target_pairs={{0,1},{1,2},{2,3},{3,4},{4,5},{5,6},{6,7},{8,9},{9,10},{10,11},{11... | collective-permute-start | bytes 24584 | tf_op jit(solution)/shard_map/ppermute | solution.py:20
  192.9 50.9 %collective-permute-start.2 = (f32[1,2,1024]{2,1,0:T(2,128)}, f32[1,2,1024]{2,1,0:T(2,128)}, u32[]{:S(2)}, u32[]{:S(2)}) collective-permute-start(f32[1,2,1024]{2,1,0:T(2,128)} %stack_reshape_squeeze.38), channel_id=1, source_target_pairs={{1,0},{2,1},{3,2},{4,3},{5,4},{6,5},{7,6},{9,8},{10,9},{11,10},{12... | collective-permute-start | bytes 24584 | tf_op jit(solution)/shard_map/ppermute | solution.py:23
  302.3 12.4 %copy-start.24 = (f32[2,32,1024]{2,1,0:T(8,128)S(1)}, f32[2,32,1024]{2,1,0:T(8,128)}, u32[]{:S(2)}) copy-start(f32[2,32,1024]{2,1,0:T(8,128)} %copy-done.23) | copy-start | bytes 786436
  367.5 29.8 %collective-permute-start.5 = (f32[1,2,1024]{2,1,0:T(2,128)}, f32[1,2,1024]{2,1,0:T(2,128)}, u32[]{:S(2)}, u32[]{:S(2)}) collective-permute-start(f32[1,2,1024]{2,1,0:T(2,128)} %stack_reshape_squeeze.41), channel_id=1, source_target_pairs={{0,1},{1,2},{2,3},{3,4},{4,5},{5,6},{6,7},{8,9},{9,10},{10,11},{11... | collective-permute-start | bytes 24584 | tf_op jit(solution)/shard_map/ppermute | solution.py:20
  369.4 26.5 %collective-permute-start.4 = (f32[1,2,1024]{2,1,0:T(2,128)}, f32[1,2,1024]{2,1,0:T(2,128)}, u32[]{:S(2)}, u32[]{:S(2)}) collective-permute-start(f32[1,2,1024]{2,1,0:T(2,128)} %stack_reshape_squeeze.40), channel_id=1, source_target_pairs={{1,0},{2,1},{3,2},{4,3},{5,4},{6,5},{7,6},{9,8},{10,9},{11,10},{12... | collective-permute-start | bytes 24584 | tf_op jit(solution)/shard_map/ppermute | solution.py:23
  434.4 11.9 %copy-start.19 = (f32[2,32,1024]{2,1,0:T(8,128)S(1)}, f32[2,32,1024]{2,1,0:T(8,128)}, u32[]{:S(2)}) copy-start(f32[2,32,1024]{2,1,0:T(8,128)} %copy-done.18) | copy-start | bytes 786436
  454.1 47.6 %collective-permute-start.7 = (f32[1,2,1024]{2,1,0:T(2,128)}, f32[1,2,1024]{2,1,0:T(2,128)}, u32[]{:S(2)}, u32[]{:S(2)}) collective-permute-start(f32[1,2,1024]{2,1,0:T(2,128)} %stack_reshape_squeeze.43), channel_id=1, source_target_pairs={{0,1},{1,2},{2,3},{3,4},{4,5},{5,6},{6,7},{8,9},{9,10},{10,11},{11... | collective-permute-start | bytes 24584 | tf_op jit(solution)/shard_map/ppermute | solution.py:20
  459.2 48.3 %collective-permute-start.6 = (f32[1,2,1024]{2,1,0:T(2,128)}, f32[1,2,1024]{2,1,0:T(2,128)}, u32[]{:S(2)}, u32[]{:S(2)}) collective-permute-start(f32[1,2,1024]{2,1,0:T(2,128)} %stack_reshape_squeeze.42), channel_id=1, source_target_pairs={{1,0},{2,1},{3,2},{4,3},{5,4},{6,5},{7,6},{9,8},{10,9},{11,10},{12... | collective-permute-start | bytes 24584 | tf_op jit(solution)/shard_map/ppermute | solution.py:23
  636.2 31.1 %collective-permute-start.9 = (f32[1,2,1024]{2,1,0:T(2,128)}, f32[1,2,1024]{2,1,0:T(2,128)}, u32[]{:S(2)}, u32[]{:S(2)}) collective-permute-start(f32[1,2,1024]{2,1,0:T(2,128)} %stack_reshape_squeeze.45), channel_id=1, source_target_pairs={{0,1},{1,2},{2,3},{3,4},{4,5},{5,6},{6,7},{8,9},{9,10},{10,11},{11... | collective-permute-start | bytes 24584 | tf_op jit(solution)/shard_map/ppermute | solution.py:20
  638.1 27.8 %collective-permute-start.8 = (f32[1,2,1024]{2,1,0:T(2,128)}, f32[1,2,1024]{2,1,0:T(2,128)}, u32[]{:S(2)}, u32[]{:S(2)}) collective-permute-start(f32[1,2,1024]{2,1,0:T(2,128)} %stack_reshape_squeeze.44), channel_id=1, source_target_pairs={{1,0},{2,1},{3,2},{4,3},{5,4},{6,5},{7,6},{9,8},{10,9},{11,10},{12... | collective-permute-start | bytes 24584 | tf_op jit(solution)/shard_map/ppermute | solution.py:23
  661.4 7.3 copy-start.50
  661.4 7.3 copy-start.59
  689.9 6.3 copy-start.13
  689.9 6.3 copy-start.14
  689.9 6.3 copy-start.15
  689.9 6.3 copy-start.31
  689.9 6.3 copy-start.33
  689.9 6.3 copy-start.44
  689.9 6.3 copy-start.45
  689.9 6.3 copy-start.52
  717.5 34.6 %collective-permute-start.11 = (f32[1,2,1024]{2,1,0:T(2,128)S(1)}, f32[1,2,1024]{2,1,0:T(2,128)S(1)}, u32[]{:S(2)}, u32[]{:S(2)}) collective-permute-start(f32[1,2,1024]{2,1,0:T(2,128)S(1)} %stack_reshape_squeeze.47), channel_id=1, source_target_pairs={{0,1},{1,2},{2,3},{3,4},{4,5},{5,6},{6,7},{8,9},{9,10},{10,11},{11... | collective-permute-start | bytes 24584 | tf_op jit(solution)/shard_map/ppermute | solution.py:20
  722.1 36.2 %collective-permute-start.10 = (f32[1,2,1024]{2,1,0:T(2,128)}, f32[1,2,1024]{2,1,0:T(2,128)S(1)}, u32[]{:S(2)}, u32[]{:S(2)}) collective-permute-start(f32[1,2,1024]{2,1,0:T(2,128)} %stack_reshape_squeeze.46), channel_id=1, source_target_pairs={{1,0},{2,1},{3,2},{4,3},{5,4},{6,5},{7,6},{9,8},{10,9},{11,10},{12... | collective-permute-start | bytes 24584 | tf_op jit(solution)/shard_map/ppermute | solution.py:23
  764.5 47.8 %copy-start.39 = (pred[32,1024]{1,0:T(8,128)(4,1)S(1)}, pred[32,1024]{1,0:T(8,128)(4,1)}, u32[]{:S(2)}) copy-start(pred[32,1024]{1,0:T(8,128)(4,1)} %copy-done.38) | copy-start | bytes 98308
  764.5 47.8 %copy-start.41 = (pred[32,1024]{1,0:T(8,128)(4,1)S(1)}, pred[32,1024]{1,0:T(8,128)(4,1)}, u32[]{:S(2)}) copy-start(pred[32,1024]{1,0:T(8,128)(4,1)} %copy-done.40) | copy-start | bytes 98308
  812.4 6.1 copy-start.37
  (47 other events, 129.3 us)
where the time goes:
time: 835 us; the launch traced here: 820 us
  local copies, waits for them, and re-layouts  375 us (45%)
  blocking collectives  236 us (28%)
  other arithmetic  155 us (19%)
  starting transfers between devices  32.4 us (4%)
  between operations  18.2 us (2%)
    psum x3, blocking collectives, paired(): lax.psum((jnp.sum(first_terms), jnp.sum(second_terms)), ('brick', 'grp'))  122 us
    another operation x3, blocking collectives, coarse_solve(): lax.linalg.triangular_solve(factor, gathered_terms, left_side=True, lower...  58.5 us
    broadcast_in_dim x26, local copies, waits for them, and re-layouts, apply_operator(): jnp.where(cube_third == BS - 1, from_above, jnp.roll(cube, -1, axis=3))  47.8 us
    broadcast_in_dim x26, local copies, waits for them, and re-layouts, apply_operator(): jnp.where(cube_third == 0, from_below, jnp.roll(cube, 1, axis=3))  47.6 us
    add x5, other arithmetic, precondition(): return smoothed + coarse_solve(residual_field)[:, None, None]  42.9 us
    all_gather x6, blocking collectives, apply_operator(): portion = lax.all_gather(outgoing_sides[None], 'brick', axis=0, tiled=True)  33.8 us
    concatenate x12, local copies, waits for them, and re-layouts, apply_operator(): jnp.roll(cube, -1, axis=3)  29.1 us
    concatenate x12, local copies, waits for them, and re-layouts, apply_operator(): jnp.roll(cube, 1, axis=3)  27.8 us
  transfers between devices with their start and end apart: 12, of which 0 were waited for; matrix products, arithmetic and copies ran while one was open for 28% of the time, Pallas kernels for 0%

commit v1 on v0

v1 whole, which is shorter than its diff:
```python
import functools

import jax
import jax.numpy as jnp
from jax import lax
from jax.experimental import pallas as pl
from jax.experimental.pallas import tpu as pltpu
from jax.sharding import PartitionSpec as P

BS = 32
CHUNKS = 16
OMEGA = 0.6
ITERS = 3
F32 = jnp.float32
FIELD = (CHUNKS, BS, 128)

XY_X1, XY_XP, XY_Y, XY_S = 0, 16, 32, 64
XY_ROWS = 72
XY_XD, XY_YC, XY_K = 72, 88, 120
XY_ROWS_FIRST = 128
Z_Y1, Z_Q, Z_Y, Z_X = 0, 32, 64, 96
Z_ROWS = 104
Z_D = 104
Z_ROWS_FIRST = 136
H_X1, H_XP, H_Y, H_Z1, H_ZQ, H_YZ, H_R = 0, 16, 32, 64, 96, 128, 160
H_ROWS = 168
C_XD, C_YC, C_ZD, C_K = 0, 16, 48, 80
C_ROWS = 88
E_XP, E_XM, E_YP, E_YM = 0, 16, 32, 64
E_ROWS = 96


def roll(block, shift):
    return pltpu.roll(block, shift % 128, axis=1)


def roll_row(row, shift):
    return pltpu.roll(jnp.broadcast_to(row, (8, 128)), shift % 128, axis=1)[0:1]


def lanes(rows=BS):
    return lax.broadcasted_iota(jnp.int32, (rows, 128), 1)


def rows_of(height=BS):
    return lax.broadcasted_iota(jnp.int32, (height, 128), 0)


def pack(chunks):
    height = chunks[0].shape[0]
    pair = (lanes(height) % BS) // 2
    total = jnp.zeros((height, 128), F32)
    for c in range(CHUNKS):
        moved = roll(chunks[c], 2 * c - 31) if height > 1 else roll_row(chunks[c], 2 * c - 31)
        total = jnp.where(pair == c, moved, total)
    return total


def stencil(field, effective, diagonal, x_halo, y_low, y_high, z_halo):
    lane = lanes()
    height = rows_of()
    depth = lane % BS
    zero = jnp.zeros((BS, 128), F32)
    back = [roll(f, -32) for f in field]
    forth = [roll(f, 32) for f in field]
    out = []
    for c in range(CHUNKS):
        f = field[c]
        x_row = zero if x_halo is None else x_halo[c : c + 1]
        total = diagonal(c) * f
        total -= effective(0, c) * jnp.where(height == BS - 1, x_row, pltpu.roll(f, BS - 1, axis=0))
        total -= effective(1, c) * jnp.where(height == 0, x_row, pltpu.roll(f, 1, axis=0))
        following = back[c + 1] if c < CHUNKS - 1 else (zero if y_high is None else y_high)
        previous = forth[c - 1] if c > 0 else (zero if y_low is None else y_low)
        total -= effective(2, c) * jnp.where(lane < 96, back[c], following)
        total -= effective(3, c) * jnp.where(lane >= 32, forth[c], previous)
        ends = zero if z_halo is None else roll(z_halo, 31 - 2 * c)
        total -= effective(4, c) * jnp.where(depth == BS - 1, ends, roll(f, -1))
        total -= effective(5, c) * jnp.where(depth == 0, ends, roll(f, 1))
        out.append(total)
    return out


def total_of(blocks):
    acc = blocks[0]
    for block in blocks[1:]:
        acc = acc + block
    return jnp.sum(jnp.sum(acc, axis=0, keepdims=True), axis=1, keepdims=True)


def facing(block, row):
    return jnp.where(row == 0, block[BS - 1 : BS], block[0:1])


def side_blocks(low_first, high_first, low_second, high_second):
    group = lanes() // 32
    return jnp.where(
        group == 0,
        low_first,
        jnp.where(
            group == 1,
            roll(high_first, 64),
            jnp.where(group == 2, roll(low_second, 64), high_second),
        ),
    )


def write_xy(xy_ref, row, y1, partial):
    for c in range(CHUNKS):
        xy_ref[XY_X1 + c : XY_X1 + c + 1] = facing(y1[c], row)
        xy_ref[XY_XP + c : XY_XP + c + 1] = facing(partial[c], row)
    last = CHUNKS - 1
    xy_ref[XY_Y : XY_Y + BS] = side_blocks(y1[0], y1[last], partial[0], partial[last])


def write_scalars(ref, start, values):
    for i, value in enumerate(values):
        ref[start + i : start + i + 1] = jnp.broadcast_to(value, (1, 128))
    for i in range(len(values), 8):
        ref[start + i : start + i + 1] = jnp.zeros((1, 128), F32)


def locate(bricks, place_ref, assignment_ref):
    across = bricks // 2
    place = place_ref[0]
    slab = place // bricks
    patch = assignment_ref[place % bricks]
    row = patch // across
    column = patch % across
    return slab, patch, row, column


def setup_kernel(
    slabs, bricks, place_ref, assignment_ref, occupancy_ref, source_ref, uptake_ref, conductance_ref,
    info_ref, effective_ref, diagonal_ref, relax_ref, residual_ref, partial_ref, edge_ref, xy_ref,
):
    across = bricks // 2
    slab, patch, row, column = locate(bricks, place_ref, assignment_ref)

    def holder(row_target, column_target):
        inside = (column_target >= 0) & (column_target < across)
        wanted = jnp.where(inside, row_target * across + column_target, patch)
        found = jnp.int32(0)
        for b in range(bricks):
            found = jnp.where(assignment_ref[b] == wanted, b, found)
        return found

    info_ref[0] = row
    info_ref[1] = slab
    info_ref[2] = holder(row, column)
    info_ref[3] = holder(1 - row, column)
    info_ref[4] = holder(row, column - 1)
    info_ref[5] = holder(row, column + 1)
    info_ref[6] = holder(1 - row, column - 1)
    info_ref[7] = holder(1 - row, column + 1)

    breadth = 2 * across

    def live_at(g, x, y):
        inside = (g >= 0) & (g < slabs) & (x >= 0) & (x < 2) & (y >= 0) & (y < breadth)
        index = (jnp.clip(g, 0, slabs - 1) * 2 + jnp.clip(x, 0, 1)) * breadth + jnp.clip(y, 0, breadth - 1)
        return jnp.where(inside, occupancy_ref[index], 0).astype(F32)

    lane = lanes()
    height = rows_of()
    depth = lane % BS
    absorbed = []
    low_ends = []
    high_ends = []
    first_y = None
    second_y = None
    y1 = []
    for s in range(2):
        y = column * 2 + s
        here = live_at(slab, row, y)
        around = [
            here * live_at(slab, row + 1, y),
            here * live_at(slab, row - 1, y),
            here * live_at(slab, row, y + 1),
            here * live_at(slab, row, y - 1),
            here * live_at(slab + 1, row, y),
            here * live_at(slab - 1, row, y),
        ]
        borders = [height == BS - 1, height == 0, lane >= 96, lane < 32, depth == BS - 1, depth == 0]
        for k in range(8):
            c = 8 * s + k
            part = pl.ds(128 * k, 128)
            taken = uptake_ref[s, :, part]
            absorbed.append(taken)
            diagonal = taken
            for d in range(6):
                bond = conductance_ref[d, s, :, part]
                if (d == 2 and k < 7) or (d == 3 and k > 0):
                    value = bond * here
                else:
                    value = bond * jnp.where(borders[d], around[d], here)
                effective_ref[d, c] = value
                diagonal = diagonal + value
                if d == 2 and c == 7:
                    first_y = jnp.where(borders[d], value, 0.0)
                if d == 3 and c == 8:
                    second_y = jnp.where(borders[d], value, 0.0)
                if d == 4:
                    high_ends.append(jnp.where(borders[d], value, 0.0))
                if d == 5:
                    low_ends.append(jnp.where(borders[d], value, 0.0))
            relax = OMEGA / diagonal
            diagonal_ref[c] = diagonal
            relax_ref[c] = relax
            forcing = source_ref[s, :, part] * here
            residual_ref[c] = forcing
            y1.append(relax * forcing)

    outcome = stencil(
        y1, lambda d, c: effective_ref[d, c], lambda c: diagonal_ref[c], None, None, None, None
    )
    partial = []
    for c in range(CHUNKS):
        value = y1[c] + relax_ref[c] * (residual_ref[c] - outcome[c])
        partial_ref[c] = value
        partial.append(value)
    write_xy(xy_ref, row, y1, partial)

    first_coupling = total_of([first_y])
    high_sums = [total_of(high_ends[8 * s : 8 * s + 8]) for s in range(2)]
    low_sums = [total_of(low_ends[8 * s : 8 * s + 8]) for s in range(2)]
    taken_sums = [total_of(absorbed[8 * s : 8 * s + 8]) for s in range(2)]
    residual_sums = [total_of([residual_ref[8 * s + k] for k in range(8)]) for s in range(2)]
    write_scalars(
        xy_ref,
        XY_S,
        [
            residual_sums[0],
            residual_sums[1],
            taken_sums[0] + first_coupling + high_sums[0] + low_sums[0],
            taken_sums[1] + total_of([second_y]) + high_sums[1] + low_sums[1],
            first_coupling,
            high_sums[0],
            high_sums[1],
        ],
    )

    last = CHUNKS - 1
    z_ends = [relax_ref[c] * (high_ends[c] + low_ends[c]) for c in range(CHUNKS)]
    for c in range(CHUNKS):
        xy_ref[XY_XD + c : XY_XD + c + 1] = facing(relax_ref[c], row)
        edge_ref[E_XP + c : E_XP + c + 1] = (relax_ref[c] * effective_ref[0, c])[BS - 1 : BS]
        edge_ref[E_XM + c : E_XM + c + 1] = (relax_ref[c] * effective_ref[1, c])[0:1]
    high_y = jnp.where(lane >= 96, relax_ref[last] * effective_ref[2, last], 0.0)
    low_y = jnp.where(lane < 32, relax_ref[0] * effective_ref[3, 0], 0.0)
    edge_ref[E_YP : E_YP + BS] = high_y
    edge_ref[E_YM : E_YM + BS] = low_y
    xy_ref[XY_YC : XY_YC + BS] = side_blocks(relax_ref[0], relax_ref[last], z_ends[0], z_ends[last])
    xy_ref[XY_K : XY_K + 1] = facing(low_y + high_y, row)
    xy_ref[XY_K + 1 : XY_K + 2] = pack([facing(z, row) for z in z_ends])
    toward_low = facing_terms(relax_ref, effective_ref, 0)
    toward_high = facing_terms(relax_ref, effective_ref, last)
    lane_row = lanes(1)
    xy_ref[XY_K + 2 : XY_K + 3] = jnp.where(lane_row < 32, toward_low, roll_row(toward_high, 64))
    xy_ref[XY_K + 3 : XY_K + 8] = jnp.zeros((5, 128), F32)


def facing_terms(relax_ref, effective_ref, c):
    upper = (relax_ref[c] * effective_ref[0, c])[BS - 1 : BS]
    lower = (relax_ref[c] * effective_ref[1, c])[0:1]
    return upper + lower


def swap_sides(from_low, from_high):
    rows = from_low.shape[0]
    if rows == 1:
        low, high = roll_row(from_low, -32), roll_row(from_high, 32)
    else:
        low, high = roll(from_low, -32), roll(from_high, 32)
    return jnp.where((lanes(rows) // 32) % 2 == 0, low, high)


def middle_kernel(
    first, bricks, info_ref, xy_ref, field_ref, relax_ref, partial_ref, edge_ref, z_ref, tile_ref
):
    lane = lanes()
    height = rows_of()
    x_holder = info_ref[3]
    x_halo = xy_ref[x_holder, XY_X1 : XY_X1 + CHUNKS]
    sides = swap_sides(
        xy_ref[info_ref[4], XY_Y : XY_Y + BS], xy_ref[info_ref[5], XY_Y : XY_Y + BS]
    )
    upper = edge_ref[E_XP : E_XP + CHUNKS] * x_halo
    lower = edge_ref[E_XM : E_XM + CHUNKS] * x_halo
    y1 = []
    whole = []
    for c in range(CHUNKS):
        y1.append(relax_ref[c] * field_ref[c])
        value = partial_ref[c]
        value = value + jnp.where(height == BS - 1, upper[c : c + 1], 0.0)
        value = value + jnp.where(height == 0, lower[c : c + 1], 0.0)
        if c == 0:
            value = value + jnp.where(lane < 32, edge_ref[E_YM : E_YM + BS] * sides, 0.0)
        if c == CHUNKS - 1:
            value = value + jnp.where(
                lane >= 96, edge_ref[E_YP : E_YP + BS] * roll(sides, 64), 0.0
            )
        whole.append(value)
    z_ref[Z_Y1 : Z_Y1 + BS] = pack(y1)
    z_ref[Z_Q : Z_Q + BS] = pack(whole)
    z_ref[Z_Y : Z_Y + BS] = sides
    x_ends = pack([x_halo[c : c + 1] for c in range(CHUNKS)])
    z_ref[Z_X : Z_X + 8] = jnp.broadcast_to(x_ends, (8, 128))
    if first:
        z_ref[Z_D : Z_D + BS] = pack([relax_ref[c] for c in range(CHUNKS)])
    lane_tile = lanes(8)
    mixed = jnp.zeros((8, 128), F32)
    for q in range(4):
        mixed = jnp.where(lane_tile == q, xy_ref[info_ref[2 + q], XY_S : XY_S + 8], mixed)
    if not first:
        summed = xy_ref[0, XY_S : XY_S + 8]
        for b in range(1, bricks):
            summed = summed + xy_ref[b, XY_S : XY_S + 8]
        mixed = jnp.where(rows_of(8) < 2, mixed, summed)
    tile_ref[...] = mixed


def search_scalars(tiles, scalars, iteration):
    energy = tiles[2:3, 0:1]
    curvature = tiles[3:4, 0:1]
    if iteration == 0:
        return energy, curvature, energy / curvature, None
    growth = energy / scalars[0:1, 0:1]
    curvature = curvature + growth * (2.0 * tiles[4:5, 0:1] + growth * scalars[1:2, 0:1])
    return energy, curvature, energy / curvature, growth


def sum_tiles(ref, count):
    total = ref[0:8]
    for g in range(1, count):
        total = total + ref[8 * g : 8 * g + 8]
    return total


def step_kernel(iteration, slabs, bricks, *refs):
    first = iteration == 0
    last = iteration == ITERS - 1
    refs = list(refs)
    take = lambda count: [refs.pop(0) for _ in range(count)]
    info_ref, xy_ref, above_ref, below_ref, tiles_ref = take(5)
    effective_ref, diagonal_ref, relax_ref, residual_ref = take(4)
    if not first:
        mapped_ref, halo_in, constant_ref, factor_ref, sums_in, scalars_in = take(6)
    if iteration > 1:
        search_in, search_halo_in, search_sums_in = take(3)
    smoothed_ref, mapped_out = take(2)
    if first:
        constant_ref, factor_ref, halo_ref, sums_ref = take(4)
    else:
        residual_out, search_ref, scalars_ref = take(3)
        if not last:
            halo_ref, sums_ref, search_halo_ref, search_sums_ref = take(4)
    xy_out = take(1)[0]
    if not last:
        partial_ref = take(1)[0]

    row = info_ref[0]
    slab = info_ref[1]
    lane = lanes()
    height = rows_of()
    depth = lane % BS
    lane_row = lanes(1)
    even = lane % 2 == 0
    even_row = lane_row % 2 == 0
    low_holder, high_holder = info_ref[4], info_ref[5]
    low_corner, high_corner = info_ref[6], info_ref[7]
    x_holder = info_ref[3]

    def merge(start):
        up = roll(above_ref[start : start + BS], 31)
        down = roll(below_ref[start : start + BS], -31)
        return jnp.where(even, up, down)

    x_sides = xy_ref[x_holder, XY_X1 : XY_X1 + 2 * CHUNKS]
    y_sides = swap_sides(
        xy_ref[low_holder, XY_Y : XY_Y + BS], xy_ref[high_holder, XY_Y : XY_Y + BS]
    )
    z_first = merge(Z_Y1)
    z_second = merge(Z_Q)
    y_up = roll(above_ref[Z_Y : Z_Y + BS], 31)
    y_down = roll(below_ref[Z_Y : Z_Y + BS], -31)
    y_ends = jnp.where(depth == BS - 1, y_up, jnp.where(depth == 0, y_down, 0.0))
    x_ends = jnp.where(
        even_row,
        roll_row(above_ref[Z_X : Z_X + 1], 31),
        roll_row(below_ref[Z_X : Z_X + 1], -31),
    )
    corner_y = jnp.where(
        lane_row < 32,
        roll_row(xy_ref[low_corner, XY_X1 + CHUNKS - 1 : XY_X1 + CHUNKS], 32),
        roll_row(xy_ref[high_corner, XY_X1 : XY_X1 + 1], -32),
    )
    low_row = jnp.where(
        row == 0,
        xy_ref[low_corner, XY_Y : XY_Y + 1],
        xy_ref[low_corner, XY_Y + BS - 1 : XY_Y + BS],
    )
    high_row = jnp.where(
        row == 0,
        xy_ref[high_corner, XY_Y : XY_Y + 1],
        xy_ref[high_corner, XY_Y + BS - 1 : XY_Y + BS],
    )
    corner_x = swap_sides(low_row, high_row)
    ends = jnp.concatenate([x_ends, corner_y, corner_x, jnp.zeros((5, 128), F32)], axis=0)
    halo = [x_sides, y_sides, z_first, z_second, y_ends, ends]
    starts = [H_X1, H_Y, H_Z1, H_ZQ, H_YZ, H_R]
    sums = tiles_ref[...]

    if first:
        residual = [residual_ref[c] for c in range(CHUNKS)]
        constant_ref[C_XD : C_XD + CHUNKS] = xy_ref[x_holder, XY_XD : XY_XD + CHUNKS]
        constant_ref[C_YC : C_YC + BS] = swap_sides(
            xy_ref[low_holder, XY_YC : XY_YC + BS], xy_ref[high_holder, XY_YC : XY_YC + BS]
        )
        constant_ref[C_ZD : C_ZD + BS] = merge(Z_D)
        constant_ref[C_K : C_K + 8] = jnp.concatenate(
            [
                xy_ref[x_holder, XY_K : XY_K + 2],
                swap_sides(
                    xy_ref[low_holder, XY_K + 2 : XY_K + 3],
                    xy_ref[high_holder, XY_K + 2 : XY_K + 3],
                ),
                jnp.zeros((5, 128), F32),
            ],
            axis=0,
        )
        for g in range(slabs):
            tile = sums[8 * g : 8 * g + 8]
            a, b, off = tile[2:3], tile[3:4], tile[4:5]
            t0, t1 = tile[5:6], tile[6:7]
            if g > 0:
                a = a - u0 * u0 * i00
                b = b - u1 * u1 * i11
                off = off + u0 * u1 * i01
            a = jnp.where(lane_row < 4, a, 1.0)
            b = jnp.where(lane_row < 4, b, 1.0)
            scale = 1.0 / (a * b - off * off)
            i00, i01, i11 = b * scale, off * scale, a * scale
            u0, u1 = t0, t1
            factor_ref[8 * g : 8 * g + 8] = jnp.concatenate(
                [i00, i01, i11, t0, t1, jnp.zeros((3, 128), F32)], axis=0
            )
    else:
        scalars = None if iteration == 1 else scalars_in[...]
        energy, curvature, step, growth = search_scalars(
            sum_tiles(tiles_ref, slabs), scalars, iteration - 1
        )
        step_row = jnp.broadcast_to(step, (1, 128))
        residual = []
        for c in range(CHUNKS):
            mapped = mapped_ref[c]
            if growth is not None:
                mapped = mapped + growth * search_in[c]
            search_ref[c] = mapped
            value = residual_ref[c] - step * mapped
            residual_out[c] = value
            residual.append(value)
        old_halo = halo
        halo = []
        for start, block in zip(starts, old_halo):
            span = slice(start, start + block.shape[0])
            if growth is not None:
                block = block + growth * search_halo_in[span]
            if not last:
                search_halo_ref[span] = block
            halo.append(halo_in[span] - step * block)
        if growth is not None:
            sums = sums + growth * search_sums_in[...]
        if not last:
            search_sums_ref[...] = sums
        sums = sums_in[...] - step * sums
        kept = [energy, curvature, step]
        if growth is not None:
            kept = [energy, curvature, scalars[2:3, 0:1], step, growth]
        write_scalars(scalars_ref, 0, kept)

    if not last:
        for start, block in zip(starts, halo):
            halo_ref[start : start + block.shape[0]] = block
        sums_ref[...] = sums
    x_sides, y_sides, z_first, z_second, y_ends, ends = halo

    forward = []
    for g in range(slabs):
        t0, t1 = sums[8 * g : 8 * g + 1], sums[8 * g + 1 : 8 * g + 2]
        if g > 0:
            t0 = t0 + w0 * v0
            t1 = t1 + w1 * v1
        factor = factor_ref[8 * g : 8 * g + 8]
        v0 = factor[0:1] * t0 + factor[1:2] * t1
        v1 = factor[1:2] * t0 + factor[2:3] * t1
        w0, w1 = factor[3:4], factor[4:5]
        forward.append((v0, v1))
    blank = jnp.zeros((1, 128), F32)
    below0, below1, here0, here1, above0, above1 = [blank] * 6
    for g in reversed(range(slabs)):
        v0, v1 = forward[g]
        if g < slabs - 1:
            factor = factor_ref[8 * g : 8 * g + 8]
            s0, s1 = factor[3:4] * n0, factor[4:5] * n1
            v0 = v0 + factor[0:1] * s0 + factor[1:2] * s1
            v1 = v1 + factor[1:2] * s0 + factor[2:3] * s1
        n0, n1 = v0, v1
        here0 = jnp.where(slab == g, n0, here0)
        here1 = jnp.where(slab == g, n1, here1)
        above0 = jnp.where(slab + 1 == g, n0, above0)
        above1 = jnp.where(slab + 1 == g, n1, above1)
        below0 = jnp.where(slab - 1 == g, n0, below0)
        below1 = jnp.where(slab - 1 == g, n1, below1)
    own = [here0[:, 0:1], here1[:, 0:1]]

    effective = lambda d, c: effective_ref[d, c]
    diagonal = lambda c: diagonal_ref[c]
    end = CHUNKS - 1

    y1 = [relax_ref[c] * residual[c] for c in range(CHUNKS)]
    outcome = stencil(
        y1, effective, diagonal, x_sides[:CHUNKS], y_sides, roll(y_sides, 64), z_first
    )
    smoothed = []
    for c in range(CHUNKS):
        value = y1[c] + relax_ref[c] * (residual[c] - outcome[c]) + own[c // 8]
        smoothed_ref[c] = value
        smoothed.append(value)
    keys = constant_ref[C_K : C_K + 8]
    crossing = jnp.concatenate(
        [
            effective(0, c)[BS - 1 : BS] * y1[c][BS - 1 : BS] + effective(1, c)[0:1] * y1[c][0:1]
            for c in range(CHUNKS)
        ],
        axis=0,
    )
    end_row = keys[1:2] * ends[0:1]
    corner_row = keys[0:1] * ends[1:2]
    depth_row = lane_row % BS
    additions = []
    for c in range(CHUNKS):
        value = jnp.where(
            (depth_row == BS - 1) | (depth_row == 0), roll_row(end_row, 31 - 2 * c), 0.0
        )
        if c == 0:
            value = value + jnp.where(lane_row < 32, corner_row, 0.0)
        if c == end:
            value = value + jnp.where(lane_row >= 96, corner_row, 0.0)
        value = value + (here0 if c < 8 else here1)[:, 1:2]
        additions.append(value)
    x_next = (
        x_sides[CHUNKS:]
        + constant_ref[C_XD : C_XD + CHUNKS] * crossing
        + jnp.concatenate(additions, axis=0)
    )
    y_constant = constant_ref[C_YC : C_YC + BS]
    y_crossing = jnp.where(
        lane < 32, effective(3, 0) * y1[0], roll(effective(2, end) * y1[end], 64)
    )
    x_side_row = jnp.where(row == 0, BS - 1, 0)
    y_next = (
        roll(y_sides, 64)
        + y_constant * y_crossing
        + roll(y_constant, 64) * y_ends
        + jnp.where(height == x_side_row, keys[2:3] * ends[2:3], 0.0)
        + jnp.where(lane < 32, here1[:, 2:3], here0[:, 3:4])
    )
    z_crossing = pack(
        [
            jnp.where(depth == BS - 1, effective(4, c), effective(5, c)) * y1[c]
            for c in range(CHUNKS)
        ]
    )
    z_coarse = jnp.where(
        even_row,
        jnp.where(depth_row < 16, above0[:, 0:1], above1[:, 0:1]),
        jnp.where(depth_row < 16, below0[:, 0:1], below1[:, 0:1]),
    )
    z_next = z_second + constant_ref[C_ZD : C_ZD + BS] * z_crossing + z_coarse
    mapped = stencil(smoothed, effective, diagonal, x_next, y_next, roll(y_next, 64), z_next)
    for c in range(CHUNKS):
        mapped_out[c] = mapped[c]

    values = [
        total_of(mapped[:8]),
        total_of(mapped[8:]),
        total_of([residual[c] * smoothed[c] for c in range(CHUNKS)]),
        total_of([mapped[c] * smoothed[c] for c in range(CHUNKS)]),
    ]
    if not first:
        values.append(total_of([search_ref[c] * smoothed[c] for c in range(CHUNKS)]))
    if last:
        write_scalars(xy_out, 0, values)
        return
    write_scalars(xy_out, XY_S, values)
    y1 = [relax_ref[c] * mapped[c] for c in range(CHUNKS)]
    outcome = stencil(y1, effective, diagonal, None, None, None, None)
    partial = []
    for c in range(CHUNKS):
        value = y1[c] + relax_ref[c] * (mapped[c] - outcome[c])
        partial_ref[c] = value
        partial.append(value)
    write_xy(xy_out, row, y1, partial)


def finish_kernel(
    count, tiles_ref, scalars_ref, residual_ref, mapped_ref, search_ref, first_ref, second_ref, third_ref,
    solution_ref, residual_out,
):
    scalars = scalars_ref[...]
    _, _, step, growth = search_scalars(sum_tiles(tiles_ref, count), scalars, ITERS - 1)
    first_step, second_step, second_growth = scalars[2:3, 0:1], scalars[3:4, 0:1], scalars[4:5, 0:1]
    third_weight = step
    second_weight = second_step + growth * step
    first_weight = first_step + second_growth * second_weight
    for c in range(CHUNKS):
        s, part = c // 8, pl.ds(128 * (c % 8), 128)
        solution_ref[s, :, part] = (
            first_weight * first_ref[c] + second_weight * second_ref[c] + third_weight * third_ref[c]
        )
        residual_out[s, :, part] = residual_ref[c] - step * (mapped_ref[c] + growth * search_ref[c])


def call(kernel, name, outs, operands, scalar_operands=0, scalar_outs=0):
    vmem = pl.BlockSpec(memory_space=pltpu.VMEM)
    smem = pl.BlockSpec(memory_space=pltpu.SMEM)
    return pl.pallas_call(
        kernel,
        out_shape=tuple(outs),
        in_specs=[smem] * scalar_operands + [vmem] * (len(operands) - scalar_operands),
        out_specs=tuple([smem] * scalar_outs + [vmem] * (len(outs) - scalar_outs)),
        compiler_params=pltpu.CompilerParams(vmem_limit_bytes=40 * 1024 * 1024),
        name=name,
    )(*operands)


def array(*shape):
    return jax.ShapeDtypeStruct(shape, F32)


def gather_bricks(message):
    return lax.all_gather(message, "brick", axis=0, tiled=False)


def gather_slabs(tile):
    return lax.all_gather(tile, "grp", axis=0, tiled=True)


def exchange_slabs(message):
    count = lax.axis_size("grp")
    upward = [(i, i + 1) for i in range(count - 1)]
    downward = [(i + 1, i) for i in range(count - 1)]
    return lax.ppermute(message, "grp", downward), lax.ppermute(message, "grp", upward)


def on_device(source, uptake, conductance, occupancy, assignment):
    slabs = lax.axis_size("grp")
    bricks = lax.axis_size("brick")
    place = (lax.axis_index("grp") * bricks + lax.axis_index("brick")).astype(jnp.int32).reshape(1)
    field = array(*FIELD)
    info, effective, diagonal, relax, residual, partial, edge, message = call(
        functools.partial(setup_kernel, slabs, bricks),
        "setup",
        [
            jax.ShapeDtypeStruct((8,), jnp.int32), array(6, *FIELD), field, field, field, field,
            array(E_ROWS, 128), array(XY_ROWS_FIRST, 128),
        ],
        [place, assignment, occupancy.reshape(-1), source[0, 0], uptake[0, 0], conductance[0, 0]],
        scalar_operands=3,
        scalar_outs=1,
    )
    mapped = residual
    directions = []
    state = {}
    for iteration in range(ITERS):
        first, last = iteration == 0, iteration == ITERS - 1
        gathered = gather_bricks(message)
        z_message, tile = call(
            functools.partial(middle_kernel, first, bricks),
            f"middle_{iteration}",
            [array(Z_ROWS_FIRST if first else Z_ROWS, 128), array(8, 128)],
            [info, gathered, mapped, relax, partial, edge],
            scalar_operands=1,
        )
        above, below = exchange_slabs(z_message)
        tiles = gather_slabs(tile)
        operands = [info, gathered, above, below, tiles, effective, diagonal, relax, residual]
        tall = array(8 * slabs, 128)
        outs = {"smoothed": field, "mapped": field}
        if not first:
            operands += [mapped] + [state[k] for k in ("halo", "constant", "factor", "sums", "scalars")]
        if iteration > 1:
            operands += [state[k] for k in ("search", "search_halo", "search_sums")]
        if first:
            outs |= {"constant": array(C_ROWS, 128), "factor": tall, "halo": array(H_ROWS, 128), "sums": tall}
        else:
            outs |= {"residual": field, "search": field, "scalars": array(8, 128)}
            if not last:
                outs |= {
                    "halo": array(H_ROWS, 128), "sums": tall,
                    "search_halo": array(H_ROWS, 128), "search_sums": tall,
                }
        outs["message"] = array(8 if last else XY_ROWS, 128)
        if not last:
            outs["partial"] = field
        results = call(
            functools.partial(step_kernel, iteration, slabs, bricks),
            f"step_{iteration}",
            list(outs.values()),
            operands,
            scalar_operands=1,
        )
        state |= dict(zip(outs, results))
        if first:
            state["scalars"] = jnp.zeros((8, 128), F32)
        mapped, message, partial = state["mapped"], state["message"], state.get("partial")
        residual = state.get("residual", residual)
        directions.append(state["smoothed"])
    tiles = gather_slabs(gather_bricks(message).reshape(bricks * 8, 128))
    brick_pair = array(2, BS, BS * BS)
    solution_field, residual = call(
        functools.partial(finish_kernel, slabs * bricks),
        "finish",
        [brick_pair, brick_pair],
        [tiles, state["scalars"], residual, mapped, state["search"]] + directions,
    )
    return solution_field[None, None], residual[None, None]


def solution(mesh):
    return jax.shard_map(
        on_device,
        mesh=mesh,
        in_specs=(
            P("grp", "brick", None, None, None),
            P("grp", "brick", None, None, None),
            P("grp", "brick", None, None, None, None),
            P(),
            P(),
        ),
        out_specs=(P("grp", "brick", None, None, None), P("grp", "brick", None, None, None)),
        check_vma=False,
    )
```

time: 835 us -> 179 us (0.21); the launches traced: 820 us -> 179 us
  local copies, waits for them, and re-layouts: 375 us -> 4.82 us
  other arithmetic: 155 us -> 0 us
  blocking collectives: 236 us -> 149 us
  starting transfers between devices: 32.4 us -> 13.7 us
  between operations: 18.2 us -> 0.75 us
  Pallas kernels: 0 us -> 10.9 us
    concatenate x76 -> x0, local copies, waits for them, and re-layouts: 141 us -> none  [the longest x12 29.1 us: apply_operator(): jnp.roll(cube, -1, axis=3)]
    psum x3 -> x0, blocking collectives: 122 us -> none  [paired(): lax.psum((jnp.sum(first_terms), jnp.sum(second_terms)), ('brick', 'grp'))]
    broadcast_in_dim x53 -> x1, local copies, waits for them, and re-layouts: 96.2 us -> 0.01 us  [on_device(): state['scalars'] = jnp.zeros((8, 128), F32)]
    all_gather x7 -> x8, blocking collectives: 55.7 us -> 149 us  [the longest x4 125 us: gather_slabs(): return lax.all_gather(tile, 'grp', axis=0, tiled=True)]
    another operation x3 -> x0, blocking collectives: 58.5 us -> none  [coarse_solve(): lax.linalg.triangular_solve(factor, gathered_terms, left_side=True, lower...]
    slice x47 -> x0, local copies, waits for them, and re-layouts: 49.7 us -> none  [the longest x6 12.9 us: apply_operator(): lower_z = cube[:, :, :, 0].reshape(slot_count, face_size)]
    add x9 -> x0, other arithmetic: 44.8 us -> none  [the longest x5 42.9 us: precondition(): return smoothed + coarse_solve(residual_field)[:, None, None]]
    another operation x52 -> x0, local copies, waits for them, and re-layouts: 33.9 us -> none  [the longest x12 13.6 us: apply_operator(): stacked = jnp.stack([lower_z, upper_z])]
  transfers between devices with their start and end apart: 12 -> 6, of which waited for: 0 -> 0; matrix products, arithmetic and copies ran while one was open for 28% -> 0% of each run, Pallas kernels for 0% -> 0%
where the time goes in v1:
time: 179 us
  blocking collectives  149 us (83%)
  starting transfers between devices  13.7 us (8%)
  Pallas kernels  10.9 us (6%)
  local copies, waits for them, and re-layouts  4.82 us (3%)
    all_gather x4, blocking collectives, gather_slabs(): return lax.all_gather(tile, 'grp', axis=0, tiled=True)  125 us
    all_gather x4, blocking collectives, gather_bricks(): return lax.all_gather(message, 'brick', axis=0, tiled=False)  23.3 us
    pallas_call x8, Pallas kernels, call(): pl.pallas_call(kernel, out_shape=tuple(outs), in_specs=[smem] * scalar_op...  10.9 us
    ppermute x3, starting transfers between devices, exchange_slabs(): lax.ppermute(message, 'grp', upward)  9.83 us
    unnamed x9, local copies, waits for them, and re-layouts  4.73 us
    ppermute x3, starting transfers between devices, exchange_slabs(): lax.ppermute(message, 'grp', downward)  3.88 us
  transfers between devices with their start and end apart: 6, of which 0 were waited for; matrix products, arithmetic and copies ran while one was open for 0% of the time, Pallas kernels for 0%

profile of v1, /device:TPU:0, one launch (start us, length us, event | category | flops | bytes accessed | tf_op | source)
XLA Modules:
  0.0 178.9 jit_solution(10876024479119801680)
XLA Ops:
  0.6 0.8 copy.8
  1.4 0.1 reshape.14.occupancy_ref
  1.5 0.0 copy-start
  1.5 1.4 copy-done
  2.9 0.0 copy-start.1
  2.9 0.9 copy-done.1
  3.9 0.0 copy-start.2
  3.9 0.9 copy-done.2
  4.8 0.0 copy-start.3
  4.8 0.7 copy-done.3
  5.5 1.8 setup.1
  7.3 7.2 %all-gather = f32[512,128]{1,0:T(8,128)S(1)} all-gather(f32[128,128]{1,0:T(8,128)S(1)} %get-tuple-element.44), channel_id=2, replica_groups=mesh['brick'=4,'grp'=8] {'brick'}, dimensions={0}, use_global_device_ids=true | all-gather | bytes 327680 | tf_op jit(solution)/shard_map/all_gather | solution.py:643
  14.5 0.8 middle_0.1
  15.3 3.4 %collective-permute-start.1 = (f32[136,128]{1,0:T(8,128)S(1)}, f32[136,128]{1,0:T(8,128)S(1)}, u32[]{:S(2)}, u32[]{:S(2)}) collective-permute-start(f32[136,128]{1,0:T(8,128)S(1)} %get-tuple-element.49), channel_id=1, source_target_pairs={{0,1},{1,2},{2,3},{3,4},{4,5},{5,6},{6,7},{8,9},{9,10},{10,11},{11... | collective-permute-start | bytes 208904 | tf_op jit(solution)/shard_map/ppermute | solution.py:654
  18.8 1.3 collective-permute-start
  20.1 32.8 %all_gather.38.refs_4_ = f32[64,128]{1,0:T(8,128)S(1)} all-gather(f32[8,128]{1,0:T(8,128)S(1)} %get-tuple-element.50), channel_id=1, replica_groups=mesh['brick'=4,'grp'=8] {'grp'}, dimensions={0}, use_global_device_ids=true | all-gather | bytes 36864 | tf_op jit(solution)/shard_map/all_gather | solution.py:647
  52.9 0.0 collective-permute-done.1.refs_3_
  52.9 0.0 collective-permute-done.refs_2_
  52.9 2.0 %step_0.1 = (f32[16,32,128]{2,1,0:T(8,128)S(1)}, f32[16,32,128]{2,1,0:T(8,128)S(1)}, f32[88,128]{1,0:T(8,128)S(1)}, f32[64,128]{1,0:T(8,128)S(1)}, f32[168,128]{...) custom-call(s32[8]{0:T(128)S(1)} %get-tuple-element.43.info_ref.refs_0_, ...), custom_call_target="tpu_custom_call" | custom-call | tf_op jit(solution)/shard_map/step_0/pallas_call | solution.py:628
  54.9 5.5 %all-gather.1 = f32[288,128]{1,0:T(8,128)S(1)} all-gather(f32[72,128]{1,0:T(8,128)S(1)} %get-tuple-element.53), channel_id=3, replica_groups=mesh['brick'=4,'grp'=8] {'brick'}, dimensions={0}, use_global_device_ids=true | all-gather | bytes 184320 | tf_op jit(solution)/shard_map/all_gather | solution.py:643
  60.4 0.8 middle_1.1
  61.1 2.5 %collective-permute-start.3 = (f32[104,128]{1,0:T(8,128)S(1)}, f32[104,128]{1,0:T(8,128)S(1)}, u32[]{:S(2)}, u32[]{:S(2)}) collective-permute-start(f32[104,128]{1,0:T(8,128)S(1)} %get-tuple-element.56), channel_id=1, source_target_pairs={{0,1},{1,2},{2,3},{3,4},{4,5},{5,6},{6,7},{8,9},{9,10},{10,11},{11... | collective-permute-start | bytes 159752 | tf_op jit(solution)/shard_map/ppermute | solution.py:654
  63.7 1.3 collective-permute-start.2
  65.0 31.0 %all_gather.41.refs_4_ = f32[64,128]{1,0:T(8,128)S(1)} all-gather(f32[8,128]{1,0:T(8,128)S(1)} %get-tuple-element.57), channel_id=1, replica_groups=mesh['brick'=4,'grp'=8] {'grp'}, dimensions={0}, use_global_device_ids=true | all-gather | bytes 36864 | tf_op jit(solution)/shard_map/all_gather | solution.py:647
  96.0 0.0 collective-permute-done.3.refs_3_
  96.0 0.0 collective-permute-done.2.refs_2_
  96.0 2.0 %step_1.1 = (f32[16,32,128]{2,1,0:T(8,128)S(1)}, f32[16,32,128]{2,1,0:T(8,128)S(1)}, f32[16,32,128]{2,1,0:T(8,128)S(1)}, f32[16,32,128]{2,1,0:T(8,128)S(1)}, f32...) custom-call(s32[8]{0:T(128)S(1)} %get-tuple-element.43.info_ref.refs, ...), custom_call_target="tpu_custom_call" | custom-call | tf_op jit(solution)/shard_map/step_1/pallas_call | solution.py:628
  98.0 5.5 %all-gather.2 = f32[288,128]{1,0:T(8,128)S(1)} all-gather(f32[72,128]{1,0:T(8,128)S(1)} %get-tuple-element.62), channel_id=4, replica_groups=mesh['brick'=4,'grp'=8] {'brick'}, dimensions={0}, use_global_device_ids=true | all-gather | bytes 184320 | tf_op jit(solution)/shard_map/all_gather | solution.py:643
  103.5 0.8 middle_2.1
  104.3 3.9 %collective-permute-start.5 = (f32[104,128]{1,0:T(8,128)S(1)}, f32[104,128]{1,0:T(8,128)S(1)}, u32[]{:S(2)}, u32[]{:S(2)}) collective-permute-start(f32[104,128]{1,0:T(8,128)S(1)} %get-tuple-element.65), channel_id=1, source_target_pairs={{0,1},{1,2},{2,3},{3,4},{4,5},{5,6},{6,7},{8,9},{9,10},{10,11},{11... | collective-permute-start | bytes 159752 | tf_op jit(solution)/shard_map/ppermute | solution.py:654
  108.2 1.3 collective-permute-start.4
  109.5 31.0 %all_gather.44.refs_4_ = f32[64,128]{1,0:T(8,128)S(1)} all-gather(f32[8,128]{1,0:T(8,128)S(1)} %get-tuple-element.66), channel_id=1, replica_groups=mesh['brick'=4,'grp'=8] {'grp'}, dimensions={0}, use_global_device_ids=true | all-gather | bytes 36864 | tf_op jit(solution)/shard_map/all_gather | solution.py:647
  140.5 0.0 collective-permute-done.5.refs_3_
  140.5 0.0 collective-permute-done.4.refs_2_
  140.6 1.7 step_2.1
  142.3 5.2 %all-gather.3 = f32[32,128]{1,0:T(8,128)S(1)} all-gather(f32[8,128]{1,0:T(8,128)S(1)} %get-tuple-element.74), channel_id=5, replica_groups=mesh['brick'=4,'grp'=8] {'brick'}, dimensions={0}, use_global_device_ids=true | all-gather | bytes 20480 | tf_op jit(solution)/shard_map/all_gather | solution.py:643
  147.5 30.5 %all_gather.47.tiles_ref = f32[256,128]{1,0:T(8,128)S(1)} all-gather(f32[32,128]{1,0:T(8,128)S(1)} %all-gather.3), channel_id=1, replica_groups=mesh['brick'=4,'grp'=8] {'grp'}, dimensions={0}, use_global_device_ids=true | all-gather | bytes 147456 | tf_op jit(solution)/shard_map/all_gather | solution.py:647
  178.0 1.0 finish.1
  (1 shorter events, 0.0 us)
Async XLA Ops:
  1.5 1.4 copy-start
  2.9 0.9 copy-start.1
  3.9 0.9 copy-start.2
  4.8 0.7 copy-start.3
  15.3 37.5 %collective-permute-start.1 = (f32[136,128]{1,0:T(8,128)S(1)}, f32[136,128]{1,0:T(8,128)S(1)}, u32[]{:S(2)}, u32[]{:S(2)}) collective-permute-start(f32[136,128]{1,0:T(8,128)S(1)} %get-tuple-element.49), channel_id=1, source_target_pairs={{0,1},{1,2},{2,3},{3,4},{4,5},{5,6},{6,7},{8,9},{9,10},{10,11},{11... | collective-permute-start | bytes 208904 | tf_op jit(solution)/shard_map/ppermute | solution.py:654
  18.8 34.1 %collective-permute-start = (f32[136,128]{1,0:T(8,128)S(1)}, f32[136,128]{1,0:T(8,128)S(1)}, u32[]{:S(2)}, u32[]{:S(2)}) collective-permute-start(f32[136,128]{1,0:T(8,128)S(1)} %get-tuple-element.49), channel_id=1, source_target_pairs={{1,0},{2,1},{3,2},{4,3},{5,4},{6,5},{7,6},{9,8},{10,9},{11,10},{12... | collective-permute-start | bytes 208904 | tf_op jit(solution)/shard_map/ppermute | solution.py:654
  61.1 34.8 %collective-permute-start.3 = (f32[104,128]{1,0:T(8,128)S(1)}, f32[104,128]{1,0:T(8,128)S(1)}, u32[]{:S(2)}, u32[]{:S(2)}) collective-permute-start(f32[104,128]{1,0:T(8,128)S(1)} %get-tuple-element.56), channel_id=1, source_target_pairs={{0,1},{1,2},{2,3},{3,4},{4,5},{5,6},{6,7},{8,9},{9,10},{10,11},{11... | collective-permute-start | bytes 159752 | tf_op jit(solution)/shard_map/ppermute | solution.py:654
  63.7 32.3 %collective-permute-start.2 = (f32[104,128]{1,0:T(8,128)S(1)}, f32[104,128]{1,0:T(8,128)S(1)}, u32[]{:S(2)}, u32[]{:S(2)}) collective-permute-start(f32[104,128]{1,0:T(8,128)S(1)} %get-tuple-element.56), channel_id=1, source_target_pairs={{1,0},{2,1},{3,2},{4,3},{5,4},{6,5},{7,6},{9,8},{10,9},{11,10},{12... | collective-permute-start | bytes 159752 | tf_op jit(solution)/shard_map/ppermute | solution.py:654
  104.3 36.3 %collective-permute-start.5 = (f32[104,128]{1,0:T(8,128)S(1)}, f32[104,128]{1,0:T(8,128)S(1)}, u32[]{:S(2)}, u32[]{:S(2)}) collective-permute-start(f32[104,128]{1,0:T(8,128)S(1)} %get-tuple-element.65), channel_id=1, source_target_pairs={{0,1},{1,2},{2,3},{3,4},{4,5},{5,6},{6,7},{8,9},{9,10},{10,11},{11... | collective-permute-start | bytes 159752 | tf_op jit(solution)/shard_map/ppermute | solution.py:654
  108.2 32.3 %collective-permute-start.4 = (f32[104,128]{1,0:T(8,128)S(1)}, f32[104,128]{1,0:T(8,128)S(1)}, u32[]{:S(2)}, u32[]{:S(2)}) collective-permute-start(f32[104,128]{1,0:T(8,128)S(1)} %get-tuple-element.65), channel_id=1, source_target_pairs={{1,0},{2,1},{3,2},{4,3},{5,4},{6,5},{7,6},{9,8},{10,9},{11,10},{12... | collective-permute-start | bytes 159752 | tf_op jit(solution)/shard_map/ppermute | solution.py:654

commit v2 on v1

--- a/solution.py
+++ b/solution.py
@@ -644,7 +644,13 @@
 
 
 def gather_slabs(tile):
-    return lax.all_gather(tile, "grp", axis=0, tiled=True)
+    count = lax.axis_size("grp")
+    inner = max(count // 4, 1)
+    outer = count // inner
+    near = [[i * inner + j for j in range(inner)] for i in range(outer)]
+    far = [[i * inner + j for i in range(outer)] for j in range(inner)]
+    pairs = lax.all_gather(tile, "grp", axis=0, tiled=True, axis_index_groups=near)
+    return lax.all_gather(pairs, "grp", axis=0, tiled=True, axis_index_groups=far)
 
 
 def exchange_slabs(message):

time: 179 us -> 130 us (0.73)
  blocking collectives: 149 us -> 101 us
    all_gather x4 -> x8, blocking collectives: 125 us -> 77.5 us  [the longest x4 57.3 us: gather_slabs(): lax.all_gather(pairs, 'grp', axis=0, tiled=True, axis_index_groups=far)]
where the time goes in v2:
time: 130 us
  blocking collectives  101 us (78%)
  starting transfers between devices  12.6 us (10%)
  Pallas kernels  10.9 us (8%)
  local copies, waits for them, and re-layouts  4.82 us (4%)
    all_gather x4, blocking collectives, gather_slabs(): lax.all_gather(pairs, 'grp', axis=0, tiled=True, axis_index_groups=far)  57.3 us
    all_gather x4, blocking collectives, gather_bricks(): return lax.all_gather(message, 'brick', axis=0, tiled=False)  23.3 us
    all_gather x4, blocking collectives, gather_slabs(): lax.all_gather(tile, 'grp', axis=0, tiled=True, axis_index_groups=near)  20.2 us
    pallas_call x8, Pallas kernels, call(): pl.pallas_call(kernel, out_shape=tuple(outs), in_specs=[smem] * scalar_op...  10.9 us
    ppermute x3, starting transfers between devices, exchange_slabs(): lax.ppermute(message, 'grp', upward)  8.77 us
    unnamed x9, local copies, waits for them, and re-layouts  4.73 us
    ppermute x3, starting transfers between devices, exchange_slabs(): lax.ppermute(message, 'grp', downward)  3.88 us
  transfers between devices with their start and end apart: 6, of which 0 were waited for; matrix products, arithmetic and copies ran while one was open for 0% of the time, Pallas kernels for 0%

profile of v2, /device:TPU:0, one launch (start us, length us, event | category | flops | bytes accessed | tf_op | source)
XLA Modules:
  0.0 130.0 jit_solution(3565535892800432549)
XLA Ops:
  0.6 0.8 copy.8
  1.4 0.1 reshape.14.occupancy_ref
  1.5 0.0 copy-start
  1.5 1.4 %copy-done = f32[1,1,6,2,32,1024]{5,4,3,2,1,0:T(8,128)S(1)} copy-done((f32[1,1,6,2,32,1024]{5,4,3,2,1,0:T(8,128)S(1)}, f32[1,1,6,2,32,1024]{5,4,3,2,1,0:T(8,128)}, u32[]{:S(2)}) %copy-start) | copy-done | bytes 1572888
  2.9 0.0 copy-start.1
  2.9 0.9 copy-done.1
  3.9 0.0 copy-start.2
  3.9 0.9 copy-done.2
  4.8 0.0 copy-start.3
  4.8 0.7 copy-done.3
  5.5 1.8 %setup.1 = (s32[8]{0:T(128)S(1)}, f32[6,16,32,128]{3,2,1,0:T(8,128)S(1)}, f32[16,32,128]{2,1,0:T(8,128)S(1)}, f32[16,32,128]{2,1,0:T(8,128)S(1)}, f32[16,32,128]...) custom-call(s32[1]{0:T(128)} %bitcast.place_ref, s32[4]{0:T(128)S(1)} %copy-done.3, ...), custom_call_target="tpu_custom_call" | custom-call | tf_op jit(solution)/shard_map/setup/pallas_call | solution.py:628
  7.3 7.2 %all-gather = f32[512,128]{1,0:T(8,128)S(1)} all-gather(f32[128,128]{1,0:T(8,128)S(1)} %get-tuple-element.44), channel_id=2, replica_groups=mesh['brick'=4,'grp'=8] {'brick'}, dimensions={0}, use_global_device_ids=true | all-gather | bytes 327680 | tf_op jit(solution)/shard_map/all_gather | solution.py:643
  14.5 0.8 middle_0.1
  15.3 3.4 %collective-permute-start.1 = (f32[136,128]{1,0:T(8,128)S(1)}, f32[136,128]{1,0:T(8,128)S(1)}, u32[]{:S(2)}, u32[]{:S(2)}) collective-permute-start(f32[136,128]{1,0:T(8,128)S(1)} %get-tuple-element.49), channel_id=1, source_target_pairs={{0,1},{1,2},{2,3},{3,4},{4,5},{5,6},{6,7},{8,9},{9,10},{10,11},{11... | collective-permute-start | bytes 208904 | tf_op jit(solution)/shard_map/ppermute | solution.py:660
  18.8 1.3 collective-permute-start
  20.1 5.0 %all_gather.50 = f32[16,128]{1,0:T(8,128)S(1)} all-gather(f32[8,128]{1,0:T(8,128)S(1)} %get-tuple-element.50), channel_id=1, replica_groups={{0,1},{2,3},{4,5},{6,7},{8,9},{10,11},{12,13},{14,15},{16,17},{18,19},{..., dimensions={0}, use_global_device_ids=true | all-gather | bytes 12288 | tf_op jit(solution)/shard_map/all_gather | solution.py:652
  25.1 14.7 %all_gather.51.refs_4_ = f32[64,128]{1,0:T(8,128)S(1)} all-gather(f32[16,128]{1,0:T(8,128)S(1)} %all_gather.50), channel_id=1, replica_groups={{0,2,4,6},{1,3,5,7},{8,10,12,14},{9,11,13,15},{16,18,20,22},{17,19,21,2..., dimensions={0}, use_global_device_ids=true | all-gather | bytes 40960 | tf_op jit(solution)/shard_map/all_gather | solution.py:653
  39.8 0.0 collective-permute-done.1.refs_3_
  39.8 0.0 collective-permute-done.refs_2_
  39.8 2.0 %step_0.1 = (f32[16,32,128]{2,1,0:T(8,128)S(1)}, f32[16,32,128]{2,1,0:T(8,128)S(1)}, f32[88,128]{1,0:T(8,128)S(1)}, f32[64,128]{1,0:T(8,128)S(1)}, f32[168,128]{...) custom-call(s32[8]{0:T(128)S(1)} %get-tuple-element.43.info_ref.refs_0_, ...), custom_call_target="tpu_custom_call" | custom-call | tf_op jit(solution)/shard_map/step_0/pallas_call | solution.py:628
  41.8 5.5 %all-gather.1 = f32[288,128]{1,0:T(8,128)S(1)} all-gather(f32[72,128]{1,0:T(8,128)S(1)} %get-tuple-element.53), channel_id=3, replica_groups=mesh['brick'=4,'grp'=8] {'brick'}, dimensions={0}, use_global_device_ids=true | all-gather | bytes 184320 | tf_op jit(solution)/shard_map/all_gather | solution.py:643
  47.3 0.8 middle_1.1
  48.1 2.9 %collective-permute-start.3 = (f32[104,128]{1,0:T(8,128)S(1)}, f32[104,128]{1,0:T(8,128)S(1)}, u32[]{:S(2)}, u32[]{:S(2)}) collective-permute-start(f32[104,128]{1,0:T(8,128)S(1)} %get-tuple-element.56), channel_id=1, source_target_pairs={{0,1},{1,2},{2,3},{3,4},{4,5},{5,6},{6,7},{8,9},{9,10},{10,11},{11... | collective-permute-start | bytes 159752 | tf_op jit(solution)/shard_map/ppermute | solution.py:660
  51.0 1.3 collective-permute-start.2
  52.3 5.0 %all_gather.54 = f32[16,128]{1,0:T(8,128)S(1)} all-gather(f32[8,128]{1,0:T(8,128)S(1)} %get-tuple-element.57), channel_id=1, replica_groups={{0,1},{2,3},{4,5},{6,7},{8,9},{10,11},{12,13},{14,15},{16,17},{18,19},{..., dimensions={0}, use_global_device_ids=true | all-gather | bytes 12288 | tf_op jit(solution)/shard_map/all_gather | solution.py:652
  57.3 14.6 %all_gather.55.refs_4_ = f32[64,128]{1,0:T(8,128)S(1)} all-gather(f32[16,128]{1,0:T(8,128)S(1)} %all_gather.54), channel_id=1, replica_groups={{0,2,4,6},{1,3,5,7},{8,10,12,14},{9,11,13,15},{16,18,20,22},{17,19,21,2..., dimensions={0}, use_global_device_ids=true | all-gather | bytes 40960 | tf_op jit(solution)/shard_map/all_gather | solution.py:653
  71.9 0.0 collective-permute-done.3.refs_3_
  71.9 0.0 collective-permute-done.2.refs_2_
  71.9 2.0 %step_1.1 = (f32[16,32,128]{2,1,0:T(8,128)S(1)}, f32[16,32,128]{2,1,0:T(8,128)S(1)}, f32[16,32,128]{2,1,0:T(8,128)S(1)}, f32[16,32,128]{2,1,0:T(8,128)S(1)}, f32...) custom-call(s32[8]{0:T(128)S(1)} %get-tuple-element.43.info_ref.refs, ...), custom_call_target="tpu_custom_call" | custom-call | tf_op jit(solution)/shard_map/step_1/pallas_call | solution.py:628
  73.9 5.5 %all-gather.2 = f32[288,128]{1,0:T(8,128)S(1)} all-gather(f32[72,128]{1,0:T(8,128)S(1)} %get-tuple-element.62), channel_id=4, replica_groups=mesh['brick'=4,'grp'=8] {'brick'}, dimensions={0}, use_global_device_ids=true | all-gather | bytes 184320 | tf_op jit(solution)/shard_map/all_gather | solution.py:643
  79.4 0.8 middle_2.1
  80.1 2.5 %collective-permute-start.5 = (f32[104,128]{1,0:T(8,128)S(1)}, f32[104,128]{1,0:T(8,128)S(1)}, u32[]{:S(2)}, u32[]{:S(2)}) collective-permute-start(f32[104,128]{1,0:T(8,128)S(1)} %get-tuple-element.65), channel_id=1, source_target_pairs={{0,1},{1,2},{2,3},{3,4},{4,5},{5,6},{6,7},{8,9},{9,10},{10,11},{11... | collective-permute-start | bytes 159752 | tf_op jit(solution)/shard_map/ppermute | solution.py:660
  82.6 1.3 collective-permute-start.4
  83.9 5.8 %all_gather.58 = f32[16,128]{1,0:T(8,128)S(1)} all-gather(f32[8,128]{1,0:T(8,128)S(1)} %get-tuple-element.66), channel_id=1, replica_groups={{0,1},{2,3},{4,5},{6,7},{8,9},{10,11},{12,13},{14,15},{16,17},{18,19},{..., dimensions={0}, use_global_device_ids=true | all-gather | bytes 12288 | tf_op jit(solution)/shard_map/all_gather | solution.py:652
  89.8 14.6 %all_gather.59.refs_4_ = f32[64,128]{1,0:T(8,128)S(1)} all-gather(f32[16,128]{1,0:T(8,128)S(1)} %all_gather.58), channel_id=1, replica_groups={{0,2,4,6},{1,3,5,7},{8,10,12,14},{9,11,13,15},{16,18,20,22},{17,19,21,2..., dimensions={0}, use_global_device_ids=true | all-gather | bytes 40960 | tf_op jit(solution)/shard_map/all_gather | solution.py:653
  104.4 0.0 collective-permute-done.5.refs_3_
  104.4 0.0 collective-permute-done.4.refs_2_
  104.4 1.7 %step_2.1 = (f32[16,32,128]{2,1,0:T(8,128)S(1)}, f32[16,32,128]{2,1,0:T(8,128)S(1)}, f32[16,32,128]{2,1,0:T(8,128)S(1)}, f32[16,32,128]{2,1,0:T(8,128)S(1)}, f32[8,128]{1,0:T(8,128)S(1)}, /*index=5*/f32[8,128]{1,0:T(8,128)S(1)}) custom-call(s32[8]{0:T(128)S(1)} %get-tuple-element.43.info_ref.refs_0_, f32[4,72,128]{2,1,0:T(8,128)S(1)} %bitcast.13, ...), custom_call_target="tpu_custom_call" | custom-call | tf_op jit(solution)/shard_map/step_2/pallas_call | solution.py:628
  106.1 5.2 %all-gather.3 = f32[32,128]{1,0:T(8,128)S(1)} all-gather(f32[8,128]{1,0:T(8,128)S(1)} %get-tuple-element.74), channel_id=5, replica_groups=mesh['brick'=4,'grp'=8] {'brick'}, dimensions={0}, use_global_device_ids=true | all-gather | bytes 20480 | tf_op jit(solution)/shard_map/all_gather | solution.py:643
  111.3 4.4 %all_gather.62 = f32[64,128]{1,0:T(8,128)S(1)} all-gather(f32[32,128]{1,0:T(8,128)S(1)} %all-gather.3), channel_id=1, replica_groups={{0,1},{2,3},{4,5},{6,7},{8,9},{10,11},{12,13},{14,15},{16,17},{18,19},{..., dimensions={0}, use_global_device_ids=true | all-gather | bytes 49152 | tf_op jit(solution)/shard_map/all_gather | solution.py:652
  115.7 13.3 %all_gather.63.tiles_ref = f32[256,128]{1,0:T(8,128)S(1)} all-gather(f32[64,128]{1,0:T(8,128)S(1)} %all_gather.62), channel_id=1, replica_groups={{0,2,4,6},{1,3,5,7},{8,10,12,14},{9,11,13,15},{16,18,20,22},{17,19,21,2..., dimensions={0}, use_global_device_ids=true | all-gather | bytes 163840 | tf_op jit(solution)/shard_map/all_gather | solution.py:653
  129.0 1.0 finish.1
  (1 shorter events, 0.0 us)
Async XLA Ops:
  1.5 1.4 %copy-start = (f32[1,1,6,2,32,1024]{5,4,3,2,1,0:T(8,128)S(1)}, f32[1,1,6,2,32,1024]{5,4,3,2,1,0:T(8,128)}, u32[]{:S(2)}) copy-start(f32[1,1,6,2,32,1024]{5,4,3,2,1,0:T(8,128)} %param.7) | copy-start | bytes 4718596
  2.9 0.9 copy-start.1
  3.9 0.9 copy-start.2
  4.8 0.7 copy-start.3
  15.3 24.5 %collective-permute-start.1 = (f32[136,128]{1,0:T(8,128)S(1)}, f32[136,128]{1,0:T(8,128)S(1)}, u32[]{:S(2)}, u32[]{:S(2)}) collective-permute-start(f32[136,128]{1,0:T(8,128)S(1)} %get-tuple-element.49), channel_id=1, source_target_pairs={{0,1},{1,2},{2,3},{3,4},{4,5},{5,6},{6,7},{8,9},{9,10},{10,11},{11... | collective-permute-start | bytes 208904 | tf_op jit(solution)/shard_map/ppermute | solution.py:660
  18.8 21.0 %collective-permute-start = (f32[136,128]{1,0:T(8,128)S(1)}, f32[136,128]{1,0:T(8,128)S(1)}, u32[]{:S(2)}, u32[]{:S(2)}) collective-permute-start(f32[136,128]{1,0:T(8,128)S(1)} %get-tuple-element.49), channel_id=1, source_target_pairs={{1,0},{2,1},{3,2},{4,3},{5,4},{6,5},{7,6},{9,8},{10,9},{11,10},{12... | collective-permute-start | bytes 208904 | tf_op jit(solution)/shard_map/ppermute | solution.py:660
  48.1 23.8 %collective-permute-start.3 = (f32[104,128]{1,0:T(8,128)S(1)}, f32[104,128]{1,0:T(8,128)S(1)}, u32[]{:S(2)}, u32[]{:S(2)}) collective-permute-start(f32[104,128]{1,0:T(8,128)S(1)} %get-tuple-element.56), channel_id=1, source_target_pairs={{0,1},{1,2},{2,3},{3,4},{4,5},{5,6},{6,7},{8,9},{9,10},{10,11},{11... | collective-permute-start | bytes 159752 | tf_op jit(solution)/shard_map/ppermute | solution.py:660
  51.0 20.9 %collective-permute-start.2 = (f32[104,128]{1,0:T(8,128)S(1)}, f32[104,128]{1,0:T(8,128)S(1)}, u32[]{:S(2)}, u32[]{:S(2)}) collective-permute-start(f32[104,128]{1,0:T(8,128)S(1)} %get-tuple-element.56), channel_id=1, source_target_pairs={{1,0},{2,1},{3,2},{4,3},{5,4},{6,5},{7,6},{9,8},{10,9},{11,10},{12... | collective-permute-start | bytes 159752 | tf_op jit(solution)/shard_map/ppermute | solution.py:660
  80.1 24.2 %collective-permute-start.5 = (f32[104,128]{1,0:T(8,128)S(1)}, f32[104,128]{1,0:T(8,128)S(1)}, u32[]{:S(2)}, u32[]{:S(2)}) collective-permute-start(f32[104,128]{1,0:T(8,128)S(1)} %get-tuple-element.65), channel_id=1, source_target_pairs={{0,1},{1,2},{2,3},{3,4},{4,5},{5,6},{6,7},{8,9},{9,10},{10,11},{11... | collective-permute-start | bytes 159752 | tf_op jit(solution)/shard_map/ppermute | solution.py:660
  82.6 21.7 %collective-permute-start.4 = (f32[104,128]{1,0:T(8,128)S(1)}, f32[104,128]{1,0:T(8,128)S(1)}, u32[]{:S(2)}, u32[]{:S(2)}) collective-permute-start(f32[104,128]{1,0:T(8,128)S(1)} %get-tuple-element.65), channel_id=1, source_target_pairs={{1,0},{2,1},{3,2},{4,3},{5,4},{6,5},{7,6},{9,8},{10,9},{11,10},{12... | collective-permute-start | bytes 159752 | tf_op jit(solution)/shard_map/ppermute | solution.py:660

commit v3 on v1

--- a/solution.py
+++ b/solution.py
@@ -18,10 +18,10 @@
 XY_ROWS = 72
 XY_XD, XY_YC, XY_K = 72, 88, 120
 XY_ROWS_FIRST = 128
-Z_Y1, Z_Q, Z_Y, Z_X = 0, 32, 64, 96
-Z_ROWS = 104
-Z_D = 104
-Z_ROWS_FIRST = 136
+Z_Y1, Z_Q, Z_Y, Z_X, Z_T = 0, 32, 64, 96, 104
+Z_ROWS = 112
+Z_D = 112
+Z_ROWS_FIRST = 144
 H_X1, H_XP, H_Y, H_Z1, H_ZQ, H_YZ, H_R = 0, 16, 32, 64, 96, 128, 160
 H_ROWS = 168
 C_XD, C_YC, C_ZD, C_K = 0, 16, 48, 80
@@ -317,6 +317,7 @@
         for b in range(1, bricks):
             summed = summed + xy_ref[b, XY_S : XY_S + 8]
         mixed = jnp.where(rows_of(8) < 2, mixed, summed)
+    z_ref[Z_T : Z_T + 8] = mixed
     tile_ref[...] = mixed
 
 
@@ -342,7 +343,8 @@
     last = iteration == ITERS - 1
     refs = list(refs)
     take = lambda count: [refs.pop(0) for _ in range(count)]
-    info_ref, xy_ref, above_ref, below_ref, tiles_ref = take(5)
+    info_ref, xy_ref, above_ref, below_ref = take(4)
+    shift_refs = take(slabs - 2)
     effective_ref, diagonal_ref, relax_ref, residual_ref = take(4)
     if not first:
         mapped_ref, halo_in, constant_ref, factor_ref, sums_in, scalars_in = take(6)
@@ -358,9 +360,19 @@
     xy_out = take(1)[0]
     if not last:
         partial_ref = take(1)[0]
+    tiles_ref = take(1)[0]
 
     row = info_ref[0]
     slab = info_ref[1]
+    for d in range(slabs):
+        if d == 1:
+            tile = below_ref[Z_T : Z_T + 8]
+        elif d == slabs - 1:
+            tile = above_ref[Z_T : Z_T + 8]
+        else:
+            tile = shift_refs[max(d - 1, 0)][...]
+        start = pl.multiple_of(8 * lax.rem(slab - d + slabs, slabs), 8)
+        tiles_ref[pl.ds(start, 8)] = tile
     lane = lanes()
     height = rows_of()
     depth = lane % BS
@@ -604,12 +616,15 @@
     write_xy(xy_out, row, y1, partial)
 
 
-def finish_kernel(
-    count, tiles_ref, scalars_ref, residual_ref, mapped_ref, search_ref, first_ref, second_ref, third_ref,
-    solution_ref, residual_out,
-):
+def finish_kernel(slabs, bricks, *refs):
+    tile_refs = refs[:slabs]
+    scalars_ref, residual_ref, mapped_ref, search_ref, first_ref, second_ref, third_ref = refs[slabs:-2]
+    solution_ref, residual_out = refs[-2:]
     scalars = scalars_ref[...]
-    _, _, step, growth = search_scalars(sum_tiles(tiles_ref, count), scalars, ITERS - 1)
+    tiles = sum_tiles(tile_refs[0], bricks)
+    for ref in tile_refs[1:]:
+        tiles = tiles + sum_tiles(ref, bricks)
+    _, _, step, growth = search_scalars(tiles, scalars, ITERS - 1)
     first_step, second_step, second_growth = scalars[2:3, 0:1], scalars[3:4, 0:1], scalars[4:5, 0:1]
     third_weight = step
     second_weight = second_step + growth * step
@@ -622,7 +637,7 @@
         residual_out[s, :, part] = residual_ref[c] - step * (mapped_ref[c] + growth * search_ref[c])
 
 
-def call(kernel, name, outs, operands, scalar_operands=0, scalar_outs=0):
+def call(kernel, name, outs, operands, scalar_operands=0, scalar_outs=0, scratch=()):
     vmem = pl.BlockSpec(memory_space=pltpu.VMEM)
     smem = pl.BlockSpec(memory_space=pltpu.SMEM)
     return pl.pallas_call(
@@ -630,6 +645,7 @@
         out_shape=tuple(outs),
         in_specs=[smem] * scalar_operands + [vmem] * (len(operands) - scalar_operands),
         out_specs=tuple([smem] * scalar_outs + [vmem] * (len(outs) - scalar_outs)),
+        scratch_shapes=list(scratch),
         compiler_params=pltpu.CompilerParams(vmem_limit_bytes=40 * 1024 * 1024),
         name=name,
     )(*operands)
@@ -643,15 +659,9 @@
     return lax.all_gather(message, "brick", axis=0, tiled=False)
 
 
-def gather_slabs(tile):
-    return lax.all_gather(tile, "grp", axis=0, tiled=True)
-
-
-def exchange_slabs(message):
+def shifted(block, shift):
     count = lax.axis_size("grp")
-    upward = [(i, i + 1) for i in range(count - 1)]
-    downward = [(i + 1, i) for i in range(count - 1)]
-    return lax.ppermute(message, "grp", downward), lax.ppermute(message, "grp", upward)
+    return lax.ppermute(block, "grp", [(i, (i + shift) % count) for i in range(count)])
 
 
 def on_device(source, uptake, conductance, occupancy, assignment):
@@ -683,9 +693,9 @@
             [info, gathered, mapped, relax, partial, edge],
             scalar_operands=1,
         )
-        above, below = exchange_slabs(z_message)
-        tiles = gather_slabs(tile)
-        operands = [info, gathered, above, below, tiles, effective, diagonal, relax, residual]
+        above, below = shifted(z_message, -1), shifted(z_message, 1)
+        tiles = [tile] + [shifted(tile, d) for d in range(2, slabs - 1)]
+        operands = [info, gathered, above, below] + tiles + [effective, diagonal, relax, residual]
         tall = array(8 * slabs, 128)
         outs = {"smoothed": field, "mapped": field}
         if not first:
@@ -710,6 +720,7 @@
             list(outs.values()),
             operands,
             scalar_operands=1,
+            scratch=[pltpu.VMEM((8 * slabs, 128), F32)],
         )
         state |= dict(zip(outs, results))
         if first:
@@ -717,13 +728,14 @@
         mapped, message, partial = state["mapped"], state["message"], state.get("partial")
         residual = state.get("residual", residual)
         directions.append(state["smoothed"])
-    tiles = gather_slabs(gather_bricks(message).reshape(bricks * 8, 128))
+    summed = gather_bricks(message).reshape(bricks * 8, 128)
+    tiles = [summed] + [shifted(summed, d) for d in range(1, slabs)]
     brick_pair = array(2, BS, BS * BS)
     solution_field, residual = call(
-        functools.partial(finish_kernel, slabs * bricks),
+        functools.partial(finish_kernel, slabs, bricks),
         "finish",
         [brick_pair, brick_pair],
-        [tiles, state["scalars"], residual, mapped, state["search"]] + directions,
+        tiles + [state["scalars"], residual, mapped, state["search"]] + directions,
     )
     return solution_field[None, None], residual[None, None]
 

time: 179 us -> 101 us (0.56)
  blocking collectives: 149 us -> 23.3 us
  starting transfers between devices: 13.7 us -> 37.7 us
  waiting for transfers between devices: 0.02 us -> 23.2 us
    all_gather x4 -> x0, blocking collectives: 125 us -> none  [gather_slabs(): return lax.all_gather(tile, 'grp', axis=0, tiled=True)]
    ppermute x6 -> x28, starting transfers between devices: 13.7 us -> 37.7 us  [shifted(): lax.ppermute(block, 'grp', [(i, (i + shift) % count) for i in range(count)])]
    ppermute x6 -> x28, waiting for transfers between devices: 0.02 us -> 23.2 us  [shifted(): lax.ppermute(block, 'grp', [(i, (i + shift) % count) for i in range(count)])]
  transfers between devices with their start and end apart: 6 -> 28, of which waited for: 0 -> 14; matrix products, arithmetic and copies ran while one was open for 0% -> 0% of each run, Pallas kernels for 0% -> 0%
where the time goes in v3:
time: 101 us
  starting transfers between devices  37.7 us (37%)
  blocking collectives  23.3 us (23%)
  waiting for transfers between devices  23.2 us (23%)
  Pallas kernels  10.9 us (11%)
  local copies, waits for them, and re-layouts  4.82 us (5%)
    ppermute x28, starting transfers between devices, shifted(): lax.ppermute(block, 'grp', [(i, (i + shift) % count) for i in range(count)])  37.7 us
    all_gather x4, blocking collectives, gather_bricks(): return lax.all_gather(message, 'brick', axis=0, tiled=False)  23.3 us
    ppermute x28, waiting for transfers between devices, shifted(): lax.ppermute(block, 'grp', [(i, (i + shift) % count) for i in range(count)])  23.2 us
    pallas_call x8, Pallas kernels, call(): pl.pallas_call(kernel, out_shape=tuple(outs), in_specs=[smem] * scalar_op...  10.9 us
    unnamed x9, local copies, waits for them, and re-layouts  4.73 us
  transfers between devices with their start and end apart: 28, of which 14 were waited for; matrix products, arithmetic and copies ran while one was open for 0% of the time, Pallas kernels for 0%

profile of v3, /device:TPU:0, one launch (start us, length us, event | category | flops | bytes accessed | tf_op | source)
XLA Modules:
  0.0 100.7 jit_solution(11052251345877484229)
XLA Ops:
  0.6 0.8 copy.8
  1.5 1.4 %copy-done = f32[1,1,6,2,32,1024]{5,4,3,2,1,0:T(8,128)S(1)} copy-done((f32[1,1,6,2,32,1024]{5,4,3,2,1,0:T(8,128)S(1)}, f32[1,1,6,2,32,1024]{5,4,3,2,1,0:T(8,128)}, u32[]{:S(2)}) %copy-start) | copy-done | bytes 1572888
  2.9 0.9 copy-done.1
  3.9 0.9 copy-done.2
  4.8 0.7 copy-done.3
  5.5 1.8 %setup.1 = (s32[8]{0:T(128)S(1)}, f32[6,16,32,128]{3,2,1,0:T(8,128)S(1)}, f32[16,32,128]{2,1,0:T(8,128)S(1)}, f32[16,32,128]{2,1,0:T(8,128)S(1)}, f32[16,32,128]...) custom-call(s32[1]{0:T(128)} %bitcast.place_ref, s32[4]{0:T(128)S(1)} %copy-done.3, ...), custom_call_target="tpu_custom_call" | custom-call | tf_op jit(solution)/shard_map/setup/pallas_call | solution.py:643
  7.3 7.2 %all-gather = f32[512,128]{1,0:T(8,128)S(1)} all-gather(f32[128,128]{1,0:T(8,128)S(1)} %get-tuple-element.44), channel_id=2, replica_groups=mesh['brick'=4,'grp'=8] {'brick'}, dimensions={0}, use_global_device_ids=true | all-gather | bytes 327680 | tf_op jit(solution)/shard_map/all_gather | solution.py:659
  14.5 0.8 middle_0.1
  15.3 1.6 %collective-permute-start.1 = (f32[144,128]{1,0:T(8,128)S(1)}, f32[144,128]{1,0:T(8,128)S(1)}, u32[]{:S(2)}, u32[]{:S(2)}) collective-permute-start(f32[144,128]{1,0:T(8,128)S(1)} %get-tuple-element.49), channel_id=1, source_target_pairs={{0,1},{1,2},{2,3},{3,4},{4,5},{5,6},{6,7},{7,0},{8,9},{9,10},{10,1... | collective-permute-start | bytes 221192 | tf_op jit(solution)/shard_map/ppermute | solution.py:664
  16.9 3.2 %collective-permute-start = (f32[144,128]{1,0:T(8,128)S(1)}, f32[144,128]{1,0:T(8,128)S(1)}, u32[]{:S(2)}, u32[]{:S(2)}) collective-permute-start(f32[144,128]{1,0:T(8,128)S(1)} %get-tuple-element.49), channel_id=1, source_target_pairs={{0,7},{1,0},{2,1},{3,2},{4,3},{5,4},{6,5},{7,6},{8,15},{9,8},{10,9... | collective-permute-start | bytes 221192 | tf_op jit(solution)/shard_map/ppermute | solution.py:664
  20.1 1.8 %collective-permute-start.6 = (f32[8,128]{1,0:T(8,128)S(1)}, f32[8,128]{1,0:T(8,128)S(1)}, u32[]{:S(2)}, u32[]{:S(2)}) collective-permute-start(f32[8,128]{1,0:T(8,128)S(1)} %get-tuple-element.50.refs_4_), channel_id=1, source_target_pairs={{0,6},{1,7},{2,0},{3,1},{4,2},{5,3},{6,4},{7,5},{8,14},{9,15},{10,... | collective-permute-start | bytes 12296 | tf_op jit(solution)/shard_map/ppermute | solution.py:664
  21.9 3.0 %collective-permute-start.4 = (f32[8,128]{1,0:T(8,128)S(1)}, f32[8,128]{1,0:T(8,128)S(1)}, u32[]{:S(2)}, u32[]{:S(2)}) collective-permute-start(f32[8,128]{1,0:T(8,128)S(1)} %get-tuple-element.50.refs_4_), channel_id=1, source_target_pairs={{0,4},{1,5},{2,6},{3,7},{4,0},{5,1},{6,2},{7,3},{8,12},{9,13},{10,... | collective-permute-start | bytes 12296 | tf_op jit(solution)/shard_map/ppermute | solution.py:664
  24.9 1.5 %collective-permute-done.5.refs_8_ = f32[8,128]{1,0:T(8,128)S(1)} collective-permute-done((f32[8,128]{1,0:T(8,128)S(1)}, f32[8,128]{1,0:T(8,128)S(1)}, u32[]{:S(2)}, u32[]{:S(2)}) %collective-permute-start.5) | collective-permute-done | bytes 4128 | tf_op jit(solution)/shard_map/ppermute | solution.py:664
  26.8 3.5 %collective-permute-done.3.refs_6_ = f32[8,128]{1,0:T(8,128)S(1)} collective-permute-done((f32[8,128]{1,0:T(8,128)S(1)}, f32[8,128]{1,0:T(8,128)S(1)}, u32[]{:S(2)}, u32[]{:S(2)}) %collective-permute-start.3) | collective-permute-done | bytes 4128 | tf_op jit(solution)/shard_map/ppermute | solution.py:664
  30.3 1.5 %collective-permute-done.2.refs_5_ = f32[8,128]{1,0:T(8,128)S(1)} collective-permute-done((f32[8,128]{1,0:T(8,128)S(1)}, f32[8,128]{1,0:T(8,128)S(1)}, u32[]{:S(2)}, u32[]{:S(2)}) %collective-permute-start.2) | collective-permute-done | bytes 4128 | tf_op jit(solution)/shard_map/ppermute | solution.py:664
  31.9 2.0 %step_0.1 = (f32[16,32,128]{2,1,0:T(8,128)S(1)}, f32[16,32,128]{2,1,0:T(8,128)S(1)}, f32[88,128]{1,0:T(8,128)S(1)}, f32[64,128]{1,0:T(8,128)S(1)}, f32[168,128]{...) custom-call(s32[8]{0:T(128)S(1)} %get-tuple-element.43.info_ref.refs_0_, ...), custom_call_target="tpu_custom_call" | custom-call | tf_op jit(solution)/shard_map/step_0/pallas_call | solution.py:643
  33.9 5.5 %all-gather.1 = f32[288,128]{1,0:T(8,128)S(1)} all-gather(f32[72,128]{1,0:T(8,128)S(1)} %get-tuple-element.53), channel_id=3, replica_groups=mesh['brick'=4,'grp'=8] {'brick'}, dimensions={0}, use_global_device_ids=true | all-gather | bytes 184320 | tf_op jit(solution)/shard_map/all_gather | solution.py:659
  39.3 0.8 middle_1.1
  40.1 1.5 %collective-permute-start.8 = (f32[112,128]{1,0:T(8,128)S(1)}, f32[112,128]{1,0:T(8,128)S(1)}, u32[]{:S(2)}, u32[]{:S(2)}) collective-permute-start(f32[112,128]{1,0:T(8,128)S(1)} %get-tuple-element.56), channel_id=1, source_target_pairs={{0,1},{1,2},{2,3},{3,4},{4,5},{5,6},{6,7},{7,0},{8,9},{9,10},{10,1... | collective-permute-start | bytes 172040 | tf_op jit(solution)/shard_map/ppermute | solution.py:664
  41.7 3.2 %collective-permute-start.7 = (f32[112,128]{1,0:T(8,128)S(1)}, f32[112,128]{1,0:T(8,128)S(1)}, u32[]{:S(2)}, u32[]{:S(2)}) collective-permute-start(f32[112,128]{1,0:T(8,128)S(1)} %get-tuple-element.56), channel_id=1, source_target_pairs={{0,7},{1,0},{2,1},{3,2},{4,3},{5,4},{6,5},{7,6},{8,15},{9,8},{10,9... | collective-permute-start | bytes 172040 | tf_op jit(solution)/shard_map/ppermute | solution.py:664
  44.9 2.9 %collective-permute-start.11 = (f32[8,128]{1,0:T(8,128)S(1)}, f32[8,128]{1,0:T(8,128)S(1)}, u32[]{:S(2)}, u32[]{:S(2)}) collective-permute-start(f32[8,128]{1,0:T(8,128)S(1)} %get-tuple-element.57.refs_4_), channel_id=1, source_target_pairs={{0,4},{1,5},{2,6},{3,7},{4,0},{5,1},{6,2},{7,3},{8,12},{9,13},{10,... | collective-permute-start | bytes 12296 | tf_op jit(solution)/shard_map/ppermute | solution.py:664
  47.8 0.7 collective-permute-done.13.refs_9_
  48.5 0.9 collective-permute-done.12.refs_8_
  49.4 2.0 %collective-permute-start.9 = (f32[8,128]{1,0:T(8,128)S(1)}, f32[8,128]{1,0:T(8,128)S(1)}, u32[]{:S(2)}, u32[]{:S(2)}) collective-permute-start(f32[8,128]{1,0:T(8,128)S(1)} %get-tuple-element.57.refs_4_), channel_id=1, source_target_pairs={{0,2},{1,3},{2,4},{3,5},{4,6},{5,7},{6,0},{7,1},{8,10},{9,11},{10,... | collective-permute-start | bytes 12296 | tf_op jit(solution)/shard_map/ppermute | solution.py:664
  51.4 2.5 %collective-permute-done.10.refs_6_ = f32[8,128]{1,0:T(8,128)S(1)} collective-permute-done((f32[8,128]{1,0:T(8,128)S(1)}, f32[8,128]{1,0:T(8,128)S(1)}, u32[]{:S(2)}, u32[]{:S(2)}) %collective-permute-start.10) | collective-permute-done | bytes 4128 | tf_op jit(solution)/shard_map/ppermute | solution.py:664
  53.9 0.9 collective-permute-done.9.refs_5_
  54.8 2.1 %step_1.1 = (f32[16,32,128]{2,1,0:T(8,128)S(1)}, f32[16,32,128]{2,1,0:T(8,128)S(1)}, f32[16,32,128]{2,1,0:T(8,128)S(1)}, f32[16,32,128]{2,1,0:T(8,128)S(1)}, f32...) custom-call(s32[8]{0:T(128)S(1)} %get-tuple-element.43.info_ref.refs, ...), custom_call_target="tpu_custom_call" | custom-call | tf_op jit(solution)/shard_map/step_1/pallas_call | solution.py:643
  56.9 5.5 %all-gather.2 = f32[288,128]{1,0:T(8,128)S(1)} all-gather(f32[72,128]{1,0:T(8,128)S(1)} %get-tuple-element.62), channel_id=4, replica_groups=mesh['brick'=4,'grp'=8] {'brick'}, dimensions={0}, use_global_device_ids=true | all-gather | bytes 184320 | tf_op jit(solution)/shard_map/all_gather | solution.py:659
  62.4 0.8 middle_2.1
  63.1 1.6 %collective-permute-start.15 = (f32[112,128]{1,0:T(8,128)S(1)}, f32[112,128]{1,0:T(8,128)S(1)}, u32[]{:S(2)}, u32[]{:S(2)}) collective-permute-start(f32[112,128]{1,0:T(8,128)S(1)} %get-tuple-element.65), channel_id=1, source_target_pairs={{0,1},{1,2},{2,3},{3,4},{4,5},{5,6},{6,7},{7,0},{8,9},{9,10},{10,1... | collective-permute-start | bytes 172040 | tf_op jit(solution)/shard_map/ppermute | solution.py:664
  64.7 3.2 %collective-permute-start.14 = (f32[112,128]{1,0:T(8,128)S(1)}, f32[112,128]{1,0:T(8,128)S(1)}, u32[]{:S(2)}, u32[]{:S(2)}) collective-permute-start(f32[112,128]{1,0:T(8,128)S(1)} %get-tuple-element.65), channel_id=1, source_target_pairs={{0,7},{1,0},{2,1},{3,2},{4,3},{5,4},{6,5},{7,6},{8,15},{9,8},{10,9... | collective-permute-start | bytes 172040 | tf_op jit(solution)/shard_map/ppermute | solution.py:664
  68.0 2.8 %collective-permute-start.18 = (f32[8,128]{1,0:T(8,128)S(1)}, f32[8,128]{1,0:T(8,128)S(1)}, u32[]{:S(2)}, u32[]{:S(2)}) collective-permute-start(f32[8,128]{1,0:T(8,128)S(1)} %get-tuple-element.66.refs_4_), channel_id=1, source_target_pairs={{0,4},{1,5},{2,6},{3,7},{4,0},{5,1},{6,2},{7,3},{8,12},{9,13},{10,... | collective-permute-start | bytes 12296 | tf_op jit(solution)/shard_map/ppermute | solution.py:664
  70.8 0.7 collective-permute-done.20.refs_9_
  71.5 1.0 %collective-permute-done.19.refs_8_ = f32[8,128]{1,0:T(8,128)S(1)} collective-permute-done((f32[8,128]{1,0:T(8,128)S(1)}, f32[8,128]{1,0:T(8,128)S(1)}, u32[]{:S(2)}, u32[]{:S(2)}) %collective-permute-start.19) | collective-permute-done | bytes 4128 | tf_op jit(solution)/shard_map/ppermute | solution.py:664
  72.5 1.9 %collective-permute-start.16 = (f32[8,128]{1,0:T(8,128)S(1)}, f32[8,128]{1,0:T(8,128)S(1)}, u32[]{:S(2)}, u32[]{:S(2)}) collective-permute-start(f32[8,128]{1,0:T(8,128)S(1)} %get-tuple-element.66.refs_4_), channel_id=1, source_target_pairs={{0,2},{1,3},{2,4},{3,5},{4,6},{5,7},{6,0},{7,1},{8,10},{9,11},{10,... | collective-permute-start | bytes 12296 | tf_op jit(solution)/shard_map/ppermute | solution.py:664
  74.5 2.5 %collective-permute-done.17.refs_6_ = f32[8,128]{1,0:T(8,128)S(1)} collective-permute-done((f32[8,128]{1,0:T(8,128)S(1)}, f32[8,128]{1,0:T(8,128)S(1)}, u32[]{:S(2)}, u32[]{:S(2)}) %collective-permute-start.17) | collective-permute-done | bytes 4128 | tf_op jit(solution)/shard_map/ppermute | solution.py:664
  76.9 1.0 %collective-permute-done.16.refs_5_ = f32[8,128]{1,0:T(8,128)S(1)} collective-permute-done((f32[8,128]{1,0:T(8,128)S(1)}, f32[8,128]{1,0:T(8,128)S(1)}, u32[]{:S(2)}, u32[]{:S(2)}) %collective-permute-start.16) | collective-permute-done | bytes 4128 | tf_op jit(solution)/shard_map/ppermute | solution.py:664
  78.0 1.7 %step_2.1 = (f32[16,32,128]{2,1,0:T(8,128)S(1)}, f32[16,32,128]{2,1,0:T(8,128)S(1)}, f32[16,32,128]{2,1,0:T(8,128)S(1)}, f32[16,32,128]{2,1,0:T(8,128)S(1)}, f32[8,128]{1,0:T(8,128)S(1)}, /*index=5*/f32[8,128]{1,0:T(8,128)S(1)}) custom-call(s32[8]{0:T(128)S(1)} %get-tuple-element.43.info_ref.refs_0_, f32[4,72,128]{2,1,0:T(8,128)S(1)} %bitcast.13, ...), custom_call_target="tpu_custom_call" | custom-call | tf_op jit(solution)/shard_map/step_2/pallas_call | solution.py:643
  79.7 5.2 %all-gather.3.refs_0_ = f32[32,128]{1,0:T(8,128)S(1)} all-gather(f32[8,128]{1,0:T(8,128)S(1)} %get-tuple-element.74), channel_id=5, replica_groups=mesh['brick'=4,'grp'=8] {'brick'}, dimensions={0}, use_global_device_ids=true | all-gather | bytes 20480 | tf_op jit(solution)/shard_map/all_gather | solution.py:659
  84.9 0.6 collective-permute-start.27
  85.5 1.9 %collective-permute-start.26 = (f32[32,128]{1,0:T(8,128)S(1)}, f32[32,128]{1,0:T(8,128)S(1)}, u32[]{:S(2)}, u32[]{:S(2)}) collective-permute-start(f32[32,128]{1,0:T(8,128)S(1)} %all-gather.3.refs_0_), channel_id=1, source_target_pairs={{0,6},{1,7},{2,0},{3,1},{4,2},{5,3},{6,4},{7,5},{8,14},{9,15},{10,... | collective-permute-start | bytes 49160 | tf_op jit(solution)/shard_map/ppermute | solution.py:664
  87.9 3.1 %collective-permute-start.24 = (f32[32,128]{1,0:T(8,128)S(1)}, f32[32,128]{1,0:T(8,128)S(1)}, u32[]{:S(2)}, u32[]{:S(2)}) collective-permute-start(f32[32,128]{1,0:T(8,128)S(1)} %all-gather.3.refs_0_), channel_id=1, source_target_pairs={{0,4},{1,5},{2,6},{3,7},{4,0},{5,1},{6,2},{7,3},{8,12},{9,13},{10,... | collective-permute-start | bytes 49160 | tf_op jit(solution)/shard_map/ppermute | solution.py:664
  91.0 1.1 %collective-permute-start.23 = (f32[32,128]{1,0:T(8,128)S(1)}, f32[32,128]{1,0:T(8,128)S(1)}, u32[]{:S(2)}, u32[]{:S(2)}) collective-permute-start(f32[32,128]{1,0:T(8,128)S(1)} %all-gather.3.refs_0_), channel_id=1, source_target_pairs={{0,3},{1,4},{2,5},{3,6},{4,7},{5,0},{6,1},{7,2},{8,11},{9,12},{10,... | collective-permute-start | bytes 49160 | tf_op jit(solution)/shard_map/ppermute | solution.py:664
  92.1 1.2 %collective-permute-start.22 = (f32[32,128]{1,0:T(8,128)S(1)}, f32[32,128]{1,0:T(8,128)S(1)}, u32[]{:S(2)}, u32[]{:S(2)}) collective-permute-start(f32[32,128]{1,0:T(8,128)S(1)} %all-gather.3.refs_0_), channel_id=1, source_target_pairs={{0,2},{1,3},{2,4},{3,5},{4,6},{5,7},{6,0},{7,1},{8,10},{9,11},{10,... | collective-permute-start | bytes 49160 | tf_op jit(solution)/shard_map/ppermute | solution.py:664
  93.3 3.3 %collective-permute-done.23.refs_3_ = f32[32,128]{1,0:T(8,128)S(1)} collective-permute-done((f32[32,128]{1,0:T(8,128)S(1)}, f32[32,128]{1,0:T(8,128)S(1)}, u32[]{:S(2)}, u32[]{:S(2)}) %collective-permute-start.23) | collective-permute-done | bytes 16416 | tf_op jit(solution)/shard_map/ppermute | solution.py:664
  96.6 1.1 %collective-permute-done.22.refs_2_ = f32[32,128]{1,0:T(8,128)S(1)} collective-permute-done((f32[32,128]{1,0:T(8,128)S(1)}, f32[32,128]{1,0:T(8,128)S(1)}, u32[]{:S(2)}, u32[]{:S(2)}) %collective-permute-start.22) | collective-permute-done | bytes 16416 | tf_op jit(solution)/shard_map/ppermute | solution.py:664
  97.6 2.1 %collective-permute-done.21.refs_1_ = f32[32,128]{1,0:T(8,128)S(1)} collective-permute-done((f32[32,128]{1,0:T(8,128)S(1)}, f32[32,128]{1,0:T(8,128)S(1)}, u32[]{:S(2)}, u32[]{:S(2)}) %collective-permute-start.21) | collective-permute-done | bytes 16416 | tf_op jit(solution)/shard_map/ppermute | solution.py:664
  99.7 1.0 finish.1
  (31 shorter events, 1.2 us)
Async XLA Ops:
  1.5 1.4 %copy-start = (f32[1,1,6,2,32,1024]{5,4,3,2,1,0:T(8,128)S(1)}, f32[1,1,6,2,32,1024]{5,4,3,2,1,0:T(8,128)}, u32[]{:S(2)}) copy-start(f32[1,1,6,2,32,1024]{5,4,3,2,1,0:T(8,128)} %param.7) | copy-start | bytes 4718596
  2.9 0.9 copy-start.1
  3.9 0.9 copy-start.2
  4.8 0.7 copy-start.3
  15.3 16.5 %collective-permute-start.1 = (f32[144,128]{1,0:T(8,128)S(1)}, f32[144,128]{1,0:T(8,128)S(1)}, u32[]{:S(2)}, u32[]{:S(2)}) collective-permute-start(f32[144,128]{1,0:T(8,128)S(1)} %get-tuple-element.49), channel_id=1, source_target_pairs={{0,1},{1,2},{2,3},{3,4},{4,5},{5,6},{6,7},{7,0},{8,9},{9,10},{10,1... | collective-permute-start | bytes 221192 | tf_op jit(solution)/shard_map/ppermute | solution.py:664
  16.9 15.0 %collective-permute-start = (f32[144,128]{1,0:T(8,128)S(1)}, f32[144,128]{1,0:T(8,128)S(1)}, u32[]{:S(2)}, u32[]{:S(2)}) collective-permute-start(f32[144,128]{1,0:T(8,128)S(1)} %get-tuple-element.49), channel_id=1, source_target_pairs={{0,7},{1,0},{2,1},{3,2},{4,3},{5,4},{6,5},{7,6},{8,15},{9,8},{10,9... | collective-permute-start | bytes 221192 | tf_op jit(solution)/shard_map/ppermute | solution.py:664
  20.1 4.8 %collective-permute-start.6 = (f32[8,128]{1,0:T(8,128)S(1)}, f32[8,128]{1,0:T(8,128)S(1)}, u32[]{:S(2)}, u32[]{:S(2)}) collective-permute-start(f32[8,128]{1,0:T(8,128)S(1)} %get-tuple-element.50.refs_4_), channel_id=1, source_target_pairs={{0,6},{1,7},{2,0},{3,1},{4,2},{5,3},{6,4},{7,5},{8,14},{9,15},{10,... | collective-permute-start | bytes 12296 | tf_op jit(solution)/shard_map/ppermute | solution.py:664
  21.9 4.5 %collective-permute-start.5 = (f32[8,128]{1,0:T(8,128)S(1)}, f32[8,128]{1,0:T(8,128)S(1)}, u32[]{:S(2)}, u32[]{:S(2)}) collective-permute-start(f32[8,128]{1,0:T(8,128)S(1)} %get-tuple-element.50.refs_4_), channel_id=1, source_target_pairs={{0,5},{1,6},{2,7},{3,0},{4,1},{5,2},{6,3},{7,4},{8,13},{9,14},{10,... | collective-permute-start | bytes 12296 | tf_op jit(solution)/shard_map/ppermute | solution.py:664
  21.9 4.8 %collective-permute-start.4 = (f32[8,128]{1,0:T(8,128)S(1)}, f32[8,128]{1,0:T(8,128)S(1)}, u32[]{:S(2)}, u32[]{:S(2)}) collective-permute-start(f32[8,128]{1,0:T(8,128)S(1)} %get-tuple-element.50.refs_4_), channel_id=1, source_target_pairs={{0,4},{1,5},{2,6},{3,7},{4,0},{5,1},{6,2},{7,3},{8,12},{9,13},{10,... | collective-permute-start | bytes 12296 | tf_op jit(solution)/shard_map/ppermute | solution.py:664
  24.9 5.4 %collective-permute-start.3 = (f32[8,128]{1,0:T(8,128)S(1)}, f32[8,128]{1,0:T(8,128)S(1)}, u32[]{:S(2)}, u32[]{:S(2)}) collective-permute-start(f32[8,128]{1,0:T(8,128)S(1)} %get-tuple-element.50.refs_4_), channel_id=1, source_target_pairs={{0,3},{1,4},{2,5},{3,6},{4,7},{5,0},{6,1},{7,2},{8,11},{9,12},{10,... | collective-permute-start | bytes 12296 | tf_op jit(solution)/shard_map/ppermute | solution.py:664
  26.4 5.4 %collective-permute-start.2 = (f32[8,128]{1,0:T(8,128)S(1)}, f32[8,128]{1,0:T(8,128)S(1)}, u32[]{:S(2)}, u32[]{:S(2)}) collective-permute-start(f32[8,128]{1,0:T(8,128)S(1)} %get-tuple-element.50.refs_4_), channel_id=1, source_target_pairs={{0,2},{1,3},{2,4},{3,5},{4,6},{5,7},{6,0},{7,1},{8,10},{9,11},{10,... | collective-permute-start | bytes 12296 | tf_op jit(solution)/shard_map/ppermute | solution.py:664
  40.1 14.7 %collective-permute-start.8 = (f32[112,128]{1,0:T(8,128)S(1)}, f32[112,128]{1,0:T(8,128)S(1)}, u32[]{:S(2)}, u32[]{:S(2)}) collective-permute-start(f32[112,128]{1,0:T(8,128)S(1)} %get-tuple-element.56), channel_id=1, source_target_pairs={{0,1},{1,2},{2,3},{3,4},{4,5},{5,6},{6,7},{7,0},{8,9},{9,10},{10,1... | collective-permute-start | bytes 172040 | tf_op jit(solution)/shard_map/ppermute | solution.py:664
  41.7 13.2 %collective-permute-start.7 = (f32[112,128]{1,0:T(8,128)S(1)}, f32[112,128]{1,0:T(8,128)S(1)}, u32[]{:S(2)}, u32[]{:S(2)}) collective-permute-start(f32[112,128]{1,0:T(8,128)S(1)} %get-tuple-element.56), channel_id=1, source_target_pairs={{0,7},{1,0},{2,1},{3,2},{4,3},{5,4},{6,5},{7,6},{8,15},{9,8},{10,9... | collective-permute-start | bytes 172040 | tf_op jit(solution)/shard_map/ppermute | solution.py:664
  44.9 3.6 %collective-permute-start.13 = (f32[8,128]{1,0:T(8,128)S(1)}, f32[8,128]{1,0:T(8,128)S(1)}, u32[]{:S(2)}, u32[]{:S(2)}) collective-permute-start(f32[8,128]{1,0:T(8,128)S(1)} %get-tuple-element.57.refs_4_), channel_id=1, source_target_pairs={{0,6},{1,7},{2,0},{3,1},{4,2},{5,3},{6,4},{7,5},{8,14},{9,15},{10,... | collective-permute-start | bytes 12296 | tf_op jit(solution)/shard_map/ppermute | solution.py:664
  44.9 4.5 %collective-permute-start.12 = (f32[8,128]{1,0:T(8,128)S(1)}, f32[8,128]{1,0:T(8,128)S(1)}, u32[]{:S(2)}, u32[]{:S(2)}) collective-permute-start(f32[8,128]{1,0:T(8,128)S(1)} %get-tuple-element.57.refs_4_), channel_id=1, source_target_pairs={{0,5},{1,6},{2,7},{3,0},{4,1},{5,2},{6,3},{7,4},{8,13},{9,14},{10,... | collective-permute-start | bytes 12296 | tf_op jit(solution)/shard_map/ppermute | solution.py:664
  44.9 6.5 %collective-permute-start.11 = (f32[8,128]{1,0:T(8,128)S(1)}, f32[8,128]{1,0:T(8,128)S(1)}, u32[]{:S(2)}, u32[]{:S(2)}) collective-permute-start(f32[8,128]{1,0:T(8,128)S(1)} %get-tuple-element.57.refs_4_), channel_id=1, source_target_pairs={{0,4},{1,5},{2,6},{3,7},{4,0},{5,1},{6,2},{7,3},{8,12},{9,13},{10,... | collective-permute-start | bytes 12296 | tf_op jit(solution)/shard_map/ppermute | solution.py:664
  48.5 5.4 %collective-permute-start.10 = (f32[8,128]{1,0:T(8,128)S(1)}, f32[8,128]{1,0:T(8,128)S(1)}, u32[]{:S(2)}, u32[]{:S(2)}) collective-permute-start(f32[8,128]{1,0:T(8,128)S(1)} %get-tuple-element.57.refs_4_), channel_id=1, source_target_pairs={{0,3},{1,4},{2,5},{3,6},{4,7},{5,0},{6,1},{7,2},{8,11},{9,12},{10,... | collective-permute-start | bytes 12296 | tf_op jit(solution)/shard_map/ppermute | solution.py:664
  49.4 5.4 %collective-permute-start.9 = (f32[8,128]{1,0:T(8,128)S(1)}, f32[8,128]{1,0:T(8,128)S(1)}, u32[]{:S(2)}, u32[]{:S(2)}) collective-permute-start(f32[8,128]{1,0:T(8,128)S(1)} %get-tuple-element.57.refs_4_), channel_id=1, source_target_pairs={{0,2},{1,3},{2,4},{3,5},{4,6},{5,7},{6,0},{7,1},{8,10},{9,11},{10,... | collective-permute-start | bytes 12296 | tf_op jit(solution)/shard_map/ppermute | solution.py:664
  63.1 14.8 %collective-permute-start.15 = (f32[112,128]{1,0:T(8,128)S(1)}, f32[112,128]{1,0:T(8,128)S(1)}, u32[]{:S(2)}, u32[]{:S(2)}) collective-permute-start(f32[112,128]{1,0:T(8,128)S(1)} %get-tuple-element.65), channel_id=1, source_target_pairs={{0,1},{1,2},{2,3},{3,4},{4,5},{5,6},{6,7},{7,0},{8,9},{9,10},{10,1... | collective-permute-start | bytes 172040 | tf_op jit(solution)/shard_map/ppermute | solution.py:664
  64.7 13.3 %collective-permute-start.14 = (f32[112,128]{1,0:T(8,128)S(1)}, f32[112,128]{1,0:T(8,128)S(1)}, u32[]{:S(2)}, u32[]{:S(2)}) collective-permute-start(f32[112,128]{1,0:T(8,128)S(1)} %get-tuple-element.65), channel_id=1, source_target_pairs={{0,7},{1,0},{2,1},{3,2},{4,3},{5,4},{6,5},{7,6},{8,15},{9,8},{10,9... | collective-permute-start | bytes 172040 | tf_op jit(solution)/shard_map/ppermute | solution.py:664
  67.9 3.6 %collective-permute-start.20 = (f32[8,128]{1,0:T(8,128)S(1)}, f32[8,128]{1,0:T(8,128)S(1)}, u32[]{:S(2)}, u32[]{:S(2)}) collective-permute-start(f32[8,128]{1,0:T(8,128)S(1)} %get-tuple-element.66.refs_4_), channel_id=1, source_target_pairs={{0,6},{1,7},{2,0},{3,1},{4,2},{5,3},{6,4},{7,5},{8,14},{9,15},{10,... | collective-permute-start | bytes 12296 | tf_op jit(solution)/shard_map/ppermute | solution.py:664
  68.0 4.5 %collective-permute-start.19 = (f32[8,128]{1,0:T(8,128)S(1)}, f32[8,128]{1,0:T(8,128)S(1)}, u32[]{:S(2)}, u32[]{:S(2)}) collective-permute-start(f32[8,128]{1,0:T(8,128)S(1)} %get-tuple-element.66.refs_4_), channel_id=1, source_target_pairs={{0,5},{1,6},{2,7},{3,0},{4,1},{5,2},{6,3},{7,4},{8,13},{9,14},{10,... | collective-permute-start | bytes 12296 | tf_op jit(solution)/shard_map/ppermute | solution.py:664
  68.0 6.4 %collective-permute-start.18 = (f32[8,128]{1,0:T(8,128)S(1)}, f32[8,128]{1,0:T(8,128)S(1)}, u32[]{:S(2)}, u32[]{:S(2)}) collective-permute-start(f32[8,128]{1,0:T(8,128)S(1)} %get-tuple-element.66.refs_4_), channel_id=1, source_target_pairs={{0,4},{1,5},{2,6},{3,7},{4,0},{5,1},{6,2},{7,3},{8,12},{9,13},{10,... | collective-permute-start | bytes 12296 | tf_op jit(solution)/shard_map/ppermute | solution.py:664
  71.5 5.4 %collective-permute-start.17 = (f32[8,128]{1,0:T(8,128)S(1)}, f32[8,128]{1,0:T(8,128)S(1)}, u32[]{:S(2)}, u32[]{:S(2)}) collective-permute-start(f32[8,128]{1,0:T(8,128)S(1)} %get-tuple-element.66.refs_4_), channel_id=1, source_target_pairs={{0,3},{1,4},{2,5},{3,6},{4,7},{5,0},{6,1},{7,2},{8,11},{9,12},{10,... | collective-permute-start | bytes 12296 | tf_op jit(solution)/shard_map/ppermute | solution.py:664
  72.5 5.4 %collective-permute-start.16 = (f32[8,128]{1,0:T(8,128)S(1)}, f32[8,128]{1,0:T(8,128)S(1)}, u32[]{:S(2)}, u32[]{:S(2)}) collective-permute-start(f32[8,128]{1,0:T(8,128)S(1)} %get-tuple-element.66.refs_4_), channel_id=1, source_target_pairs={{0,2},{1,3},{2,4},{3,5},{4,6},{5,7},{6,0},{7,1},{8,10},{9,11},{10,... | collective-permute-start | bytes 12296 | tf_op jit(solution)/shard_map/ppermute | solution.py:664
  84.9 7.2 %collective-permute-start.27 = (f32[32,128]{1,0:T(8,128)S(1)}, f32[32,128]{1,0:T(8,128)S(1)}, u32[]{:S(2)}, u32[]{:S(2)}) collective-permute-start(f32[32,128]{1,0:T(8,128)S(1)} %all-gather.3.refs_0_), channel_id=1, source_target_pairs={{0,7},{1,0},{2,1},{3,2},{4,3},{5,4},{6,5},{7,6},{8,15},{9,8},{10,9... | collective-permute-start | bytes 49160 | tf_op jit(solution)/shard_map/ppermute | solution.py:664
  85.5 7.8 %collective-permute-start.26 = (f32[32,128]{1,0:T(8,128)S(1)}, f32[32,128]{1,0:T(8,128)S(1)}, u32[]{:S(2)}, u32[]{:S(2)}) collective-permute-start(f32[32,128]{1,0:T(8,128)S(1)} %all-gather.3.refs_0_), channel_id=1, source_target_pairs={{0,6},{1,7},{2,0},{3,1},{4,2},{5,3},{6,4},{7,5},{8,14},{9,15},{10,... | collective-permute-start | bytes 49160 | tf_op jit(solution)/shard_map/ppermute | solution.py:664
  87.3 6.0 %collective-permute-start.25 = (f32[32,128]{1,0:T(8,128)S(1)}, f32[32,128]{1,0:T(8,128)S(1)}, u32[]{:S(2)}, u32[]{:S(2)}) collective-permute-start(f32[32,128]{1,0:T(8,128)S(1)} %all-gather.3.refs_0_), channel_id=1, source_target_pairs={{0,5},{1,6},{2,7},{3,0},{4,1},{5,2},{6,3},{7,4},{8,13},{9,14},{10,... | collective-permute-start | bytes 49160 | tf_op jit(solution)/shard_map/ppermute | solution.py:664
  87.9 5.4 %collective-permute-start.24 = (f32[32,128]{1,0:T(8,128)S(1)}, f32[32,128]{1,0:T(8,128)S(1)}, u32[]{:S(2)}, u32[]{:S(2)}) collective-permute-start(f32[32,128]{1,0:T(8,128)S(1)} %all-gather.3.refs_0_), channel_id=1, source_target_pairs={{0,4},{1,5},{2,6},{3,7},{4,0},{5,1},{6,2},{7,3},{8,12},{9,13},{10,... | collective-permute-start | bytes 49160 | tf_op jit(solution)/shard_map/ppermute | solution.py:664
  91.0 5.5 %collective-permute-start.23 = (f32[32,128]{1,0:T(8,128)S(1)}, f32[32,128]{1,0:T(8,128)S(1)}, u32[]{:S(2)}, u32[]{:S(2)}) collective-permute-start(f32[32,128]{1,0:T(8,128)S(1)} %all-gather.3.refs_0_), channel_id=1, source_target_pairs={{0,3},{1,4},{2,5},{3,6},{4,7},{5,0},{6,1},{7,2},{8,11},{9,12},{10,... | collective-permute-start | bytes 49160 | tf_op jit(solution)/shard_map/ppermute | solution.py:664
  92.1 5.5 %collective-permute-start.22 = (f32[32,128]{1,0:T(8,128)S(1)}, f32[32,128]{1,0:T(8,128)S(1)}, u32[]{:S(2)}, u32[]{:S(2)}) collective-permute-start(f32[32,128]{1,0:T(8,128)S(1)} %all-gather.3.refs_0_), channel_id=1, source_target_pairs={{0,2},{1,3},{2,4},{3,5},{4,6},{5,7},{6,0},{7,1},{8,10},{9,11},{10,... | collective-permute-start | bytes 49160 | tf_op jit(solution)/shard_map/ppermute | solution.py:664
  93.3 6.4 %collective-permute-start.21 = (f32[32,128]{1,0:T(8,128)S(1)}, f32[32,128]{1,0:T(8,128)S(1)}, u32[]{:S(2)}, u32[]{:S(2)}) collective-permute-start(f32[32,128]{1,0:T(8,128)S(1)} %all-gather.3.refs_0_), channel_id=1, source_target_pairs={{0,1},{1,2},{2,3},{3,4},{4,5},{5,6},{6,7},{7,0},{8,9},{9,10},{10,1... | collective-permute-start | bytes 49160 | tf_op jit(solution)/shard_map/ppermute | solution.py:664

commit v4 on v1

--- a/solution.py
+++ b/solution.py
@@ -317,7 +317,8 @@
         for b in range(1, bricks):
             summed = summed + xy_ref[b, XY_S : XY_S + 8]
         mixed = jnp.where(rows_of(8) < 2, mixed, summed)
-    tile_ref[...] = mixed
+    for g in range(tile_ref.shape[0] // 8):
+        tile_ref[8 * g : 8 * g + 8] = mixed
 
 
 def search_scalars(tiles, scalars, iteration):
@@ -592,6 +593,9 @@
         values.append(total_of([search_ref[c] * smoothed[c] for c in range(CHUNKS)]))
     if last:
         write_scalars(xy_out, 0, values)
+        tile = xy_out[0:8]
+        for k in range(1, slabs * bricks):
+            xy_out[8 * k : 8 * k + 8] = tile
         return
     write_scalars(xy_out, XY_S, values)
     y1 = [relax_ref[c] * mapped[c] for c in range(CHUNKS)]
@@ -605,11 +609,12 @@
 
 
 def finish_kernel(
-    count, tiles_ref, scalars_ref, residual_ref, mapped_ref, search_ref, first_ref, second_ref, third_ref,
+    tiles_ref, scalars_ref, residual_ref, mapped_ref, search_ref, first_ref, second_ref, third_ref,
     solution_ref, residual_out,
 ):
     scalars = scalars_ref[...]
-    _, _, step, growth = search_scalars(sum_tiles(tiles_ref, count), scalars, ITERS - 1)
+    tiles = sum_tiles(tiles_ref, tiles_ref.shape[0] // 8)
+    _, _, step, growth = search_scalars(tiles, scalars, ITERS - 1)
     first_step, second_step, second_growth = scalars[2:3, 0:1], scalars[3:4, 0:1], scalars[4:5, 0:1]
     third_weight = step
     second_weight = second_step + growth * step
@@ -643,8 +648,8 @@
     return lax.all_gather(message, "brick", axis=0, tiled=False)
 
 
-def gather_slabs(tile):
-    return lax.all_gather(tile, "grp", axis=0, tiled=True)
+def to_all(copies, axes):
+    return lax.all_to_all(copies, axes, 0, 0, tiled=True)
 
 
 def exchange_slabs(message):
@@ -679,12 +684,12 @@
         z_message, tile = call(
             functools.partial(middle_kernel, first, bricks),
             f"middle_{iteration}",
-            [array(Z_ROWS_FIRST if first else Z_ROWS, 128), array(8, 128)],
+            [array(Z_ROWS_FIRST if first else Z_ROWS, 128), array(8 * slabs, 128)],
             [info, gathered, mapped, relax, partial, edge],
             scalar_operands=1,
         )
         above, below = exchange_slabs(z_message)
-        tiles = gather_slabs(tile)
+        tiles = to_all(tile, "grp")
         operands = [info, gathered, above, below, tiles, effective, diagonal, relax, residual]
         tall = array(8 * slabs, 128)
         outs = {"smoothed": field, "mapped": field}
@@ -701,7 +706,7 @@
                     "halo": array(H_ROWS, 128), "sums": tall,
                     "search_halo": array(H_ROWS, 128), "search_sums": tall,
                 }
-        outs["message"] = array(8 if last else XY_ROWS, 128)
+        outs["message"] = array(8 * slabs * bricks if last else XY_ROWS, 128)
         if not last:
             outs["partial"] = field
         results = call(
@@ -717,10 +722,10 @@
         mapped, message, partial = state["mapped"], state["message"], state.get("partial")
         residual = state.get("residual", residual)
         directions.append(state["smoothed"])
-    tiles = gather_slabs(gather_bricks(message).reshape(bricks * 8, 128))
+    tiles = to_all(message, ("brick", "grp"))
     brick_pair = array(2, BS, BS * BS)
     solution_field, residual = call(
-        functools.partial(finish_kernel, slabs * bricks),
+        finish_kernel,
         "finish",
         [brick_pair, brick_pair],
         [tiles, state["scalars"], residual, mapped, state["search"]] + directions,

time: 179 us -> 107 us (0.60)
  blocking collectives: 149 us -> 44.6 us
  local copies, waits for them, and re-layouts: 4.82 us -> 16.1 us
  starting transfers between devices: 13.7 us -> 23.8 us
  waiting for transfers between devices: 0.02 us -> 8.23 us
    all_gather x4 -> x0, blocking collectives: 125 us -> none  [gather_slabs(): return lax.all_gather(tile, 'grp', axis=0, tiled=True)]
    all_to_all x0 -> x2, blocking collectives: none -> 26.5 us  [to_all(): return lax.all_to_all(copies, axes, 0, 0, tiled=True)]
    unnamed x9 -> x57, local copies, waits for them, and re-layouts: 4.73 us -> 16.1 us
    all_to_all x0 -> x2, starting transfers between devices: none -> 8.81 us  [to_all(): return lax.all_to_all(copies, axes, 0, 0, tiled=True)]
    ppermute x3, waiting for transfers between devices: 0.01 us -> 7.29 us  [exchange_slabs(): lax.ppermute(message, 'grp', downward)]
    all_gather x4 -> x3, blocking collectives: 23.3 us -> 18.2 us  [gather_bricks(): return lax.all_gather(message, 'brick', axis=0, tiled=False)]
  transfers between devices with their start and end apart: 6 -> 8, of which waited for: 0 -> 4; matrix products, arithmetic and copies ran while one was open for 0% -> 0% of each run, Pallas kernels for 0% -> 0%
where the time goes in v4:
time: 107 us; the launch traced here: 106 us
  blocking collectives  44.6 us (42%)
  starting transfers between devices  23.8 us (22%)
  local copies, waits for them, and re-layouts  16.1 us (15%)
  Pallas kernels  11.9 us (11%)
  waiting for transfers between devices  8.23 us (8%)
    all_to_all x2, blocking collectives, to_all(): return lax.all_to_all(copies, axes, 0, 0, tiled=True)  26.5 us
    all_gather x3, blocking collectives, gather_bricks(): return lax.all_gather(message, 'brick', axis=0, tiled=False)  18.2 us
    unnamed x57, local copies, waits for them, and re-layouts  16.1 us
    pallas_call x8, Pallas kernels, call(): pl.pallas_call(kernel, out_shape=tuple(outs), in_specs=[smem] * scalar_op...  11.9 us
    ppermute x3, starting transfers between devices, exchange_slabs(): lax.ppermute(message, 'grp', upward)  11.1 us
    all_to_all x2, starting transfers between devices, to_all(): return lax.all_to_all(copies, axes, 0, 0, tiled=True)  8.81 us
    ppermute x3, waiting for transfers between devices, exchange_slabs(): lax.ppermute(message, 'grp', downward)  7.29 us
    ppermute x3, starting transfers between devices, exchange_slabs(): lax.ppermute(message, 'grp', downward)  3.88 us
  transfers between devices with their start and end apart: 8, of which 4 were waited for; matrix products, arithmetic and copies ran while one was open for 0% of the time, Pallas kernels for 0%

profile of v4, /device:TPU:0, one launch (start us, length us, event | category | flops | bytes accessed | tf_op | source)
XLA Modules:
  0.0 105.6 jit_solution(9455922534786058391)
XLA Ops:
  0.6 0.8 copy.8
  1.4 0.1 reshape.19.occupancy_ref
  1.5 0.0 copy-start
  1.5 1.4 %copy-done = f32[1,1,6,2,32,1024]{5,4,3,2,1,0:T(8,128)S(1)} copy-done((f32[1,1,6,2,32,1024]{5,4,3,2,1,0:T(8,128)S(1)}, f32[1,1,6,2,32,1024]{5,4,3,2,1,0:T(8,128)}, u32[]{:S(2)}) %copy-start) | copy-done | bytes 1572888
  2.9 0.9 copy-done.1
  3.9 0.9 copy-done.2
  4.8 0.7 copy-done.27
  5.5 1.8 %setup.1 = (s32[8]{0:T(128)S(1)}, f32[6,16,32,128]{3,2,1,0:T(8,128)S(1)}, f32[16,32,128]{2,1,0:T(8,128)S(1)}, f32[16,32,128]{2,1,0:T(8,128)S(1)}, f32[16,32,128]...) custom-call(s32[1]{0:T(128)} %bitcast.place_ref, s32[4]{0:T(128)S(1)} %copy-done.27, ...), custom_call_target="tpu_custom_call" | custom-call | tf_op jit(solution)/shard_map/setup/pallas_call | solution.py:633
  7.3 7.2 %all-gather = f32[512,128]{1,0:T(8,128)S(1)} all-gather(f32[128,128]{1,0:T(8,128)S(1)} %get-tuple-element.44), channel_id=2, replica_groups=mesh['brick'=4,'grp'=8] {'brick'}, dimensions={0}, use_global_device_ids=true | all-gather | bytes 327680 | tf_op jit(solution)/shard_map/all_gather | solution.py:648
  14.5 0.8 middle_0.1
  15.3 3.4 %collective-permute-start.1 = (f32[136,128]{1,0:T(8,128)S(1)}, f32[136,128]{1,0:T(8,128)S(1)}, u32[]{:S(2)}, u32[]{:S(2)}) collective-permute-start(f32[136,128]{1,0:T(8,128)S(1)} %get-tuple-element.49), channel_id=1, source_target_pairs={{0,1},{1,2},{2,3},{3,4},{4,5},{5,6},{6,7},{8,9},{9,10},{10,11},{11... | collective-permute-start | bytes 208904 | tf_op jit(solution)/shard_map/ppermute | solution.py:659
  18.8 1.3 %collective-permute-start = (f32[136,128]{1,0:T(8,128)S(1)}, f32[136,128]{1,0:T(8,128)S(1)}, u32[]{:S(2)}, u32[]{:S(2)}) collective-permute-start(f32[136,128]{1,0:T(8,128)S(1)} %get-tuple-element.49), channel_id=1, source_target_pairs={{1,0},{2,1},{3,2},{4,3},{5,4},{6,5},{7,6},{9,8},{10,9},{11,10},{12... | collective-permute-start | bytes 208904 | tf_op jit(solution)/shard_map/ppermute | solution.py:659
  20.1 13.4 %all_to_all.44 = f32[8,8,128]{2,1,0:T(8,128)S(1)} all-to-all(f32[8,8,128]{2,1,0:T(8,128)S(1)} %bitcast.31), channel_id=1, replica_groups=mesh['brick'=4,'grp'=8] {'grp'}, dimensions={0} | all-to-all | bytes 65536 | tf_op jit(solution)/shard_map/all_to_all | solution.py:652
  33.5 2.0 %step_0.1 = (f32[16,32,128]{2,1,0:T(8,128)S(1)}, f32[16,32,128]{2,1,0:T(8,128)S(1)}, f32[88,128]{1,0:T(8,128)S(1)}, f32[64,128]{1,0:T(8,128)S(1)}, f32[168,128]{...) custom-call(s32[8]{0:T(128)S(1)} %get-tuple-element.43.info_ref.refs_0_, ...), custom_call_target="tpu_custom_call" | custom-call | tf_op jit(solution)/shard_map/step_0/pallas_call | solution.py:633
  35.5 0.6 copy-done.25
  36.1 5.5 %all-gather.1 = f32[288,128]{1,0:T(8,128)S(1)} all-gather(f32[72,128]{1,0:T(8,128)S(1)} %get-tuple-element.53), channel_id=3, replica_groups=mesh['brick'=4,'grp'=8] {'brick'}, dimensions={0}, use_global_device_ids=true | all-gather | bytes 184320 | tf_op jit(solution)/shard_map/all_gather | solution.py:648
  41.6 1.3 %middle_1.1 = (f32[104,128]{1,0:T(8,128)S(1)}, f32[64,128]{1,0:T(8,128)}) custom-call(s32[8]{0:T(128)S(1)} %get-tuple-element.43.info_ref.refs_0_, f32[4,72,128]{2,1,0:T(8,128)S(1)} %bitcast.22, f32[16,32,128]{2,1,0:T(8,128)S(1)} %get-tuple-element.54.field_ref.refs_9_, f32[16,32,128]{2,1,0:T(8,128)S(1)} %get-tuple-element.46.relax_ref.refs_7_, ...), custom_call_target="tpu_custom_call" | custom-call | tf_op jit(solution)/shard_map/middle_1/pallas_call | solution.py:633
  42.9 3.3 %all-to-all-start.1 = ((f32[8,8,128]{2,1,0:T(8,128)}), f32[8,8,128]{2,1,0:T(8,128)S(1)}, u32[]{:S(2)}, u32[]{:S(2)}) async-start(f32[8,8,128]{2,1,0:T(8,128)} %bitcast.8), calls=%async_computation.1 | async-start | bytes 65536 | tf_op jit(solution)/shard_map/all_to_all | solution.py:652
  46.2 3.8 %collective-permute-start.3 = (f32[104,128]{1,0:T(8,128)S(1)}, f32[104,128]{1,0:T(8,128)S(1)}, u32[]{:S(2)}, u32[]{:S(2)}) collective-permute-start(f32[104,128]{1,0:T(8,128)S(1)} %get-tuple-element.56), channel_id=1, source_target_pairs={{0,1},{1,2},{2,3},{3,4},{4,5},{5,6},{6,7},{8,9},{9,10},{10,11},{11... | collective-permute-start | bytes 159752 | tf_op jit(solution)/shard_map/ppermute | solution.py:659
  50.0 1.3 %collective-permute-start.2 = (f32[104,128]{1,0:T(8,128)S(1)}, f32[104,128]{1,0:T(8,128)S(1)}, u32[]{:S(2)}, u32[]{:S(2)}) collective-permute-start(f32[104,128]{1,0:T(8,128)S(1)} %get-tuple-element.56), channel_id=1, source_target_pairs={{1,0},{2,1},{3,2},{4,3},{5,4},{6,5},{7,6},{9,8},{10,9},{11,10},{12... | collective-permute-start | bytes 159752 | tf_op jit(solution)/shard_map/ppermute | solution.py:659
  51.3 0.5 collective-permute-done.3.refs_3_
  51.8 0.6 copy-done.15
  52.4 3.6 %collective-permute-done.2.refs_2_ = f32[104,128]{1,0:T(8,128)S(1)} collective-permute-done((f32[104,128]{1,0:T(8,128)S(1)}, f32[104,128]{1,0:T(8,128)S(1)}, u32[]{:S(2)}, u32[]{:S(2)}) %collective-permute-start.2) | collective-permute-done | bytes 53280 | tf_op jit(solution)/shard_map/ppermute | solution.py:659
  56.1 0.6 copy-done.19
  56.7 0.9 copy-done.12
  57.6 0.8 copy-done.16
  58.4 0.8 copy-done.20
  59.2 0.8 copy-done.26
  60.0 2.0 %step_1.1 = (f32[16,32,128]{2,1,0:T(8,128)S(1)}, f32[16,32,128]{2,1,0:T(8,128)S(1)}, f32[16,32,128]{2,1,0:T(8,128)S(1)}, f32[16,32,128]{2,1,0:T(8,128)S(1)}, f32...) custom-call(s32[8]{0:T(128)S(1)} %get-tuple-element.43.info_ref.refs, ...), custom_call_target="tpu_custom_call" | custom-call | tf_op jit(solution)/shard_map/step_1/pallas_call | solution.py:633
  61.9 0.0 copy-start.3
  62.0 5.5 %all-gather.2 = f32[288,128]{1,0:T(8,128)S(1)} all-gather(f32[72,128]{1,0:T(8,128)S(1)} %get-tuple-element.62), channel_id=4, replica_groups=mesh['brick'=4,'grp'=8] {'brick'}, dimensions={0}, use_global_device_ids=true | all-gather | bytes 184320 | tf_op jit(solution)/shard_map/all_gather | solution.py:648
  67.5 1.3 %middle_2.1 = (f32[104,128]{1,0:T(8,128)S(1)}, f32[64,128]{1,0:T(8,128)}) custom-call(s32[8]{0:T(128)S(1)} %get-tuple-element.43.info_ref.refs_0_, f32[4,72,128]{2,1,0:T(8,128)S(1)} %bitcast.20, f32[16,32,128]{2,1,0:T(8,128)S(1)} %get-tuple-element.63.field_ref.refs_9_, f32[16,32,128]{2,1,0:T(8,128)S(1)} %get-tuple-element.46.relax_ref.refs_7_, ...), custom_call_target="tpu_custom_call" | custom-call | tf_op jit(solution)/shard_map/middle_2/pallas_call | solution.py:633
  68.8 5.5 %all-to-all-start.2 = ((f32[8,8,128]{2,1,0:T(8,128)}), f32[8,8,128]{2,1,0:T(8,128)S(1)}, u32[]{:S(2)}, u32[]{:S(2)}) async-start(f32[8,8,128]{2,1,0:T(8,128)} %bitcast.11), calls=%async_computation.2 | async-start | bytes 65536 | tf_op jit(solution)/shard_map/all_to_all | solution.py:652
  74.3 3.9 %collective-permute-start.5 = (f32[104,128]{1,0:T(8,128)S(1)}, f32[104,128]{1,0:T(8,128)S(1)}, u32[]{:S(2)}, u32[]{:S(2)}) collective-permute-start(f32[104,128]{1,0:T(8,128)S(1)} %get-tuple-element.65), channel_id=1, source_target_pairs={{0,1},{1,2},{2,3},{3,4},{4,5},{5,6},{6,7},{8,9},{9,10},{10,11},{11... | collective-permute-start | bytes 159752 | tf_op jit(solution)/shard_map/ppermute | solution.py:659
  78.2 1.3 %collective-permute-start.4 = (f32[104,128]{1,0:T(8,128)S(1)}, f32[104,128]{1,0:T(8,128)S(1)}, u32[]{:S(2)}, u32[]{:S(2)}) collective-permute-start(f32[104,128]{1,0:T(8,128)S(1)} %get-tuple-element.65), channel_id=1, source_target_pairs={{1,0},{2,1},{3,2},{4,3},{5,4},{6,5},{7,6},{9,8},{10,9},{11,10},{12... | collective-permute-start | bytes 159752 | tf_op jit(solution)/shard_map/ppermute | solution.py:659
  79.5 0.5 collective-permute-done.5.refs_3_
  80.0 0.6 copy-done.13
  80.6 3.6 %collective-permute-done.4.refs_2_ = f32[104,128]{1,0:T(8,128)S(1)} collective-permute-done((f32[104,128]{1,0:T(8,128)S(1)}, f32[104,128]{1,0:T(8,128)S(1)}, u32[]{:S(2)}, u32[]{:S(2)}) %collective-permute-start.4) | collective-permute-done | bytes 53280 | tf_op jit(solution)/shard_map/ppermute | solution.py:659
  84.2 0.6 copy-done.17
  84.9 0.9 copy-done.4
  85.8 0.9 copy-done.10
  86.7 0.8 copy-done.14
  87.5 0.8 copy-done.18
  88.3 0.8 copy-done.22
  89.1 0.8 copy-done.24
  89.8 1.7 %step_2.1 = (f32[16,32,128]{2,1,0:T(8,128)S(1)}, f32[16,32,128]{2,1,0:T(8,128)S(1)}, f32[16,32,128]{2,1,0:T(8,128)S(1)}, f32[16,32,128]{2,1,0:T(8,128)S(1)}, f32...) custom-call(s32[8]{0:T(128)S(1)} %get-tuple-element.43.info_ref.refs_0_, f32[4,72,128]{2,1,0:T(8,128)S(1)} %bitcast.21, ...), custom_call_target="tpu_custom_call" | custom-call | tf_op jit(solution)/shard_map/step_2/pallas_call | solution.py:633
  91.6 13.0 %all_to_all.45 = f32[32,8,128]{2,1,0:T(8,128)S(1)} all-to-all(f32[32,8,128]{2,1,0:T(8,128)S(1)} %bitcast.30), channel_id=1, replica_groups=mesh['brick'=4,'grp'=8] {'brick','grp'}, dimensions={0} | all-to-all | bytes 262144 | tf_op jit(solution)/shard_map/all_to_all | solution.py:652
  104.6 1.0 finish.1
  (40 shorter events, 0.1 us)
Async XLA Ops:
  1.5 1.4 %copy-start = (f32[1,1,6,2,32,1024]{5,4,3,2,1,0:T(8,128)S(1)}, f32[1,1,6,2,32,1024]{5,4,3,2,1,0:T(8,128)}, u32[]{:S(2)}) copy-start(f32[1,1,6,2,32,1024]{5,4,3,2,1,0:T(8,128)} %param.7) | copy-start | bytes 4718596
  2.9 0.9 copy-start.1
  3.9 0.9 copy-start.2
  4.8 0.7 copy-start.27
  15.3 18.2 %collective-permute-start.1 = (f32[136,128]{1,0:T(8,128)S(1)}, f32[136,128]{1,0:T(8,128)S(1)}, u32[]{:S(2)}, u32[]{:S(2)}) collective-permute-start(f32[136,128]{1,0:T(8,128)S(1)} %get-tuple-element.49), channel_id=1, source_target_pairs={{0,1},{1,2},{2,3},{3,4},{4,5},{5,6},{6,7},{8,9},{9,10},{10,11},{11... | collective-permute-start | bytes 208904 | tf_op jit(solution)/shard_map/ppermute | solution.py:659
  18.8 14.7 %collective-permute-start = (f32[136,128]{1,0:T(8,128)S(1)}, f32[136,128]{1,0:T(8,128)S(1)}, u32[]{:S(2)}, u32[]{:S(2)}) collective-permute-start(f32[136,128]{1,0:T(8,128)S(1)} %get-tuple-element.49), channel_id=1, source_target_pairs={{1,0},{2,1},{3,2},{4,3},{5,4},{6,5},{7,6},{9,8},{10,9},{11,10},{12... | collective-permute-start | bytes 208904 | tf_op jit(solution)/shard_map/ppermute | solution.py:659
  35.5 0.6 copy-start.25
  36.1 6.8 %copy-start.5 = (f32[16,32,128]{2,1,0:T(8,128)}, f32[16,32,128]{2,1,0:T(8,128)S(1)}, u32[]{:S(2)}) copy-start(f32[16,32,128]{2,1,0:T(8,128)S(1)} %get-tuple-element.79.first_ref) | copy-start | bytes 786436
  36.1 6.8 %copy-start.11 = (f32[168,128]{1,0:T(8,128)}, f32[168,128]{1,0:T(8,128)S(1)}, u32[]{:S(2)}) copy-start(f32[168,128]{1,0:T(8,128)S(1)} %get-tuple-element.58.refs_10_) | copy-start | bytes 258052
  42.9 13.8 %all-to-all-start.1 = ((f32[8,8,128]{2,1,0:T(8,128)}), f32[8,8,128]{2,1,0:T(8,128)S(1)}, u32[]{:S(2)}, u32[]{:S(2)}) async-start(f32[8,8,128]{2,1,0:T(8,128)} %bitcast.8), calls=%async_computation.1 | async-start | bytes 65536 | tf_op jit(solution)/shard_map/all_to_all | solution.py:652
  46.2 5.6 %collective-permute-start.3 = (f32[104,128]{1,0:T(8,128)S(1)}, f32[104,128]{1,0:T(8,128)S(1)}, u32[]{:S(2)}, u32[]{:S(2)}) collective-permute-start(f32[104,128]{1,0:T(8,128)S(1)} %get-tuple-element.56), channel_id=1, source_target_pairs={{0,1},{1,2},{2,3},{3,4},{4,5},{5,6},{6,7},{8,9},{9,10},{10,11},{11... | collective-permute-start | bytes 159752 | tf_op jit(solution)/shard_map/ppermute | solution.py:659
  50.0 6.0 %collective-permute-start.2 = (f32[104,128]{1,0:T(8,128)S(1)}, f32[104,128]{1,0:T(8,128)S(1)}, u32[]{:S(2)}, u32[]{:S(2)}) collective-permute-start(f32[104,128]{1,0:T(8,128)S(1)} %get-tuple-element.56), channel_id=1, source_target_pairs={{1,0},{2,1},{3,2},{4,3},{5,4},{6,5},{7,6},{9,8},{10,9},{11,10},{12... | collective-permute-start | bytes 159752 | tf_op jit(solution)/shard_map/ppermute | solution.py:659
  51.8 0.6 copy-start.15
  56.1 0.6 copy-start.19
  56.7 0.9 copy-start.12
  57.6 0.8 copy-start.16
  58.4 0.8 copy-start.20
  59.2 0.8 copy-start.26
  61.9 6.8 %copy-start.3 = (f32[16,32,128]{2,1,0:T(8,128)}, f32[16,32,128]{2,1,0:T(8,128)S(1)}, u32[]{:S(2)}) copy-start(f32[16,32,128]{2,1,0:T(8,128)S(1)} %get-tuple-element.71.refs_15_) | copy-start | bytes 786436
  61.9 6.8 %copy-start.7 = (f32[16,32,128]{2,1,0:T(8,128)}, f32[16,32,128]{2,1,0:T(8,128)S(1)}, u32[]{:S(2)}) copy-start(f32[16,32,128]{2,1,0:T(8,128)S(1)} %get-tuple-element.80.second_ref) | copy-start | bytes 786436
  61.9 6.8 %copy-start.9 = (f32[168,128]{1,0:T(8,128)}, f32[168,128]{1,0:T(8,128)S(1)}, u32[]{:S(2)}) copy-start(f32[168,128]{1,0:T(8,128)S(1)} %get-tuple-element.72.refs_16_) | copy-start | bytes 258052
  62.0 6.8 %copy-start.21 = (f32[64,128]{1,0:T(8,128)}, f32[64,128]{1,0:T(8,128)S(1)}, u32[]{:S(2)}) copy-start(f32[64,128]{1,0:T(8,128)S(1)} %get-tuple-element.69.refs_13_) | copy-start | bytes 98308
  62.0 6.8 %copy-start.23 = (f32[64,128]{1,0:T(8,128)}, f32[64,128]{1,0:T(8,128)S(1)}, u32[]{:S(2)}) copy-start(f32[64,128]{1,0:T(8,128)S(1)} %get-tuple-element.73.refs_17_) | copy-start | bytes 98308
  68.8 16.1 %all-to-all-start.2 = ((f32[8,8,128]{2,1,0:T(8,128)}), f32[8,8,128]{2,1,0:T(8,128)S(1)}, u32[]{:S(2)}, u32[]{:S(2)}) async-start(f32[8,8,128]{2,1,0:T(8,128)} %bitcast.11), calls=%async_computation.2 | async-start | bytes 65536 | tf_op jit(solution)/shard_map/all_to_all | solution.py:652
  74.3 5.7 %collective-permute-start.5 = (f32[104,128]{1,0:T(8,128)S(1)}, f32[104,128]{1,0:T(8,128)S(1)}, u32[]{:S(2)}, u32[]{:S(2)}) collective-permute-start(f32[104,128]{1,0:T(8,128)S(1)} %get-tuple-element.65), channel_id=1, source_target_pairs={{0,1},{1,2},{2,3},{3,4},{4,5},{5,6},{6,7},{8,9},{9,10},{10,11},{11... | collective-permute-start | bytes 159752 | tf_op jit(solution)/shard_map/ppermute | solution.py:659
  78.2 6.0 %collective-permute-start.4 = (f32[104,128]{1,0:T(8,128)S(1)}, f32[104,128]{1,0:T(8,128)S(1)}, u32[]{:S(2)}, u32[]{:S(2)}) collective-permute-start(f32[104,128]{1,0:T(8,128)S(1)} %get-tuple-element.65), channel_id=1, source_target_pairs={{1,0},{2,1},{3,2},{4,3},{5,4},{6,5},{7,6},{9,8},{10,9},{11,10},{12... | collective-permute-start | bytes 159752 | tf_op jit(solution)/shard_map/ppermute | solution.py:659
  80.0 0.6 copy-start.13
  84.2 0.6 copy-start.17
  84.8 1.0 copy-start.4
  85.8 0.9 copy-start.10
  86.7 0.8 copy-start.14
  87.5 0.8 copy-start.18
  88.3 0.8 copy-start.22
  89.1 0.8 copy-start.24
  89.8 14.8 %copy-start.6 = (f32[16,32,128]{2,1,0:T(8,128)S(1)}, f32[16,32,128]{2,1,0:T(8,128)}, u32[]{:S(2)}) copy-start(f32[16,32,128]{2,1,0:T(8,128)} %copy-done.5) | copy-start | bytes 786436
  89.8 14.8 %copy-start.8 = (f32[16,32,128]{2,1,0:T(8,128)S(1)}, f32[16,32,128]{2,1,0:T(8,128)}, u32[]{:S(2)}) copy-start(f32[16,32,128]{2,1,0:T(8,128)} %copy-done.7) | copy-start | bytes 786436

commit v5 on v4

--- a/solution.py
+++ b/solution.py
@@ -14,20 +14,19 @@
 F32 = jnp.float32
 FIELD = (CHUNKS, BS, 128)
 
-XY_X1, XY_XP, XY_Y, XY_S = 0, 16, 32, 64
-XY_ROWS = 72
-XY_XD, XY_YC, XY_K = 72, 88, 120
-XY_ROWS_FIRST = 128
-Z_Y1, Z_Q, Z_Y, Z_X = 0, 32, 64, 96
-Z_ROWS = 104
-Z_D = 104
+XY_X1, XY_XP, XY_Y = 0, 16, 32
+XY_ROWS = 64
+XY_XD, XY_YC, XY_K = 64, 80, 112
+XY_ROWS_FIRST = 120
+Z_Y1, Z_P = 0, 32
+Z_ROWS = 64
+Z_D, Z_K, Z_X = 64, 96, 128
 Z_ROWS_FIRST = 136
-H_X1, H_XP, H_Y, H_Z1, H_ZQ, H_YZ, H_R = 0, 16, 32, 64, 96, 128, 160
+T_N, T_Y = 16, 64
+H_X1, H_Y, H_Z1, H_ZP, H_E, H_R = 0, 32, 64, 96, 128, 160
 H_ROWS = 168
-C_XD, C_YC, C_ZD, C_K = 0, 16, 48, 80
-C_ROWS = 88
-E_XP, E_XM, E_YP, E_YM = 0, 16, 32, 64
-E_ROWS = 96
+C_XD, C_YC, C_ZD, C_ZK, C_K = 0, 16, 48, 80, 112
+C_ROWS = 120
 
 
 def roll(block, shift):
@@ -120,6 +119,37 @@
         ref[start + i : start + i + 1] = jnp.zeros((1, 128), F32)
 
 
+def tile_of(values, y1=None):
+    lane = lanes(8)
+    level = rows_of(8)
+    tile = jnp.zeros((8, 128), F32)
+    for i, value in enumerate(values):
+        tile = jnp.where((level == i) & (lane >= T_N) & (lane < T_Y), value, tile)
+    if y1 is None:
+        return tile
+    row, low, high = y1
+    tile = jnp.where((level == 0) & (lane >= T_Y), row, tile)
+    tile = jnp.where((level == 1) & (lane >= T_Y), roll_row(row, 64), tile)
+    wide = lanes()
+    edges = jnp.where(wide == 0, low, 0.0)
+    edges = jnp.where(wide == 1, roll(low, -30), edges)
+    edges = jnp.where(wide == 2, roll(high, -94), edges)
+    edges = jnp.where(wide == 3, roll(high, -124), edges)
+    for t in range(4):
+        tile = tile + roll(edges[8 * t : 8 * t + 8], 4 * t)
+    return tile
+
+
+def write_copies(ref, tile):
+    for k in range(ref.shape[0] // 8):
+        ref[8 * k : 8 * k + 8] = tile
+
+
+def edge_tile(y1, row, values):
+    line = pack([facing(f, row) for f in y1])
+    return tile_of(values, (line, y1[0], y1[CHUNKS - 1]))
+
+
 def locate(bricks, place_ref, assignment_ref):
     across = bricks // 2
     place = place_ref[0]
@@ -132,7 +162,7 @@
 
 def setup_kernel(
     slabs, bricks, place_ref, assignment_ref, occupancy_ref, source_ref, uptake_ref, conductance_ref,
-    info_ref, effective_ref, diagonal_ref, relax_ref, residual_ref, partial_ref, edge_ref, xy_ref,
+    info_ref, effective_ref, diagonal_ref, relax_ref, residual_ref, xy_ref, z_ref, tile_ref,
 ):
     across = bricks // 2
     slab, patch, row, column = locate(bricks, place_ref, assignment_ref)
@@ -216,40 +246,37 @@
     )
     partial = []
     for c in range(CHUNKS):
-        value = y1[c] + relax_ref[c] * (residual_ref[c] - outcome[c])
-        partial_ref[c] = value
-        partial.append(value)
+        partial.append(y1[c] + relax_ref[c] * (residual_ref[c] - outcome[c]))
     write_xy(xy_ref, row, y1, partial)
+    z_ref[Z_Y1 : Z_Y1 + BS] = pack(y1)
+    z_ref[Z_P : Z_P + BS] = pack(partial)
 
     first_coupling = total_of([first_y])
     high_sums = [total_of(high_ends[8 * s : 8 * s + 8]) for s in range(2)]
     low_sums = [total_of(low_ends[8 * s : 8 * s + 8]) for s in range(2)]
     taken_sums = [total_of(absorbed[8 * s : 8 * s + 8]) for s in range(2)]
     residual_sums = [total_of([residual_ref[8 * s + k] for k in range(8)]) for s in range(2)]
-    write_scalars(
-        xy_ref,
-        XY_S,
-        [
-            residual_sums[0],
-            residual_sums[1],
-            taken_sums[0] + first_coupling + high_sums[0] + low_sums[0],
-            taken_sums[1] + total_of([second_y]) + high_sums[1] + low_sums[1],
-            first_coupling,
-            high_sums[0],
-            high_sums[1],
-        ],
-    )
+    numbers = [
+        residual_sums[0],
+        residual_sums[1],
+        taken_sums[0] + first_coupling + high_sums[0] + low_sums[0],
+        taken_sums[1] + total_of([second_y]) + high_sums[1] + low_sums[1],
+        first_coupling,
+        high_sums[0],
+        high_sums[1],
+    ]
+    write_copies(tile_ref, edge_tile(y1, row, numbers))
 
     last = CHUNKS - 1
     z_ends = [relax_ref[c] * (high_ends[c] + low_ends[c]) for c in range(CHUNKS)]
     for c in range(CHUNKS):
         xy_ref[XY_XD + c : XY_XD + c + 1] = facing(relax_ref[c], row)
-        edge_ref[E_XP + c : E_XP + c + 1] = (relax_ref[c] * effective_ref[0, c])[BS - 1 : BS]
-        edge_ref[E_XM + c : E_XM + c + 1] = (relax_ref[c] * effective_ref[1, c])[0:1]
     high_y = jnp.where(lane >= 96, relax_ref[last] * effective_ref[2, last], 0.0)
     low_y = jnp.where(lane < 32, relax_ref[0] * effective_ref[3, 0], 0.0)
-    edge_ref[E_YP : E_YP + BS] = high_y
-    edge_ref[E_YM : E_YM + BS] = low_y
+    z_ref[Z_D : Z_D + BS] = pack([relax_ref[c] for c in range(CHUNKS)])
+    z_ref[Z_K : Z_K + BS] = pack([low_y] + [jnp.zeros((BS, 128), F32)] * (CHUNKS - 2) + [high_y])
+    x_row = pack([facing_terms(relax_ref, effective_ref, c) for c in range(CHUNKS)])
+    z_ref[Z_X : Z_X + 8] = jnp.broadcast_to(x_row, (8, 128))
     xy_ref[XY_YC : XY_YC + BS] = side_blocks(relax_ref[0], relax_ref[last], z_ends[0], z_ends[last])
     xy_ref[XY_K : XY_K + 1] = facing(low_y + high_y, row)
     xy_ref[XY_K + 1 : XY_K + 2] = pack([facing(z, row) for z in z_ends])
@@ -275,59 +302,13 @@
     return jnp.where((lanes(rows) // 32) % 2 == 0, low, high)
 
 
-def middle_kernel(
-    first, bricks, info_ref, xy_ref, field_ref, relax_ref, partial_ref, edge_ref, z_ref, tile_ref
-):
-    lane = lanes()
-    height = rows_of()
-    x_holder = info_ref[3]
-    x_halo = xy_ref[x_holder, XY_X1 : XY_X1 + CHUNKS]
-    sides = swap_sides(
-        xy_ref[info_ref[4], XY_Y : XY_Y + BS], xy_ref[info_ref[5], XY_Y : XY_Y + BS]
-    )
-    upper = edge_ref[E_XP : E_XP + CHUNKS] * x_halo
-    lower = edge_ref[E_XM : E_XM + CHUNKS] * x_halo
-    y1 = []
-    whole = []
-    for c in range(CHUNKS):
-        y1.append(relax_ref[c] * field_ref[c])
-        value = partial_ref[c]
-        value = value + jnp.where(height == BS - 1, upper[c : c + 1], 0.0)
-        value = value + jnp.where(height == 0, lower[c : c + 1], 0.0)
-        if c == 0:
-            value = value + jnp.where(lane < 32, edge_ref[E_YM : E_YM + BS] * sides, 0.0)
-        if c == CHUNKS - 1:
-            value = value + jnp.where(
-                lane >= 96, edge_ref[E_YP : E_YP + BS] * roll(sides, 64), 0.0
-            )
-        whole.append(value)
-    z_ref[Z_Y1 : Z_Y1 + BS] = pack(y1)
-    z_ref[Z_Q : Z_Q + BS] = pack(whole)
-    z_ref[Z_Y : Z_Y + BS] = sides
-    x_ends = pack([x_halo[c : c + 1] for c in range(CHUNKS)])
-    z_ref[Z_X : Z_X + 8] = jnp.broadcast_to(x_ends, (8, 128))
-    if first:
-        z_ref[Z_D : Z_D + BS] = pack([relax_ref[c] for c in range(CHUNKS)])
-    lane_tile = lanes(8)
-    mixed = jnp.zeros((8, 128), F32)
-    for q in range(4):
-        mixed = jnp.where(lane_tile == q, xy_ref[info_ref[2 + q], XY_S : XY_S + 8], mixed)
-    if not first:
-        summed = xy_ref[0, XY_S : XY_S + 8]
-        for b in range(1, bricks):
-            summed = summed + xy_ref[b, XY_S : XY_S + 8]
-        mixed = jnp.where(rows_of(8) < 2, mixed, summed)
-    for g in range(tile_ref.shape[0] // 8):
-        tile_ref[8 * g : 8 * g + 8] = mixed
-
-
 def search_scalars(tiles, scalars, iteration):
-    energy = tiles[2:3, 0:1]
-    curvature = tiles[3:4, 0:1]
+    energy = tiles[2:3, T_N : T_N + 1]
+    curvature = tiles[3:4, T_N : T_N + 1]
     if iteration == 0:
         return energy, curvature, energy / curvature, None
     growth = energy / scalars[0:1, 0:1]
-    curvature = curvature + growth * (2.0 * tiles[4:5, 0:1] + growth * scalars[1:2, 0:1])
+    curvature = curvature + growth * (2.0 * tiles[4:5, T_N : T_N + 1] + growth * scalars[1:2, 0:1])
     return energy, curvature, energy / curvature, growth
 
 
@@ -356,9 +337,9 @@
         residual_out, search_ref, scalars_ref = take(3)
         if not last:
             halo_ref, sums_ref, search_halo_ref, search_sums_ref = take(4)
-    xy_out = take(1)[0]
+    tile_out = take(1)[0]
     if not last:
-        partial_ref = take(1)[0]
+        xy_out, z_out = take(2)
 
     row = info_ref[0]
     slab = info_ref[1]
@@ -382,14 +363,38 @@
         xy_ref[low_holder, XY_Y : XY_Y + BS], xy_ref[high_holder, XY_Y : XY_Y + BS]
     )
     z_first = merge(Z_Y1)
-    z_second = merge(Z_Q)
-    y_up = roll(above_ref[Z_Y : Z_Y + BS], 31)
-    y_down = roll(below_ref[Z_Y : Z_Y + BS], -31)
-    y_ends = jnp.where(depth == BS - 1, y_up, jnp.where(depth == 0, y_down, 0.0))
+    z_second = merge(Z_P)
+
+    def tile_at(holder, g):
+        return tiles_ref[pl.ds(pl.multiple_of((holder * slabs + g) * 8, 8), 8)]
+
+    slab_above = jnp.minimum(slab + 1, slabs - 1)
+    slab_below = jnp.maximum(slab - 1, 0)
+
+    def edge_row(tile):
+        return jnp.where(lane_row >= T_Y, tile[0:1], roll_row(tile[1:2], 64))
+
     x_ends = jnp.where(
         even_row,
-        roll_row(above_ref[Z_X : Z_X + 1], 31),
-        roll_row(below_ref[Z_X : Z_X + 1], -31),
+        roll_row(edge_row(tile_at(x_holder, slab_above)), 31),
+        roll_row(edge_row(tile_at(x_holder, slab_below)), -31),
+    )
+    kind = lanes(8) % 4
+    mixed = jnp.where(
+        kind == 0,
+        roll(tile_at(low_holder, slab_above), -2),
+        jnp.where(
+            kind == 1,
+            roll(tile_at(low_holder, slab_below), -2),
+            jnp.where(
+                kind == 2,
+                roll(tile_at(high_holder, slab_above), 2),
+                roll(tile_at(high_holder, slab_below), 2),
+            ),
+        ),
+    )
+    y_edges = jnp.where(
+        lane < 4, jnp.concatenate([roll(mixed, -4 * t) for t in range(4)], axis=0), 0.0
     )
     corner_y = jnp.where(
         lane_row < 32,
@@ -408,9 +413,16 @@
     )
     corner_x = swap_sides(low_row, high_row)
     ends = jnp.concatenate([x_ends, corner_y, corner_x, jnp.zeros((5, 128), F32)], axis=0)
-    halo = [x_sides, y_sides, z_first, z_second, y_ends, ends]
-    starts = [H_X1, H_Y, H_Z1, H_ZQ, H_YZ, H_R]
-    sums = tiles_ref[...]
+    halo = [x_sides, y_sides, z_first, z_second, y_edges, ends]
+    starts = [H_X1, H_Y, H_Z1, H_ZP, H_E, H_R]
+    lane_tile = lanes(8)
+    slab_tiles = []
+    for g in range(slabs):
+        tile = tile_at(info_ref[2], g)
+        for q in range(1, 4):
+            tile = jnp.where(lane_tile == T_N + q, tile_at(info_ref[2 + q], g), tile)
+        slab_tiles.append(tile)
+    sums = jnp.concatenate(slab_tiles, axis=0)
 
     if first:
         residual = [residual_ref[c] for c in range(CHUNKS)]
@@ -419,6 +431,7 @@
             xy_ref[low_holder, XY_YC : XY_YC + BS], xy_ref[high_holder, XY_YC : XY_YC + BS]
         )
         constant_ref[C_ZD : C_ZD + BS] = merge(Z_D)
+        constant_ref[C_ZK : C_ZK + BS] = merge(Z_K)
         constant_ref[C_K : C_K + 8] = jnp.concatenate(
             [
                 xy_ref[x_holder, XY_K : XY_K + 2],
@@ -426,7 +439,12 @@
                     xy_ref[low_holder, XY_K + 2 : XY_K + 3],
                     xy_ref[high_holder, XY_K + 2 : XY_K + 3],
                 ),
-                jnp.zeros((5, 128), F32),
+                jnp.where(
+                    even_row,
+                    roll_row(above_ref[Z_X : Z_X + 1], 31),
+                    roll_row(below_ref[Z_X : Z_X + 1], -31),
+                ),
+                jnp.zeros((4, 128), F32),
             ],
             axis=0,
         )
@@ -438,8 +456,12 @@
                 a = a - u0 * u0 * i00
                 b = b - u1 * u1 * i11
                 off = off + u0 * u1 * i01
-            a = jnp.where(lane_row < 4, a, 1.0)
-            b = jnp.where(lane_row < 4, b, 1.0)
+            used = (lane_row >= T_N) & (lane_row < T_N + 4)
+            a = jnp.where(used, a, 1.0)
+            b = jnp.where(used, b, 1.0)
+            off = jnp.where(used, off, 0.0)
+            t0 = jnp.where(used, t0, 0.0)
+            t1 = jnp.where(used, t1, 0.0)
             scale = 1.0 / (a * b - off * off)
             i00, i01, i11 = b * scale, off * scale, a * scale
             u0, u1 = t0, t1
@@ -449,7 +471,7 @@
     else:
         scalars = None if iteration == 1 else scalars_in[...]
         energy, curvature, step, growth = search_scalars(
-            sum_tiles(tiles_ref, slabs), scalars, iteration - 1
+            sum_tiles(tiles_ref, slabs * bricks), scalars, iteration - 1
         )
         step_row = jnp.broadcast_to(step, (1, 128))
         residual = []
@@ -484,7 +506,7 @@
         for start, block in zip(starts, halo):
             halo_ref[start : start + block.shape[0]] = block
         sums_ref[...] = sums
-    x_sides, y_sides, z_first, z_second, y_ends, ends = halo
+    x_sides, y_sides, z_first, z_second, y_edges, ends = halo
 
     forward = []
     for g in range(slabs):
@@ -513,7 +535,10 @@
         above1 = jnp.where(slab + 1 == g, n1, above1)
         below0 = jnp.where(slab - 1 == g, n0, below0)
         below1 = jnp.where(slab - 1 == g, n1, below1)
-    own = [here0[:, 0:1], here1[:, 0:1]]
+    def coarse_of(row, q):
+        return row[:, T_N + q : T_N + q + 1]
+
+    own = [coarse_of(here0, 0), coarse_of(here1, 0)]
 
     effective = lambda d, c: effective_ref[d, c]
     diagonal = lambda c: diagonal_ref[c]
@@ -548,7 +573,7 @@
             value = value + jnp.where(lane_row < 32, corner_row, 0.0)
         if c == end:
             value = value + jnp.where(lane_row >= 96, corner_row, 0.0)
-        value = value + (here0 if c < 8 else here1)[:, 1:2]
+        value = value + coarse_of(here0 if c < 8 else here1, 1)
         additions.append(value)
     x_next = (
         x_sides[CHUNKS:]
@@ -560,12 +585,20 @@
         lane < 32, effective(3, 0) * y1[0], roll(effective(2, end) * y1[end], 64)
     )
     x_side_row = jnp.where(row == 0, BS - 1, 0)
+    y_ends = jnp.where(lane == 0, roll(y_edges, -1), 0.0)
+    y_ends = jnp.where(lane == 31, roll(y_edges, 31), y_ends)
+    y_ends = jnp.where(lane == 32, roll(y_edges, 29), y_ends)
+    y_ends = jnp.where(lane == 63, roll(y_edges, 61), y_ends)
+    z_sides = jnp.where(lane == 0, y_edges, 0.0)
+    z_sides = jnp.where(lane == 97, roll(y_edges, 96), z_sides)
+    z_sides = jnp.where(lane == 126, roll(y_edges, 124), z_sides)
+    z_sides = jnp.where(lane == 95, roll(y_edges, 92), z_sides)
     y_next = (
         roll(y_sides, 64)
         + y_constant * y_crossing
         + roll(y_constant, 64) * y_ends
         + jnp.where(height == x_side_row, keys[2:3] * ends[2:3], 0.0)
-        + jnp.where(lane < 32, here1[:, 2:3], here0[:, 3:4])
+        + jnp.where(lane < 32, coarse_of(here1, 2), coarse_of(here0, 3))
     )
     z_crossing = pack(
         [
@@ -575,10 +608,16 @@
     )
     z_coarse = jnp.where(
         even_row,
-        jnp.where(depth_row < 16, above0[:, 0:1], above1[:, 0:1]),
-        jnp.where(depth_row < 16, below0[:, 0:1], below1[:, 0:1]),
-    )
-    z_next = z_second + constant_ref[C_ZD : C_ZD + BS] * z_crossing + z_coarse
+        jnp.where(depth_row < 16, coarse_of(above0, 0), coarse_of(above1, 0)),
+        jnp.where(depth_row < 16, coarse_of(below0, 0), coarse_of(below1, 0)),
+    )
+    z_next = (
+        z_second
+        + constant_ref[C_ZD : C_ZD + BS] * z_crossing
+        + constant_ref[C_ZK : C_ZK + BS] * z_sides
+        + jnp.where(height == x_side_row, keys[3:4] * ends[0:1], 0.0)
+        + z_coarse
+    )
     mapped = stencil(smoothed, effective, diagonal, x_next, y_next, roll(y_next, 64), z_next)
     for c in range(CHUNKS):
         mapped_out[c] = mapped[c]
@@ -592,20 +631,15 @@
     if not first:
         values.append(total_of([search_ref[c] * smoothed[c] for c in range(CHUNKS)]))
     if last:
-        write_scalars(xy_out, 0, values)
-        tile = xy_out[0:8]
-        for k in range(1, slabs * bricks):
-            xy_out[8 * k : 8 * k + 8] = tile
+        write_copies(tile_out, tile_of(values))
         return
-    write_scalars(xy_out, XY_S, values)
     y1 = [relax_ref[c] * mapped[c] for c in range(CHUNKS)]
+    write_copies(tile_out, edge_tile(y1, row, values))
     outcome = stencil(y1, effective, diagonal, None, None, None, None)
-    partial = []
-    for c in range(CHUNKS):
-        value = y1[c] + relax_ref[c] * (mapped[c] - outcome[c])
-        partial_ref[c] = value
-        partial.append(value)
+    partial = [y1[c] + relax_ref[c] * (mapped[c] - outcome[c]) for c in range(CHUNKS)]
     write_xy(xy_out, row, y1, partial)
+    z_out[Z_Y1 : Z_Y1 + BS] = pack(y1)
+    z_out[Z_P : Z_P + BS] = pack(partial)
 
 
 def finish_kernel(
@@ -635,7 +669,7 @@
         out_shape=tuple(outs),
         in_specs=[smem] * scalar_operands + [vmem] * (len(operands) - scalar_operands),
         out_specs=tuple([smem] * scalar_outs + [vmem] * (len(outs) - scalar_outs)),
-        compiler_params=pltpu.CompilerParams(vmem_limit_bytes=40 * 1024 * 1024),
+        compiler_params=pltpu.CompilerParams(vmem_limit_bytes=16 * 1024 * 1024),
         name=name,
     )(*operands)
 
@@ -664,12 +698,13 @@
     bricks = lax.axis_size("brick")
     place = (lax.axis_index("grp") * bricks + lax.axis_index("brick")).astype(jnp.int32).reshape(1)
     field = array(*FIELD)
-    info, effective, diagonal, relax, residual, partial, edge, message = call(
+    copies = array(8 * slabs * bricks, 128)
+    info, effective, diagonal, relax, residual, sides, ends, tile = call(
         functools.partial(setup_kernel, slabs, bricks),
         "setup",
         [
-            jax.ShapeDtypeStruct((8,), jnp.int32), array(6, *FIELD), field, field, field, field,
-            array(E_ROWS, 128), array(XY_ROWS_FIRST, 128),
+            jax.ShapeDtypeStruct((8,), jnp.int32), array(6, *FIELD), field, field, field,
+            array(XY_ROWS_FIRST, 128), array(Z_ROWS_FIRST, 128), copies,
         ],
         [place, assignment, occupancy.reshape(-1), source[0, 0], uptake[0, 0], conductance[0, 0]],
         scalar_operands=3,
@@ -680,16 +715,9 @@
     state = {}
     for iteration in range(ITERS):
         first, last = iteration == 0, iteration == ITERS - 1
-        gathered = gather_bricks(message)
-        z_message, tile = call(
-            functools.partial(middle_kernel, first, bricks),
-            f"middle_{iteration}",
-            [array(Z_ROWS_FIRST if first else Z_ROWS, 128), array(8 * slabs, 128)],
-            [info, gathered, mapped, relax, partial, edge],
-            scalar_operands=1,
-        )
-        above, below = exchange_slabs(z_message)
-        tiles = to_all(tile, "grp")
+        tiles = to_all(tile, ("brick", "grp"))
+        above, below = exchange_slabs(ends)
+        gathered = gather_bricks(sides)
         operands = [info, gathered, above, below, tiles, effective, diagonal, relax, residual]
         tall = array(8 * slabs, 128)
         outs = {"smoothed": field, "mapped": field}
@@ -706,9 +734,9 @@
                     "halo": array(H_ROWS, 128), "sums": tall,
                     "search_halo": array(H_ROWS, 128), "search_sums": tall,
                 }
-        outs["message"] = array(8 * slabs * bricks if last else XY_ROWS, 128)
+        outs["tile"] = copies
         if not last:
-            outs["partial"] = field
+            outs |= {"sides": array(XY_ROWS, 128), "ends": array(Z_ROWS, 128)}
         results = call(
             functools.partial(step_kernel, iteration, slabs, bricks),
             f"step_{iteration}",
@@ -719,10 +747,11 @@
         state |= dict(zip(outs, results))
         if first:
             state["scalars"] = jnp.zeros((8, 128), F32)
-        mapped, message, partial = state["mapped"], state["message"], state.get("partial")
+        mapped, tile = state["mapped"], state["tile"]
+        sides, ends = state.get("sides"), state.get("ends")
         residual = state.get("residual", residual)
         directions.append(state["smoothed"])
-    tiles = to_all(message, ("brick", "grp"))
+    tiles = to_all(tile, ("brick", "grp"))
     brick_pair = array(2, BS, BS * BS)
     solution_field, residual = call(
         finish_kernel,

time: 107 us -> 102 us (0.953)
  blocking collectives: 44.6 us -> 31.1 us
  starting transfers between devices: 23.8 us -> 35.6 us
  waiting for transfers between devices: 8.23 us -> 0.02 us
  local copies, waits for them, and re-layouts: 16.1 us -> 23.1 us
  Pallas kernels: 11.9 us -> 10.7 us
    all_to_all x2 -> x1, blocking collectives: 26.5 us -> 14.3 us  [to_all(): return lax.all_to_all(copies, axes, 0, 0, tiled=True)]
    all_to_all x2 -> x3, starting transfers between devices: 8.81 us -> 20.7 us  [to_all(): return lax.all_to_all(copies, axes, 0, 0, tiled=True)]
    ppermute x3, waiting for transfers between devices: 7.29 us -> 0.01 us  [exchange_slabs(): lax.ppermute(message, 'grp', downward)]
    unnamed x57 -> x59, local copies, waits for them, and re-layouts: 16.1 us -> 23 us
    all_gather x3, blocking collectives: 18.2 us -> 16.8 us  [gather_bricks(): return lax.all_gather(message, 'brick', axis=0, tiled=False)]
    pallas_call x8 -> x5, Pallas kernels: 11.9 us -> 10.7 us  [call(): pl.pallas_call(kernel, out_shape=tuple(outs), in_specs=[smem] * scalar_op...]
  transfers between devices with their start and end apart: 8 -> 9, of which waited for: 4 -> 0; matrix products, arithmetic and copies ran while one was open for 0% -> 0% of each run, Pallas kernels for 0% -> 0%
where the time goes in v5:
time: 102 us; the launch traced here: 101 us
  starting transfers between devices  35.6 us (35%)
  blocking collectives  31.1 us (30%)
  local copies, waits for them, and re-layouts  23.1 us (23%)
  Pallas kernels  10.7 us (10%)
    unnamed x59, local copies, waits for them, and re-layouts  23 us
    all_to_all x3, starting transfers between devices, to_all(): return lax.all_to_all(copies, axes, 0, 0, tiled=True)  20.7 us
    all_gather x3, blocking collectives, gather_bricks(): return lax.all_gather(message, 'brick', axis=0, tiled=False)  16.8 us
    all_to_all x1, blocking collectives, to_all(): return lax.all_to_all(copies, axes, 0, 0, tiled=True)  14.3 us
    ppermute x3, starting transfers between devices, exchange_slabs(): lax.ppermute(message, 'grp', upward)  11 us
    pallas_call x5, Pallas kernels, call(): pl.pallas_call(kernel, out_shape=tuple(outs), in_specs=[smem] * scalar_op...  10.7 us
    ppermute x3, starting transfers between devices, exchange_slabs(): lax.ppermute(message, 'grp', downward)  3.88 us
  transfers between devices with their start and end apart: 9, of which 0 were waited for; matrix products, arithmetic and copies ran while one was open for 0% of the time, Pallas kernels for 0%

profile of v5, /device:TPU:0, one launch (start us, length us, event | category | flops | bytes accessed | tf_op | source)
XLA Modules:
  0.0 101.2 jit_solution(3902454154549668797)
XLA Ops:
  0.6 0.8 copy.8
  1.5 1.4 %copy-done = f32[1,1,6,2,32,1024]{5,4,3,2,1,0:T(8,128)S(1)} copy-done((f32[1,1,6,2,32,1024]{5,4,3,2,1,0:T(8,128)S(1)}, f32[1,1,6,2,32,1024]{5,4,3,2,1,0:T(8,128)}, u32[]{:S(2)}) %copy-start) | copy-done | bytes 1572888
  2.9 0.9 copy-done.1
  3.9 0.9 copy-done.2
  4.8 0.7 copy-done.27
  5.5 2.2 %setup.1 = (s32[8]{0:T(128)S(1)}, f32[6,16,32,128]{3,2,1,0:T(8,128)S(1)}, f32[16,32,128]{2,1,0:T(8,128)S(1)}, f32[16,32,128]{2,1,0:T(8,128)S(1)}, f32[16,32,128]...) custom-call(s32[1]{0:T(128)} %bitcast.place_ref, s32[4]{0:T(128)S(1)} %copy-done.27, ...), custom_call_target="tpu_custom_call" | custom-call | tf_op jit(solution)/shard_map/setup/pallas_call | solution.py:667
  7.7 7.3 %all-to-all-start = ((f32[32,8,128]{2,1,0:T(8,128)}), f32[32,8,128]{2,1,0:T(8,128)S(1)}, u32[]{:S(2)}, u32[]{:S(2)}) async-start(f32[32,8,128]{2,1,0:T(8,128)} %bitcast.5), calls=%async_computation | async-start | bytes 262144 | tf_op jit(solution)/shard_map/all_to_all | solution.py:686
  15.0 3.7 %collective-permute-start.1 = (f32[136,128]{1,0:T(8,128)S(1)}, f32[136,128]{1,0:T(8,128)S(1)}, u32[]{:S(2)}, u32[]{:S(2)}) collective-permute-start(f32[136,128]{1,0:T(8,128)S(1)} %get-tuple-element.41), channel_id=1, source_target_pairs={{0,1},{1,2},{2,3},{3,4},{4,5},{5,6},{6,7},{8,9},{9,10},{10,11},{11... | collective-permute-start | bytes 208904 | tf_op jit(solution)/shard_map/ppermute | solution.py:693
  18.7 1.3 %collective-permute-start = (f32[136,128]{1,0:T(8,128)S(1)}, f32[136,128]{1,0:T(8,128)S(1)}, u32[]{:S(2)}, u32[]{:S(2)}) collective-permute-start(f32[136,128]{1,0:T(8,128)S(1)} %get-tuple-element.41), channel_id=1, source_target_pairs={{1,0},{2,1},{3,2},{4,3},{5,4},{6,5},{7,6},{9,8},{10,9},{11,10},{12... | collective-permute-start | bytes 208904 | tf_op jit(solution)/shard_map/ppermute | solution.py:693
  20.0 5.7 %all-gather = f32[480,128]{1,0:T(8,128)S(1)} all-gather(f32[120,128]{1,0:T(8,128)S(1)} %get-tuple-element.40), channel_id=2, replica_groups=mesh['brick'=4,'grp'=8] {'brick'}, dimensions={0}, use_global_device_ids=true | all-gather | bytes 307200 | tf_op jit(solution)/shard_map/all_gather | solution.py:682
  25.7 3.0 %step_0.1 = (f32[16,32,128]{2,1,0:T(8,128)S(1)}, f32[16,32,128]{2,1,0:T(8,128)S(1)}, f32[120,128]{1,0:T(8,128)S(1)}, f32[64,128]{1,0:T(8,128)S(1)}, f32[168,128]...) custom-call(s32[8]{0:T(128)S(1)} %get-tuple-element.39.refs_0_, ...), custom_call_target="tpu_custom_call" | custom-call | tf_op jit(solution)/shard_map/step_0/pallas_call | solution.py:667
  28.7 0.7 copy-done.7
  29.4 0.6 copy-done.9
  30.1 0.6 copy-done.16
  30.7 6.7 %all-to-all-start.1 = ((f32[32,8,128]{2,1,0:T(8,128)}), f32[32,8,128]{2,1,0:T(8,128)S(1)}, u32[]{:S(2)}, u32[]{:S(2)}) async-start(f32[32,8,128]{2,1,0:T(8,128)} %bitcast.8), calls=%async_computation.1 | async-start | bytes 262144 | tf_op jit(solution)/shard_map/all_to_all | solution.py:686
  37.4 3.7 %collective-permute-start.3 = (f32[64,128]{1,0:T(8,128)S(1)}, f32[64,128]{1,0:T(8,128)S(1)}, u32[]{:S(2)}, u32[]{:S(2)}) collective-permute-start(f32[64,128]{1,0:T(8,128)S(1)} %get-tuple-element.48), channel_id=1, source_target_pairs={{0,1},{1,2},{2,3},{3,4},{4,5},{5,6},{6,7},{8,9},{9,10},{10,11},{11... | collective-permute-start | bytes 98312 | tf_op jit(solution)/shard_map/ppermute | solution.py:693
  41.1 1.3 %collective-permute-start.2 = (f32[64,128]{1,0:T(8,128)S(1)}, f32[64,128]{1,0:T(8,128)S(1)}, u32[]{:S(2)}, u32[]{:S(2)}) collective-permute-start(f32[64,128]{1,0:T(8,128)S(1)} %get-tuple-element.48), channel_id=1, source_target_pairs={{1,0},{2,1},{3,2},{4,3},{5,4},{6,5},{7,6},{9,8},{10,9},{11,10},{12... | collective-permute-start | bytes 98312 | tf_op jit(solution)/shard_map/ppermute | solution.py:693
  42.4 5.4 %all-gather.1 = f32[256,128]{1,0:T(8,128)S(1)} all-gather(f32[64,128]{1,0:T(8,128)S(1)} %get-tuple-element.47), channel_id=3, replica_groups=mesh['brick'=4,'grp'=8] {'brick'}, dimensions={0}, use_global_device_ids=true | all-gather | bytes 163840 | tf_op jit(solution)/shard_map/all_gather | solution.py:682
  47.8 0.6 copy-done.18
  48.4 0.6 copy-done.20
  49.0 0.9 copy-done.8
  50.0 0.8 copy-done.10
  50.8 0.9 copy-done.17
  51.7 0.8 copy-done.19
  52.5 0.8 copy-done.21
  53.2 2.5 %step_1.1 = (f32[16,32,128]{2,1,0:T(8,128)S(1)}, f32[16,32,128]{2,1,0:T(8,128)S(1)}, f32[16,32,128]{2,1,0:T(8,128)S(1)}, f32[16,32,128]{2,1,0:T(8,128)S(1)}, f32...) custom-call(s32[8]{0:T(128)S(1)} %get-tuple-element.39.refs_0_, ...), custom_call_target="tpu_custom_call" | custom-call | tf_op jit(solution)/shard_map/step_1/pallas_call | solution.py:667
  55.7 0.7 copy-done.3
  56.4 0.7 copy-done.5
  57.1 0.6 copy-done.11
  57.8 0.6 copy-done.12
  58.4 0.6 copy-done.14
  59.0 0.6 copy-done.22
  59.6 0.6 copy-done.23
  60.2 0.6 copy-done.25
  60.8 0.6 copy-done.28
  61.4 6.7 %all-to-all-start.2 = ((f32[32,8,128]{2,1,0:T(8,128)}), f32[32,8,128]{2,1,0:T(8,128)S(1)}, u32[]{:S(2)}, u32[]{:S(2)}) async-start(f32[32,8,128]{2,1,0:T(8,128)} %bitcast.27), calls=%async_computation.2 | async-start | bytes 262144 | tf_op jit(solution)/shard_map/all_to_all | solution.py:686
  68.2 3.7 %collective-permute-start.5 = (f32[64,128]{1,0:T(8,128)}, f32[64,128]{1,0:T(8,128)S(1)}, u32[]{:S(2)}, u32[]{:S(2)}) collective-permute-start(f32[64,128]{1,0:T(8,128)} %copy-done.28), channel_id=1, source_target_pairs={{0,1},{1,2},{2,3},{3,4},{4,5},{5,6},{6,7},{8,9},{9,10},{10,11},{11... | collective-permute-start | bytes 98312 | tf_op jit(solution)/shard_map/ppermute | solution.py:693
  71.8 1.3 %collective-permute-start.4 = (f32[64,128]{1,0:T(8,128)}, f32[64,128]{1,0:T(8,128)S(1)}, u32[]{:S(2)}, u32[]{:S(2)}) collective-permute-start(f32[64,128]{1,0:T(8,128)} %copy-done.28), channel_id=1, source_target_pairs={{1,0},{2,1},{3,2},{4,3},{5,4},{6,5},{7,6},{9,8},{10,9},{11,10},{12... | collective-permute-start | bytes 98312 | tf_op jit(solution)/shard_map/ppermute | solution.py:693
  73.1 5.6 %all-gather.2 = f32[256,128]{1,0:T(8,128)S(1)} all-gather(f32[64,128]{1,0:T(8,128)} %copy-done.22), channel_id=4, replica_groups=mesh['brick'=4,'grp'=8] {'brick'}, dimensions={0}, use_global_device_ids=true | all-gather | bytes 163840 | tf_op jit(solution)/shard_map/all_gather | solution.py:682
  78.8 0.9 copy-done.4
  79.7 0.9 copy-done.6
  80.7 0.9 copy-done.13
  81.6 0.9 copy-done.15
  82.5 0.8 copy-done.24
  83.2 0.8 copy-done.26
  84.0 1.9 %step_2.1 = (f32[16,32,128]{2,1,0:T(8,128)S(1)}, f32[16,32,128]{2,1,0:T(8,128)S(1)}, f32[16,32,128]{2,1,0:T(8,128)S(1)}, f32[16,32,128]{2,1,0:T(8,128)S(1)}, f32...) custom-call(s32[8]{0:T(128)S(1)} %get-tuple-element.39.refs_0_, f32[4,64,128]{2,1,0:T(8,128)S(1)} %bitcast.23, ...), custom_call_target="tpu_custom_call" | custom-call | tf_op jit(solution)/shard_map/step_2/pallas_call | solution.py:667
  85.9 14.3 %all_to_all.44 = f32[32,8,128]{2,1,0:T(8,128)S(1)} all-to-all(f32[32,8,128]{2,1,0:T(8,128)S(1)} %bitcast.28), channel_id=1, replica_groups=mesh['brick'=4,'grp'=8] {'brick','grp'}, dimensions={0} | all-to-all | bytes 262144 | tf_op jit(solution)/shard_map/all_to_all | solution.py:686
  100.2 1.0 %finish.1 = (f32[2,32,1024]{2,1,0:T(8,128)}, f32[2,32,1024]{2,1,0:T(8,128)}) custom-call(f32[256,128]{1,0:T(8,128)S(1)} %bitcast.20, f32[8,128]{1,0:T(8,128)S(1)} %get-tuple-element.67.scalars_ref, f32[16,32,128]{2,1,0:T(8,128)S(1)} %get-tuple-element.68.residual_ref, f32[16,32,128]{2,1,0:T(8,128)S(1)} %get-tuple-element.69.mapped_ref, ...), custom_call_target="tpu_custom_call" | custom-call | tf_op jit(solution)/shard_map/finish/pallas_call | solution.py:667
  (40 shorter events, 0.2 us)
Async XLA Ops:
  1.5 1.4 %copy-start = (f32[1,1,6,2,32,1024]{5,4,3,2,1,0:T(8,128)S(1)}, f32[1,1,6,2,32,1024]{5,4,3,2,1,0:T(8,128)}, u32[]{:S(2)}) copy-start(f32[1,1,6,2,32,1024]{5,4,3,2,1,0:T(8,128)} %param.7) | copy-start | bytes 4718596
  2.9 0.9 copy-start.1
  3.9 0.9 copy-start.2
  4.8 0.7 copy-start.27
  7.7 18.0 %all-to-all-start = ((f32[32,8,128]{2,1,0:T(8,128)}), f32[32,8,128]{2,1,0:T(8,128)S(1)}, u32[]{:S(2)}, u32[]{:S(2)}) async-start(f32[32,8,128]{2,1,0:T(8,128)} %bitcast.5), calls=%async_computation | async-start | bytes 262144 | tf_op jit(solution)/shard_map/all_to_all | solution.py:686
  15.0 10.7 %collective-permute-start.1 = (f32[136,128]{1,0:T(8,128)S(1)}, f32[136,128]{1,0:T(8,128)S(1)}, u32[]{:S(2)}, u32[]{:S(2)}) collective-permute-start(f32[136,128]{1,0:T(8,128)S(1)} %get-tuple-element.41), channel_id=1, source_target_pairs={{0,1},{1,2},{2,3},{3,4},{4,5},{5,6},{6,7},{8,9},{9,10},{10,11},{11... | collective-permute-start | bytes 208904 | tf_op jit(solution)/shard_map/ppermute | solution.py:693
  18.7 7.0 %collective-permute-start = (f32[136,128]{1,0:T(8,128)S(1)}, f32[136,128]{1,0:T(8,128)S(1)}, u32[]{:S(2)}, u32[]{:S(2)}) collective-permute-start(f32[136,128]{1,0:T(8,128)S(1)} %get-tuple-element.41), channel_id=1, source_target_pairs={{1,0},{2,1},{3,2},{4,3},{5,4},{6,5},{7,6},{9,8},{10,9},{11,10},{12... | collective-permute-start | bytes 208904 | tf_op jit(solution)/shard_map/ppermute | solution.py:693
  28.7 0.7 copy-start.7
  29.4 0.6 copy-start.9
  30.1 0.6 copy-start.16
  30.7 18.3 %all-to-all-start.1 = ((f32[32,8,128]{2,1,0:T(8,128)}), f32[32,8,128]{2,1,0:T(8,128)S(1)}, u32[]{:S(2)}, u32[]{:S(2)}) async-start(f32[32,8,128]{2,1,0:T(8,128)} %bitcast.8), calls=%async_computation.1 | async-start | bytes 262144 | tf_op jit(solution)/shard_map/all_to_all | solution.py:686
  37.4 10.4 %collective-permute-start.3 = (f32[64,128]{1,0:T(8,128)S(1)}, f32[64,128]{1,0:T(8,128)S(1)}, u32[]{:S(2)}, u32[]{:S(2)}) collective-permute-start(f32[64,128]{1,0:T(8,128)S(1)} %get-tuple-element.48), channel_id=1, source_target_pairs={{0,1},{1,2},{2,3},{3,4},{4,5},{5,6},{6,7},{8,9},{9,10},{10,11},{11... | collective-permute-start | bytes 98312 | tf_op jit(solution)/shard_map/ppermute | solution.py:693
  41.1 7.3 %collective-permute-start.2 = (f32[64,128]{1,0:T(8,128)S(1)}, f32[64,128]{1,0:T(8,128)S(1)}, u32[]{:S(2)}, u32[]{:S(2)}) collective-permute-start(f32[64,128]{1,0:T(8,128)S(1)} %get-tuple-element.48), channel_id=1, source_target_pairs={{1,0},{2,1},{3,2},{4,3},{5,4},{6,5},{7,6},{9,8},{10,9},{11,10},{12... | collective-permute-start | bytes 98312 | tf_op jit(solution)/shard_map/ppermute | solution.py:693
  47.8 0.6 copy-start.18
  48.4 0.6 copy-start.20
  49.0 1.0 copy-start.8
  50.0 0.8 copy-start.10
  50.8 0.9 copy-start.17
  51.7 0.8 copy-start.19
  52.5 0.8 copy-start.21
  55.7 0.7 copy-start.3
  56.4 0.7 copy-start.5
  57.1 0.6 copy-start.11
  57.8 0.6 copy-start.12
  58.4 0.6 copy-start.14
  59.0 0.6 copy-start.22
  59.6 0.6 copy-start.23
  60.2 0.6 copy-start.25
  60.8 0.6 copy-start.28
  61.4 17.3 %all-to-all-start.2 = ((f32[32,8,128]{2,1,0:T(8,128)}), f32[32,8,128]{2,1,0:T(8,128)S(1)}, u32[]{:S(2)}, u32[]{:S(2)}) async-start(f32[32,8,128]{2,1,0:T(8,128)} %bitcast.27), calls=%async_computation.2 | async-start | bytes 262144 | tf_op jit(solution)/shard_map/all_to_all | solution.py:686
  68.2 10.6 %collective-permute-start.5 = (f32[64,128]{1,0:T(8,128)}, f32[64,128]{1,0:T(8,128)S(1)}, u32[]{:S(2)}, u32[]{:S(2)}) collective-permute-start(f32[64,128]{1,0:T(8,128)} %copy-done.28), channel_id=1, source_target_pairs={{0,1},{1,2},{2,3},{3,4},{4,5},{5,6},{6,7},{8,9},{9,10},{10,11},{11... | collective-permute-start | bytes 98312 | tf_op jit(solution)/shard_map/ppermute | solution.py:693
  71.8 6.9 %collective-permute-start.4 = (f32[64,128]{1,0:T(8,128)}, f32[64,128]{1,0:T(8,128)S(1)}, u32[]{:S(2)}, u32[]{:S(2)}) collective-permute-start(f32[64,128]{1,0:T(8,128)} %copy-done.28), channel_id=1, source_target_pairs={{1,0},{2,1},{3,2},{4,3},{5,4},{6,5},{7,6},{9,8},{10,9},{11,10},{12... | collective-permute-start | bytes 98312 | tf_op jit(solution)/shard_map/ppermute | solution.py:693
  78.8 1.0 copy-start.4
  79.7 0.9 copy-start.6
  80.7 0.9 copy-start.13
  81.6 0.9 copy-start.15
  82.5 0.8 copy-start.24
  83.2 0.8 copy-start.26

commit v6 on v5

--- a/solution.py
+++ b/solution.py
@@ -27,6 +27,8 @@
 H_ROWS = 168
 C_XD, C_YC, C_ZD, C_ZK, C_K = 0, 16, 48, 80, 112
 C_ROWS = 120
+B_XP, B_XM, B_YP, B_YM, B_Z = 0, 16, 32, 64, 96
+B_ROWS = 128
 
 
 def roll(block, shift):
@@ -55,27 +57,34 @@
     return total
 
 
-def stencil(field, effective, diagonal, x_halo, y_low, y_high, z_halo):
+def stencil(field, bonds, diagonal, outer=None):
     lane = lanes()
     height = rows_of()
     depth = lane % BS
-    zero = jnp.zeros((BS, 128), F32)
+    at_end = (depth == BS - 1) | (depth == 0)
     back = [roll(f, -32) for f in field]
-    forth = [roll(f, 32) for f in field]
+    forth = [roll(bonds(1, c) * field[c], 32) for c in range(CHUNKS)]
     out = []
     for c in range(CHUNKS):
         f = field[c]
-        x_row = zero if x_halo is None else x_halo[c : c + 1]
         total = diagonal(c) * f
-        total -= effective(0, c) * jnp.where(height == BS - 1, x_row, pltpu.roll(f, BS - 1, axis=0))
-        total -= effective(1, c) * jnp.where(height == 0, x_row, pltpu.roll(f, 1, axis=0))
-        following = back[c + 1] if c < CHUNKS - 1 else (zero if y_high is None else y_high)
-        previous = forth[c - 1] if c > 0 else (zero if y_low is None else y_low)
-        total -= effective(2, c) * jnp.where(lane < 96, back[c], following)
-        total -= effective(3, c) * jnp.where(lane >= 32, forth[c], previous)
-        ends = zero if z_halo is None else roll(z_halo, 31 - 2 * c)
-        total -= effective(4, c) * jnp.where(depth == BS - 1, ends, roll(f, -1))
-        total -= effective(5, c) * jnp.where(depth == 0, ends, roll(f, 1))
+        total -= bonds(0, c) * pltpu.roll(f, BS - 1, axis=0)
+        total -= pltpu.roll(bonds(0, c) * f, 1, axis=0)
+        following = back[c + 1] if c < CHUNKS - 1 else back[c]
+        previous = forth[c - 1] if c > 0 else jnp.zeros((BS, 128), F32)
+        total -= bonds(1, c) * jnp.where(lane < 96, back[c], following)
+        total -= jnp.where(lane >= 32, forth[c], previous)
+        total -= bonds(2, c) * roll(f, -1)
+        total -= roll(bonds(2, c) * f, 1)
+        if outer is not None:
+            x_up, x_down, y_low, y_high, z_ends = outer
+            total -= jnp.where(height == BS - 1, x_up[c : c + 1], 0.0)
+            total -= jnp.where(height == 0, x_down[c : c + 1], 0.0)
+            total -= jnp.where(at_end, roll(z_ends, 31 - 2 * c), 0.0)
+            if c == 0:
+                total -= jnp.where(lane < 32, y_low, 0.0)
+            if c == CHUNKS - 1:
+                total -= jnp.where(lane >= 96, y_high, 0.0)
         out.append(total)
     return out
 
@@ -161,9 +170,24 @@
 
 
 def setup_kernel(
-    slabs, bricks, place_ref, assignment_ref, occupancy_ref, source_ref, uptake_ref, conductance_ref,
-    info_ref, effective_ref, diagonal_ref, relax_ref, residual_ref, xy_ref, z_ref, tile_ref,
+    slabs, bricks, place_ref, assignment_hbm, occupancy_hbm, source_hbm, uptake_hbm, conductance_hbm,
+    info_ref, bonds_ref, outer_ref, diagonal_ref, residual_ref, xy_ref, z_ref, tile_ref,
+    assignment_ref, occupancy_ref, source_ref, uptake_ref, conductance_ref, relax_ref, y1_ref, arrived,
 ):
+    pairs = [
+        (assignment_hbm, assignment_ref),
+        (occupancy_hbm, occupancy_ref),
+        (source_hbm, source_ref),
+        (uptake_hbm, uptake_ref),
+        (conductance_hbm, conductance_ref),
+    ]
+    copies = [
+        pltpu.make_async_copy(there, here, arrived.at[i]) for i, (there, here) in enumerate(pairs)
+    ]
+    for copy in copies:
+        copy.start()
+    for copy in copies:
+        copy.wait()
     across = bricks // 2
     slab, patch, row, column = locate(bricks, place_ref, assignment_ref)
 
@@ -188,8 +212,8 @@
 
     def live_at(g, x, y):
         inside = (g >= 0) & (g < slabs) & (x >= 0) & (x < 2) & (y >= 0) & (y < breadth)
-        index = (jnp.clip(g, 0, slabs - 1) * 2 + jnp.clip(x, 0, 1)) * breadth + jnp.clip(y, 0, breadth - 1)
-        return jnp.where(inside, occupancy_ref[index], 0).astype(F32)
+        taken = occupancy_ref[jnp.clip(x, 0, 1), jnp.clip(y, 0, breadth - 1), jnp.clip(g, 0, slabs - 1)]
+        return jnp.where(inside, taken, 0).astype(F32)
 
     lane = lanes()
     height = rows_of()
@@ -199,7 +223,6 @@
     high_ends = []
     first_y = None
     second_y = None
-    y1 = []
     for s in range(2):
         y = column * 2 + s
         here = live_at(slab, row, y)
@@ -218,35 +241,44 @@
             taken = uptake_ref[s, :, part]
             absorbed.append(taken)
             diagonal = taken
+            values = []
             for d in range(6):
                 bond = conductance_ref[d, s, :, part]
                 if (d == 2 and k < 7) or (d == 3 and k > 0):
                     value = bond * here
                 else:
                     value = bond * jnp.where(borders[d], around[d], here)
-                effective_ref[d, c] = value
+                values.append(value)
                 diagonal = diagonal + value
-                if d == 2 and c == 7:
-                    first_y = jnp.where(borders[d], value, 0.0)
-                if d == 3 and c == 8:
-                    second_y = jnp.where(borders[d], value, 0.0)
-                if d == 4:
-                    high_ends.append(jnp.where(borders[d], value, 0.0))
-                if d == 5:
-                    low_ends.append(jnp.where(borders[d], value, 0.0))
+            if c == 7:
+                first_y = jnp.where(borders[2], values[2], 0.0)
+            if c == 8:
+                second_y = jnp.where(borders[3], values[3], 0.0)
+            high_ends.append(jnp.where(borders[4], values[4], 0.0))
+            low_ends.append(jnp.where(borders[5], values[5], 0.0))
+            outer_ref[B_XP + c : B_XP + c + 1] = values[0][BS - 1 : BS]
+            outer_ref[B_XM + c : B_XM + c + 1] = values[1][0:1]
+            bonds_ref[0, c] = jnp.where(borders[0], 0.0, values[0])
+            if c == CHUNKS - 1:
+                outer_ref[B_YP : B_YP + BS] = jnp.where(borders[2], values[2], 0.0)
+                bonds_ref[1, c] = jnp.where(borders[2], 0.0, values[2])
+            else:
+                bonds_ref[1, c] = values[2]
+            if c == 0:
+                outer_ref[B_YM : B_YM + BS] = jnp.where(borders[3], values[3], 0.0)
+            bonds_ref[2, c] = jnp.where(borders[4], 0.0, values[4])
             relax = OMEGA / diagonal
             diagonal_ref[c] = diagonal
             relax_ref[c] = relax
             forcing = source_ref[s, :, part] * here
             residual_ref[c] = forcing
-            y1.append(relax * forcing)
-
-    outcome = stencil(
-        y1, lambda d, c: effective_ref[d, c], lambda c: diagonal_ref[c], None, None, None, None
-    )
-    partial = []
-    for c in range(CHUNKS):
-        partial.append(y1[c] + relax_ref[c] * (residual_ref[c] - outcome[c]))
+            y1_ref[c] = relax * forcing
+
+    ends = [high_ends[c] + low_ends[c] for c in range(CHUNKS)]
+    outer_ref[B_Z : B_Z + BS] = pack(ends)
+    y1 = [y1_ref[c] for c in range(CHUNKS)]
+    outcome = stencil(y1, lambda d, c: bonds_ref[d, c], lambda c: diagonal_ref[c])
+    partial = [y1[c] + relax_ref[c] * (residual_ref[c] - outcome[c]) for c in range(CHUNKS)]
     write_xy(xy_ref, row, y1, partial)
     z_ref[Z_Y1 : Z_Y1 + BS] = pack(y1)
     z_ref[Z_P : Z_P + BS] = pack(partial)
@@ -268,29 +300,24 @@
     write_copies(tile_ref, edge_tile(y1, row, numbers))
 
     last = CHUNKS - 1
-    z_ends = [relax_ref[c] * (high_ends[c] + low_ends[c]) for c in range(CHUNKS)]
+    z_ends = [relax_ref[c] * ends[c] for c in range(CHUNKS)]
     for c in range(CHUNKS):
         xy_ref[XY_XD + c : XY_XD + c + 1] = facing(relax_ref[c], row)
-    high_y = jnp.where(lane >= 96, relax_ref[last] * effective_ref[2, last], 0.0)
-    low_y = jnp.where(lane < 32, relax_ref[0] * effective_ref[3, 0], 0.0)
-    z_ref[Z_D : Z_D + BS] = pack([relax_ref[c] for c in range(CHUNKS)])
-    z_ref[Z_K : Z_K + BS] = pack([low_y] + [jnp.zeros((BS, 128), F32)] * (CHUNKS - 2) + [high_y])
-    x_row = pack([facing_terms(relax_ref, effective_ref, c) for c in range(CHUNKS)])
-    z_ref[Z_X : Z_X + 8] = jnp.broadcast_to(x_row, (8, 128))
+    high_y = relax_ref[last] * outer_ref[B_YP : B_YP + BS]
+    low_y = relax_ref[0] * outer_ref[B_YM : B_YM + BS]
     xy_ref[XY_YC : XY_YC + BS] = side_blocks(relax_ref[0], relax_ref[last], z_ends[0], z_ends[last])
     xy_ref[XY_K : XY_K + 1] = facing(low_y + high_y, row)
     xy_ref[XY_K + 1 : XY_K + 2] = pack([facing(z, row) for z in z_ends])
-    toward_low = facing_terms(relax_ref, effective_ref, 0)
-    toward_high = facing_terms(relax_ref, effective_ref, last)
-    lane_row = lanes(1)
-    xy_ref[XY_K + 2 : XY_K + 3] = jnp.where(lane_row < 32, toward_low, roll_row(toward_high, 64))
+    toward = [
+        relax_ref[c][BS - 1 : BS] * outer_ref[B_XP + c : B_XP + c + 1]
+        + relax_ref[c][0:1] * outer_ref[B_XM + c : B_XM + c + 1]
+        for c in range(CHUNKS)
+    ]
+    xy_ref[XY_K + 2 : XY_K + 3] = jnp.where(lanes(1) < 32, toward[0], roll_row(toward[last], 64))
     xy_ref[XY_K + 3 : XY_K + 8] = jnp.zeros((5, 128), F32)
-
-
-def facing_terms(relax_ref, effective_ref, c):
-    upper = (relax_ref[c] * effective_ref[0, c])[BS - 1 : BS]
-    lower = (relax_ref[c] * effective_ref[1, c])[0:1]
-    return upper + lower
+    z_ref[Z_D : Z_D + BS] = pack([relax_ref[c] for c in range(CHUNKS)])
+    z_ref[Z_K : Z_K + BS] = pack([low_y] + [jnp.zeros((BS, 128), F32)] * (CHUNKS - 2) + [high_y])
+    z_ref[Z_X : Z_X + 8] = jnp.broadcast_to(pack(toward), (8, 128))
 
 
 def swap_sides(from_low, from_high):
@@ -325,7 +352,7 @@
     refs = list(refs)
     take = lambda count: [refs.pop(0) for _ in range(count)]
     info_ref, xy_ref, above_ref, below_ref, tiles_ref = take(5)
-    effective_ref, diagonal_ref, relax_ref, residual_ref = take(4)
+    bonds_ref, outer_ref, diagonal_ref, residual_ref = take(4)
     if not first:
         mapped_ref, halo_in, constant_ref, factor_ref, sums_in, scalars_in = take(6)
     if iteration > 1:
@@ -340,6 +367,9 @@
     tile_out = take(1)[0]
     if not last:
         xy_out, z_out = take(2)
+    relax_ref = take(1)[0]
+    for c in range(CHUNKS):
+        relax_ref[c] = OMEGA / diagonal_ref[c]
 
     row = info_ref[0]
     slab = info_ref[1]
@@ -540,27 +570,34 @@
 
     own = [coarse_of(here0, 0), coarse_of(here1, 0)]
 
-    effective = lambda d, c: effective_ref[d, c]
+    bonds = lambda d, c: bonds_ref[d, c]
     diagonal = lambda c: diagonal_ref[c]
     end = CHUNKS - 1
+    x_plus = outer_ref[B_XP : B_XP + CHUNKS]
+    x_minus = outer_ref[B_XM : B_XM + CHUNKS]
+    y_plus = outer_ref[B_YP : B_YP + BS]
+    y_minus = outer_ref[B_YM : B_YM + BS]
+    z_bonds = outer_ref[B_Z : B_Z + BS]
+
+    def brought(x_rows, y_block, z_block):
+        return (
+            x_plus * x_rows,
+            x_minus * x_rows,
+            y_minus * y_block,
+            y_plus * roll(y_block, 64),
+            z_bonds * z_block,
+        )
 
     y1 = [relax_ref[c] * residual[c] for c in range(CHUNKS)]
-    outcome = stencil(
-        y1, effective, diagonal, x_sides[:CHUNKS], y_sides, roll(y_sides, 64), z_first
-    )
+    outcome = stencil(y1, bonds, diagonal, brought(x_sides[:CHUNKS], y_sides, z_first))
     smoothed = []
     for c in range(CHUNKS):
         value = y1[c] + relax_ref[c] * (residual[c] - outcome[c]) + own[c // 8]
         smoothed_ref[c] = value
         smoothed.append(value)
     keys = constant_ref[C_K : C_K + 8]
-    crossing = jnp.concatenate(
-        [
-            effective(0, c)[BS - 1 : BS] * y1[c][BS - 1 : BS] + effective(1, c)[0:1] * y1[c][0:1]
-            for c in range(CHUNKS)
-        ],
-        axis=0,
-    )
+    crossing = x_plus * jnp.concatenate([f[BS - 1 : BS] for f in y1], axis=0)
+    crossing += x_minus * jnp.concatenate([f[0:1] for f in y1], axis=0)
     end_row = keys[1:2] * ends[0:1]
     corner_row = keys[0:1] * ends[1:2]
     depth_row = lane_row % BS
@@ -581,9 +618,7 @@
         + jnp.concatenate(additions, axis=0)
     )
     y_constant = constant_ref[C_YC : C_YC + BS]
-    y_crossing = jnp.where(
-        lane < 32, effective(3, 0) * y1[0], roll(effective(2, end) * y1[end], 64)
-    )
+    y_crossing = jnp.where(lane < 32, y_minus * y1[0], roll(y_plus * y1[end], 64))
     x_side_row = jnp.where(row == 0, BS - 1, 0)
     y_ends = jnp.where(lane == 0, roll(y_edges, -1), 0.0)
     y_ends = jnp.where(lane == 31, roll(y_edges, 31), y_ends)
@@ -600,12 +635,7 @@
         + jnp.where(height == x_side_row, keys[2:3] * ends[2:3], 0.0)
         + jnp.where(lane < 32, coarse_of(here1, 2), coarse_of(here0, 3))
     )
-    z_crossing = pack(
-        [
-            jnp.where(depth == BS - 1, effective(4, c), effective(5, c)) * y1[c]
-            for c in range(CHUNKS)
-        ]
-    )
+    z_crossing = z_bonds * pack(y1)
     z_coarse = jnp.where(
         even_row,
         jnp.where(depth_row < 16, coarse_of(above0, 0), coarse_of(above1, 0)),
@@ -618,7 +648,7 @@
         + jnp.where(height == x_side_row, keys[3:4] * ends[0:1], 0.0)
         + z_coarse
     )
-    mapped = stencil(smoothed, effective, diagonal, x_next, y_next, roll(y_next, 64), z_next)
+    mapped = stencil(smoothed, bonds, diagonal, brought(x_next, y_next, z_next))
     for c in range(CHUNKS):
         mapped_out[c] = mapped[c]
 
@@ -635,7 +665,7 @@
         return
     y1 = [relax_ref[c] * mapped[c] for c in range(CHUNKS)]
     write_copies(tile_out, edge_tile(y1, row, values))
-    outcome = stencil(y1, effective, diagonal, None, None, None, None)
+    outcome = stencil(y1, bonds, diagonal)
     partial = [y1[c] + relax_ref[c] * (mapped[c] - outcome[c]) for c in range(CHUNKS)]
     write_xy(xy_out, row, y1, partial)
     z_out[Z_Y1 : Z_Y1 + BS] = pack(y1)
@@ -661,14 +691,16 @@
         residual_out[s, :, part] = residual_ref[c] - step * (mapped_ref[c] + growth * search_ref[c])
 
 
-def call(kernel, name, outs, operands, scalar_operands=0, scalar_outs=0):
-    vmem = pl.BlockSpec(memory_space=pltpu.VMEM)
-    smem = pl.BlockSpec(memory_space=pltpu.SMEM)
+def call(kernel, name, outs, in_spaces, out_spaces, operands, scratch=()):
+    spec = lambda space: pl.BlockSpec(memory_space=space)
+    in_spaces = list(in_spaces) + [pltpu.VMEM] * (len(operands) - len(in_spaces))
+    out_spaces = list(out_spaces) + [pltpu.VMEM] * (len(outs) - len(out_spaces))
     return pl.pallas_call(
         kernel,
         out_shape=tuple(outs),
-        in_specs=[smem] * scalar_operands + [vmem] * (len(operands) - scalar_operands),
-        out_specs=tuple([smem] * scalar_outs + [vmem] * (len(outs) - scalar_outs)),
+        in_specs=[spec(space) for space in in_spaces],
+        out_specs=tuple(spec(space) for space in out_spaces),
+        scratch_shapes=list(scratch),
         compiler_params=pltpu.CompilerParams(vmem_limit_bytes=16 * 1024 * 1024),
         name=name,
     )(*operands)
@@ -699,16 +731,25 @@
     place = (lax.axis_index("grp") * bricks + lax.axis_index("brick")).astype(jnp.int32).reshape(1)
     field = array(*FIELD)
     copies = array(8 * slabs * bricks, 128)
-    info, effective, diagonal, relax, residual, sides, ends, tile = call(
+    info, bonds, outer, diagonal, residual, sides, ends, tile = call(
         functools.partial(setup_kernel, slabs, bricks),
         "setup",
         [
-            jax.ShapeDtypeStruct((8,), jnp.int32), array(6, *FIELD), field, field, field,
+            jax.ShapeDtypeStruct((8,), jnp.int32), array(3, *FIELD), array(B_ROWS, 128), field, field,
             array(XY_ROWS_FIRST, 128), array(Z_ROWS_FIRST, 128), copies,
         ],
-        [place, assignment, occupancy.reshape(-1), source[0, 0], uptake[0, 0], conductance[0, 0]],
-        scalar_operands=3,
-        scalar_outs=1,
+        [pltpu.SMEM] + [pl.ANY] * 5,
+        [pltpu.SMEM],
+        [
+            place, assignment, jnp.transpose(occupancy, (1, 2, 0)),
+            source[0, 0], uptake[0, 0], conductance[0, 0],
+        ],
+        [
+            pltpu.SMEM((bricks,), jnp.int32), pltpu.SMEM((2, bricks, slabs), jnp.int32),
+            pltpu.VMEM((2, BS, BS * BS), F32), pltpu.VMEM((2, BS, BS * BS), F32),
+            pltpu.VMEM((6, 2, BS, BS * BS), F32), pltpu.VMEM(FIELD, F32), pltpu.VMEM(FIELD, F32),
+            pltpu.SemaphoreType.DMA((5,)),
+        ],
     )
     mapped = residual
     directions = []
@@ -718,7 +759,7 @@
         tiles = to_all(tile, ("brick", "grp"))
         above, below = exchange_slabs(ends)
         gathered = gather_bricks(sides)
-        operands = [info, gathered, above, below, tiles, effective, diagonal, relax, residual]
+        operands = [info, gathered, above, below, tiles, bonds, outer, diagonal, residual]
         tall = array(8 * slabs, 128)
         outs = {"smoothed": field, "mapped": field}
         if not first:
@@ -741,8 +782,10 @@
             functools.partial(step_kernel, iteration, slabs, bricks),
             f"step_{iteration}",
             list(outs.values()),
+            [pltpu.SMEM],
+            [],
             operands,
-            scalar_operands=1,
+            [pltpu.VMEM(FIELD, F32)],
         )
         state |= dict(zip(outs, results))
         if first:
@@ -757,6 +800,8 @@
         finish_kernel,
         "finish",
         [brick_pair, brick_pair],
+        [],
+        [],
         [tiles, state["scalars"], residual, mapped, state["search"]] + directions,
     )
     return solution_field[None, None], residual[None, None]

time: 102 us -> 92.4 us (0.906)
  local copies, waits for them, and re-layouts: 23.1 us -> 12.8 us
    unnamed x59 -> x34, local copies, waits for them, and re-layouts: 23 us -> 12.8 us
where the time goes in v6:
time: 92.4 us; the launch traced here: 91.6 us
  starting transfers between devices  35.6 us (39%)
  blocking collectives  31.1 us (34%)
  local copies, waits for them, and re-layouts  12.8 us (14%)
  Pallas kernels  11.3 us (12%)
    all_to_all x3, starting transfers between devices, to_all(): return lax.all_to_all(copies, axes, 0, 0, tiled=True)  20.7 us
    all_gather x3, blocking collectives, gather_bricks(): return lax.all_gather(message, 'brick', axis=0, tiled=False)  16.8 us
    all_to_all x1, blocking collectives, to_all(): return lax.all_to_all(copies, axes, 0, 0, tiled=True)  14.3 us
    unnamed x34, local copies, waits for them, and re-layouts  12.8 us
    pallas_call x5, Pallas kernels, call(): pl.pallas_call(kernel, out_shape=tuple(outs), in_specs=[spec(space) for s...  11.3 us
    ppermute x3, starting transfers between devices, exchange_slabs(): lax.ppermute(message, 'grp', upward)  11 us
    ppermute x3, starting transfers between devices, exchange_slabs(): lax.ppermute(message, 'grp', downward)  3.88 us
  transfers between devices with their start and end apart: 9, of which 0 were waited for; matrix products, arithmetic and copies ran while one was open for 0% of the time, Pallas kernels for 0%

profile of v6, /device:TPU:0, one launch (start us, length us, event | category | flops | bytes accessed | tf_op | source)
XLA Modules:
  0.0 91.6 jit_solution(2549144413277149064)
XLA Ops:
  0.6 0.0 copy-start
  0.6 1.4 %copy-done = f32[1,1,6,2,32,1024]{5,4,3,2,1,0:T(8,128)S(1)} copy-done((f32[1,1,6,2,32,1024]{5,4,3,2,1,0:T(8,128)S(1)}, f32[1,1,6,2,32,1024]{5,4,3,2,1,0:T(8,128)}, u32[]{:S(2)}) %copy-start) | copy-done | bytes 1572888
  2.0 0.0 copy-start.1
  2.0 0.9 %copy-done.1 = f32[1,1,2,32,1024]{4,3,2,1,0:T(8,128)S(1)} copy-done((f32[1,1,2,32,1024]{4,3,2,1,0:T(8,128)S(1)}, f32[1,1,2,32,1024]{4,3,2,1,0:T(8,128)}, u32[]{:S(2)}) %copy-start.1) | copy-done | bytes 262168
  3.0 0.0 copy-start.2
  3.0 0.9 %copy-done.2 = f32[1,1,2,32,1024]{4,3,2,1,0:T(8,128)S(1)} copy-done((f32[1,1,2,32,1024]{4,3,2,1,0:T(8,128)S(1)}, f32[1,1,2,32,1024]{4,3,2,1,0:T(8,128)}, u32[]{:S(2)}) %copy-start.2) | copy-done | bytes 262168
  3.9 0.7 copy-done.14
  4.6 0.7 copy-done.15
  5.3 2.3 %setup.1 = (s32[8]{0:T(128)S(1)}, f32[3,16,32,128]{3,2,1,0:T(8,128)S(1)}, f32[128,128]{1,0:T(8,128)S(1)}, f32[16,32,128]{2,1,0:T(8,128)S(1)}, f32[16,32,128]{2,1...) custom-call(s32[1]{0:T(128)} %bitcast.place_ref, s32[4]{0:T(128)S(1)} %copy-done.15, ...), custom_call_target="tpu_custom_call" | custom-call | tf_op jit(solution)/shard_map/setup/pallas_call | solution.py:698
  7.6 7.3 %all-to-all-start = ((f32[32,8,128]{2,1,0:T(8,128)}), f32[32,8,128]{2,1,0:T(8,128)S(1)}, u32[]{:S(2)}, u32[]{:S(2)}) async-start(f32[32,8,128]{2,1,0:T(8,128)} %bitcast.6), calls=%async_computation | async-start | bytes 262144 | tf_op jit(solution)/shard_map/all_to_all | solution.py:718
  14.9 3.7 %collective-permute-start.1 = (f32[136,128]{1,0:T(8,128)S(1)}, f32[136,128]{1,0:T(8,128)S(1)}, u32[]{:S(2)}, u32[]{:S(2)}) collective-permute-start(f32[136,128]{1,0:T(8,128)S(1)} %get-tuple-element.41), channel_id=1, source_target_pairs={{0,1},{1,2},{2,3},{3,4},{4,5},{5,6},{6,7},{8,9},{9,10},{10,11},{11... | collective-permute-start | bytes 208904 | tf_op jit(solution)/shard_map/ppermute | solution.py:725
  18.6 1.3 %collective-permute-start = (f32[136,128]{1,0:T(8,128)S(1)}, f32[136,128]{1,0:T(8,128)S(1)}, u32[]{:S(2)}, u32[]{:S(2)}) collective-permute-start(f32[136,128]{1,0:T(8,128)S(1)} %get-tuple-element.41), channel_id=1, source_target_pairs={{1,0},{2,1},{3,2},{4,3},{5,4},{6,5},{7,6},{9,8},{10,9},{11,10},{12... | collective-permute-start | bytes 208904 | tf_op jit(solution)/shard_map/ppermute | solution.py:725
  19.9 5.7 %all-gather = f32[480,128]{1,0:T(8,128)S(1)} all-gather(f32[120,128]{1,0:T(8,128)S(1)} %get-tuple-element.40), channel_id=2, replica_groups=mesh['brick'=4,'grp'=8] {'brick'}, dimensions={0}, use_global_device_ids=true | all-gather | bytes 307200 | tf_op jit(solution)/shard_map/all_gather | solution.py:714
  25.7 0.0 collective-permute-done.1.refs_3_
  25.7 0.0 collective-permute-done.refs_2_
  25.7 0.0 all-to-all-done
  25.7 2.9 %step_0.1 = (f32[16,32,128]{2,1,0:T(8,128)S(1)}, f32[16,32,128]{2,1,0:T(8,128)S(1)}, f32[120,128]{1,0:T(8,128)S(1)}, f32[64,128]{1,0:T(8,128)S(1)}, f32[168,128]...) custom-call(s32[8]{0:T(128)S(1)} %get-tuple-element.39.refs_0_, ...), custom_call_target="tpu_custom_call" | custom-call | tf_op jit(solution)/shard_map/step_0/pallas_call | solution.py:698
  28.6 0.6 copy-done.3
  29.3 0.6 copy-done.7
  29.9 6.7 %all-to-all-start.1 = ((f32[32,8,128]{2,1,0:T(8,128)}), f32[32,8,128]{2,1,0:T(8,128)S(1)}, u32[]{:S(2)}, u32[]{:S(2)}) async-start(f32[32,8,128]{2,1,0:T(8,128)} %bitcast.9), calls=%async_computation.1 | async-start | bytes 262144 | tf_op jit(solution)/shard_map/all_to_all | solution.py:718
  36.6 3.7 %collective-permute-start.3 = (f32[64,128]{1,0:T(8,128)S(1)}, f32[64,128]{1,0:T(8,128)S(1)}, u32[]{:S(2)}, u32[]{:S(2)}) collective-permute-start(f32[64,128]{1,0:T(8,128)S(1)} %get-tuple-element.48), channel_id=1, source_target_pairs={{0,1},{1,2},{2,3},{3,4},{4,5},{5,6},{6,7},{8,9},{9,10},{10,11},{11... | collective-permute-start | bytes 98312 | tf_op jit(solution)/shard_map/ppermute | solution.py:725
  40.3 1.3 %collective-permute-start.2 = (f32[64,128]{1,0:T(8,128)S(1)}, f32[64,128]{1,0:T(8,128)S(1)}, u32[]{:S(2)}, u32[]{:S(2)}) collective-permute-start(f32[64,128]{1,0:T(8,128)S(1)} %get-tuple-element.48), channel_id=1, source_target_pairs={{1,0},{2,1},{3,2},{4,3},{5,4},{6,5},{7,6},{9,8},{10,9},{11,10},{12... | collective-permute-start | bytes 98312 | tf_op jit(solution)/shard_map/ppermute | solution.py:725
  41.6 5.4 %all-gather.1 = f32[256,128]{1,0:T(8,128)S(1)} all-gather(f32[64,128]{1,0:T(8,128)S(1)} %get-tuple-element.47), channel_id=3, replica_groups=mesh['brick'=4,'grp'=8] {'brick'}, dimensions={0}, use_global_device_ids=true | all-gather | bytes 163840 | tf_op jit(solution)/shard_map/all_gather | solution.py:714
  47.0 0.0 collective-permute-done.3.refs_3_
  47.0 0.6 copy-done.9
  47.6 0.0 collective-permute-done.2.refs_2_
  47.6 0.6 copy-done.11
  48.2 0.0 all-to-all-done.1
  48.2 0.9 copy-done.4
  49.1 0.8 copy-done.8
  49.9 0.8 copy-done.10
  50.6 0.8 copy-done.12
  51.4 3.0 %step_1.1 = (f32[16,32,128]{2,1,0:T(8,128)S(1)}, f32[16,32,128]{2,1,0:T(8,128)S(1)}, f32[16,32,128]{2,1,0:T(8,128)S(1)}, f32[16,32,128]{2,1,0:T(8,128)S(1)}, f32...) custom-call(s32[8]{0:T(128)S(1)} %get-tuple-element.39.refs_0_, ...), custom_call_target="tpu_custom_call" | custom-call | tf_op jit(solution)/shard_map/step_1/pallas_call | solution.py:698
  54.4 0.6 copy-done.5
  55.0 0.6 copy-done.13
  55.6 0.6 copy-done.16
  56.2 6.7 %all-to-all-start.2 = ((f32[32,8,128]{2,1,0:T(8,128)}), f32[32,8,128]{2,1,0:T(8,128)S(1)}, u32[]{:S(2)}, u32[]{:S(2)}) async-start(f32[32,8,128]{2,1,0:T(8,128)} %bitcast.12), calls=%async_computation.2 | async-start | bytes 262144 | tf_op jit(solution)/shard_map/all_to_all | solution.py:718
  62.9 3.7 %collective-permute-start.5 = (f32[64,128]{1,0:T(8,128)}, f32[64,128]{1,0:T(8,128)S(1)}, u32[]{:S(2)}, u32[]{:S(2)}) collective-permute-start(f32[64,128]{1,0:T(8,128)} %copy-done.16), channel_id=1, source_target_pairs={{0,1},{1,2},{2,3},{3,4},{4,5},{5,6},{6,7},{8,9},{9,10},{10,11},{11... | collective-permute-start | bytes 98312 | tf_op jit(solution)/shard_map/ppermute | solution.py:725
  66.6 1.3 %collective-permute-start.4 = (f32[64,128]{1,0:T(8,128)}, f32[64,128]{1,0:T(8,128)S(1)}, u32[]{:S(2)}, u32[]{:S(2)}) collective-permute-start(f32[64,128]{1,0:T(8,128)} %copy-done.16), channel_id=1, source_target_pairs={{1,0},{2,1},{3,2},{4,3},{5,4},{6,5},{7,6},{9,8},{10,9},{11,10},{12... | collective-permute-start | bytes 98312 | tf_op jit(solution)/shard_map/ppermute | solution.py:725
  67.9 5.6 %all-gather.2 = f32[256,128]{1,0:T(8,128)S(1)} all-gather(f32[64,128]{1,0:T(8,128)} %copy-done.13), channel_id=4, replica_groups=mesh['brick'=4,'grp'=8] {'brick'}, dimensions={0}, use_global_device_ids=true | all-gather | bytes 163840 | tf_op jit(solution)/shard_map/all_gather | solution.py:714
  73.5 0.0 collective-permute-done.5.refs_3_
  73.5 0.0 collective-permute-done.4.refs_2_
  73.5 0.0 all-to-all-done.2
  73.5 0.0 copy-start.6
  73.5 0.7 copy-done.6
  74.3 2.0 %step_2.1 = (f32[16,32,128]{2,1,0:T(8,128)S(1)}, f32[16,32,128]{2,1,0:T(8,128)S(1)}, f32[16,32,128]{2,1,0:T(8,128)S(1)}, f32[16,32,128]{2,1,0:T(8,128)S(1)}, f32...) custom-call(s32[8]{0:T(128)S(1)} %get-tuple-element.39.refs_0_, f32[4,64,128]{2,1,0:T(8,128)S(1)} %bitcast.20, ...), custom_call_target="tpu_custom_call" | custom-call | tf_op jit(solution)/shard_map/step_2/pallas_call | solution.py:698
  76.3 14.3 %all_to_all.44 = f32[32,8,128]{2,1,0:T(8,128)S(1)} all-to-all(f32[32,8,128]{2,1,0:T(8,128)S(1)} %bitcast.28), channel_id=1, replica_groups=mesh['brick'=4,'grp'=8] {'brick','grp'}, dimensions={0} | all-to-all | bytes 262144 | tf_op jit(solution)/shard_map/all_to_all | solution.py:718
  90.5 1.0 %finish.1 = (f32[2,32,1024]{2,1,0:T(8,128)}, f32[2,32,1024]{2,1,0:T(8,128)}) custom-call(f32[256,128]{1,0:T(8,128)S(1)} %bitcast.25, f32[8,128]{1,0:T(8,128)S(1)} %get-tuple-element.67.scalars_ref, f32[16,32,128]{2,1,0:T(8,128)S(1)} %get-tuple-element.68.residual_ref, f32[16,32,128]{2,1,0:T(8,128)S(1)} %get-tuple-element.69.mapped_ref, ...), custom_call_target="tpu_custom_call" | custom-call | tf_op jit(solution)/shard_map/finish/pallas_call | solution.py:698
  (14 shorter events, 0.0 us)
Async XLA Ops:
  0.6 1.4 %copy-start = (f32[1,1,6,2,32,1024]{5,4,3,2,1,0:T(8,128)S(1)}, f32[1,1,6,2,32,1024]{5,4,3,2,1,0:T(8,128)}, u32[]{:S(2)}) copy-start(f32[1,1,6,2,32,1024]{5,4,3,2,1,0:T(8,128)} %param.7) | copy-start | bytes 4718596
  2.0 0.9 %copy-start.1 = (f32[1,1,2,32,1024]{4,3,2,1,0:T(8,128)S(1)}, f32[1,1,2,32,1024]{4,3,2,1,0:T(8,128)}, u32[]{:S(2)}) copy-start(f32[1,1,2,32,1024]{4,3,2,1,0:T(8,128)} %param.5) | copy-start | bytes 786436
  3.0 0.9 %copy-start.2 = (f32[1,1,2,32,1024]{4,3,2,1,0:T(8,128)S(1)}, f32[1,1,2,32,1024]{4,3,2,1,0:T(8,128)}, u32[]{:S(2)}) copy-start(f32[1,1,2,32,1024]{4,3,2,1,0:T(8,128)} %param.6) | copy-start | bytes 786436
  3.9 0.7 copy-start.14
  4.6 0.7 copy-start.15
  7.6 18.0 %all-to-all-start = ((f32[32,8,128]{2,1,0:T(8,128)}), f32[32,8,128]{2,1,0:T(8,128)S(1)}, u32[]{:S(2)}, u32[]{:S(2)}) async-start(f32[32,8,128]{2,1,0:T(8,128)} %bitcast.6), calls=%async_computation | async-start | bytes 262144 | tf_op jit(solution)/shard_map/all_to_all | solution.py:718
  14.9 10.7 %collective-permute-start.1 = (f32[136,128]{1,0:T(8,128)S(1)}, f32[136,128]{1,0:T(8,128)S(1)}, u32[]{:S(2)}, u32[]{:S(2)}) collective-permute-start(f32[136,128]{1,0:T(8,128)S(1)} %get-tuple-element.41), channel_id=1, source_target_pairs={{0,1},{1,2},{2,3},{3,4},{4,5},{5,6},{6,7},{8,9},{9,10},{10,11},{11... | collective-permute-start | bytes 208904 | tf_op jit(solution)/shard_map/ppermute | solution.py:725
  18.6 7.0 %collective-permute-start = (f32[136,128]{1,0:T(8,128)S(1)}, f32[136,128]{1,0:T(8,128)S(1)}, u32[]{:S(2)}, u32[]{:S(2)}) collective-permute-start(f32[136,128]{1,0:T(8,128)S(1)} %get-tuple-element.41), channel_id=1, source_target_pairs={{1,0},{2,1},{3,2},{4,3},{5,4},{6,5},{7,6},{9,8},{10,9},{11,10},{12... | collective-permute-start | bytes 208904 | tf_op jit(solution)/shard_map/ppermute | solution.py:725
  28.6 0.6 copy-start.3
  29.3 0.6 copy-start.7
  29.9 18.3 %all-to-all-start.1 = ((f32[32,8,128]{2,1,0:T(8,128)}), f32[32,8,128]{2,1,0:T(8,128)S(1)}, u32[]{:S(2)}, u32[]{:S(2)}) async-start(f32[32,8,128]{2,1,0:T(8,128)} %bitcast.9), calls=%async_computation.1 | async-start | bytes 262144 | tf_op jit(solution)/shard_map/all_to_all | solution.py:718
  36.6 10.4 %collective-permute-start.3 = (f32[64,128]{1,0:T(8,128)S(1)}, f32[64,128]{1,0:T(8,128)S(1)}, u32[]{:S(2)}, u32[]{:S(2)}) collective-permute-start(f32[64,128]{1,0:T(8,128)S(1)} %get-tuple-element.48), channel_id=1, source_target_pairs={{0,1},{1,2},{2,3},{3,4},{4,5},{5,6},{6,7},{8,9},{9,10},{10,11},{11... | collective-permute-start | bytes 98312 | tf_op jit(solution)/shard_map/ppermute | solution.py:725
  40.3 7.3 %collective-permute-start.2 = (f32[64,128]{1,0:T(8,128)S(1)}, f32[64,128]{1,0:T(8,128)S(1)}, u32[]{:S(2)}, u32[]{:S(2)}) collective-permute-start(f32[64,128]{1,0:T(8,128)S(1)} %get-tuple-element.48), channel_id=1, source_target_pairs={{1,0},{2,1},{3,2},{4,3},{5,4},{6,5},{7,6},{9,8},{10,9},{11,10},{12... | collective-permute-start | bytes 98312 | tf_op jit(solution)/shard_map/ppermute | solution.py:725
  47.0 0.6 copy-start.9
  47.6 0.6 copy-start.11
  48.2 0.9 copy-start.4
  49.1 0.8 copy-start.8
  49.9 0.8 copy-start.10
  50.6 0.8 copy-start.12
  54.4 0.6 copy-start.5
  55.0 0.6 copy-start.13
  55.6 0.6 copy-start.16
  56.2 17.3 %all-to-all-start.2 = ((f32[32,8,128]{2,1,0:T(8,128)}), f32[32,8,128]{2,1,0:T(8,128)S(1)}, u32[]{:S(2)}, u32[]{:S(2)}) async-start(f32[32,8,128]{2,1,0:T(8,128)} %bitcast.12), calls=%async_computation.2 | async-start | bytes 262144 | tf_op jit(solution)/shard_map/all_to_all | solution.py:718
  62.9 10.6 %collective-permute-start.5 = (f32[64,128]{1,0:T(8,128)}, f32[64,128]{1,0:T(8,128)S(1)}, u32[]{:S(2)}, u32[]{:S(2)}) collective-permute-start(f32[64,128]{1,0:T(8,128)} %copy-done.16), channel_id=1, source_target_pairs={{0,1},{1,2},{2,3},{3,4},{4,5},{5,6},{6,7},{8,9},{9,10},{10,11},{11... | collective-permute-start | bytes 98312 | tf_op jit(solution)/shard_map/ppermute | solution.py:725
  66.6 6.9 %collective-permute-start.4 = (f32[64,128]{1,0:T(8,128)}, f32[64,128]{1,0:T(8,128)S(1)}, u32[]{:S(2)}, u32[]{:S(2)}) collective-permute-start(f32[64,128]{1,0:T(8,128)} %copy-done.16), channel_id=1, source_target_pairs={{1,0},{2,1},{3,2},{4,3},{5,4},{6,5},{7,6},{9,8},{10,9},{11,10},{12... | collective-permute-start | bytes 98312 | tf_op jit(solution)/shard_map/ppermute | solution.py:725
  73.5 0.8 copy-start.6

commit v7 on v6

--- a/solution.py
+++ b/solution.py
@@ -23,10 +23,8 @@
 Z_D, Z_K, Z_X = 64, 96, 128
 Z_ROWS_FIRST = 136
 T_N, T_Y = 16, 64
-H_X1, H_Y, H_Z1, H_ZP, H_E, H_R = 0, 32, 64, 96, 128, 160
-H_ROWS = 168
-C_XD, C_YC, C_ZD, C_ZK, C_K = 0, 16, 48, 80, 112
-C_ROWS = 120
+H_X1, H_Y, H_Z1, H_ZP, H_E, H_R, H_S = 0, 32, 64, 96, 128, 160, 168
+C_XD, C_YC, C_ZD, C_ZK, C_K, C_F = 0, 16, 48, 80, 112, 120
 B_XP, B_XM, B_YP, B_YM, B_Z = 0, 16, 32, 64, 96
 B_ROWS = 128
 
@@ -147,6 +145,11 @@
     for t in range(4):
         tile = tile + roll(edges[8 * t : 8 * t + 8], 4 * t)
     return tile
+
+
+def repeat_message(ref, rows):
+    for k in range(1, ref.shape[0] // rows):
+        ref[k * rows : (k + 1) * rows] = ref[0:rows]
 
 
 def write_copies(ref, tile):
@@ -318,6 +321,7 @@
     z_ref[Z_D : Z_D + BS] = pack([relax_ref[c] for c in range(CHUNKS)])
     z_ref[Z_K : Z_K + BS] = pack([low_y] + [jnp.zeros((BS, 128), F32)] * (CHUNKS - 2) + [high_y])
     z_ref[Z_X : Z_X + 8] = jnp.broadcast_to(pack(toward), (8, 128))
+    repeat_message(xy_ref, XY_ROWS_FIRST)
 
 
 def swap_sides(from_low, from_high):
@@ -354,20 +358,20 @@
     info_ref, xy_ref, above_ref, below_ref, tiles_ref = take(5)
     bonds_ref, outer_ref, diagonal_ref, residual_ref = take(4)
     if not first:
-        mapped_ref, halo_in, constant_ref, factor_ref, sums_in, scalars_in = take(6)
+        mapped_ref, halo_in, constant_ref, scalars_in = take(4)
     if iteration > 1:
-        search_in, search_halo_in, search_sums_in = take(3)
-    smoothed_ref, mapped_out = take(2)
+        search_in, search_halo_in = take(2)
+    smoothed_hbm, mapped_out = take(2)
     if first:
-        constant_ref, factor_ref, halo_ref, sums_ref = take(4)
+        constant_ref, halo_ref = take(2)
     else:
         residual_out, search_ref, scalars_ref = take(3)
         if not last:
-            halo_ref, sums_ref, search_halo_ref, search_sums_ref = take(4)
+            halo_ref, search_halo_ref = take(2)
     tile_out = take(1)[0]
     if not last:
         xy_out, z_out = take(2)
-    relax_ref = take(1)[0]
+    relax_ref, smoothed_ref, written = take(3)
     for c in range(CHUNKS):
         relax_ref[c] = OMEGA / diagonal_ref[c]
 
@@ -443,8 +447,6 @@
     )
     corner_x = swap_sides(low_row, high_row)
     ends = jnp.concatenate([x_ends, corner_y, corner_x, jnp.zeros((5, 128), F32)], axis=0)
-    halo = [x_sides, y_sides, z_first, z_second, y_edges, ends]
-    starts = [H_X1, H_Y, H_Z1, H_ZP, H_E, H_R]
     lane_tile = lanes(8)
     slab_tiles = []
     for g in range(slabs):
@@ -453,6 +455,8 @@
             tile = jnp.where(lane_tile == T_N + q, tile_at(info_ref[2 + q], g), tile)
         slab_tiles.append(tile)
     sums = jnp.concatenate(slab_tiles, axis=0)
+    halo = [x_sides, y_sides, z_first, z_second, y_edges, ends, sums]
+    starts = [H_X1, H_Y, H_Z1, H_ZP, H_E, H_R, H_S]
 
     if first:
         residual = [residual_ref[c] for c in range(CHUNKS)]
@@ -495,7 +499,7 @@
             scale = 1.0 / (a * b - off * off)
             i00, i01, i11 = b * scale, off * scale, a * scale
             u0, u1 = t0, t1
-            factor_ref[8 * g : 8 * g + 8] = jnp.concatenate(
+            constant_ref[C_F + 8 * g : C_F + 8 * g + 8] = jnp.concatenate(
                 [i00, i01, i11, t0, t1, jnp.zeros((3, 128), F32)], axis=0
             )
     else:
@@ -522,11 +526,6 @@
             if not last:
                 search_halo_ref[span] = block
             halo.append(halo_in[span] - step * block)
-        if growth is not None:
-            sums = sums + growth * search_sums_in[...]
-        if not last:
-            search_sums_ref[...] = sums
-        sums = sums_in[...] - step * sums
         kept = [energy, curvature, step]
         if growth is not None:
             kept = [energy, curvature, scalars[2:3, 0:1], step, growth]
@@ -535,8 +534,7 @@
     if not last:
         for start, block in zip(starts, halo):
             halo_ref[start : start + block.shape[0]] = block
-        sums_ref[...] = sums
-    x_sides, y_sides, z_first, z_second, y_edges, ends = halo
+    x_sides, y_sides, z_first, z_second, y_edges, ends, sums = halo
 
     forward = []
     for g in range(slabs):
@@ -544,7 +542,7 @@
         if g > 0:
             t0 = t0 + w0 * v0
             t1 = t1 + w1 * v1
-        factor = factor_ref[8 * g : 8 * g + 8]
+        factor = constant_ref[C_F + 8 * g : C_F + 8 * g + 8]
         v0 = factor[0:1] * t0 + factor[1:2] * t1
         v1 = factor[1:2] * t0 + factor[2:3] * t1
         w0, w1 = factor[3:4], factor[4:5]
@@ -554,7 +552,7 @@
     for g in reversed(range(slabs)):
         v0, v1 = forward[g]
         if g < slabs - 1:
-            factor = factor_ref[8 * g : 8 * g + 8]
+            factor = constant_ref[C_F + 8 * g : C_F + 8 * g + 8]
             s0, s1 = factor[3:4] * n0, factor[4:5] * n1
             v0 = v0 + factor[0:1] * s0 + factor[1:2] * s1
             v1 = v1 + factor[1:2] * s0 + factor[2:3] * s1
@@ -595,6 +593,8 @@
         value = y1[c] + relax_ref[c] * (residual[c] - outcome[c]) + own[c // 8]
         smoothed_ref[c] = value
         smoothed.append(value)
+    writing = pltpu.make_async_copy(smoothed_ref, smoothed_hbm, written)
+    writing.start()
     keys = constant_ref[C_K : C_K + 8]
     crossing = x_plus * jnp.concatenate([f[BS - 1 : BS] for f in y1], axis=0)
     crossing += x_minus * jnp.concatenate([f[0:1] for f in y1], axis=0)
@@ -662,6 +662,7 @@
         values.append(total_of([search_ref[c] * smoothed[c] for c in range(CHUNKS)]))
     if last:
         write_copies(tile_out, tile_of(values))
+        writing.wait()
         return
     y1 = [relax_ref[c] * mapped[c] for c in range(CHUNKS)]
     write_copies(tile_out, edge_tile(y1, row, values))
@@ -670,6 +671,8 @@
     write_xy(xy_out, row, y1, partial)
     z_out[Z_Y1 : Z_Y1 + BS] = pack(y1)
     z_out[Z_P : Z_P + BS] = pack(partial)
+    repeat_message(xy_out, XY_ROWS)
+    writing.wait()
 
 
 def finish_kernel(
@@ -710,10 +713,6 @@
     return jax.ShapeDtypeStruct(shape, F32)
 
 
-def gather_bricks(message):
-    return lax.all_gather(message, "brick", axis=0, tiled=False)
-
-
 def to_all(copies, axes):
     return lax.all_to_all(copies, axes, 0, 0, tiled=True)
 
@@ -736,9 +735,9 @@
         "setup",
         [
             jax.ShapeDtypeStruct((8,), jnp.int32), array(3, *FIELD), array(B_ROWS, 128), field, field,
-            array(XY_ROWS_FIRST, 128), array(Z_ROWS_FIRST, 128), copies,
+            array(bricks * XY_ROWS_FIRST, 128), array(Z_ROWS_FIRST, 128), copies,
         ],
-        [pltpu.SMEM] + [pl.ANY] * 5,
+        [pltpu.SMEM] + [pltpu.HBM] * 5,
         [pltpu.SMEM],
         [
             place, assignment, jnp.transpose(occupancy, (1, 2, 0)),
@@ -758,34 +757,31 @@
         first, last = iteration == 0, iteration == ITERS - 1
         tiles = to_all(tile, ("brick", "grp"))
         above, below = exchange_slabs(ends)
-        gathered = gather_bricks(sides)
+        gathered = to_all(sides, "brick").reshape(bricks, -1, 128)
         operands = [info, gathered, above, below, tiles, bonds, outer, diagonal, residual]
-        tall = array(8 * slabs, 128)
+        tall = array(H_S + 8 * slabs, 128)
         outs = {"smoothed": field, "mapped": field}
         if not first:
-            operands += [mapped] + [state[k] for k in ("halo", "constant", "factor", "sums", "scalars")]
+            operands += [mapped] + [state[k] for k in ("halo", "constant", "scalars")]
         if iteration > 1:
-            operands += [state[k] for k in ("search", "search_halo", "search_sums")]
+            operands += [state[k] for k in ("search", "search_halo")]
         if first:
-            outs |= {"constant": array(C_ROWS, 128), "factor": tall, "halo": array(H_ROWS, 128), "sums": tall}
+            outs |= {"constant": array(C_F + 8 * slabs, 128), "halo": tall}
         else:
             outs |= {"residual": field, "search": field, "scalars": array(8, 128)}
             if not last:
-                outs |= {
-                    "halo": array(H_ROWS, 128), "sums": tall,
-                    "search_halo": array(H_ROWS, 128), "search_sums": tall,
-                }
+                outs |= {"halo": tall, "search_halo": tall}
         outs["tile"] = copies
         if not last:
-            outs |= {"sides": array(XY_ROWS, 128), "ends": array(Z_ROWS, 128)}
+            outs |= {"sides": array(bricks * XY_ROWS, 128), "ends": array(Z_ROWS, 128)}
         results = call(
             functools.partial(step_kernel, iteration, slabs, bricks),
             f"step_{iteration}",
             list(outs.values()),
             [pltpu.SMEM],
-            [],
+            [pltpu.HBM],
             operands,
-            [pltpu.VMEM(FIELD, F32)],
+            [pltpu.VMEM(FIELD, F32), pltpu.VMEM(FIELD, F32), pltpu.SemaphoreType.DMA],
         )
         state |= dict(zip(outs, results))
         if first:

time: 92.4 us -> 100 us (1.082)
  waiting for transfers between devices: 0.02 us -> 13.9 us
  starting transfers between devices: 35.6 us -> 29 us
  local copies, waits for them, and re-layouts: 12.8 us -> 6.46 us
  blocking collectives: 31.1 us -> 37.3 us
    all_to_all x1 -> x4, blocking collectives: 14.3 us -> 37.3 us  [to_all(): return lax.all_to_all(copies, axes, 0, 0, tiled=True)]
    all_gather x3 -> x0, blocking collectives: 16.8 us -> none  [gather_bricks(): return lax.all_gather(message, 'brick', axis=0, tiled=False)]
    ppermute x3, waiting for transfers between devices: 0.01 us -> 12.5 us  [exchange_slabs(): lax.ppermute(message, 'grp', downward)]
    all_to_all x3, starting transfers between devices: 20.7 us -> 14.1 us  [to_all(): return lax.all_to_all(copies, axes, 0, 0, tiled=True)]
    unnamed x34 -> x18, local copies, waits for them, and re-layouts: 12.8 us -> 6.46 us
    ppermute x3, waiting for transfers between devices: 0.01 us -> 1.38 us  [exchange_slabs(): lax.ppermute(message, 'grp', upward)]
  transfers between devices with their start and end apart: 9 -> 9, of which waited for: 0 -> 6; matrix products, arithmetic and copies ran while one was open for 0% -> 0% of each run, Pallas kernels for 0% -> 0%
where the time goes in v7:
time: 100 us; the launch traced here: 99.3 us
  blocking collectives  37.3 us (37%)
  starting transfers between devices  29 us (29%)
  waiting for transfers between devices  13.9 us (14%)
  Pallas kernels  11.8 us (12%)
  local copies, waits for them, and re-layouts  6.46 us (6%)
    all_to_all x4, blocking collectives, to_all(): return lax.all_to_all(copies, axes, 0, 0, tiled=True)  37.3 us
    all_to_all x3, starting transfers between devices, to_all(): return lax.all_to_all(copies, axes, 0, 0, tiled=True)  14.1 us
    ppermute x3, waiting for transfers between devices, exchange_slabs(): lax.ppermute(message, 'grp', downward)  12.5 us
    pallas_call x5, Pallas kernels, call(): pl.pallas_call(kernel, out_shape=tuple(outs), in_specs=[spec(space) for s...  11.8 us
    ppermute x3, starting transfers between devices, exchange_slabs(): lax.ppermute(message, 'grp', upward)  11 us
    unnamed x18, local copies, waits for them, and re-layouts  6.46 us
    ppermute x3, starting transfers between devices, exchange_slabs(): lax.ppermute(message, 'grp', downward)  3.88 us
  transfers between devices with their start and end apart: 9, of which 6 were waited for; matrix products, arithmetic and copies ran while one was open for 0% of the time, Pallas kernels for 0%

profile of v7, /device:TPU:0, one launch (start us, length us, event | category | flops | bytes accessed | tf_op | source)
XLA Modules:
  0.0 99.3 jit_solution(3797167896732836857)
XLA Ops:
  0.6 0.0 copy-start
  0.6 1.4 %copy-done = f32[1,1,6,2,32,1024]{5,4,3,2,1,0:T(8,128)S(1)} copy-done((f32[1,1,6,2,32,1024]{5,4,3,2,1,0:T(8,128)S(1)}, f32[1,1,6,2,32,1024]{5,4,3,2,1,0:T(8,128)}, u32[]{:S(2)}) %copy-start) | copy-done | bytes 1572888
  2.0 0.0 copy-start.1
  2.0 0.9 copy-done.1
  3.0 0.0 copy-start.2
  3.0 0.9 copy-done.2
  3.9 0.0 copy-start.7
  3.9 0.7 copy-done.7
  4.6 0.0 copy-start.8
  4.6 0.7 copy-done.8
  5.3 2.3 %setup.1 = (s32[8]{0:T(128)S(1)}, f32[3,16,32,128]{3,2,1,0:T(8,128)S(1)}, f32[128,128]{1,0:T(8,128)S(1)}, f32[16,32,128]{2,1,0:T(8,128)S(1)}, f32[16,32,128]{2,1...) custom-call(s32[1]{0:T(128)} %bitcast.place_ref, s32[4]{0:T(128)S(1)} %copy-done.8, ...), custom_call_target="tpu_custom_call" | custom-call | tf_op jit(solution)/shard_map/setup/pallas_call | solution.py:701
  7.6 9.9 %all_to_all.71.refs_1_ = f32[4,120,128]{2,1,0:T(8,128)S(1)} all-to-all(f32[4,120,128]{2,1,0:T(8,128)S(1)} %bitcast.25), channel_id=1, replica_groups=mesh['brick'=4,'grp'=8] {'brick'}, dimensions={0} | all-to-all | bytes 491520 | tf_op jit(solution)/shard_map/all_to_all | solution.py:717
  17.5 4.9 %all-to-all-start.1 = ((f32[32,8,128]{2,1,0:T(8,128)}), f32[32,8,128]{2,1,0:T(8,128)S(1)}, u32[]{:S(2)}, u32[]{:S(2)}) async-start(f32[32,8,128]{2,1,0:T(8,128)} %bitcast.6), calls=%async_computation.1 | async-start | bytes 262144 | tf_op jit(solution)/shard_map/all_to_all | solution.py:717
  22.4 3.7 %collective-permute-start.1 = (f32[136,128]{1,0:T(8,128)S(1)}, f32[136,128]{1,0:T(8,128)S(1)}, u32[]{:S(2)}, u32[]{:S(2)}) collective-permute-start(f32[136,128]{1,0:T(8,128)S(1)} %get-tuple-element.37), channel_id=1, source_target_pairs={{0,1},{1,2},{2,3},{3,4},{4,5},{5,6},{6,7},{8,9},{9,10},{10,11},{11... | collective-permute-start | bytes 208904 | tf_op jit(solution)/shard_map/ppermute | solution.py:724
  26.1 1.3 %collective-permute-start = (f32[136,128]{1,0:T(8,128)S(1)}, f32[136,128]{1,0:T(8,128)S(1)}, u32[]{:S(2)}, u32[]{:S(2)}) collective-permute-start(f32[136,128]{1,0:T(8,128)S(1)} %get-tuple-element.37), channel_id=1, source_target_pairs={{1,0},{2,1},{3,2},{4,3},{5,4},{6,5},{7,6},{9,8},{10,9},{11,10},{12... | collective-permute-start | bytes 208904 | tf_op jit(solution)/shard_map/ppermute | solution.py:724
  27.4 0.8 collective-permute-done.1.refs_3_
  28.3 4.1 %collective-permute-done.refs_2_ = f32[136,128]{1,0:T(8,128)S(1)} collective-permute-done((f32[136,128]{1,0:T(8,128)S(1)}, f32[136,128]{1,0:T(8,128)S(1)}, u32[]{:S(2)}, u32[]{:S(2)}) %collective-permute-start) | collective-permute-done | bytes 69664 | tf_op jit(solution)/shard_map/ppermute | solution.py:724
  32.3 0.0 all-to-all-done.1
  32.3 3.1 %step_0.1 = (f32[16,32,128]{2,1,0:T(8,128)S(1)}, f32[16,32,128]{2,1,0:T(8,128)S(1)}, f32[184,128]{1,0:T(8,128)S(1)}, f32[232,128]{1,0:T(8,128)S(1)}, f32[256,128...) custom-call(s32[8]{0:T(128)S(1)} %get-tuple-element.35.refs_0_, f32[4,120,128]{2,1,0:T(8,128)S(1)} %all_to_all.71.refs_1_, ...), custom_call_target="tpu_custom_call" | custom-call | tf_op jit(solution)/shard_map/step_0/pallas_call | solution.py:701
  35.5 0.0 copy-start.5
  35.5 7.2 %all_to_all.72.refs_1_ = f32[4,64,128]{2,1,0:T(8,128)S(1)} all-to-all(f32[4,64,128]{2,1,0:T(8,128)S(1)} %bitcast.28), channel_id=1, replica_groups=mesh['brick'=4,'grp'=8] {'brick'}, dimensions={0} | all-to-all | bytes 262144 | tf_op jit(solution)/shard_map/all_to_all | solution.py:717
  42.7 0.0 copy-done.5
  42.7 4.6 %all-to-all-start.3 = ((f32[32,8,128]{2,1,0:T(8,128)}), f32[32,8,128]{2,1,0:T(8,128)S(1)}, u32[]{:S(2)}, u32[]{:S(2)}) async-start(f32[32,8,128]{2,1,0:T(8,128)} %bitcast.9), calls=%async_computation.3 | async-start | bytes 262144 | tf_op jit(solution)/shard_map/all_to_all | solution.py:717
  47.3 3.7 %collective-permute-start.3 = (f32[64,128]{1,0:T(8,128)S(1)}, f32[64,128]{1,0:T(8,128)S(1)}, u32[]{:S(2)}, u32[]{:S(2)}) collective-permute-start(f32[64,128]{1,0:T(8,128)S(1)} %get-tuple-element.44), channel_id=1, source_target_pairs={{0,1},{1,2},{2,3},{3,4},{4,5},{5,6},{6,7},{8,9},{9,10},{10,11},{11... | collective-permute-start | bytes 98312 | tf_op jit(solution)/shard_map/ppermute | solution.py:724
  51.0 1.3 %collective-permute-start.2 = (f32[64,128]{1,0:T(8,128)S(1)}, f32[64,128]{1,0:T(8,128)S(1)}, u32[]{:S(2)}, u32[]{:S(2)}) collective-permute-start(f32[64,128]{1,0:T(8,128)S(1)} %get-tuple-element.44), channel_id=1, source_target_pairs={{1,0},{2,1},{3,2},{4,3},{5,4},{6,5},{7,6},{9,8},{10,9},{11,10},{12... | collective-permute-start | bytes 98312 | tf_op jit(solution)/shard_map/ppermute | solution.py:724
  52.3 0.3 collective-permute-done.3.refs_3_
  52.5 4.2 %collective-permute-done.2.refs_2_ = f32[64,128]{1,0:T(8,128)S(1)} collective-permute-done((f32[64,128]{1,0:T(8,128)S(1)}, f32[64,128]{1,0:T(8,128)S(1)}, u32[]{:S(2)}, u32[]{:S(2)}) %collective-permute-start.2) | collective-permute-done | bytes 32800 | tf_op jit(solution)/shard_map/ppermute | solution.py:724
  56.8 0.0 all-to-all-done.3
  56.8 0.0 copy-start.6
  56.8 0.9 copy-done.6
  57.7 3.3 %step_1.1 = (f32[16,32,128]{2,1,0:T(8,128)S(1)}, f32[16,32,128]{2,1,0:T(8,128)S(1)}, f32[16,32,128]{2,1,0:T(8,128)S(1)}, f32[16,32,128]{2,1,0:T(8,128)S(1)}, f32...) custom-call(s32[8]{0:T(128)S(1)} %get-tuple-element.35.refs_0_, ...), custom_call_target="tpu_custom_call" | custom-call | tf_op jit(solution)/shard_map/step_1/pallas_call | solution.py:701
  60.9 0.0 copy-start.3
  61.0 7.2 %all_to_all.73.refs_1_ = f32[4,64,128]{2,1,0:T(8,128)S(1)} all-to-all(f32[4,64,128]{2,1,0:T(8,128)S(1)} %bitcast.27), channel_id=1, replica_groups=mesh['brick'=4,'grp'=8] {'brick'}, dimensions={0} | all-to-all | bytes 262144 | tf_op jit(solution)/shard_map/all_to_all | solution.py:717
  68.1 0.0 copy-done.3
  68.1 4.6 %all-to-all-start.5 = ((f32[32,8,128]{2,1,0:T(8,128)}), f32[32,8,128]{2,1,0:T(8,128)S(1)}, u32[]{:S(2)}, u32[]{:S(2)}) async-start(f32[32,8,128]{2,1,0:T(8,128)} %bitcast.12), calls=%async_computation.5 | async-start | bytes 262144 | tf_op jit(solution)/shard_map/all_to_all | solution.py:717
  72.7 3.7 %collective-permute-start.5 = (f32[64,128]{1,0:T(8,128)S(1)}, f32[64,128]{1,0:T(8,128)S(1)}, u32[]{:S(2)}, u32[]{:S(2)}) collective-permute-start(f32[64,128]{1,0:T(8,128)S(1)} %get-tuple-element.50), channel_id=1, source_target_pairs={{0,1},{1,2},{2,3},{3,4},{4,5},{5,6},{6,7},{8,9},{9,10},{10,11},{11... | collective-permute-start | bytes 98312 | tf_op jit(solution)/shard_map/ppermute | solution.py:724
  76.4 1.3 %collective-permute-start.4 = (f32[64,128]{1,0:T(8,128)S(1)}, f32[64,128]{1,0:T(8,128)S(1)}, u32[]{:S(2)}, u32[]{:S(2)}) collective-permute-start(f32[64,128]{1,0:T(8,128)S(1)} %get-tuple-element.50), channel_id=1, source_target_pairs={{1,0},{2,1},{3,2},{4,3},{5,4},{6,5},{7,6},{9,8},{10,9},{11,10},{12... | collective-permute-start | bytes 98312 | tf_op jit(solution)/shard_map/ppermute | solution.py:724
  77.7 0.3 collective-permute-done.5.refs_3_
  78.0 4.2 %collective-permute-done.4.refs_2_ = f32[64,128]{1,0:T(8,128)S(1)} collective-permute-done((f32[64,128]{1,0:T(8,128)S(1)}, f32[64,128]{1,0:T(8,128)S(1)}, u32[]{:S(2)}, u32[]{:S(2)}) %collective-permute-start.4) | collective-permute-done | bytes 32800 | tf_op jit(solution)/shard_map/ppermute | solution.py:724
  82.2 0.0 all-to-all-done.5
  82.2 0.0 copy-start.4
  82.2 0.9 copy-done.4
  83.1 2.0 %step_2.1 = (f32[16,32,128]{2,1,0:T(8,128)S(1)}, f32[16,32,128]{2,1,0:T(8,128)S(1)}, f32[16,32,128]{2,1,0:T(8,128)S(1)}, f32[16,32,128]{2,1,0:T(8,128)S(1)}, f32...) custom-call(s32[8]{0:T(128)S(1)} %get-tuple-element.35.refs_0_, f32[4,64,128]{2,1,0:T(8,128)S(1)} %all_to_all.73.refs_1_, ...), custom_call_target="tpu_custom_call" | custom-call | tf_op jit(solution)/shard_map/step_2/pallas_call | solution.py:701
  85.2 13.1 %all_to_all.74 = f32[32,8,128]{2,1,0:T(8,128)S(1)} all-to-all(f32[32,8,128]{2,1,0:T(8,128)S(1)} %bitcast.26), channel_id=1, replica_groups=mesh['brick'=4,'grp'=8] {'brick','grp'}, dimensions={0} | all-to-all | bytes 262144 | tf_op jit(solution)/shard_map/all_to_all | solution.py:717
  98.3 1.0 %finish.1 = (f32[2,32,1024]{2,1,0:T(8,128)}, f32[2,32,1024]{2,1,0:T(8,128)}) custom-call(f32[256,128]{1,0:T(8,128)S(1)} %bitcast.22, f32[8,128]{1,0:T(8,128)S(1)} %get-tuple-element.59.scalars_ref, f32[16,32,128]{2,1,0:T(8,128)S(1)} %get-tuple-element.60.residual_ref, f32[16,32,128]{2,1,0:T(8,128)S(1)} %get-tuple-element.61.mapped_ref, ...), custom_call_target="tpu_custom_call" | custom-call | tf_op jit(solution)/shard_map/finish/pallas_call | solution.py:701
  (1 shorter events, 0.0 us)
Async XLA Ops:
  0.6 1.4 %copy-start = (f32[1,1,6,2,32,1024]{5,4,3,2,1,0:T(8,128)S(1)}, f32[1,1,6,2,32,1024]{5,4,3,2,1,0:T(8,128)}, u32[]{:S(2)}) copy-start(f32[1,1,6,2,32,1024]{5,4,3,2,1,0:T(8,128)} %param.7) | copy-start | bytes 4718596
  2.0 0.9 copy-start.1
  3.0 0.9 copy-start.2
  3.9 0.7 copy-start.7
  4.6 0.7 copy-start.8
  17.5 14.8 %all-to-all-start.1 = ((f32[32,8,128]{2,1,0:T(8,128)}), f32[32,8,128]{2,1,0:T(8,128)S(1)}, u32[]{:S(2)}, u32[]{:S(2)}) async-start(f32[32,8,128]{2,1,0:T(8,128)} %bitcast.6), calls=%async_computation.1 | async-start | bytes 262144 | tf_op jit(solution)/shard_map/all_to_all | solution.py:717
  22.4 5.8 %collective-permute-start.1 = (f32[136,128]{1,0:T(8,128)S(1)}, f32[136,128]{1,0:T(8,128)S(1)}, u32[]{:S(2)}, u32[]{:S(2)}) collective-permute-start(f32[136,128]{1,0:T(8,128)S(1)} %get-tuple-element.37), channel_id=1, source_target_pairs={{0,1},{1,2},{2,3},{3,4},{4,5},{5,6},{6,7},{8,9},{9,10},{10,11},{11... | collective-permute-start | bytes 208904 | tf_op jit(solution)/shard_map/ppermute | solution.py:724
  26.1 6.2 %collective-permute-start = (f32[136,128]{1,0:T(8,128)S(1)}, f32[136,128]{1,0:T(8,128)S(1)}, u32[]{:S(2)}, u32[]{:S(2)}) collective-permute-start(f32[136,128]{1,0:T(8,128)S(1)} %get-tuple-element.37), channel_id=1, source_target_pairs={{1,0},{2,1},{3,2},{4,3},{5,4},{6,5},{7,6},{9,8},{10,9},{11,10},{12... | collective-permute-start | bytes 208904 | tf_op jit(solution)/shard_map/ppermute | solution.py:724
  35.5 7.2 %copy-start.5 = (f32[232,128]{1,0:T(8,128)}, f32[232,128]{1,0:T(8,128)S(1)}, u32[]{:S(2)}) copy-start(f32[232,128]{1,0:T(8,128)S(1)} %get-tuple-element.47.refs_10_) | copy-start | bytes 356356
  42.7 14.1 %all-to-all-start.3 = ((f32[32,8,128]{2,1,0:T(8,128)}), f32[32,8,128]{2,1,0:T(8,128)S(1)}, u32[]{:S(2)}, u32[]{:S(2)}) async-start(f32[32,8,128]{2,1,0:T(8,128)} %bitcast.9), calls=%async_computation.3 | async-start | bytes 262144 | tf_op jit(solution)/shard_map/all_to_all | solution.py:717
  47.3 5.3 %collective-permute-start.3 = (f32[64,128]{1,0:T(8,128)S(1)}, f32[64,128]{1,0:T(8,128)S(1)}, u32[]{:S(2)}, u32[]{:S(2)}) collective-permute-start(f32[64,128]{1,0:T(8,128)S(1)} %get-tuple-element.44), channel_id=1, source_target_pairs={{0,1},{1,2},{2,3},{3,4},{4,5},{5,6},{6,7},{8,9},{9,10},{10,11},{11... | collective-permute-start | bytes 98312 | tf_op jit(solution)/shard_map/ppermute | solution.py:724
  51.0 5.8 %collective-permute-start.2 = (f32[64,128]{1,0:T(8,128)S(1)}, f32[64,128]{1,0:T(8,128)S(1)}, u32[]{:S(2)}, u32[]{:S(2)}) collective-permute-start(f32[64,128]{1,0:T(8,128)S(1)} %get-tuple-element.44), channel_id=1, source_target_pairs={{1,0},{2,1},{3,2},{4,3},{5,4},{6,5},{7,6},{9,8},{10,9},{11,10},{12... | collective-permute-start | bytes 98312 | tf_op jit(solution)/shard_map/ppermute | solution.py:724
  56.8 0.9 copy-start.6
  60.9 7.2 %copy-start.3 = (f32[232,128]{1,0:T(8,128)}, f32[232,128]{1,0:T(8,128)S(1)}, u32[]{:S(2)}) copy-start(f32[232,128]{1,0:T(8,128)S(1)} %get-tuple-element.57.refs_14_) | copy-start | bytes 356356
  68.1 14.1 %all-to-all-start.5 = ((f32[32,8,128]{2,1,0:T(8,128)}), f32[32,8,128]{2,1,0:T(8,128)S(1)}, u32[]{:S(2)}, u32[]{:S(2)}) async-start(f32[32,8,128]{2,1,0:T(8,128)} %bitcast.12), calls=%async_computation.5 | async-start | bytes 262144 | tf_op jit(solution)/shard_map/all_to_all | solution.py:717
  72.7 5.3 %collective-permute-start.5 = (f32[64,128]{1,0:T(8,128)S(1)}, f32[64,128]{1,0:T(8,128)S(1)}, u32[]{:S(2)}, u32[]{:S(2)}) collective-permute-start(f32[64,128]{1,0:T(8,128)S(1)} %get-tuple-element.50), channel_id=1, source_target_pairs={{0,1},{1,2},{2,3},{3,4},{4,5},{5,6},{6,7},{8,9},{9,10},{10,11},{11... | collective-permute-start | bytes 98312 | tf_op jit(solution)/shard_map/ppermute | solution.py:724
  76.4 5.8 %collective-permute-start.4 = (f32[64,128]{1,0:T(8,128)S(1)}, f32[64,128]{1,0:T(8,128)S(1)}, u32[]{:S(2)}, u32[]{:S(2)}) collective-permute-start(f32[64,128]{1,0:T(8,128)S(1)} %get-tuple-element.50), channel_id=1, source_target_pairs={{1,0},{2,1},{3,2},{4,3},{5,4},{6,5},{7,6},{9,8},{10,9},{11,10},{12... | collective-permute-start | bytes 98312 | tf_op jit(solution)/shard_map/ppermute | solution.py:724
  82.2 0.9 copy-start.4

commit v8 on v7

--- a/solution.py
+++ b/solution.py
@@ -147,11 +147,6 @@
     return tile
 
 
-def repeat_message(ref, rows):
-    for k in range(1, ref.shape[0] // rows):
-        ref[k * rows : (k + 1) * rows] = ref[0:rows]
-
-
 def write_copies(ref, tile):
     for k in range(ref.shape[0] // 8):
         ref[8 * k : 8 * k + 8] = tile
@@ -173,24 +168,10 @@
 
 
 def setup_kernel(
-    slabs, bricks, place_ref, assignment_hbm, occupancy_hbm, source_hbm, uptake_hbm, conductance_hbm,
+    slabs, bricks, place_ref, assignment_ref, occupancy_ref, source_ref, uptake_ref, conductance_ref,
     info_ref, bonds_ref, outer_ref, diagonal_ref, residual_ref, xy_ref, z_ref, tile_ref,
-    assignment_ref, occupancy_ref, source_ref, uptake_ref, conductance_ref, relax_ref, y1_ref, arrived,
+    relax_ref, y1_ref,
 ):
-    pairs = [
-        (assignment_hbm, assignment_ref),
-        (occupancy_hbm, occupancy_ref),
-        (source_hbm, source_ref),
-        (uptake_hbm, uptake_ref),
-        (conductance_hbm, conductance_ref),
-    ]
-    copies = [
-        pltpu.make_async_copy(there, here, arrived.at[i]) for i, (there, here) in enumerate(pairs)
-    ]
-    for copy in copies:
-        copy.start()
-    for copy in copies:
-        copy.wait()
     across = bricks // 2
     slab, patch, row, column = locate(bricks, place_ref, assignment_ref)
 
@@ -321,7 +302,6 @@
     z_ref[Z_D : Z_D + BS] = pack([relax_ref[c] for c in range(CHUNKS)])
     z_ref[Z_K : Z_K + BS] = pack([low_y] + [jnp.zeros((BS, 128), F32)] * (CHUNKS - 2) + [high_y])
     z_ref[Z_X : Z_X + 8] = jnp.broadcast_to(pack(toward), (8, 128))
-    repeat_message(xy_ref, XY_ROWS_FIRST)
 
 
 def swap_sides(from_low, from_high):
@@ -671,7 +651,6 @@
     write_xy(xy_out, row, y1, partial)
     z_out[Z_Y1 : Z_Y1 + BS] = pack(y1)
     z_out[Z_P : Z_P + BS] = pack(partial)
-    repeat_message(xy_out, XY_ROWS)
     writing.wait()
 
 
@@ -735,19 +714,16 @@
         "setup",
         [
             jax.ShapeDtypeStruct((8,), jnp.int32), array(3, *FIELD), array(B_ROWS, 128), field, field,
-            array(bricks * XY_ROWS_FIRST, 128), array(Z_ROWS_FIRST, 128), copies,
+            array(XY_ROWS_FIRST, 128), array(Z_ROWS_FIRST, 128), copies,
         ],
-        [pltpu.SMEM] + [pltpu.HBM] * 5,
+        [pltpu.SMEM] * 3,
         [pltpu.SMEM],
         [
             place, assignment, jnp.transpose(occupancy, (1, 2, 0)),
             source[0, 0], uptake[0, 0], conductance[0, 0],
         ],
         [
-            pltpu.SMEM((bricks,), jnp.int32), pltpu.SMEM((2, bricks, slabs), jnp.int32),
-            pltpu.VMEM((2, BS, BS * BS), F32), pltpu.VMEM((2, BS, BS * BS), F32),
-            pltpu.VMEM((6, 2, BS, BS * BS), F32), pltpu.VMEM(FIELD, F32), pltpu.VMEM(FIELD, F32),
-            pltpu.SemaphoreType.DMA((5,)),
+            pltpu.VMEM(FIELD, F32), pltpu.VMEM(FIELD, F32),
         ],
     )
     mapped = residual
@@ -757,7 +733,7 @@
         first, last = iteration == 0, iteration == ITERS - 1
         tiles = to_all(tile, ("brick", "grp"))
         above, below = exchange_slabs(ends)
-        gathered = to_all(sides, "brick").reshape(bricks, -1, 128)
+        gathered = lax.all_gather(sides, "brick", axis=0, tiled=False)
         operands = [info, gathered, above, below, tiles, bonds, outer, diagonal, residual]
         tall = array(H_S + 8 * slabs, 128)
         outs = {"smoothed": field, "mapped": field}
@@ -773,7 +749,7 @@
                 outs |= {"halo": tall, "search_halo": tall}
         outs["tile"] = copies
         if not last:
-            outs |= {"sides": array(bricks * XY_ROWS, 128), "ends": array(Z_ROWS, 128)}
+            outs |= {"sides": array(XY_ROWS, 128), "ends": array(Z_ROWS, 128)}
         results = call(
             functools.partial(step_kernel, iteration, slabs, bricks),
             f"step_{iteration}",

time: 100 us -> 88 us (0.88)
  waiting for transfers between devices: 13.9 us -> 0.02 us
  starting transfers between devices: 29 us -> 35.6 us
  blocking collectives: 37.3 us -> 30.8 us
  local copies, waits for them, and re-layouts: 6.46 us -> 8.33 us
    all_to_all x4 -> x1, blocking collectives: 37.3 us -> 14.3 us  [to_all(): return lax.all_to_all(copies, axes, 0, 0, tiled=True)]
    all_gather x0 -> x3, blocking collectives: none -> 16.6 us  [on_device(): gathered = lax.all_gather(sides, 'brick', axis=0, tiled=False)]
    ppermute x3, waiting for transfers between devices: 12.5 us -> 0.01 us  [exchange_slabs(): lax.ppermute(message, 'grp', downward)]
    all_to_all x3, starting transfers between devices: 14.1 us -> 20.7 us  [to_all(): return lax.all_to_all(copies, axes, 0, 0, tiled=True)]
    unnamed x18 -> x20, local copies, waits for them, and re-layouts: 6.46 us -> 8.33 us
    ppermute x3, waiting for transfers between devices: 1.38 us -> 0.01 us  [exchange_slabs(): lax.ppermute(message, 'grp', upward)]
  transfers between devices with their start and end apart: 9 -> 9, of which waited for: 6 -> 0; matrix products, arithmetic and copies ran while one was open for 0% -> 0% of each run, Pallas kernels for 0% -> 0%
where the time goes in v8:
time: 88 us; the launch traced here: 87.4 us
  starting transfers between devices  35.6 us (40%)
  blocking collectives  30.8 us (35%)
  Pallas kernels  11.8 us (13%)
  local copies, waits for them, and re-layouts  8.33 us (9%)
    all_to_all x3, starting transfers between devices, to_all(): return lax.all_to_all(copies, axes, 0, 0, tiled=True)  20.7 us
    all_gather x3, blocking collectives, on_device(): gathered = lax.all_gather(sides, 'brick', axis=0, tiled=False)  16.6 us
    all_to_all x1, blocking collectives, to_all(): return lax.all_to_all(copies, axes, 0, 0, tiled=True)  14.3 us
    pallas_call x5, Pallas kernels, call(): pl.pallas_call(kernel, out_shape=tuple(outs), in_specs=[spec(space) for s...  11.8 us
    ppermute x3, starting transfers between devices, exchange_slabs(): lax.ppermute(message, 'grp', upward)  11 us
    unnamed x20, local copies, waits for them, and re-layouts  8.33 us
    ppermute x3, starting transfers between devices, exchange_slabs(): lax.ppermute(message, 'grp', downward)  3.88 us
  transfers between devices with their start and end apart: 9, of which 0 were waited for; matrix products, arithmetic and copies ran while one was open for 0% of the time, Pallas kernels for 0%

profile of v8, /device:TPU:0, one launch (start us, length us, event | category | flops | bytes accessed | tf_op | source)
XLA Modules:
  0.0 87.4 jit_solution(9020958577690221806)
XLA Ops:
  0.6 0.0 copy-start
  0.6 1.4 %copy-done = f32[1,1,6,2,32,1024]{5,4,3,2,1,0:T(8,128)S(1)} copy-done((f32[1,1,6,2,32,1024]{5,4,3,2,1,0:T(8,128)S(1)}, f32[1,1,6,2,32,1024]{5,4,3,2,1,0:T(8,128)}, u32[]{:S(2)}) %copy-start) | copy-done | bytes 1572888
  2.0 0.0 copy-start.1
  2.0 0.9 %copy-done.1 = f32[1,1,2,32,1024]{4,3,2,1,0:T(8,128)S(1)} copy-done((f32[1,1,2,32,1024]{4,3,2,1,0:T(8,128)S(1)}, f32[1,1,2,32,1024]{4,3,2,1,0:T(8,128)}, u32[]{:S(2)}) %copy-start.1) | copy-done | bytes 262168
  3.0 0.0 copy-start.2
  3.0 0.9 %copy-done.2 = f32[1,1,2,32,1024]{4,3,2,1,0:T(8,128)S(1)} copy-done((f32[1,1,2,32,1024]{4,3,2,1,0:T(8,128)S(1)}, f32[1,1,2,32,1024]{4,3,2,1,0:T(8,128)}, u32[]{:S(2)}) %copy-start.2) | copy-done | bytes 262168
  3.9 0.0 copy-start.7
  3.9 0.7 copy-done.7
  4.6 0.0 copy-start.8
  4.6 0.7 copy-done.8
  5.3 2.3 %setup.1 = (s32[8]{0:T(128)S(1)}, f32[3,16,32,128]{3,2,1,0:T(8,128)S(1)}, f32[128,128]{1,0:T(8,128)S(1)}, f32[16,32,128]{2,1,0:T(8,128)S(1)}, f32[16,32,128]{2,1...) custom-call(s32[1]{0:T(128)} %bitcast.place_ref, s32[4]{0:T(128)S(1)} %copy-done.8, ...), custom_call_target="tpu_custom_call" | custom-call | tf_op jit(solution)/shard_map/setup/pallas_call | solution.py:680
  7.6 7.3 %all-to-all-start = ((f32[32,8,128]{2,1,0:T(8,128)}), f32[32,8,128]{2,1,0:T(8,128)S(1)}, u32[]{:S(2)}, u32[]{:S(2)}) async-start(f32[32,8,128]{2,1,0:T(8,128)} %bitcast.6), calls=%async_computation | async-start | bytes 262144 | tf_op jit(solution)/shard_map/all_to_all | solution.py:696
  14.9 3.7 %collective-permute-start.1 = (f32[136,128]{1,0:T(8,128)S(1)}, f32[136,128]{1,0:T(8,128)S(1)}, u32[]{:S(2)}, u32[]{:S(2)}) collective-permute-start(f32[136,128]{1,0:T(8,128)S(1)} %get-tuple-element.37), channel_id=1, source_target_pairs={{0,1},{1,2},{2,3},{3,4},{4,5},{5,6},{6,7},{8,9},{9,10},{10,11},{11... | collective-permute-start | bytes 208904 | tf_op jit(solution)/shard_map/ppermute | solution.py:703
  18.6 1.3 %collective-permute-start = (f32[136,128]{1,0:T(8,128)S(1)}, f32[136,128]{1,0:T(8,128)S(1)}, u32[]{:S(2)}, u32[]{:S(2)}) collective-permute-start(f32[136,128]{1,0:T(8,128)S(1)} %get-tuple-element.37), channel_id=1, source_target_pairs={{1,0},{2,1},{3,2},{4,3},{5,4},{6,5},{7,6},{9,8},{10,9},{11,10},{12... | collective-permute-start | bytes 208904 | tf_op jit(solution)/shard_map/ppermute | solution.py:703
  19.9 5.7 %all-gather = f32[480,128]{1,0:T(8,128)S(1)} all-gather(f32[120,128]{1,0:T(8,128)S(1)} %get-tuple-element.36), channel_id=2, replica_groups=mesh['brick'=4,'grp'=8] {'brick'}, dimensions={0}, use_global_device_ids=true | all-gather | bytes 307200 | tf_op jit(solution)/shard_map/all_gather | solution.py:736
  25.6 0.0 collective-permute-done.1.refs_3_
  25.6 0.0 collective-permute-done.refs_2_
  25.6 0.0 all-to-all-done
  25.7 3.1 %step_0.1 = (f32[16,32,128]{2,1,0:T(8,128)S(1)}, f32[16,32,128]{2,1,0:T(8,128)S(1)}, f32[184,128]{1,0:T(8,128)S(1)}, f32[232,128]{1,0:T(8,128)S(1)}, f32[256,128...) custom-call(s32[8]{0:T(128)S(1)} %get-tuple-element.35.refs_0_, f32[4,120,128]{2,1,0:T(8,128)S(1)} %bitcast.19, ...), custom_call_target="tpu_custom_call" | custom-call | tf_op jit(solution)/shard_map/step_0/pallas_call | solution.py:680
  28.8 0.0 copy-start.5
  28.8 0.6 copy-done.5
  29.5 6.7 %all-to-all-start.1 = ((f32[32,8,128]{2,1,0:T(8,128)}), f32[32,8,128]{2,1,0:T(8,128)S(1)}, u32[]{:S(2)}, u32[]{:S(2)}) async-start(f32[32,8,128]{2,1,0:T(8,128)} %bitcast.9), calls=%async_computation.1 | async-start | bytes 262144 | tf_op jit(solution)/shard_map/all_to_all | solution.py:696
  36.2 3.7 %collective-permute-start.3 = (f32[64,128]{1,0:T(8,128)S(1)}, f32[64,128]{1,0:T(8,128)S(1)}, u32[]{:S(2)}, u32[]{:S(2)}) collective-permute-start(f32[64,128]{1,0:T(8,128)S(1)} %get-tuple-element.44), channel_id=1, source_target_pairs={{0,1},{1,2},{2,3},{3,4},{4,5},{5,6},{6,7},{8,9},{9,10},{10,11},{11... | collective-permute-start | bytes 98312 | tf_op jit(solution)/shard_map/ppermute | solution.py:703
  39.9 1.3 %collective-permute-start.2 = (f32[64,128]{1,0:T(8,128)S(1)}, f32[64,128]{1,0:T(8,128)S(1)}, u32[]{:S(2)}, u32[]{:S(2)}) collective-permute-start(f32[64,128]{1,0:T(8,128)S(1)} %get-tuple-element.44), channel_id=1, source_target_pairs={{1,0},{2,1},{3,2},{4,3},{5,4},{6,5},{7,6},{9,8},{10,9},{11,10},{12... | collective-permute-start | bytes 98312 | tf_op jit(solution)/shard_map/ppermute | solution.py:703
  41.1 5.4 %all-gather.1 = f32[256,128]{1,0:T(8,128)S(1)} all-gather(f32[64,128]{1,0:T(8,128)S(1)} %get-tuple-element.43), channel_id=3, replica_groups=mesh['brick'=4,'grp'=8] {'brick'}, dimensions={0}, use_global_device_ids=true | all-gather | bytes 163840 | tf_op jit(solution)/shard_map/all_gather | solution.py:736
  46.6 0.0 collective-permute-done.3.refs_3_
  46.6 0.0 collective-permute-done.2.refs_2_
  46.6 0.0 all-to-all-done.1
  46.6 0.0 copy-start.6
  46.6 0.9 %copy-done.6 = f32[232,128]{1,0:T(8,128)S(1)} copy-done((f32[232,128]{1,0:T(8,128)S(1)}, f32[232,128]{1,0:T(8,128)}, u32[]{:S(2)}) %copy-start.6) | copy-done | bytes 118808
  47.5 3.2 %step_1.1 = (f32[16,32,128]{2,1,0:T(8,128)S(1)}, f32[16,32,128]{2,1,0:T(8,128)S(1)}, f32[16,32,128]{2,1,0:T(8,128)S(1)}, f32[16,32,128]{2,1,0:T(8,128)S(1)}, f32...) custom-call(s32[8]{0:T(128)S(1)} %get-tuple-element.35.refs_0_, ...), custom_call_target="tpu_custom_call" | custom-call | tf_op jit(solution)/shard_map/step_1/pallas_call | solution.py:680
  50.8 0.0 copy-start.3
  50.8 0.6 copy-done.3
  51.4 0.0 copy-start.9
  51.4 0.6 copy-done.9
  52.0 6.7 %all-to-all-start.2 = ((f32[32,8,128]{2,1,0:T(8,128)}), f32[32,8,128]{2,1,0:T(8,128)S(1)}, u32[]{:S(2)}, u32[]{:S(2)}) async-start(f32[32,8,128]{2,1,0:T(8,128)} %bitcast.12), calls=%async_computation.2 | async-start | bytes 262144 | tf_op jit(solution)/shard_map/all_to_all | solution.py:696
  58.7 3.7 %collective-permute-start.5 = (f32[64,128]{1,0:T(8,128)}, f32[64,128]{1,0:T(8,128)S(1)}, u32[]{:S(2)}, u32[]{:S(2)}) collective-permute-start(f32[64,128]{1,0:T(8,128)} %copy-done.9), channel_id=1, source_target_pairs={{0,1},{1,2},{2,3},{3,4},{4,5},{5,6},{6,7},{8,9},{9,10},{10,11},{11... | collective-permute-start | bytes 98312 | tf_op jit(solution)/shard_map/ppermute | solution.py:703
  62.4 1.3 %collective-permute-start.4 = (f32[64,128]{1,0:T(8,128)}, f32[64,128]{1,0:T(8,128)S(1)}, u32[]{:S(2)}, u32[]{:S(2)}) collective-permute-start(f32[64,128]{1,0:T(8,128)} %copy-done.9), channel_id=1, source_target_pairs={{1,0},{2,1},{3,2},{4,3},{5,4},{6,5},{7,6},{9,8},{10,9},{11,10},{12... | collective-permute-start | bytes 98312 | tf_op jit(solution)/shard_map/ppermute | solution.py:703
  63.7 5.4 %all-gather.2 = f32[256,128]{1,0:T(8,128)S(1)} all-gather(f32[64,128]{1,0:T(8,128)S(1)} %get-tuple-element.49), channel_id=4, replica_groups=mesh['brick'=4,'grp'=8] {'brick'}, dimensions={0}, use_global_device_ids=true | all-gather | bytes 163840 | tf_op jit(solution)/shard_map/all_gather | solution.py:736
  69.1 0.0 collective-permute-done.5.refs_3_
  69.1 0.0 collective-permute-done.4.refs_2_
  69.1 0.0 all-to-all-done.2
  69.2 0.0 copy-start.4
  69.2 0.9 %copy-done.4 = f32[232,128]{1,0:T(8,128)S(1)} copy-done((f32[232,128]{1,0:T(8,128)S(1)}, f32[232,128]{1,0:T(8,128)}, u32[]{:S(2)}) %copy-start.4) | copy-done | bytes 118808
  70.1 2.0 %step_2.1 = (f32[16,32,128]{2,1,0:T(8,128)S(1)}, f32[16,32,128]{2,1,0:T(8,128)S(1)}, f32[16,32,128]{2,1,0:T(8,128)S(1)}, f32[16,32,128]{2,1,0:T(8,128)S(1)}, f32...) custom-call(s32[8]{0:T(128)S(1)} %get-tuple-element.35.refs_0_, f32[4,64,128]{2,1,0:T(8,128)S(1)} %bitcast.20, ...), custom_call_target="tpu_custom_call" | custom-call | tf_op jit(solution)/shard_map/step_2/pallas_call | solution.py:680
  72.1 14.3 %all_to_all.44 = f32[32,8,128]{2,1,0:T(8,128)S(1)} all-to-all(f32[32,8,128]{2,1,0:T(8,128)S(1)} %bitcast.28), channel_id=1, replica_groups=mesh['brick'=4,'grp'=8] {'brick','grp'}, dimensions={0} | all-to-all | bytes 262144 | tf_op jit(solution)/shard_map/all_to_all | solution.py:696
  86.4 1.0 %finish.1 = (f32[2,32,1024]{2,1,0:T(8,128)}, f32[2,32,1024]{2,1,0:T(8,128)}) custom-call(f32[256,128]{1,0:T(8,128)S(1)} %bitcast.25, f32[8,128]{1,0:T(8,128)S(1)} %get-tuple-element.59.scalars_ref, f32[16,32,128]{2,1,0:T(8,128)S(1)} %get-tuple-element.60.residual_ref, f32[16,32,128]{2,1,0:T(8,128)S(1)} %get-tuple-element.61.mapped_ref, ...), custom_call_target="tpu_custom_call" | custom-call | tf_op jit(solution)/shard_map/finish/pallas_call | solution.py:680
  (1 shorter events, 0.0 us)
Async XLA Ops:
  0.6 1.4 %copy-start = (f32[1,1,6,2,32,1024]{5,4,3,2,1,0:T(8,128)S(1)}, f32[1,1,6,2,32,1024]{5,4,3,2,1,0:T(8,128)}, u32[]{:S(2)}) copy-start(f32[1,1,6,2,32,1024]{5,4,3,2,1,0:T(8,128)} %param.7) | copy-start | bytes 4718596
  2.0 0.9 %copy-start.1 = (f32[1,1,2,32,1024]{4,3,2,1,0:T(8,128)S(1)}, f32[1,1,2,32,1024]{4,3,2,1,0:T(8,128)}, u32[]{:S(2)}) copy-start(f32[1,1,2,32,1024]{4,3,2,1,0:T(8,128)} %param.5) | copy-start | bytes 786436
  3.0 0.9 %copy-start.2 = (f32[1,1,2,32,1024]{4,3,2,1,0:T(8,128)S(1)}, f32[1,1,2,32,1024]{4,3,2,1,0:T(8,128)}, u32[]{:S(2)}) copy-start(f32[1,1,2,32,1024]{4,3,2,1,0:T(8,128)} %param.6) | copy-start | bytes 786436
  3.9 0.7 copy-start.7
  4.6 0.7 copy-start.8
  7.6 18.0 %all-to-all-start = ((f32[32,8,128]{2,1,0:T(8,128)}), f32[32,8,128]{2,1,0:T(8,128)S(1)}, u32[]{:S(2)}, u32[]{:S(2)}) async-start(f32[32,8,128]{2,1,0:T(8,128)} %bitcast.6), calls=%async_computation | async-start | bytes 262144 | tf_op jit(solution)/shard_map/all_to_all | solution.py:696
  14.9 10.7 %collective-permute-start.1 = (f32[136,128]{1,0:T(8,128)S(1)}, f32[136,128]{1,0:T(8,128)S(1)}, u32[]{:S(2)}, u32[]{:S(2)}) collective-permute-start(f32[136,128]{1,0:T(8,128)S(1)} %get-tuple-element.37), channel_id=1, source_target_pairs={{0,1},{1,2},{2,3},{3,4},{4,5},{5,6},{6,7},{8,9},{9,10},{10,11},{11... | collective-permute-start | bytes 208904 | tf_op jit(solution)/shard_map/ppermute | solution.py:703
  18.6 7.0 %collective-permute-start = (f32[136,128]{1,0:T(8,128)S(1)}, f32[136,128]{1,0:T(8,128)S(1)}, u32[]{:S(2)}, u32[]{:S(2)}) collective-permute-start(f32[136,128]{1,0:T(8,128)S(1)} %get-tuple-element.37), channel_id=1, source_target_pairs={{1,0},{2,1},{3,2},{4,3},{5,4},{6,5},{7,6},{9,8},{10,9},{11,10},{12... | collective-permute-start | bytes 208904 | tf_op jit(solution)/shard_map/ppermute | solution.py:703
  28.8 0.7 copy-start.5
  29.5 17.1 %all-to-all-start.1 = ((f32[32,8,128]{2,1,0:T(8,128)}), f32[32,8,128]{2,1,0:T(8,128)S(1)}, u32[]{:S(2)}, u32[]{:S(2)}) async-start(f32[32,8,128]{2,1,0:T(8,128)} %bitcast.9), calls=%async_computation.1 | async-start | bytes 262144 | tf_op jit(solution)/shard_map/all_to_all | solution.py:696
  36.2 10.4 %collective-permute-start.3 = (f32[64,128]{1,0:T(8,128)S(1)}, f32[64,128]{1,0:T(8,128)S(1)}, u32[]{:S(2)}, u32[]{:S(2)}) collective-permute-start(f32[64,128]{1,0:T(8,128)S(1)} %get-tuple-element.44), channel_id=1, source_target_pairs={{0,1},{1,2},{2,3},{3,4},{4,5},{5,6},{6,7},{8,9},{9,10},{10,11},{11... | collective-permute-start | bytes 98312 | tf_op jit(solution)/shard_map/ppermute | solution.py:703
  39.9 6.7 %collective-permute-start.2 = (f32[64,128]{1,0:T(8,128)S(1)}, f32[64,128]{1,0:T(8,128)S(1)}, u32[]{:S(2)}, u32[]{:S(2)}) collective-permute-start(f32[64,128]{1,0:T(8,128)S(1)} %get-tuple-element.44), channel_id=1, source_target_pairs={{1,0},{2,1},{3,2},{4,3},{5,4},{6,5},{7,6},{9,8},{10,9},{11,10},{12... | collective-permute-start | bytes 98312 | tf_op jit(solution)/shard_map/ppermute | solution.py:703
  46.6 0.9 %copy-start.6 = (f32[232,128]{1,0:T(8,128)S(1)}, f32[232,128]{1,0:T(8,128)}, u32[]{:S(2)}) copy-start(f32[232,128]{1,0:T(8,128)} %copy-done.5) | copy-start | bytes 356356
  50.8 0.7 copy-start.3
  51.4 0.6 copy-start.9
  52.0 17.1 %all-to-all-start.2 = ((f32[32,8,128]{2,1,0:T(8,128)}), f32[32,8,128]{2,1,0:T(8,128)S(1)}, u32[]{:S(2)}, u32[]{:S(2)}) async-start(f32[32,8,128]{2,1,0:T(8,128)} %bitcast.12), calls=%async_computation.2 | async-start | bytes 262144 | tf_op jit(solution)/shard_map/all_to_all | solution.py:696
  58.7 10.4 %collective-permute-start.5 = (f32[64,128]{1,0:T(8,128)}, f32[64,128]{1,0:T(8,128)S(1)}, u32[]{:S(2)}, u32[]{:S(2)}) collective-permute-start(f32[64,128]{1,0:T(8,128)} %copy-done.9), channel_id=1, source_target_pairs={{0,1},{1,2},{2,3},{3,4},{4,5},{5,6},{6,7},{8,9},{9,10},{10,11},{11... | collective-permute-start | bytes 98312 | tf_op jit(solution)/shard_map/ppermute | solution.py:703
  62.4 6.7 %collective-permute-start.4 = (f32[64,128]{1,0:T(8,128)}, f32[64,128]{1,0:T(8,128)S(1)}, u32[]{:S(2)}, u32[]{:S(2)}) collective-permute-start(f32[64,128]{1,0:T(8,128)} %copy-done.9), channel_id=1, source_target_pairs={{1,0},{2,1},{3,2},{4,3},{5,4},{6,5},{7,6},{9,8},{10,9},{11,10},{12... | collective-permute-start | bytes 98312 | tf_op jit(solution)/shard_map/ppermute | solution.py:703
  69.2 0.9 %copy-start.4 = (f32[232,128]{1,0:T(8,128)S(1)}, f32[232,128]{1,0:T(8,128)}, u32[]{:S(2)}) copy-start(f32[232,128]{1,0:T(8,128)} %copy-done.3) | copy-start | bytes 356356

commit v9 on v8

--- a/solution.py
+++ b/solution.py
@@ -313,13 +313,13 @@
     return jnp.where((lanes(rows) // 32) % 2 == 0, low, high)
 
 
-def search_scalars(tiles, scalars, iteration):
-    energy = tiles[2:3, T_N : T_N + 1]
-    curvature = tiles[3:4, T_N : T_N + 1]
+def search_scalars(sums, scalars, iteration):
+    energy = sums[0]
+    curvature = sums[1]
     if iteration == 0:
         return energy, curvature, energy / curvature, None
     growth = energy / scalars[0:1, 0:1]
-    curvature = curvature + growth * (2.0 * tiles[4:5, T_N : T_N + 1] + growth * scalars[1:2, 0:1])
+    curvature = curvature + growth * (2.0 * sums[2] + growth * scalars[1:2, 0:1])
     return energy, curvature, energy / curvature, growth
 
 
@@ -352,6 +352,8 @@
     if not last:
         xy_out, z_out = take(2)
     relax_ref, smoothed_ref, written = take(3)
+    if not last:
+        tile_ref, sent = take(2)
     for c in range(CHUNKS):
         relax_ref[c] = OMEGA / diagonal_ref[c]
 
@@ -484,8 +486,9 @@
             )
     else:
         scalars = None if iteration == 1 else scalars_in[...]
+        tile = sum_tiles(tiles_ref, slabs * bricks)
         energy, curvature, step, growth = search_scalars(
-            sum_tiles(tiles_ref, slabs * bricks), scalars, iteration - 1
+            [tile[i : i + 1, T_N : T_N + 1] for i in range(2, 5)], scalars, iteration - 1
         )
         step_row = jnp.broadcast_to(step, (1, 128))
         residual = []
@@ -571,7 +574,10 @@
     smoothed = []
     for c in range(CHUNKS):
         value = y1[c] + relax_ref[c] * (residual[c] - outcome[c]) + own[c // 8]
-        smoothed_ref[c] = value
+        if last:
+            smoothed_ref[c] = value
+        else:
+            smoothed_ref[c // 8, :, 128 * (c % 8) : 128 * (c % 8 + 1)] = value
         smoothed.append(value)
     writing = pltpu.make_async_copy(smoothed_ref, smoothed_hbm, written)
     writing.start()
@@ -641,39 +647,65 @@
     if not first:
         values.append(total_of([search_ref[c] * smoothed[c] for c in range(CHUNKS)]))
     if last:
-        write_copies(tile_out, tile_of(values))
+        level = lane_row // 16
+        line = jnp.zeros((1, 128), F32)
+        for i in range(2, 5):
+            line = jnp.where(level == i, values[i], line)
+        for k in range(tile_out.shape[0]):
+            tile_out[k] = line
         writing.wait()
         return
     y1 = [relax_ref[c] * mapped[c] for c in range(CHUNKS)]
-    write_copies(tile_out, edge_tile(y1, row, values))
+    write_copies(tile_ref, edge_tile(y1, row, values))
+    sending = pltpu.make_async_copy(tile_ref, tile_out, sent)
+    sending.start()
     outcome = stencil(y1, bonds, diagonal)
     partial = [y1[c] + relax_ref[c] * (mapped[c] - outcome[c]) for c in range(CHUNKS)]
     write_xy(xy_out, row, y1, partial)
     z_out[Z_Y1 : Z_Y1 + BS] = pack(y1)
     z_out[Z_P : Z_P + BS] = pack(partial)
     writing.wait()
+    sending.wait()
 
 
 def finish_kernel(
-    tiles_ref, scalars_ref, residual_ref, mapped_ref, search_ref, first_ref, second_ref, third_ref,
-    solution_ref, residual_out,
+    tiles_ref, scalars_ref, residual_ref, mapped_ref, search_ref, third_ref, first_hbm, second_hbm,
+    solution_hbm, residual_hbm, first_ref, second_ref, arrived,
 ):
+    copies = [
+        pltpu.make_async_copy(first_hbm, first_ref, arrived.at[0]),
+        pltpu.make_async_copy(second_hbm, second_ref, arrived.at[1]),
+    ]
+    for copy in copies:
+        copy.start()
     scalars = scalars_ref[...]
-    tiles = sum_tiles(tiles_ref, tiles_ref.shape[0] // 8)
-    _, _, step, growth = search_scalars(tiles, scalars, ITERS - 1)
+    line = tiles_ref[0]
+    for k in range(1, tiles_ref.shape[0]):
+        line = line + tiles_ref[k]
+    _, _, step, growth = search_scalars(
+        [line[:, 16 * i : 16 * i + 1] for i in range(2, 5)], scalars, ITERS - 1
+    )
     first_step, second_step, second_growth = scalars[2:3, 0:1], scalars[3:4, 0:1], scalars[4:5, 0:1]
-    third_weight = step
     second_weight = second_step + growth * step
     first_weight = first_step + second_growth * second_weight
+    for copy in copies:
+        copy.wait()
     for c in range(CHUNKS):
-        s, part = c // 8, pl.ds(128 * (c % 8), 128)
-        solution_ref[s, :, part] = (
-            first_weight * first_ref[c] + second_weight * second_ref[c] + third_weight * third_ref[c]
-        )
-        residual_out[s, :, part] = residual_ref[c] - step * (mapped_ref[c] + growth * search_ref[c])
-
-
-def call(kernel, name, outs, in_spaces, out_spaces, operands, scratch=()):
+        s, part = c // 8, slice(128 * (c % 8), 128 * (c % 8 + 1))
+        total = first_weight * first_ref[s, :, part] + second_weight * second_ref[s, :, part]
+        first_ref[s, :, part] = total + step * third_ref[c]
+        second_ref[s, :, part] = residual_ref[c] - step * (mapped_ref[c] + growth * search_ref[c])
+    copies = [
+        pltpu.make_async_copy(first_ref, solution_hbm, arrived.at[0]),
+        pltpu.make_async_copy(second_ref, residual_hbm, arrived.at[1]),
+    ]
+    for copy in copies:
+        copy.start()
+    for copy in copies:
+        copy.wait()
+
+
+def call(kernel, name, outs, in_spaces, out_spaces, operands, scratch=(), aliases=None):
     spec = lambda space: pl.BlockSpec(memory_space=space)
     in_spaces = list(in_spaces) + [pltpu.VMEM] * (len(operands) - len(in_spaces))
     out_spaces = list(out_spaces) + [pltpu.VMEM] * (len(outs) - len(out_spaces))
@@ -683,6 +715,7 @@
         in_specs=[spec(space) for space in in_spaces],
         out_specs=tuple(spec(space) for space in out_spaces),
         scratch_shapes=list(scratch),
+        input_output_aliases=aliases or {},
         compiler_params=pltpu.CompilerParams(vmem_limit_bytes=16 * 1024 * 1024),
         name=name,
     )(*operands)
@@ -708,6 +741,7 @@
     bricks = lax.axis_size("brick")
     place = (lax.axis_index("grp") * bricks + lax.axis_index("brick")).astype(jnp.int32).reshape(1)
     field = array(*FIELD)
+    brick_pair = array(2, BS, BS * BS)
     copies = array(8 * slabs * bricks, 128)
     info, bonds, outer, diagonal, residual, sides, ends, tile = call(
         functools.partial(setup_kernel, slabs, bricks),
@@ -736,7 +770,7 @@
         gathered = lax.all_gather(sides, "brick", axis=0, tiled=False)
         operands = [info, gathered, above, below, tiles, bonds, outer, diagonal, residual]
         tall = array(H_S + 8 * slabs, 128)
-        outs = {"smoothed": field, "mapped": field}
+        outs = {"smoothed": field if last else brick_pair, "mapped": field}
         if not first:
             operands += [mapped] + [state[k] for k in ("halo", "constant", "scalars")]
         if iteration > 1:
@@ -747,17 +781,23 @@
             outs |= {"residual": field, "search": field, "scalars": array(8, 128)}
             if not last:
                 outs |= {"halo": tall, "search_halo": tall}
-        outs["tile"] = copies
+        outs["tile"] = array(slabs * bricks, 1, 128) if last else copies
         if not last:
             outs |= {"sides": array(XY_ROWS, 128), "ends": array(Z_ROWS, 128)}
+        moved = ("smoothed",) if last else ("smoothed", "tile")
         results = call(
             functools.partial(step_kernel, iteration, slabs, bricks),
             f"step_{iteration}",
             list(outs.values()),
             [pltpu.SMEM],
-            [pltpu.HBM],
+            [pl.ANY if name in moved else pltpu.VMEM for name in outs],
             operands,
-            [pltpu.VMEM(FIELD, F32), pltpu.VMEM(FIELD, F32), pltpu.SemaphoreType.DMA],
+            [
+                pltpu.VMEM(FIELD, F32),
+                pltpu.VMEM(FIELD if last else (2, BS, BS * BS), F32),
+                pltpu.SemaphoreType.DMA,
+            ]
+            + ([] if last else [pltpu.VMEM(copies.shape, F32), pltpu.SemaphoreType.DMA]),
         )
         state |= dict(zip(outs, results))
         if first:
@@ -767,14 +807,18 @@
         residual = state.get("residual", residual)
         directions.append(state["smoothed"])
     tiles = to_all(tile, ("brick", "grp"))
-    brick_pair = array(2, BS, BS * BS)
     solution_field, residual = call(
         finish_kernel,
         "finish",
         [brick_pair, brick_pair],
-        [],
-        [],
-        [tiles, state["scalars"], residual, mapped, state["search"]] + directions,
+        [pltpu.VMEM] * 6 + [pl.ANY] * 2,
+        [pl.ANY] * 2,
+        [tiles, state["scalars"], residual, mapped, state["search"], directions[2]] + directions[:2],
+        [
+            pltpu.VMEM(brick_pair.shape, F32), pltpu.VMEM(brick_pair.shape, F32),
+            pltpu.SemaphoreType.DMA((2,)),
+        ],
+        {6: 0, 7: 1},
     )
     return solution_field[None, None], residual[None, None]
 

time: 88 us -> 84.4 us (0.959)
  local copies, waits for them, and re-layouts: 8.33 us -> 4.64 us
    unnamed x20 -> x10, local copies, waits for them, and re-layouts: 8.33 us -> 4.64 us
where the time goes in v9:
time: 84.4 us; the launch traced here: 83.8 us
  starting transfers between devices  35.6 us (42%)
  blocking collectives  30.2 us (36%)
  Pallas kernels  12.5 us (15%)
  local copies, waits for them, and re-layouts  4.64 us (5%)
    all_to_all x3, starting transfers between devices, to_all(): return lax.all_to_all(copies, axes, 0, 0, tiled=True)  20.7 us
    all_gather x3, blocking collectives, on_device(): gathered = lax.all_gather(sides, 'brick', axis=0, tiled=False)  16.6 us
    all_to_all x1, blocking collectives, to_all(): return lax.all_to_all(copies, axes, 0, 0, tiled=True)  13.6 us
    pallas_call x5, Pallas kernels, call(): pl.pallas_call(kernel, out_shape=tuple(outs), in_specs=[spec(space) for s...  12.5 us
    ppermute x3, starting transfers between devices, exchange_slabs(): lax.ppermute(message, 'grp', upward)  11 us
    unnamed x10, local copies, waits for them, and re-layouts  4.64 us
    ppermute x3, starting transfers between devices, exchange_slabs(): lax.ppermute(message, 'grp', downward)  3.88 us
  transfers between devices with their start and end apart: 9, of which 0 were waited for; matrix products, arithmetic and copies ran while one was open for 0% of the time, Pallas kernels for 0%

profile of v9, /device:TPU:0, one launch (start us, length us, event | category | flops | bytes accessed | tf_op | source)
XLA Modules:
  0.0 83.8 jit_solution(13491663146294952344)
XLA Ops:
  0.6 0.0 copy-start
  0.6 1.4 %copy-done = f32[1,1,6,2,32,1024]{5,4,3,2,1,0:T(8,128)S(1)} copy-done((f32[1,1,6,2,32,1024]{5,4,3,2,1,0:T(8,128)S(1)}, f32[1,1,6,2,32,1024]{5,4,3,2,1,0:T(8,128)}, u32[]{:S(2)}) %copy-start) | copy-done | bytes 1572888
  2.0 0.0 copy-start.1
  2.0 0.9 %copy-done.1 = f32[1,1,2,32,1024]{4,3,2,1,0:T(8,128)S(1)} copy-done((f32[1,1,2,32,1024]{4,3,2,1,0:T(8,128)S(1)}, f32[1,1,2,32,1024]{4,3,2,1,0:T(8,128)}, u32[]{:S(2)}) %copy-start.1) | copy-done | bytes 262168
  3.0 0.0 copy-start.2
  3.0 0.9 %copy-done.2 = f32[1,1,2,32,1024]{4,3,2,1,0:T(8,128)S(1)} copy-done((f32[1,1,2,32,1024]{4,3,2,1,0:T(8,128)S(1)}, f32[1,1,2,32,1024]{4,3,2,1,0:T(8,128)}, u32[]{:S(2)}) %copy-start.2) | copy-done | bytes 262168
  3.9 0.0 copy-start.3
  3.9 0.7 copy-done.3
  4.6 0.0 copy-start.4
  4.6 0.7 copy-done.4
  5.3 2.3 %setup.1 = (s32[8]{0:T(128)S(1)}, f32[3,16,32,128]{3,2,1,0:T(8,128)S(1)}, f32[128,128]{1,0:T(8,128)S(1)}, f32[16,32,128]{2,1,0:T(8,128)S(1)}, f32[16,32,128]{2,1...) custom-call(s32[1]{0:T(128)} %bitcast.place_ref, s32[4]{0:T(128)S(1)} %copy-done.4, ...), custom_call_target="tpu_custom_call" | custom-call | tf_op jit(solution)/shard_map/setup/pallas_call | solution.py:712
  7.6 7.3 %all-to-all-start = ((f32[32,8,128]{2,1,0:T(8,128)}), f32[32,8,128]{2,1,0:T(8,128)S(1)}, u32[]{:S(2)}, u32[]{:S(2)}) async-start(f32[32,8,128]{2,1,0:T(8,128)} %bitcast.6), calls=%async_computation | async-start | bytes 262144 | tf_op jit(solution)/shard_map/all_to_all | solution.py:729
  14.9 3.7 %collective-permute-start.1 = (f32[136,128]{1,0:T(8,128)S(1)}, f32[136,128]{1,0:T(8,128)S(1)}, u32[]{:S(2)}, u32[]{:S(2)}) collective-permute-start(f32[136,128]{1,0:T(8,128)S(1)} %get-tuple-element.37), channel_id=1, source_target_pairs={{0,1},{1,2},{2,3},{3,4},{4,5},{5,6},{6,7},{8,9},{9,10},{10,11},{11... | collective-permute-start | bytes 208904 | tf_op jit(solution)/shard_map/ppermute | solution.py:736
  18.6 1.3 %collective-permute-start = (f32[136,128]{1,0:T(8,128)S(1)}, f32[136,128]{1,0:T(8,128)S(1)}, u32[]{:S(2)}, u32[]{:S(2)}) collective-permute-start(f32[136,128]{1,0:T(8,128)S(1)} %get-tuple-element.37), channel_id=1, source_target_pairs={{1,0},{2,1},{3,2},{4,3},{5,4},{6,5},{7,6},{9,8},{10,9},{11,10},{12... | collective-permute-start | bytes 208904 | tf_op jit(solution)/shard_map/ppermute | solution.py:736
  19.9 5.7 %all-gather = f32[480,128]{1,0:T(8,128)S(1)} all-gather(f32[120,128]{1,0:T(8,128)S(1)} %get-tuple-element.36), channel_id=2, replica_groups=mesh['brick'=4,'grp'=8] {'brick'}, dimensions={0}, use_global_device_ids=true | all-gather | bytes 307200 | tf_op jit(solution)/shard_map/all_gather | solution.py:770
  25.6 0.0 collective-permute-done.1.refs_3_
  25.6 0.0 collective-permute-done.refs_2_
  25.6 0.0 all-to-all-done
  25.7 3.0 %step_0.1 = (f32[2,32,1024]{2,1,0:T(8,128)}, f32[16,32,128]{2,1,0:T(8,128)S(1)}, f32[184,128]{1,0:T(8,128)S(1)}, f32[232,128]{1,0:T(8,128)S(1)}, f32[256,128]{1,...) custom-call(s32[8]{0:T(128)S(1)} %get-tuple-element.35.refs_0_, f32[4,120,128]{2,1,0:T(8,128)S(1)} %bitcast.17, ...), custom_call_target="tpu_custom_call" | custom-call | tf_op jit(solution)/shard_map/step_0/pallas_call | solution.py:712
  28.7 6.7 %all-to-all-start.1 = ((f32[32,8,128]{2,1,0:T(8,128)}), f32[32,8,128]{2,1,0:T(8,128)S(1)}, u32[]{:S(2)}, u32[]{:S(2)}) async-start(f32[32,8,128]{2,1,0:T(8,128)} %bitcast.9), calls=%async_computation.1 | async-start | bytes 262144 | tf_op jit(solution)/shard_map/all_to_all | solution.py:729
  35.4 3.7 %collective-permute-start.3 = (f32[64,128]{1,0:T(8,128)S(1)}, f32[64,128]{1,0:T(8,128)S(1)}, u32[]{:S(2)}, u32[]{:S(2)}) collective-permute-start(f32[64,128]{1,0:T(8,128)S(1)} %get-tuple-element.44), channel_id=1, source_target_pairs={{0,1},{1,2},{2,3},{3,4},{4,5},{5,6},{6,7},{8,9},{9,10},{10,11},{11... | collective-permute-start | bytes 98312 | tf_op jit(solution)/shard_map/ppermute | solution.py:736
  39.1 1.3 %collective-permute-start.2 = (f32[64,128]{1,0:T(8,128)S(1)}, f32[64,128]{1,0:T(8,128)S(1)}, u32[]{:S(2)}, u32[]{:S(2)}) collective-permute-start(f32[64,128]{1,0:T(8,128)S(1)} %get-tuple-element.44), channel_id=1, source_target_pairs={{1,0},{2,1},{3,2},{4,3},{5,4},{6,5},{7,6},{9,8},{10,9},{11,10},{12... | collective-permute-start | bytes 98312 | tf_op jit(solution)/shard_map/ppermute | solution.py:736
  40.4 5.4 %all-gather.1 = f32[256,128]{1,0:T(8,128)S(1)} all-gather(f32[64,128]{1,0:T(8,128)S(1)} %get-tuple-element.43), channel_id=3, replica_groups=mesh['brick'=4,'grp'=8] {'brick'}, dimensions={0}, use_global_device_ids=true | all-gather | bytes 163840 | tf_op jit(solution)/shard_map/all_gather | solution.py:770
  45.8 0.0 collective-permute-done.3.refs_3_
  45.8 0.0 collective-permute-done.2.refs_2_
  45.8 0.0 all-to-all-done.1
  45.8 3.1 %step_1.1 = (f32[2,32,1024]{2,1,0:T(8,128)}, f32[16,32,128]{2,1,0:T(8,128)S(1)}, f32[16,32,128]{2,1,0:T(8,128)S(1)}, f32[16,32,128]{2,1,0:T(8,128)S(1)}, f32[8,1...) custom-call(s32[8]{0:T(128)S(1)} %get-tuple-element.35.refs_0_, ...), custom_call_target="tpu_custom_call" | custom-call | tf_op jit(solution)/shard_map/step_1/pallas_call | solution.py:712
  49.0 6.7 %all-to-all-start.2 = ((f32[32,8,128]{2,1,0:T(8,128)}), f32[32,8,128]{2,1,0:T(8,128)S(1)}, u32[]{:S(2)}, u32[]{:S(2)}) async-start(f32[32,8,128]{2,1,0:T(8,128)} %bitcast.12), calls=%async_computation.2 | async-start | bytes 262144 | tf_op jit(solution)/shard_map/all_to_all | solution.py:729
  55.7 3.7 %collective-permute-start.5 = (f32[64,128]{1,0:T(8,128)S(1)}, f32[64,128]{1,0:T(8,128)S(1)}, u32[]{:S(2)}, u32[]{:S(2)}) collective-permute-start(f32[64,128]{1,0:T(8,128)S(1)} %get-tuple-element.50), channel_id=1, source_target_pairs={{0,1},{1,2},{2,3},{3,4},{4,5},{5,6},{6,7},{8,9},{9,10},{10,11},{11... | collective-permute-start | bytes 98312 | tf_op jit(solution)/shard_map/ppermute | solution.py:736
  59.4 1.3 %collective-permute-start.4 = (f32[64,128]{1,0:T(8,128)S(1)}, f32[64,128]{1,0:T(8,128)S(1)}, u32[]{:S(2)}, u32[]{:S(2)}) collective-permute-start(f32[64,128]{1,0:T(8,128)S(1)} %get-tuple-element.50), channel_id=1, source_target_pairs={{1,0},{2,1},{3,2},{4,3},{5,4},{6,5},{7,6},{9,8},{10,9},{11,10},{12... | collective-permute-start | bytes 98312 | tf_op jit(solution)/shard_map/ppermute | solution.py:736
  60.7 5.4 %all-gather.2 = f32[256,128]{1,0:T(8,128)S(1)} all-gather(f32[64,128]{1,0:T(8,128)S(1)} %get-tuple-element.49), channel_id=4, replica_groups=mesh['brick'=4,'grp'=8] {'brick'}, dimensions={0}, use_global_device_ids=true | all-gather | bytes 163840 | tf_op jit(solution)/shard_map/all_gather | solution.py:770
  66.1 0.0 collective-permute-done.5.refs_3_
  66.1 0.0 collective-permute-done.4.refs_2_
  66.1 0.0 all-to-all-done.2
  66.1 2.1 %step_2.1 = (f32[16,32,128]{2,1,0:T(8,128)S(1)}, f32[16,32,128]{2,1,0:T(8,128)S(1)}, f32[16,32,128]{2,1,0:T(8,128)S(1)}, f32[16,32,128]{2,1,0:T(8,128)S(1)}, f32...) custom-call(s32[8]{0:T(128)S(1)} %get-tuple-element.35.refs_0_, f32[4,64,128]{2,1,0:T(8,128)S(1)} %bitcast.18, ...), custom_call_target="tpu_custom_call" | custom-call | tf_op jit(solution)/shard_map/step_2/pallas_call | solution.py:712
  68.2 13.6 %all_to_all.38.tiles_ref = f32[32,1,128]{2,1,0:T(1,128)S(1)} all-to-all(f32[32,1,128]{2,1,0:T(1,128)S(1)} %get-tuple-element.58), channel_id=1, replica_groups=mesh['brick'=4,'grp'=8] {'brick','grp'}, dimensions={0} | all-to-all | bytes 32768 | tf_op jit(solution)/shard_map/all_to_all | solution.py:729
  81.8 2.0 %finish.1 = (f32[2,32,1024]{2,1,0:T(8,128)}, f32[2,32,1024]{2,1,0:T(8,128)}) custom-call(f32[32,1,128]{2,1,0:T(1,128)S(1)} %all_to_all.38.tiles_ref, f32[8,128]{1,0:T(8,128)S(1)} %get-tuple-element.59.scalars_ref, f32[16,32,128]{2,1,0:T(8,128)S(1)} %get-tuple-element.60.residual_ref, ...), custom_call_target="tpu_custom_call", output_to_operand_aliasing={{0}: (6, {}), {1}: (7, {})} | custom-call | tf_op jit(solution)/shard_map/finish/pallas_call | solution.py:712
  (1 shorter events, 0.0 us)
Async XLA Ops:
  0.6 1.4 %copy-start = (f32[1,1,6,2,32,1024]{5,4,3,2,1,0:T(8,128)S(1)}, f32[1,1,6,2,32,1024]{5,4,3,2,1,0:T(8,128)}, u32[]{:S(2)}) copy-start(f32[1,1,6,2,32,1024]{5,4,3,2,1,0:T(8,128)} %param.7) | copy-start | bytes 4718596
  2.0 0.9 %copy-start.1 = (f32[1,1,2,32,1024]{4,3,2,1,0:T(8,128)S(1)}, f32[1,1,2,32,1024]{4,3,2,1,0:T(8,128)}, u32[]{:S(2)}) copy-start(f32[1,1,2,32,1024]{4,3,2,1,0:T(8,128)} %param.5) | copy-start | bytes 786436
  3.0 0.9 %copy-start.2 = (f32[1,1,2,32,1024]{4,3,2,1,0:T(8,128)S(1)}, f32[1,1,2,32,1024]{4,3,2,1,0:T(8,128)}, u32[]{:S(2)}) copy-start(f32[1,1,2,32,1024]{4,3,2,1,0:T(8,128)} %param.6) | copy-start | bytes 786436
  3.9 0.7 copy-start.3
  4.6 0.7 copy-start.4
  7.6 18.0 %all-to-all-start = ((f32[32,8,128]{2,1,0:T(8,128)}), f32[32,8,128]{2,1,0:T(8,128)S(1)}, u32[]{:S(2)}, u32[]{:S(2)}) async-start(f32[32,8,128]{2,1,0:T(8,128)} %bitcast.6), calls=%async_computation | async-start | bytes 262144 | tf_op jit(solution)/shard_map/all_to_all | solution.py:729
  14.9 10.7 %collective-permute-start.1 = (f32[136,128]{1,0:T(8,128)S(1)}, f32[136,128]{1,0:T(8,128)S(1)}, u32[]{:S(2)}, u32[]{:S(2)}) collective-permute-start(f32[136,128]{1,0:T(8,128)S(1)} %get-tuple-element.37), channel_id=1, source_target_pairs={{0,1},{1,2},{2,3},{3,4},{4,5},{5,6},{6,7},{8,9},{9,10},{10,11},{11... | collective-permute-start | bytes 208904 | tf_op jit(solution)/shard_map/ppermute | solution.py:736
  18.6 7.0 %collective-permute-start = (f32[136,128]{1,0:T(8,128)S(1)}, f32[136,128]{1,0:T(8,128)S(1)}, u32[]{:S(2)}, u32[]{:S(2)}) collective-permute-start(f32[136,128]{1,0:T(8,128)S(1)} %get-tuple-element.37), channel_id=1, source_target_pairs={{1,0},{2,1},{3,2},{4,3},{5,4},{6,5},{7,6},{9,8},{10,9},{11,10},{12... | collective-permute-start | bytes 208904 | tf_op jit(solution)/shard_map/ppermute | solution.py:736
  28.7 17.1 %all-to-all-start.1 = ((f32[32,8,128]{2,1,0:T(8,128)}), f32[32,8,128]{2,1,0:T(8,128)S(1)}, u32[]{:S(2)}, u32[]{:S(2)}) async-start(f32[32,8,128]{2,1,0:T(8,128)} %bitcast.9), calls=%async_computation.1 | async-start | bytes 262144 | tf_op jit(solution)/shard_map/all_to_all | solution.py:729
  35.4 10.4 %collective-permute-start.3 = (f32[64,128]{1,0:T(8,128)S(1)}, f32[64,128]{1,0:T(8,128)S(1)}, u32[]{:S(2)}, u32[]{:S(2)}) collective-permute-start(f32[64,128]{1,0:T(8,128)S(1)} %get-tuple-element.44), channel_id=1, source_target_pairs={{0,1},{1,2},{2,3},{3,4},{4,5},{5,6},{6,7},{8,9},{9,10},{10,11},{11... | collective-permute-start | bytes 98312 | tf_op jit(solution)/shard_map/ppermute | solution.py:736
  39.1 6.7 %collective-permute-start.2 = (f32[64,128]{1,0:T(8,128)S(1)}, f32[64,128]{1,0:T(8,128)S(1)}, u32[]{:S(2)}, u32[]{:S(2)}) collective-permute-start(f32[64,128]{1,0:T(8,128)S(1)} %get-tuple-element.44), channel_id=1, source_target_pairs={{1,0},{2,1},{3,2},{4,3},{5,4},{6,5},{7,6},{9,8},{10,9},{11,10},{12... | collective-permute-start | bytes 98312 | tf_op jit(solution)/shard_map/ppermute | solution.py:736
  49.0 17.1 %all-to-all-start.2 = ((f32[32,8,128]{2,1,0:T(8,128)}), f32[32,8,128]{2,1,0:T(8,128)S(1)}, u32[]{:S(2)}, u32[]{:S(2)}) async-start(f32[32,8,128]{2,1,0:T(8,128)} %bitcast.12), calls=%async_computation.2 | async-start | bytes 262144 | tf_op jit(solution)/shard_map/all_to_all | solution.py:729
  55.7 10.4 %collective-permute-start.5 = (f32[64,128]{1,0:T(8,128)S(1)}, f32[64,128]{1,0:T(8,128)S(1)}, u32[]{:S(2)}, u32[]{:S(2)}) collective-permute-start(f32[64,128]{1,0:T(8,128)S(1)} %get-tuple-element.50), channel_id=1, source_target_pairs={{0,1},{1,2},{2,3},{3,4},{4,5},{5,6},{6,7},{8,9},{9,10},{10,11},{11... | collective-permute-start | bytes 98312 | tf_op jit(solution)/shard_map/ppermute | solution.py:736
  59.4 6.7 %collective-permute-start.4 = (f32[64,128]{1,0:T(8,128)S(1)}, f32[64,128]{1,0:T(8,128)S(1)}, u32[]{:S(2)}, u32[]{:S(2)}) collective-permute-start(f32[64,128]{1,0:T(8,128)S(1)} %get-tuple-element.50), channel_id=1, source_target_pairs={{1,0},{2,1},{3,2},{4,3},{5,4},{6,5},{7,6},{9,8},{10,9},{11,10},{12... | collective-permute-start | bytes 98312 | tf_op jit(solution)/shard_map/ppermute | solution.py:736

commit v10 on v9

--- a/solution.py
+++ b/solution.py
@@ -341,7 +341,11 @@
         mapped_ref, halo_in, constant_ref, scalars_in = take(4)
     if iteration > 1:
         search_in, search_halo_in = take(2)
-    smoothed_hbm, mapped_out = take(2)
+    if last:
+        zero_hbm, one_hbm = take(2)
+        advance_ref, direction_ref, smoothed_ref, mapped_out = take(4)
+    else:
+        smoothed_hbm, mapped_out = take(2)
     if first:
         constant_ref, halo_ref = take(2)
     else:
@@ -351,9 +355,17 @@
     tile_out = take(1)[0]
     if not last:
         xy_out, z_out = take(2)
-    relax_ref, smoothed_ref, written = take(3)
-    if not last:
-        tile_ref, sent = take(2)
+    relax_ref = take(1)[0]
+    if last:
+        zero_ref, one_ref, arrived = take(3)
+        reading = [
+            pltpu.make_async_copy(zero_hbm, zero_ref, arrived.at[0]),
+            pltpu.make_async_copy(one_hbm, one_ref, arrived.at[1]),
+        ]
+        for copy in reading:
+            copy.start()
+    else:
+        smoothed_ref, written, tile_ref, sent = take(4)
     for c in range(CHUNKS):
         relax_ref[c] = OMEGA / diagonal_ref[c]
 
@@ -579,8 +591,9 @@
         else:
             smoothed_ref[c // 8, :, 128 * (c % 8) : 128 * (c % 8 + 1)] = value
         smoothed.append(value)
-    writing = pltpu.make_async_copy(smoothed_ref, smoothed_hbm, written)
-    writing.start()
+    if not last:
+        writing = pltpu.make_async_copy(smoothed_ref, smoothed_hbm, written)
+        writing.start()
     keys = constant_ref[C_K : C_K + 8]
     crossing = x_plus * jnp.concatenate([f[BS - 1 : BS] for f in y1], axis=0)
     crossing += x_minus * jnp.concatenate([f[0:1] for f in y1], axis=0)
@@ -653,7 +666,14 @@
             line = jnp.where(level == i, values[i], line)
         for k in range(tile_out.shape[0]):
             tile_out[k] = line
-        writing.wait()
+        for copy in reading:
+            copy.wait()
+        first_step = scalars_in[2:3, 0:1]
+        for c in range(CHUNKS):
+            s, part = c // 8, slice(128 * (c % 8), 128 * (c % 8 + 1))
+            direction = one_ref[s, :, part] + growth * zero_ref[s, :, part]
+            direction_ref[c] = direction
+            advance_ref[c] = first_step * zero_ref[s, :, part] + step * direction
         return
     y1 = [relax_ref[c] * mapped[c] for c in range(CHUNKS)]
     write_copies(tile_ref, edge_tile(y1, row, values))
@@ -669,15 +689,9 @@
 
 
 def finish_kernel(
-    tiles_ref, scalars_ref, residual_ref, mapped_ref, search_ref, third_ref, first_hbm, second_hbm,
-    solution_hbm, residual_hbm, first_ref, second_ref, arrived,
+    tiles_ref, scalars_ref, residual_ref, mapped_ref, search_ref, smoothed_ref, advance_ref, direction_ref,
+    first_hbm, second_hbm, solution_hbm, residual_hbm, solution_ref, change_ref, sent,
 ):
-    copies = [
-        pltpu.make_async_copy(first_hbm, first_ref, arrived.at[0]),
-        pltpu.make_async_copy(second_hbm, second_ref, arrived.at[1]),
-    ]
-    for copy in copies:
-        copy.start()
     scalars = scalars_ref[...]
     line = tiles_ref[0]
     for k in range(1, tiles_ref.shape[0]):
@@ -685,22 +699,18 @@
     _, _, step, growth = search_scalars(
         [line[:, 16 * i : 16 * i + 1] for i in range(2, 5)], scalars, ITERS - 1
     )
-    first_step, second_step, second_growth = scalars[2:3, 0:1], scalars[3:4, 0:1], scalars[4:5, 0:1]
-    second_weight = second_step + growth * step
-    first_weight = first_step + second_growth * second_weight
-    for copy in copies:
-        copy.wait()
     for c in range(CHUNKS):
         s, part = c // 8, slice(128 * (c % 8), 128 * (c % 8 + 1))
-        total = first_weight * first_ref[s, :, part] + second_weight * second_ref[s, :, part]
-        first_ref[s, :, part] = total + step * third_ref[c]
-        second_ref[s, :, part] = residual_ref[c] - step * (mapped_ref[c] + growth * search_ref[c])
+        solution_ref[s, :, part] = advance_ref[c] + step * (smoothed_ref[c] + growth * direction_ref[c])
     copies = [
-        pltpu.make_async_copy(first_ref, solution_hbm, arrived.at[0]),
-        pltpu.make_async_copy(second_ref, residual_hbm, arrived.at[1]),
+        pltpu.make_async_copy(solution_ref, solution_hbm, sent.at[0]),
+        pltpu.make_async_copy(change_ref, residual_hbm, sent.at[1]),
     ]
-    for copy in copies:
-        copy.start()
+    copies[0].start()
+    for c in range(CHUNKS):
+        s, part = c // 8, slice(128 * (c % 8), 128 * (c % 8 + 1))
+        change_ref[s, :, part] = residual_ref[c] - step * (mapped_ref[c] + growth * search_ref[c])
+    copies[1].start()
     for copy in copies:
         copy.wait()
 
@@ -770,11 +780,18 @@
         gathered = lax.all_gather(sides, "brick", axis=0, tiled=False)
         operands = [info, gathered, above, below, tiles, bonds, outer, diagonal, residual]
         tall = array(H_S + 8 * slabs, 128)
-        outs = {"smoothed": field if last else brick_pair, "mapped": field}
+        if last:
+            outs = {"advance": field, "direction": field, "smoothed": field, "mapped": field}
+        else:
+            outs = {"smoothed": brick_pair, "mapped": field}
         if not first:
             operands += [mapped] + [state[k] for k in ("halo", "constant", "scalars")]
         if iteration > 1:
             operands += [state[k] for k in ("search", "search_halo")]
+        in_spaces = [pltpu.SMEM]
+        if last:
+            in_spaces += [pltpu.VMEM] * (len(operands) - 1) + [pl.ANY] * 2
+            operands += directions
         if first:
             outs |= {"constant": array(C_F + 8 * slabs, 128), "halo": tall}
         else:
@@ -784,20 +801,24 @@
         outs["tile"] = array(slabs * bricks, 1, 128) if last else copies
         if not last:
             outs |= {"sides": array(XY_ROWS, 128), "ends": array(Z_ROWS, 128)}
-        moved = ("smoothed",) if last else ("smoothed", "tile")
+        moved = () if last else ("smoothed", "tile")
+        pair = pltpu.VMEM(brick_pair.shape, F32)
         results = call(
             functools.partial(step_kernel, iteration, slabs, bricks),
             f"step_{iteration}",
             list(outs.values()),
-            [pltpu.SMEM],
+            in_spaces,
             [pl.ANY if name in moved else pltpu.VMEM for name in outs],
             operands,
-            [
-                pltpu.VMEM(FIELD, F32),
-                pltpu.VMEM(FIELD if last else (2, BS, BS * BS), F32),
-                pltpu.SemaphoreType.DMA,
-            ]
-            + ([] if last else [pltpu.VMEM(copies.shape, F32), pltpu.SemaphoreType.DMA]),
+            [pltpu.VMEM(FIELD, F32)]
+            + (
+                [pair, pair, pltpu.SemaphoreType.DMA((2,))]
+                if last
+                else [
+                    pair, pltpu.SemaphoreType.DMA,
+                    pltpu.VMEM(copies.shape, F32), pltpu.SemaphoreType.DMA,
+                ]
+            ),
         )
         state |= dict(zip(outs, results))
         if first:
@@ -811,14 +832,18 @@
         finish_kernel,
         "finish",
         [brick_pair, brick_pair],
-        [pltpu.VMEM] * 6 + [pl.ANY] * 2,
+        [pltpu.VMEM] * 8 + [pl.ANY] * 2,
         [pl.ANY] * 2,
-        [tiles, state["scalars"], residual, mapped, state["search"], directions[2]] + directions[:2],
+        [
+            tiles, state["scalars"], residual, mapped, state["search"], directions[2],
+            state["advance"], state["direction"],
+        ]
+        + directions[:2],
         [
             pltpu.VMEM(brick_pair.shape, F32), pltpu.VMEM(brick_pair.shape, F32),
             pltpu.SemaphoreType.DMA((2,)),
         ],
-        {6: 0, 7: 1},
+        {8: 0, 9: 1},
     )
     return solution_field[None, None], residual[None, None]
 

time: 84.4 us -> 84.7 us (level)
  local copies, waits for them, and re-layouts: 4.64 us -> 5.6 us
    unnamed x10 -> x14, local copies, waits for them, and re-layouts: 4.64 us -> 5.59 us
where the time goes in v10:
time: 84.7 us; the launch traced here: 84.1 us
  starting transfers between devices  35.6 us (42%)
  blocking collectives  30.2 us (36%)
  Pallas kernels  11.8 us (14%)
  local copies, waits for them, and re-layouts  5.6 us (7%)
    all_to_all x3, starting transfers between devices, to_all(): return lax.all_to_all(copies, axes, 0, 0, tiled=True)  20.7 us
    all_gather x3, blocking collectives, on_device(): gathered = lax.all_gather(sides, 'brick', axis=0, tiled=False)  16.6 us
    all_to_all x1, blocking collectives, to_all(): return lax.all_to_all(copies, axes, 0, 0, tiled=True)  13.6 us
    pallas_call x5, Pallas kernels, call(): pl.pallas_call(kernel, out_shape=tuple(outs), in_specs=[spec(space) for s...  11.8 us
    ppermute x3, starting transfers between devices, exchange_slabs(): lax.ppermute(message, 'grp', upward)  11 us
    unnamed x14, local copies, waits for them, and re-layouts  5.59 us
    ppermute x3, starting transfers between devices, exchange_slabs(): lax.ppermute(message, 'grp', downward)  3.88 us
  transfers between devices with their start and end apart: 9, of which 0 were waited for; matrix products, arithmetic and copies ran while one was open for 0% of the time, Pallas kernels for 0%

profile of v10, /device:TPU:0, one launch (start us, length us, event | category | flops | bytes accessed | tf_op | source)
XLA Modules:
  0.0 84.1 jit_solution(385034704905801328)
XLA Ops:
  0.6 0.0 copy-start
  0.6 1.4 %copy-done = f32[1,1,6,2,32,1024]{5,4,3,2,1,0:T(8,128)S(1)} copy-done((f32[1,1,6,2,32,1024]{5,4,3,2,1,0:T(8,128)S(1)}, f32[1,1,6,2,32,1024]{5,4,3,2,1,0:T(8,128)}, u32[]{:S(2)}) %copy-start) | copy-done | bytes 1572888
  2.0 0.0 copy-start.3
  2.0 0.9 %copy-done.3 = f32[1,1,2,32,1024]{4,3,2,1,0:T(8,128)S(1)} copy-done((f32[1,1,2,32,1024]{4,3,2,1,0:T(8,128)S(1)}, f32[1,1,2,32,1024]{4,3,2,1,0:T(8,128)}, u32[]{:S(2)}) %copy-start.3) | copy-done | bytes 262168
  3.0 0.0 copy-start.4
  3.0 0.9 %copy-done.4 = f32[1,1,2,32,1024]{4,3,2,1,0:T(8,128)S(1)} copy-done((f32[1,1,2,32,1024]{4,3,2,1,0:T(8,128)S(1)}, f32[1,1,2,32,1024]{4,3,2,1,0:T(8,128)}, u32[]{:S(2)}) %copy-start.4) | copy-done | bytes 262168
  3.9 0.0 copy-start.5
  3.9 0.7 copy-done.5
  4.6 0.0 copy-start.6
  4.6 0.7 copy-done.6
  5.3 2.3 %setup.1 = (s32[8]{0:T(128)S(1)}, f32[3,16,32,128]{3,2,1,0:T(8,128)S(1)}, f32[128,128]{1,0:T(8,128)S(1)}, f32[16,32,128]{2,1,0:T(8,128)S(1)}, f32[16,32,128]{2,1...) custom-call(s32[1]{0:T(128)} %bitcast.place_ref, s32[4]{0:T(128)S(1)} %copy-done.6, ...), custom_call_target="tpu_custom_call" | custom-call | tf_op jit(solution)/shard_map/setup/pallas_call | solution.py:722
  7.6 7.3 %all-to-all-start = ((f32[32,8,128]{2,1,0:T(8,128)}), f32[32,8,128]{2,1,0:T(8,128)S(1)}, u32[]{:S(2)}, u32[]{:S(2)}) async-start(f32[32,8,128]{2,1,0:T(8,128)} %bitcast.6), calls=%async_computation | async-start | bytes 262144 | tf_op jit(solution)/shard_map/all_to_all | solution.py:739
  14.9 3.7 %collective-permute-start.1 = (f32[136,128]{1,0:T(8,128)S(1)}, f32[136,128]{1,0:T(8,128)S(1)}, u32[]{:S(2)}, u32[]{:S(2)}) collective-permute-start(f32[136,128]{1,0:T(8,128)S(1)} %get-tuple-element.39), channel_id=1, source_target_pairs={{0,1},{1,2},{2,3},{3,4},{4,5},{5,6},{6,7},{8,9},{9,10},{10,11},{11... | collective-permute-start | bytes 208904 | tf_op jit(solution)/shard_map/ppermute | solution.py:746
  18.6 1.3 %collective-permute-start = (f32[136,128]{1,0:T(8,128)S(1)}, f32[136,128]{1,0:T(8,128)S(1)}, u32[]{:S(2)}, u32[]{:S(2)}) collective-permute-start(f32[136,128]{1,0:T(8,128)S(1)} %get-tuple-element.39), channel_id=1, source_target_pairs={{1,0},{2,1},{3,2},{4,3},{5,4},{6,5},{7,6},{9,8},{10,9},{11,10},{12... | collective-permute-start | bytes 208904 | tf_op jit(solution)/shard_map/ppermute | solution.py:746
  19.9 5.7 %all-gather = f32[480,128]{1,0:T(8,128)S(1)} all-gather(f32[120,128]{1,0:T(8,128)S(1)} %get-tuple-element.38), channel_id=2, replica_groups=mesh['brick'=4,'grp'=8] {'brick'}, dimensions={0}, use_global_device_ids=true | all-gather | bytes 307200 | tf_op jit(solution)/shard_map/all_gather | solution.py:780
  25.6 0.0 collective-permute-done.1.refs_3_
  25.6 0.0 collective-permute-done.refs_2_
  25.6 0.0 all-to-all-done
  25.7 3.0 %step_0.1 = (f32[2,32,1024]{2,1,0:T(8,128)}, f32[16,32,128]{2,1,0:T(8,128)S(1)}, f32[184,128]{1,0:T(8,128)S(1)}, f32[232,128]{1,0:T(8,128)S(1)}, f32[256,128]{1,...) custom-call(s32[8]{0:T(128)S(1)} %get-tuple-element.37.refs_0_, f32[4,120,128]{2,1,0:T(8,128)S(1)} %bitcast.19, ...), custom_call_target="tpu_custom_call" | custom-call | tf_op jit(solution)/shard_map/step_0/pallas_call | solution.py:722
  28.7 0.0 copy-start.1
  28.7 6.7 %all-to-all-start.1 = ((f32[32,8,128]{2,1,0:T(8,128)}), f32[32,8,128]{2,1,0:T(8,128)S(1)}, u32[]{:S(2)}, u32[]{:S(2)}) async-start(f32[32,8,128]{2,1,0:T(8,128)} %bitcast.9), calls=%async_computation.1 | async-start | bytes 262144 | tf_op jit(solution)/shard_map/all_to_all | solution.py:739
  35.4 3.7 %collective-permute-start.3 = (f32[64,128]{1,0:T(8,128)S(1)}, f32[64,128]{1,0:T(8,128)S(1)}, u32[]{:S(2)}, u32[]{:S(2)}) collective-permute-start(f32[64,128]{1,0:T(8,128)S(1)} %get-tuple-element.46), channel_id=1, source_target_pairs={{0,1},{1,2},{2,3},{3,4},{4,5},{5,6},{6,7},{8,9},{9,10},{10,11},{11... | collective-permute-start | bytes 98312 | tf_op jit(solution)/shard_map/ppermute | solution.py:746
  39.1 1.3 %collective-permute-start.2 = (f32[64,128]{1,0:T(8,128)S(1)}, f32[64,128]{1,0:T(8,128)S(1)}, u32[]{:S(2)}, u32[]{:S(2)}) collective-permute-start(f32[64,128]{1,0:T(8,128)S(1)} %get-tuple-element.46), channel_id=1, source_target_pairs={{1,0},{2,1},{3,2},{4,3},{5,4},{6,5},{7,6},{9,8},{10,9},{11,10},{12... | collective-permute-start | bytes 98312 | tf_op jit(solution)/shard_map/ppermute | solution.py:746
  40.4 5.4 %all-gather.1 = f32[256,128]{1,0:T(8,128)S(1)} all-gather(f32[64,128]{1,0:T(8,128)S(1)} %get-tuple-element.45), channel_id=3, replica_groups=mesh['brick'=4,'grp'=8] {'brick'}, dimensions={0}, use_global_device_ids=true | all-gather | bytes 163840 | tf_op jit(solution)/shard_map/all_gather | solution.py:780
  45.8 0.0 collective-permute-done.3.refs_3_
  45.8 0.0 collective-permute-done.2.refs_2_
  45.8 0.0 all-to-all-done.1
  45.8 3.1 %step_1.1 = (f32[2,32,1024]{2,1,0:T(8,128)}, f32[16,32,128]{2,1,0:T(8,128)S(1)}, f32[16,32,128]{2,1,0:T(8,128)S(1)}, f32[16,32,128]{2,1,0:T(8,128)S(1)}, f32[8,1...) custom-call(s32[8]{0:T(128)S(1)} %get-tuple-element.37.refs_0_, ...), custom_call_target="tpu_custom_call" | custom-call | tf_op jit(solution)/shard_map/step_1/pallas_call | solution.py:722
  49.0 6.7 %all-to-all-start.2 = ((f32[32,8,128]{2,1,0:T(8,128)}), f32[32,8,128]{2,1,0:T(8,128)S(1)}, u32[]{:S(2)}, u32[]{:S(2)}) async-start(f32[32,8,128]{2,1,0:T(8,128)} %bitcast.12), calls=%async_computation.2 | async-start | bytes 262144 | tf_op jit(solution)/shard_map/all_to_all | solution.py:739
  55.7 3.7 %collective-permute-start.5 = (f32[64,128]{1,0:T(8,128)S(1)}, f32[64,128]{1,0:T(8,128)S(1)}, u32[]{:S(2)}, u32[]{:S(2)}) collective-permute-start(f32[64,128]{1,0:T(8,128)S(1)} %get-tuple-element.52), channel_id=1, source_target_pairs={{0,1},{1,2},{2,3},{3,4},{4,5},{5,6},{6,7},{8,9},{9,10},{10,11},{11... | collective-permute-start | bytes 98312 | tf_op jit(solution)/shard_map/ppermute | solution.py:746
  59.4 1.3 %collective-permute-start.4 = (f32[64,128]{1,0:T(8,128)S(1)}, f32[64,128]{1,0:T(8,128)S(1)}, u32[]{:S(2)}, u32[]{:S(2)}) collective-permute-start(f32[64,128]{1,0:T(8,128)S(1)} %get-tuple-element.52), channel_id=1, source_target_pairs={{1,0},{2,1},{3,2},{4,3},{5,4},{6,5},{7,6},{9,8},{10,9},{11,10},{12... | collective-permute-start | bytes 98312 | tf_op jit(solution)/shard_map/ppermute | solution.py:746
  60.7 5.4 %all-gather.2 = f32[256,128]{1,0:T(8,128)S(1)} all-gather(f32[64,128]{1,0:T(8,128)S(1)} %get-tuple-element.51), channel_id=4, replica_groups=mesh['brick'=4,'grp'=8] {'brick'}, dimensions={0}, use_global_device_ids=true | all-gather | bytes 163840 | tf_op jit(solution)/shard_map/all_gather | solution.py:780
  66.1 0.0 collective-permute-done.5.refs_3_
  66.1 0.0 collective-permute-done.4.refs_2_
  66.1 0.0 all-to-all-done.2
  66.1 0.0 copy-done.1
  66.1 0.0 copy-start.2
  66.1 0.9 %copy-done.2 = f32[2,32,1024]{2,1,0:T(8,128)S(1)} copy-done((f32[2,32,1024]{2,1,0:T(8,128)S(1)}, f32[2,32,1024]{2,1,0:T(8,128)}, u32[]{:S(2)}) %copy-start.2) | copy-done | bytes 262168
  67.1 2.1 %step_2.1 = (f32[16,32,128]{2,1,0:T(8,128)S(1)}, f32[16,32,128]{2,1,0:T(8,128)S(1)}, f32[16,32,128]{2,1,0:T(8,128)S(1)}, f32[16,32,128]{2,1,0:T(8,128)S(1)}, f32...) custom-call(s32[8]{0:T(128)S(1)} %get-tuple-element.37.refs_0_, ...), custom_call_target="tpu_custom_call" | custom-call | tf_op jit(solution)/shard_map/step_2/pallas_call | solution.py:722
  69.2 13.6 %all_to_all.38.tiles_ref = f32[32,1,128]{2,1,0:T(1,128)S(1)} all-to-all(f32[32,1,128]{2,1,0:T(1,128)S(1)} %get-tuple-element.62), channel_id=1, replica_groups=mesh['brick'=4,'grp'=8] {'brick','grp'}, dimensions={0} | all-to-all | bytes 32768 | tf_op jit(solution)/shard_map/all_to_all | solution.py:739
  82.8 1.3 %finish.1 = (f32[2,32,1024]{2,1,0:T(8,128)}, f32[2,32,1024]{2,1,0:T(8,128)}) custom-call(f32[32,1,128]{2,1,0:T(1,128)S(1)} %all_to_all.38.tiles_ref, f32[8,128]{1,0:T(8,128)S(1)} %get-tuple-element.63.scalars_ref, f32[16,32,128]{2,1,0:T(8,128)S(1)} %get-tuple-element.64.residual_ref, ...), custom_call_target="tpu_custom_call", output_to_operand_aliasing={{0}: (8, {}), {1}: (9, {})} | custom-call | tf_op jit(solution)/shard_map/finish/pallas_call | solution.py:722
  (1 shorter events, 0.0 us)
Async XLA Ops:
  0.6 1.4 %copy-start = (f32[1,1,6,2,32,1024]{5,4,3,2,1,0:T(8,128)S(1)}, f32[1,1,6,2,32,1024]{5,4,3,2,1,0:T(8,128)}, u32[]{:S(2)}) copy-start(f32[1,1,6,2,32,1024]{5,4,3,2,1,0:T(8,128)} %param.7) | copy-start | bytes 4718596
  2.0 0.9 %copy-start.3 = (f32[1,1,2,32,1024]{4,3,2,1,0:T(8,128)S(1)}, f32[1,1,2,32,1024]{4,3,2,1,0:T(8,128)}, u32[]{:S(2)}) copy-start(f32[1,1,2,32,1024]{4,3,2,1,0:T(8,128)} %param.5) | copy-start | bytes 786436
  3.0 0.9 %copy-start.4 = (f32[1,1,2,32,1024]{4,3,2,1,0:T(8,128)S(1)}, f32[1,1,2,32,1024]{4,3,2,1,0:T(8,128)}, u32[]{:S(2)}) copy-start(f32[1,1,2,32,1024]{4,3,2,1,0:T(8,128)} %param.6) | copy-start | bytes 786436
  3.9 0.7 copy-start.5
  4.6 0.7 copy-start.6
  7.6 18.0 %all-to-all-start = ((f32[32,8,128]{2,1,0:T(8,128)}), f32[32,8,128]{2,1,0:T(8,128)S(1)}, u32[]{:S(2)}, u32[]{:S(2)}) async-start(f32[32,8,128]{2,1,0:T(8,128)} %bitcast.6), calls=%async_computation | async-start | bytes 262144 | tf_op jit(solution)/shard_map/all_to_all | solution.py:739
  14.9 10.7 %collective-permute-start.1 = (f32[136,128]{1,0:T(8,128)S(1)}, f32[136,128]{1,0:T(8,128)S(1)}, u32[]{:S(2)}, u32[]{:S(2)}) collective-permute-start(f32[136,128]{1,0:T(8,128)S(1)} %get-tuple-element.39), channel_id=1, source_target_pairs={{0,1},{1,2},{2,3},{3,4},{4,5},{5,6},{6,7},{8,9},{9,10},{10,11},{11... | collective-permute-start | bytes 208904 | tf_op jit(solution)/shard_map/ppermute | solution.py:746
  18.6 7.0 %collective-permute-start = (f32[136,128]{1,0:T(8,128)S(1)}, f32[136,128]{1,0:T(8,128)S(1)}, u32[]{:S(2)}, u32[]{:S(2)}) collective-permute-start(f32[136,128]{1,0:T(8,128)S(1)} %get-tuple-element.39), channel_id=1, source_target_pairs={{1,0},{2,1},{3,2},{4,3},{5,4},{6,5},{7,6},{9,8},{10,9},{11,10},{12... | collective-permute-start | bytes 208904 | tf_op jit(solution)/shard_map/ppermute | solution.py:746
  28.7 37.4 %copy-start.1 = (f32[2,32,1024]{2,1,0:T(8,128)S(1)}, f32[2,32,1024]{2,1,0:T(8,128)}, u32[]{:S(2)}) copy-start(f32[2,32,1024]{2,1,0:T(8,128)} %get-tuple-element.60.refs_15_.first_hbm) | copy-start | bytes 786436
  28.7 17.1 %all-to-all-start.1 = ((f32[32,8,128]{2,1,0:T(8,128)}), f32[32,8,128]{2,1,0:T(8,128)S(1)}, u32[]{:S(2)}, u32[]{:S(2)}) async-start(f32[32,8,128]{2,1,0:T(8,128)} %bitcast.9), calls=%async_computation.1 | async-start | bytes 262144 | tf_op jit(solution)/shard_map/all_to_all | solution.py:739
  35.4 10.4 %collective-permute-start.3 = (f32[64,128]{1,0:T(8,128)S(1)}, f32[64,128]{1,0:T(8,128)S(1)}, u32[]{:S(2)}, u32[]{:S(2)}) collective-permute-start(f32[64,128]{1,0:T(8,128)S(1)} %get-tuple-element.46), channel_id=1, source_target_pairs={{0,1},{1,2},{2,3},{3,4},{4,5},{5,6},{6,7},{8,9},{9,10},{10,11},{11... | collective-permute-start | bytes 98312 | tf_op jit(solution)/shard_map/ppermute | solution.py:746
  39.1 6.7 %collective-permute-start.2 = (f32[64,128]{1,0:T(8,128)S(1)}, f32[64,128]{1,0:T(8,128)S(1)}, u32[]{:S(2)}, u32[]{:S(2)}) collective-permute-start(f32[64,128]{1,0:T(8,128)S(1)} %get-tuple-element.46), channel_id=1, source_target_pairs={{1,0},{2,1},{3,2},{4,3},{5,4},{6,5},{7,6},{9,8},{10,9},{11,10},{12... | collective-permute-start | bytes 98312 | tf_op jit(solution)/shard_map/ppermute | solution.py:746
  49.0 17.1 %all-to-all-start.2 = ((f32[32,8,128]{2,1,0:T(8,128)}), f32[32,8,128]{2,1,0:T(8,128)S(1)}, u32[]{:S(2)}, u32[]{:S(2)}) async-start(f32[32,8,128]{2,1,0:T(8,128)} %bitcast.12), calls=%async_computation.2 | async-start | bytes 262144 | tf_op jit(solution)/shard_map/all_to_all | solution.py:739
  55.7 10.4 %collective-permute-start.5 = (f32[64,128]{1,0:T(8,128)S(1)}, f32[64,128]{1,0:T(8,128)S(1)}, u32[]{:S(2)}, u32[]{:S(2)}) collective-permute-start(f32[64,128]{1,0:T(8,128)S(1)} %get-tuple-element.52), channel_id=1, source_target_pairs={{0,1},{1,2},{2,3},{3,4},{4,5},{5,6},{6,7},{8,9},{9,10},{10,11},{11... | collective-permute-start | bytes 98312 | tf_op jit(solution)/shard_map/ppermute | solution.py:746
  59.4 6.7 %collective-permute-start.4 = (f32[64,128]{1,0:T(8,128)S(1)}, f32[64,128]{1,0:T(8,128)S(1)}, u32[]{:S(2)}, u32[]{:S(2)}) collective-permute-start(f32[64,128]{1,0:T(8,128)S(1)} %get-tuple-element.52), channel_id=1, source_target_pairs={{1,0},{2,1},{3,2},{4,3},{5,4},{6,5},{7,6},{9,8},{10,9},{11,10},{12... | collective-permute-start | bytes 98312 | tf_op jit(solution)/shard_map/ppermute | solution.py:746
  66.1 1.0 %copy-start.2 = (f32[2,32,1024]{2,1,0:T(8,128)S(1)}, f32[2,32,1024]{2,1,0:T(8,128)}, u32[]{:S(2)}) copy-start(f32[2,32,1024]{2,1,0:T(8,128)} %get-tuple-element.61.refs_16_.second_hbm) | copy-start | bytes 786436

commit v11 on v10

--- a/solution.py
+++ b/solution.py
@@ -353,7 +353,9 @@
         if not last:
             halo_ref, search_halo_ref = take(2)
     tile_out = take(1)[0]
-    if not last:
+    if last:
+        take(2)
+    else:
         xy_out, z_out = take(2)
     relax_ref = take(1)[0]
     if last:
@@ -792,6 +794,7 @@
         if last:
             in_spaces += [pltpu.VMEM] * (len(operands) - 1) + [pl.ANY] * 2
             operands += directions
+            count = len(operands)
         if first:
             outs |= {"constant": array(C_F + 8 * slabs, 128), "halo": tall}
         else:
@@ -799,9 +802,13 @@
             if not last:
                 outs |= {"halo": tall, "search_halo": tall}
         outs["tile"] = array(slabs * bricks, 1, 128) if last else copies
-        if not last:
+        if last:
+            outs |= {"zero": brick_pair, "one": brick_pair}
+            aliases = {count - 2: len(outs) - 2, count - 1: len(outs) - 1}
+        else:
             outs |= {"sides": array(XY_ROWS, 128), "ends": array(Z_ROWS, 128)}
-        moved = () if last else ("smoothed", "tile")
+            aliases = {}
+        moved = ("zero", "one") if last else ("smoothed", "tile")
         pair = pltpu.VMEM(brick_pair.shape, F32)
         results = call(
             functools.partial(step_kernel, iteration, slabs, bricks),
@@ -819,6 +826,7 @@
                     pltpu.VMEM(copies.shape, F32), pltpu.SemaphoreType.DMA,
                 ]
             ),
+            aliases,
         )
         state |= dict(zip(outs, results))
         if first:
@@ -836,9 +844,8 @@
         [pl.ANY] * 2,
         [
             tiles, state["scalars"], residual, mapped, state["search"], directions[2],
-            state["advance"], state["direction"],
-        ]
-        + directions[:2],
+            state["advance"], state["direction"], state["zero"], state["one"],
+        ],
         [
             pltpu.VMEM(brick_pair.shape, F32), pltpu.VMEM(brick_pair.shape, F32),
             pltpu.SemaphoreType.DMA((2,)),

time: 84.7 us -> 84.6 us (level)
  local copies, waits for them, and re-layouts: 5.6 us -> 4.64 us
  Pallas kernels: 11.8 us -> 12.7 us
    unnamed x14 -> x10, local copies, waits for them, and re-layouts: 5.59 us -> 4.64 us
    pallas_call x5, Pallas kernels: 11.8 us -> 12.7 us  [call(): pl.pallas_call(kernel, out_shape=tuple(outs), in_specs=[spec(space) for s...]
where the time goes in v11:
time: 84.6 us; the launch traced here: 84 us
  starting transfers between devices  35.6 us (42%)
  blocking collectives  30.2 us (36%)
  Pallas kernels  12.7 us (15%)
  local copies, waits for them, and re-layouts  4.64 us (5%)
    all_to_all x3, starting transfers between devices, to_all(): return lax.all_to_all(copies, axes, 0, 0, tiled=True)  20.7 us
    all_gather x3, blocking collectives, on_device(): gathered = lax.all_gather(sides, 'brick', axis=0, tiled=False)  16.6 us
    all_to_all x1, blocking collectives, to_all(): return lax.all_to_all(copies, axes, 0, 0, tiled=True)  13.6 us
    pallas_call x5, Pallas kernels, call(): pl.pallas_call(kernel, out_shape=tuple(outs), in_specs=[spec(space) for s...  12.7 us
    ppermute x3, starting transfers between devices, exchange_slabs(): lax.ppermute(message, 'grp', upward)  11 us
    unnamed x10, local copies, waits for them, and re-layouts  4.64 us
    ppermute x3, starting transfers between devices, exchange_slabs(): lax.ppermute(message, 'grp', downward)  3.88 us
  transfers between devices with their start and end apart: 9, of which 0 were waited for; matrix products, arithmetic and copies ran while one was open for 0% of the time, Pallas kernels for 0%

profile of v11, /device:TPU:0, one launch (start us, length us, event | category | flops | bytes accessed | tf_op | source)
XLA Modules:
  0.0 84.0 jit_solution(2897174236066251933)
XLA Ops:
  0.6 0.0 copy-start
  0.6 1.4 %copy-done = f32[1,1,6,2,32,1024]{5,4,3,2,1,0:T(8,128)S(1)} copy-done((f32[1,1,6,2,32,1024]{5,4,3,2,1,0:T(8,128)S(1)}, f32[1,1,6,2,32,1024]{5,4,3,2,1,0:T(8,128)}, u32[]{:S(2)}) %copy-start) | copy-done | bytes 1572888
  2.0 0.0 copy-start.1
  2.0 0.9 %copy-done.1 = f32[1,1,2,32,1024]{4,3,2,1,0:T(8,128)S(1)} copy-done((f32[1,1,2,32,1024]{4,3,2,1,0:T(8,128)S(1)}, f32[1,1,2,32,1024]{4,3,2,1,0:T(8,128)}, u32[]{:S(2)}) %copy-start.1) | copy-done | bytes 262168
  3.0 0.0 copy-start.2
  3.0 0.9 %copy-done.2 = f32[1,1,2,32,1024]{4,3,2,1,0:T(8,128)S(1)} copy-done((f32[1,1,2,32,1024]{4,3,2,1,0:T(8,128)S(1)}, f32[1,1,2,32,1024]{4,3,2,1,0:T(8,128)}, u32[]{:S(2)}) %copy-start.2) | copy-done | bytes 262168
  3.9 0.0 copy-start.3
  3.9 0.7 copy-done.3
  4.6 0.0 copy-start.4
  4.6 0.7 copy-done.4
  5.3 2.3 %setup.1 = (s32[8]{0:T(128)S(1)}, f32[3,16,32,128]{3,2,1,0:T(8,128)S(1)}, f32[128,128]{1,0:T(8,128)S(1)}, f32[16,32,128]{2,1,0:T(8,128)S(1)}, f32[16,32,128]{2,1...) custom-call(s32[1]{0:T(128)} %bitcast.place_ref, s32[4]{0:T(128)S(1)} %copy-done.4, ...), custom_call_target="tpu_custom_call" | custom-call | tf_op jit(solution)/shard_map/setup/pallas_call | solution.py:724
  7.6 7.3 %all-to-all-start = ((f32[32,8,128]{2,1,0:T(8,128)}), f32[32,8,128]{2,1,0:T(8,128)S(1)}, u32[]{:S(2)}, u32[]{:S(2)}) async-start(f32[32,8,128]{2,1,0:T(8,128)} %bitcast.6), calls=%async_computation | async-start | bytes 262144 | tf_op jit(solution)/shard_map/all_to_all | solution.py:741
  14.9 3.7 %collective-permute-start.1 = (f32[136,128]{1,0:T(8,128)S(1)}, f32[136,128]{1,0:T(8,128)S(1)}, u32[]{:S(2)}, u32[]{:S(2)}) collective-permute-start(f32[136,128]{1,0:T(8,128)S(1)} %get-tuple-element.41), channel_id=1, source_target_pairs={{0,1},{1,2},{2,3},{3,4},{4,5},{5,6},{6,7},{8,9},{9,10},{10,11},{11... | collective-permute-start | bytes 208904 | tf_op jit(solution)/shard_map/ppermute | solution.py:748
  18.6 1.3 %collective-permute-start = (f32[136,128]{1,0:T(8,128)S(1)}, f32[136,128]{1,0:T(8,128)S(1)}, u32[]{:S(2)}, u32[]{:S(2)}) collective-permute-start(f32[136,128]{1,0:T(8,128)S(1)} %get-tuple-element.41), channel_id=1, source_target_pairs={{1,0},{2,1},{3,2},{4,3},{5,4},{6,5},{7,6},{9,8},{10,9},{11,10},{12... | collective-permute-start | bytes 208904 | tf_op jit(solution)/shard_map/ppermute | solution.py:748
  19.9 5.7 %all-gather = f32[480,128]{1,0:T(8,128)S(1)} all-gather(f32[120,128]{1,0:T(8,128)S(1)} %get-tuple-element.40), channel_id=2, replica_groups=mesh['brick'=4,'grp'=8] {'brick'}, dimensions={0}, use_global_device_ids=true | all-gather | bytes 307200 | tf_op jit(solution)/shard_map/all_gather | solution.py:782
  25.6 0.0 collective-permute-done.1.refs_3_
  25.6 0.0 collective-permute-done.refs_2_
  25.6 0.0 all-to-all-done
  25.7 3.0 %step_0.1 = (f32[2,32,1024]{2,1,0:T(8,128)}, f32[16,32,128]{2,1,0:T(8,128)S(1)}, f32[184,128]{1,0:T(8,128)S(1)}, f32[232,128]{1,0:T(8,128)S(1)}, f32[256,128]{1,...) custom-call(s32[8]{0:T(128)S(1)} %get-tuple-element.39.refs_0_, f32[4,120,128]{2,1,0:T(8,128)S(1)} %bitcast.17, ...), custom_call_target="tpu_custom_call" | custom-call | tf_op jit(solution)/shard_map/step_0/pallas_call | solution.py:724
  28.7 6.7 %all-to-all-start.1 = ((f32[32,8,128]{2,1,0:T(8,128)}), f32[32,8,128]{2,1,0:T(8,128)S(1)}, u32[]{:S(2)}, u32[]{:S(2)}) async-start(f32[32,8,128]{2,1,0:T(8,128)} %bitcast.9), calls=%async_computation.1 | async-start | bytes 262144 | tf_op jit(solution)/shard_map/all_to_all | solution.py:741
  35.4 3.7 %collective-permute-start.3 = (f32[64,128]{1,0:T(8,128)S(1)}, f32[64,128]{1,0:T(8,128)S(1)}, u32[]{:S(2)}, u32[]{:S(2)}) collective-permute-start(f32[64,128]{1,0:T(8,128)S(1)} %get-tuple-element.48), channel_id=1, source_target_pairs={{0,1},{1,2},{2,3},{3,4},{4,5},{5,6},{6,7},{8,9},{9,10},{10,11},{11... | collective-permute-start | bytes 98312 | tf_op jit(solution)/shard_map/ppermute | solution.py:748
  39.1 1.3 %collective-permute-start.2 = (f32[64,128]{1,0:T(8,128)S(1)}, f32[64,128]{1,0:T(8,128)S(1)}, u32[]{:S(2)}, u32[]{:S(2)}) collective-permute-start(f32[64,128]{1,0:T(8,128)S(1)} %get-tuple-element.48), channel_id=1, source_target_pairs={{1,0},{2,1},{3,2},{4,3},{5,4},{6,5},{7,6},{9,8},{10,9},{11,10},{12... | collective-permute-start | bytes 98312 | tf_op jit(solution)/shard_map/ppermute | solution.py:748
  40.4 5.4 %all-gather.1 = f32[256,128]{1,0:T(8,128)S(1)} all-gather(f32[64,128]{1,0:T(8,128)S(1)} %get-tuple-element.47), channel_id=3, replica_groups=mesh['brick'=4,'grp'=8] {'brick'}, dimensions={0}, use_global_device_ids=true | all-gather | bytes 163840 | tf_op jit(solution)/shard_map/all_gather | solution.py:782
  45.8 0.0 collective-permute-done.3.refs_3_
  45.8 0.0 collective-permute-done.2.refs_2_
  45.8 0.0 all-to-all-done.1
  45.8 3.1 %step_1.1 = (f32[2,32,1024]{2,1,0:T(8,128)}, f32[16,32,128]{2,1,0:T(8,128)S(1)}, f32[16,32,128]{2,1,0:T(8,128)S(1)}, f32[16,32,128]{2,1,0:T(8,128)S(1)}, f32[8,1...) custom-call(s32[8]{0:T(128)S(1)} %get-tuple-element.39.refs_0_, ...), custom_call_target="tpu_custom_call" | custom-call | tf_op jit(solution)/shard_map/step_1/pallas_call | solution.py:724
  49.0 6.7 %all-to-all-start.2 = ((f32[32,8,128]{2,1,0:T(8,128)}), f32[32,8,128]{2,1,0:T(8,128)S(1)}, u32[]{:S(2)}, u32[]{:S(2)}) async-start(f32[32,8,128]{2,1,0:T(8,128)} %bitcast.12), calls=%async_computation.2 | async-start | bytes 262144 | tf_op jit(solution)/shard_map/all_to_all | solution.py:741
  55.7 3.7 %collective-permute-start.5 = (f32[64,128]{1,0:T(8,128)S(1)}, f32[64,128]{1,0:T(8,128)S(1)}, u32[]{:S(2)}, u32[]{:S(2)}) collective-permute-start(f32[64,128]{1,0:T(8,128)S(1)} %get-tuple-element.54), channel_id=1, source_target_pairs={{0,1},{1,2},{2,3},{3,4},{4,5},{5,6},{6,7},{8,9},{9,10},{10,11},{11... | collective-permute-start | bytes 98312 | tf_op jit(solution)/shard_map/ppermute | solution.py:748
  59.4 1.3 %collective-permute-start.4 = (f32[64,128]{1,0:T(8,128)S(1)}, f32[64,128]{1,0:T(8,128)S(1)}, u32[]{:S(2)}, u32[]{:S(2)}) collective-permute-start(f32[64,128]{1,0:T(8,128)S(1)} %get-tuple-element.54), channel_id=1, source_target_pairs={{1,0},{2,1},{3,2},{4,3},{5,4},{6,5},{7,6},{9,8},{10,9},{11,10},{12... | collective-permute-start | bytes 98312 | tf_op jit(solution)/shard_map/ppermute | solution.py:748
  60.7 5.4 %all-gather.2 = f32[256,128]{1,0:T(8,128)S(1)} all-gather(f32[64,128]{1,0:T(8,128)S(1)} %get-tuple-element.53), channel_id=4, replica_groups=mesh['brick'=4,'grp'=8] {'brick'}, dimensions={0}, use_global_device_ids=true | all-gather | bytes 163840 | tf_op jit(solution)/shard_map/all_gather | solution.py:782
  66.1 0.0 collective-permute-done.5.refs_3_
  66.1 0.0 collective-permute-done.4.refs_2_
  66.1 0.0 all-to-all-done.2
  66.1 3.0 %step_2.1 = (f32[16,32,128]{2,1,0:T(8,128)S(1)}, f32[16,32,128]{2,1,0:T(8,128)S(1)}, f32[16,32,128]{2,1,0:T(8,128)S(1)}, f32[16,32,128]{2,1,0:T(8,128)S(1)}, f32...) custom-call(s32[8]{0:T(128)S(1)} %get-tuple-element.39.refs_0_, ...), custom_call_target="tpu_custom_call", output_to_operand_aliasing={{8}: (15, {}), {9}: (16, {})} | custom-call | tf_op jit(solution)/shard_map/step_2/pallas_call | solution.py:724
  69.1 13.6 %all_to_all.38.tiles_ref = f32[32,1,128]{2,1,0:T(1,128)S(1)} all-to-all(f32[32,1,128]{2,1,0:T(1,128)S(1)} %get-tuple-element.64), channel_id=1, replica_groups=mesh['brick'=4,'grp'=8] {'brick','grp'}, dimensions={0} | all-to-all | bytes 32768 | tf_op jit(solution)/shard_map/all_to_all | solution.py:741
  82.7 1.3 %finish.1 = (f32[2,32,1024]{2,1,0:T(8,128)}, f32[2,32,1024]{2,1,0:T(8,128)}) custom-call(f32[32,1,128]{2,1,0:T(1,128)S(1)} %all_to_all.38.tiles_ref, f32[8,128]{1,0:T(8,128)S(1)} %get-tuple-element.65.scalars_ref, f32[16,32,128]{2,1,0:T(8,128)S(1)} %get-tuple-element.66.residual_ref, ...), custom_call_target="tpu_custom_call", output_to_operand_aliasing={{0}: (8, {}), {1}: (9, {})} | custom-call | tf_op jit(solution)/shard_map/finish/pallas_call | solution.py:724
  (1 shorter events, 0.0 us)
Async XLA Ops:
  0.6 1.4 %copy-start = (f32[1,1,6,2,32,1024]{5,4,3,2,1,0:T(8,128)S(1)}, f32[1,1,6,2,32,1024]{5,4,3,2,1,0:T(8,128)}, u32[]{:S(2)}) copy-start(f32[1,1,6,2,32,1024]{5,4,3,2,1,0:T(8,128)} %param.7) | copy-start | bytes 4718596
  2.0 0.9 %copy-start.1 = (f32[1,1,2,32,1024]{4,3,2,1,0:T(8,128)S(1)}, f32[1,1,2,32,1024]{4,3,2,1,0:T(8,128)}, u32[]{:S(2)}) copy-start(f32[1,1,2,32,1024]{4,3,2,1,0:T(8,128)} %param.5) | copy-start | bytes 786436
  3.0 0.9 %copy-start.2 = (f32[1,1,2,32,1024]{4,3,2,1,0:T(8,128)S(1)}, f32[1,1,2,32,1024]{4,3,2,1,0:T(8,128)}, u32[]{:S(2)}) copy-start(f32[1,1,2,32,1024]{4,3,2,1,0:T(8,128)} %param.6) | copy-start | bytes 786436
  3.9 0.7 copy-start.3
  4.6 0.7 copy-start.4
  7.6 18.0 %all-to-all-start = ((f32[32,8,128]{2,1,0:T(8,128)}), f32[32,8,128]{2,1,0:T(8,128)S(1)}, u32[]{:S(2)}, u32[]{:S(2)}) async-start(f32[32,8,128]{2,1,0:T(8,128)} %bitcast.6), calls=%async_computation | async-start | bytes 262144 | tf_op jit(solution)/shard_map/all_to_all | solution.py:741
  14.9 10.7 %collective-permute-start.1 = (f32[136,128]{1,0:T(8,128)S(1)}, f32[136,128]{1,0:T(8,128)S(1)}, u32[]{:S(2)}, u32[]{:S(2)}) collective-permute-start(f32[136,128]{1,0:T(8,128)S(1)} %get-tuple-element.41), channel_id=1, source_target_pairs={{0,1},{1,2},{2,3},{3,4},{4,5},{5,6},{6,7},{8,9},{9,10},{10,11},{11... | collective-permute-start | bytes 208904 | tf_op jit(solution)/shard_map/ppermute | solution.py:748
  18.6 7.0 %collective-permute-start = (f32[136,128]{1,0:T(8,128)S(1)}, f32[136,128]{1,0:T(8,128)S(1)}, u32[]{:S(2)}, u32[]{:S(2)}) collective-permute-start(f32[136,128]{1,0:T(8,128)S(1)} %get-tuple-element.41), channel_id=1, source_target_pairs={{1,0},{2,1},{3,2},{4,3},{5,4},{6,5},{7,6},{9,8},{10,9},{11,10},{12... | collective-permute-start | bytes 208904 | tf_op jit(solution)/shard_map/ppermute | solution.py:748
  28.7 17.1 %all-to-all-start.1 = ((f32[32,8,128]{2,1,0:T(8,128)}), f32[32,8,128]{2,1,0:T(8,128)S(1)}, u32[]{:S(2)}, u32[]{:S(2)}) async-start(f32[32,8,128]{2,1,0:T(8,128)} %bitcast.9), calls=%async_computation.1 | async-start | bytes 262144 | tf_op jit(solution)/shard_map/all_to_all | solution.py:741
  35.4 10.4 %collective-permute-start.3 = (f32[64,128]{1,0:T(8,128)S(1)}, f32[64,128]{1,0:T(8,128)S(1)}, u32[]{:S(2)}, u32[]{:S(2)}) collective-permute-start(f32[64,128]{1,0:T(8,128)S(1)} %get-tuple-element.48), channel_id=1, source_target_pairs={{0,1},{1,2},{2,3},{3,4},{4,5},{5,6},{6,7},{8,9},{9,10},{10,11},{11... | collective-permute-start | bytes 98312 | tf_op jit(solution)/shard_map/ppermute | solution.py:748
  39.1 6.7 %collective-permute-start.2 = (f32[64,128]{1,0:T(8,128)S(1)}, f32[64,128]{1,0:T(8,128)S(1)}, u32[]{:S(2)}, u32[]{:S(2)}) collective-permute-start(f32[64,128]{1,0:T(8,128)S(1)} %get-tuple-element.48), channel_id=1, source_target_pairs={{1,0},{2,1},{3,2},{4,3},{5,4},{6,5},{7,6},{9,8},{10,9},{11,10},{12... | collective-permute-start | bytes 98312 | tf_op jit(solution)/shard_map/ppermute | solution.py:748
  49.0 17.1 %all-to-all-start.2 = ((f32[32,8,128]{2,1,0:T(8,128)}), f32[32,8,128]{2,1,0:T(8,128)S(1)}, u32[]{:S(2)}, u32[]{:S(2)}) async-start(f32[32,8,128]{2,1,0:T(8,128)} %bitcast.12), calls=%async_computation.2 | async-start | bytes 262144 | tf_op jit(solution)/shard_map/all_to_all | solution.py:741
  55.7 10.4 %collective-permute-start.5 = (f32[64,128]{1,0:T(8,128)S(1)}, f32[64,128]{1,0:T(8,128)S(1)}, u32[]{:S(2)}, u32[]{:S(2)}) collective-permute-start(f32[64,128]{1,0:T(8,128)S(1)} %get-tuple-element.54), channel_id=1, source_target_pairs={{0,1},{1,2},{2,3},{3,4},{4,5},{5,6},{6,7},{8,9},{9,10},{10,11},{11... | collective-permute-start | bytes 98312 | tf_op jit(solution)/shard_map/ppermute | solution.py:748
  59.4 6.7 %collective-permute-start.4 = (f32[64,128]{1,0:T(8,128)S(1)}, f32[64,128]{1,0:T(8,128)S(1)}, u32[]{:S(2)}, u32[]{:S(2)}) collective-permute-start(f32[64,128]{1,0:T(8,128)S(1)} %get-tuple-element.54), channel_id=1, source_target_pairs={{1,0},{2,1},{3,2},{4,3},{5,4},{6,5},{7,6},{9,8},{10,9},{11,10},{12... | collective-permute-start | bytes 98312 | tf_op jit(solution)/shard_map/ppermute | solution.py:748

commit v12 on v9

--- a/solution.py
+++ b/solution.py
@@ -670,7 +670,7 @@
 
 def finish_kernel(
     tiles_ref, scalars_ref, residual_ref, mapped_ref, search_ref, third_ref, first_hbm, second_hbm,
-    solution_hbm, residual_hbm, first_ref, second_ref, arrived,
+    solution_hbm, residual_hbm, first_ref, second_ref, change_ref, arrived,
 ):
     copies = [
         pltpu.make_async_copy(first_hbm, first_ref, arrived.at[0]),
@@ -688,19 +688,21 @@
     first_step, second_step, second_growth = scalars[2:3, 0:1], scalars[3:4, 0:1], scalars[4:5, 0:1]
     second_weight = second_step + growth * step
     first_weight = first_step + second_growth * second_weight
+    for c in range(CHUNKS):
+        s, part = c // 8, slice(128 * (c % 8), 128 * (c % 8 + 1))
+        change_ref[s, :, part] = residual_ref[c] - step * (mapped_ref[c] + growth * search_ref[c])
     for copy in copies:
         copy.wait()
+    copies = [
+        pltpu.make_async_copy(change_ref, residual_hbm, arrived.at[1]),
+        pltpu.make_async_copy(first_ref, solution_hbm, arrived.at[0]),
+    ]
+    copies[0].start()
     for c in range(CHUNKS):
         s, part = c // 8, slice(128 * (c % 8), 128 * (c % 8 + 1))
         total = first_weight * first_ref[s, :, part] + second_weight * second_ref[s, :, part]
         first_ref[s, :, part] = total + step * third_ref[c]
-        second_ref[s, :, part] = residual_ref[c] - step * (mapped_ref[c] + growth * search_ref[c])
-    copies = [
-        pltpu.make_async_copy(first_ref, solution_hbm, arrived.at[0]),
-        pltpu.make_async_copy(second_ref, residual_hbm, arrived.at[1]),
-    ]
-    for copy in copies:
-        copy.start()
+    copies[1].start()
     for copy in copies:
         copy.wait()
 
@@ -816,7 +818,7 @@
         [tiles, state["scalars"], residual, mapped, state["search"], directions[2]] + directions[:2],
         [
             pltpu.VMEM(brick_pair.shape, F32), pltpu.VMEM(brick_pair.shape, F32),
-            pltpu.SemaphoreType.DMA((2,)),
+            pltpu.VMEM(brick_pair.shape, F32), pltpu.SemaphoreType.DMA((2,)),
         ],
         {6: 0, 7: 1},
     )

time: 84.4 us -> 84.3 us (level)
  no operation moved by 1% of the time
where the time goes in v12:
time: 84.3 us; the launch traced here: 83.7 us
  starting transfers between devices  35.6 us (42%)
  blocking collectives  30.2 us (36%)
  Pallas kernels  12.4 us (15%)
  local copies, waits for them, and re-layouts  4.64 us (6%)
    all_to_all x3, starting transfers between devices, to_all(): return lax.all_to_all(copies, axes, 0, 0, tiled=True)  20.7 us
    all_gather x3, blocking collectives, on_device(): gathered = lax.all_gather(sides, 'brick', axis=0, tiled=False)  16.6 us
    all_to_all x1, blocking collectives, to_all(): return lax.all_to_all(copies, axes, 0, 0, tiled=True)  13.6 us
    pallas_call x5, Pallas kernels, call(): pl.pallas_call(kernel, out_shape=tuple(outs), in_specs=[spec(space) for s...  12.4 us
    ppermute x3, starting transfers between devices, exchange_slabs(): lax.ppermute(message, 'grp', upward)  11 us
    unnamed x10, local copies, waits for them, and re-layouts  4.64 us
    ppermute x3, starting transfers between devices, exchange_slabs(): lax.ppermute(message, 'grp', downward)  3.88 us
  transfers between devices with their start and end apart: 9, of which 0 were waited for; matrix products, arithmetic and copies ran while one was open for 0% of the time, Pallas kernels for 0%

profile of v12, /device:TPU:0, one launch (start us, length us, event | category | flops | bytes accessed | tf_op | source)
XLA Modules:
  0.0 83.7 jit_solution(7414960617128658370)
XLA Ops:
  0.6 0.0 copy-start
  0.6 1.4 %copy-done = f32[1,1,6,2,32,1024]{5,4,3,2,1,0:T(8,128)S(1)} copy-done((f32[1,1,6,2,32,1024]{5,4,3,2,1,0:T(8,128)S(1)}, f32[1,1,6,2,32,1024]{5,4,3,2,1,0:T(8,128)}, u32[]{:S(2)}) %copy-start) | copy-done | bytes 1572888
  2.0 0.0 copy-start.1
  2.0 0.9 %copy-done.1 = f32[1,1,2,32,1024]{4,3,2,1,0:T(8,128)S(1)} copy-done((f32[1,1,2,32,1024]{4,3,2,1,0:T(8,128)S(1)}, f32[1,1,2,32,1024]{4,3,2,1,0:T(8,128)}, u32[]{:S(2)}) %copy-start.1) | copy-done | bytes 262168
  3.0 0.0 copy-start.2
  3.0 0.9 %copy-done.2 = f32[1,1,2,32,1024]{4,3,2,1,0:T(8,128)S(1)} copy-done((f32[1,1,2,32,1024]{4,3,2,1,0:T(8,128)S(1)}, f32[1,1,2,32,1024]{4,3,2,1,0:T(8,128)}, u32[]{:S(2)}) %copy-start.2) | copy-done | bytes 262168
  3.9 0.0 copy-start.3
  3.9 0.7 copy-done.3
  4.6 0.0 copy-start.4
  4.6 0.7 copy-done.4
  5.3 2.3 %setup.1 = (s32[8]{0:T(128)S(1)}, f32[3,16,32,128]{3,2,1,0:T(8,128)S(1)}, f32[128,128]{1,0:T(8,128)S(1)}, f32[16,32,128]{2,1,0:T(8,128)S(1)}, f32[16,32,128]{2,1...) custom-call(s32[1]{0:T(128)} %bitcast.place_ref, s32[4]{0:T(128)S(1)} %copy-done.4, ...), custom_call_target="tpu_custom_call" | custom-call | tf_op jit(solution)/shard_map/setup/pallas_call | solution.py:714
  7.6 7.3 %all-to-all-start = ((f32[32,8,128]{2,1,0:T(8,128)}), f32[32,8,128]{2,1,0:T(8,128)S(1)}, u32[]{:S(2)}, u32[]{:S(2)}) async-start(f32[32,8,128]{2,1,0:T(8,128)} %bitcast.6), calls=%async_computation | async-start | bytes 262144 | tf_op jit(solution)/shard_map/all_to_all | solution.py:731
  14.9 3.7 %collective-permute-start.1 = (f32[136,128]{1,0:T(8,128)S(1)}, f32[136,128]{1,0:T(8,128)S(1)}, u32[]{:S(2)}, u32[]{:S(2)}) collective-permute-start(f32[136,128]{1,0:T(8,128)S(1)} %get-tuple-element.37), channel_id=1, source_target_pairs={{0,1},{1,2},{2,3},{3,4},{4,5},{5,6},{6,7},{8,9},{9,10},{10,11},{11... | collective-permute-start | bytes 208904 | tf_op jit(solution)/shard_map/ppermute | solution.py:738
  18.6 1.3 %collective-permute-start = (f32[136,128]{1,0:T(8,128)S(1)}, f32[136,128]{1,0:T(8,128)S(1)}, u32[]{:S(2)}, u32[]{:S(2)}) collective-permute-start(f32[136,128]{1,0:T(8,128)S(1)} %get-tuple-element.37), channel_id=1, source_target_pairs={{1,0},{2,1},{3,2},{4,3},{5,4},{6,5},{7,6},{9,8},{10,9},{11,10},{12... | collective-permute-start | bytes 208904 | tf_op jit(solution)/shard_map/ppermute | solution.py:738
  19.9 5.7 %all-gather = f32[480,128]{1,0:T(8,128)S(1)} all-gather(f32[120,128]{1,0:T(8,128)S(1)} %get-tuple-element.36), channel_id=2, replica_groups=mesh['brick'=4,'grp'=8] {'brick'}, dimensions={0}, use_global_device_ids=true | all-gather | bytes 307200 | tf_op jit(solution)/shard_map/all_gather | solution.py:772
  25.6 0.0 collective-permute-done.1.refs_3_
  25.6 0.0 collective-permute-done.refs_2_
  25.6 0.0 all-to-all-done
  25.7 3.0 %step_0.1 = (f32[2,32,1024]{2,1,0:T(8,128)}, f32[16,32,128]{2,1,0:T(8,128)S(1)}, f32[184,128]{1,0:T(8,128)S(1)}, f32[232,128]{1,0:T(8,128)S(1)}, f32[256,128]{1,...) custom-call(s32[8]{0:T(128)S(1)} %get-tuple-element.35.refs_0_, f32[4,120,128]{2,1,0:T(8,128)S(1)} %bitcast.17, ...), custom_call_target="tpu_custom_call" | custom-call | tf_op jit(solution)/shard_map/step_0/pallas_call | solution.py:714
  28.7 6.7 %all-to-all-start.1 = ((f32[32,8,128]{2,1,0:T(8,128)}), f32[32,8,128]{2,1,0:T(8,128)S(1)}, u32[]{:S(2)}, u32[]{:S(2)}) async-start(f32[32,8,128]{2,1,0:T(8,128)} %bitcast.9), calls=%async_computation.1 | async-start | bytes 262144 | tf_op jit(solution)/shard_map/all_to_all | solution.py:731
  35.4 3.7 %collective-permute-start.3 = (f32[64,128]{1,0:T(8,128)S(1)}, f32[64,128]{1,0:T(8,128)S(1)}, u32[]{:S(2)}, u32[]{:S(2)}) collective-permute-start(f32[64,128]{1,0:T(8,128)S(1)} %get-tuple-element.44), channel_id=1, source_target_pairs={{0,1},{1,2},{2,3},{3,4},{4,5},{5,6},{6,7},{8,9},{9,10},{10,11},{11... | collective-permute-start | bytes 98312 | tf_op jit(solution)/shard_map/ppermute | solution.py:738
  39.1 1.3 %collective-permute-start.2 = (f32[64,128]{1,0:T(8,128)S(1)}, f32[64,128]{1,0:T(8,128)S(1)}, u32[]{:S(2)}, u32[]{:S(2)}) collective-permute-start(f32[64,128]{1,0:T(8,128)S(1)} %get-tuple-element.44), channel_id=1, source_target_pairs={{1,0},{2,1},{3,2},{4,3},{5,4},{6,5},{7,6},{9,8},{10,9},{11,10},{12... | collective-permute-start | bytes 98312 | tf_op jit(solution)/shard_map/ppermute | solution.py:738
  40.4 5.4 %all-gather.1 = f32[256,128]{1,0:T(8,128)S(1)} all-gather(f32[64,128]{1,0:T(8,128)S(1)} %get-tuple-element.43), channel_id=3, replica_groups=mesh['brick'=4,'grp'=8] {'brick'}, dimensions={0}, use_global_device_ids=true | all-gather | bytes 163840 | tf_op jit(solution)/shard_map/all_gather | solution.py:772
  45.8 0.0 collective-permute-done.3.refs_3_
  45.8 0.0 collective-permute-done.2.refs_2_
  45.8 0.0 all-to-all-done.1
  45.8 3.1 %step_1.1 = (f32[2,32,1024]{2,1,0:T(8,128)}, f32[16,32,128]{2,1,0:T(8,128)S(1)}, f32[16,32,128]{2,1,0:T(8,128)S(1)}, f32[16,32,128]{2,1,0:T(8,128)S(1)}, f32[8,1...) custom-call(s32[8]{0:T(128)S(1)} %get-tuple-element.35.refs_0_, ...), custom_call_target="tpu_custom_call" | custom-call | tf_op jit(solution)/shard_map/step_1/pallas_call | solution.py:714
  49.0 6.7 %all-to-all-start.2 = ((f32[32,8,128]{2,1,0:T(8,128)}), f32[32,8,128]{2,1,0:T(8,128)S(1)}, u32[]{:S(2)}, u32[]{:S(2)}) async-start(f32[32,8,128]{2,1,0:T(8,128)} %bitcast.12), calls=%async_computation.2 | async-start | bytes 262144 | tf_op jit(solution)/shard_map/all_to_all | solution.py:731
  55.7 3.7 %collective-permute-start.5 = (f32[64,128]{1,0:T(8,128)S(1)}, f32[64,128]{1,0:T(8,128)S(1)}, u32[]{:S(2)}, u32[]{:S(2)}) collective-permute-start(f32[64,128]{1,0:T(8,128)S(1)} %get-tuple-element.50), channel_id=1, source_target_pairs={{0,1},{1,2},{2,3},{3,4},{4,5},{5,6},{6,7},{8,9},{9,10},{10,11},{11... | collective-permute-start | bytes 98312 | tf_op jit(solution)/shard_map/ppermute | solution.py:738
  59.4 1.3 %collective-permute-start.4 = (f32[64,128]{1,0:T(8,128)S(1)}, f32[64,128]{1,0:T(8,128)S(1)}, u32[]{:S(2)}, u32[]{:S(2)}) collective-permute-start(f32[64,128]{1,0:T(8,128)S(1)} %get-tuple-element.50), channel_id=1, source_target_pairs={{1,0},{2,1},{3,2},{4,3},{5,4},{6,5},{7,6},{9,8},{10,9},{11,10},{12... | collective-permute-start | bytes 98312 | tf_op jit(solution)/shard_map/ppermute | solution.py:738
  60.7 5.4 %all-gather.2 = f32[256,128]{1,0:T(8,128)S(1)} all-gather(f32[64,128]{1,0:T(8,128)S(1)} %get-tuple-element.49), channel_id=4, replica_groups=mesh['brick'=4,'grp'=8] {'brick'}, dimensions={0}, use_global_device_ids=true | all-gather | bytes 163840 | tf_op jit(solution)/shard_map/all_gather | solution.py:772
  66.1 0.0 collective-permute-done.5.refs_3_
  66.1 0.0 collective-permute-done.4.refs_2_
  66.1 0.0 all-to-all-done.2
  66.1 2.1 %step_2.1 = (f32[16,32,128]{2,1,0:T(8,128)S(1)}, f32[16,32,128]{2,1,0:T(8,128)S(1)}, f32[16,32,128]{2,1,0:T(8,128)S(1)}, f32[16,32,128]{2,1,0:T(8,128)S(1)}, f32...) custom-call(s32[8]{0:T(128)S(1)} %get-tuple-element.35.refs_0_, f32[4,64,128]{2,1,0:T(8,128)S(1)} %bitcast.18, ...), custom_call_target="tpu_custom_call" | custom-call | tf_op jit(solution)/shard_map/step_2/pallas_call | solution.py:714
  68.2 13.6 %all_to_all.38.tiles_ref = f32[32,1,128]{2,1,0:T(1,128)S(1)} all-to-all(f32[32,1,128]{2,1,0:T(1,128)S(1)} %get-tuple-element.58), channel_id=1, replica_groups=mesh['brick'=4,'grp'=8] {'brick','grp'}, dimensions={0} | all-to-all | bytes 32768 | tf_op jit(solution)/shard_map/all_to_all | solution.py:731
  81.8 1.9 %finish.1 = (f32[2,32,1024]{2,1,0:T(8,128)}, f32[2,32,1024]{2,1,0:T(8,128)}) custom-call(f32[32,1,128]{2,1,0:T(1,128)S(1)} %all_to_all.38.tiles_ref, f32[8,128]{1,0:T(8,128)S(1)} %get-tuple-element.59.scalars_ref, f32[16,32,128]{2,1,0:T(8,128)S(1)} %get-tuple-element.60.residual_ref, ...), custom_call_target="tpu_custom_call", output_to_operand_aliasing={{0}: (6, {}), {1}: (7, {})} | custom-call | tf_op jit(solution)/shard_map/finish/pallas_call | solution.py:714
  (1 shorter events, 0.0 us)
Async XLA Ops:
  0.6 1.4 %copy-start = (f32[1,1,6,2,32,1024]{5,4,3,2,1,0:T(8,128)S(1)}, f32[1,1,6,2,32,1024]{5,4,3,2,1,0:T(8,128)}, u32[]{:S(2)}) copy-start(f32[1,1,6,2,32,1024]{5,4,3,2,1,0:T(8,128)} %param.7) | copy-start | bytes 4718596
  2.0 0.9 %copy-start.1 = (f32[1,1,2,32,1024]{4,3,2,1,0:T(8,128)S(1)}, f32[1,1,2,32,1024]{4,3,2,1,0:T(8,128)}, u32[]{:S(2)}) copy-start(f32[1,1,2,32,1024]{4,3,2,1,0:T(8,128)} %param.5) | copy-start | bytes 786436
  3.0 0.9 %copy-start.2 = (f32[1,1,2,32,1024]{4,3,2,1,0:T(8,128)S(1)}, f32[1,1,2,32,1024]{4,3,2,1,0:T(8,128)}, u32[]{:S(2)}) copy-start(f32[1,1,2,32,1024]{4,3,2,1,0:T(8,128)} %param.6) | copy-start | bytes 786436
  3.9 0.7 copy-start.3
  4.6 0.7 copy-start.4
  7.6 18.0 %all-to-all-start = ((f32[32,8,128]{2,1,0:T(8,128)}), f32[32,8,128]{2,1,0:T(8,128)S(1)}, u32[]{:S(2)}, u32[]{:S(2)}) async-start(f32[32,8,128]{2,1,0:T(8,128)} %bitcast.6), calls=%async_computation | async-start | bytes 262144 | tf_op jit(solution)/shard_map/all_to_all | solution.py:731
  14.9 10.7 %collective-permute-start.1 = (f32[136,128]{1,0:T(8,128)S(1)}, f32[136,128]{1,0:T(8,128)S(1)}, u32[]{:S(2)}, u32[]{:S(2)}) collective-permute-start(f32[136,128]{1,0:T(8,128)S(1)} %get-tuple-element.37), channel_id=1, source_target_pairs={{0,1},{1,2},{2,3},{3,4},{4,5},{5,6},{6,7},{8,9},{9,10},{10,11},{11... | collective-permute-start | bytes 208904 | tf_op jit(solution)/shard_map/ppermute | solution.py:738
  18.6 7.0 %collective-permute-start = (f32[136,128]{1,0:T(8,128)S(1)}, f32[136,128]{1,0:T(8,128)S(1)}, u32[]{:S(2)}, u32[]{:S(2)}) collective-permute-start(f32[136,128]{1,0:T(8,128)S(1)} %get-tuple-element.37), channel_id=1, source_target_pairs={{1,0},{2,1},{3,2},{4,3},{5,4},{6,5},{7,6},{9,8},{10,9},{11,10},{12... | collective-permute-start | bytes 208904 | tf_op jit(solution)/shard_map/ppermute | solution.py:738
  28.7 17.1 %all-to-all-start.1 = ((f32[32,8,128]{2,1,0:T(8,128)}), f32[32,8,128]{2,1,0:T(8,128)S(1)}, u32[]{:S(2)}, u32[]{:S(2)}) async-start(f32[32,8,128]{2,1,0:T(8,128)} %bitcast.9), calls=%async_computation.1 | async-start | bytes 262144 | tf_op jit(solution)/shard_map/all_to_all | solution.py:731
  35.4 10.4 %collective-permute-start.3 = (f32[64,128]{1,0:T(8,128)S(1)}, f32[64,128]{1,0:T(8,128)S(1)}, u32[]{:S(2)}, u32[]{:S(2)}) collective-permute-start(f32[64,128]{1,0:T(8,128)S(1)} %get-tuple-element.44), channel_id=1, source_target_pairs={{0,1},{1,2},{2,3},{3,4},{4,5},{5,6},{6,7},{8,9},{9,10},{10,11},{11... | collective-permute-start | bytes 98312 | tf_op jit(solution)/shard_map/ppermute | solution.py:738
  39.1 6.7 %collective-permute-start.2 = (f32[64,128]{1,0:T(8,128)S(1)}, f32[64,128]{1,0:T(8,128)S(1)}, u32[]{:S(2)}, u32[]{:S(2)}) collective-permute-start(f32[64,128]{1,0:T(8,128)S(1)} %get-tuple-element.44), channel_id=1, source_target_pairs={{1,0},{2,1},{3,2},{4,3},{5,4},{6,5},{7,6},{9,8},{10,9},{11,10},{12... | collective-permute-start | bytes 98312 | tf_op jit(solution)/shard_map/ppermute | solution.py:738
  49.0 17.1 %all-to-all-start.2 = ((f32[32,8,128]{2,1,0:T(8,128)}), f32[32,8,128]{2,1,0:T(8,128)S(1)}, u32[]{:S(2)}, u32[]{:S(2)}) async-start(f32[32,8,128]{2,1,0:T(8,128)} %bitcast.12), calls=%async_computation.2 | async-start | bytes 262144 | tf_op jit(solution)/shard_map/all_to_all | solution.py:731
  55.7 10.4 %collective-permute-start.5 = (f32[64,128]{1,0:T(8,128)S(1)}, f32[64,128]{1,0:T(8,128)S(1)}, u32[]{:S(2)}, u32[]{:S(2)}) collective-permute-start(f32[64,128]{1,0:T(8,128)S(1)} %get-tuple-element.50), channel_id=1, source_target_pairs={{0,1},{1,2},{2,3},{3,4},{4,5},{5,6},{6,7},{8,9},{9,10},{10,11},{11... | collective-permute-start | bytes 98312 | tf_op jit(solution)/shard_map/ppermute | solution.py:738
  59.4 6.7 %collective-permute-start.4 = (f32[64,128]{1,0:T(8,128)S(1)}, f32[64,128]{1,0:T(8,128)S(1)}, u32[]{:S(2)}, u32[]{:S(2)}) collective-permute-start(f32[64,128]{1,0:T(8,128)S(1)} %get-tuple-element.50), channel_id=1, source_target_pairs={{1,0},{2,1},{3,2},{4,3},{5,4},{6,5},{7,6},{9,8},{10,9},{11,10},{12... | collective-permute-start | bytes 98312 | tf_op jit(solution)/shard_map/ppermute | solution.py:738
